TPU v7x, 256 devices: a whole 4x4x8 slice. The times are simulated.
256 devices in a mesh: blk: 32 (over y, x, core), mpo: 8 (over z).
Axes of the slice: x: 4, y: 4, z: 8, core: 2. Of those that a mesh axis runs over, the one named last changes fastest.
Arguments:
- wavefunction: bfloat16 [8192, 8192], P('blk'), may hold values from -6 to 6
- left_env: bfloat16 [16, 8192, 256], P('mpo', 'blk'), may hold values from -0.375 to 0.375
- right_env: bfloat16 [16, 8192, 256], P('mpo', 'blk'), may hold values from -0.09375 to 0.09375
- left_sizes: int32 [32], replicated, may hold values from 64 to 256, as said below
- right_sizes: int32 [32], replicated, may hold values from 64 to 256, as said below
Outputs:
- applied: bfloat16 [32, 256, 8192], P(None, 'mpo', 'blk')
Inputs may be any that keep to these rules, and one draw needn't show every extreme that they name: `left_sizes`: one sector has exactly 256 and one exactly 64. `right_sizes`: one sector has exactly 256 and one exactly 64.
All inputs are finite; a program needn't handle non-finite values.
Results may differ from a plain program's by a relative error of at most 0.0049.
Values may be sent and summed in bfloat16 or wider, within the bound.
No kernel may reach another device: no remote copies, remote signals or barrier semaphores. Data moves between devices by JAX's collectives and lax.ppermute only.
A program may use at most 192 MiB of HBM per device.

v0:
```python
import jax
import jax.numpy as jnp
from jax import lax
from jax.sharding import PartitionSpec as P


def local(wavefunction, left_env, right_env, left_sizes, right_sizes):
    sector = lax.axis_index("blk")
    indices = left_env.shape[0]
    left_dim = wavefunction.shape[0]
    columns_all = wavefunction.shape[1]
    right_dim = right_env.shape[2]
    sectors = columns_all // right_dim
    sector_ids = jnp.arange(sectors, dtype=jnp.int32)
    own_left = jnp.sum(jnp.where(sector_ids == sector, left_sizes, 0))
    own_right = jnp.sum(jnp.where(sector_ids == sector, right_sizes, 0))
    row_own = jnp.arange(left_dim, dtype=jnp.int32) < own_left
    col_every = (jnp.arange(right_dim, dtype=jnp.int32)[None, :] < right_sizes[:, None]).reshape(
        columns_all
    )
    masked = jnp.where(
        row_own[:, None] & col_every[None, :], wavefunction, jnp.zeros_like(wavefunction)
    )
    products = jnp.stack(
        [
            jnp.dot(left_env[mpo_index], masked, preferred_element_type=jnp.float32).astype(
                jnp.bfloat16
            )
            for mpo_index in range(indices)
        ]
    )
    relayed = lax.all_to_all(products, "blk", split_axis=2, concat_axis=1, tiled=True)
    summed_terms = jnp.einsum("wir,wrc->ic", relayed, right_env, preferred_element_type=jnp.float32)
    row_every = (jnp.arange(left_dim, dtype=jnp.int32)[None, :] < left_sizes[:, None]).reshape(
        sectors * left_dim
    )
    col_own = jnp.arange(right_dim, dtype=jnp.int32) < own_right
    summed_terms = jnp.where(row_every[:, None] & col_own[None, :], summed_terms, 0.0)
    summed_terms = summed_terms.reshape(sectors, left_dim, right_dim)
    shared = lax.psum_scatter(summed_terms, "mpo", scatter_dimension=1, tiled=True)
    return shared.astype(jnp.bfloat16)


def solution(mesh):
    placed = (P("blk", None), P("mpo", "blk", None), P("mpo", "blk", None), P(), P())
    return jax.shard_map(
        local, mesh=mesh, in_specs=placed, out_specs=P(None, "mpo", "blk"), check_vma=False
    )
```

profile of v0, /device:TPU:1, one launch (start us, length us, event | category | flops | bytes accessed | tf_op | source)
XLA Modules:
  0.0 284.6 jit_solution(2879343556874369647)
XLA Ops:
  6.5 0.0 copy-start
  6.5 1.3 fusion.8
  7.9 0.6 iota_compare_fusion.2
  8.5 0.7 iota_compare_fusion
  9.3 0.0 copy-start.3
  9.3 0.0 copy-start.4
  9.3 4.3 %fusion = bf16[1,256,8192]{1,2,0:T(8,128)(2,1)S(1)} fusion(bf16[256,8192]{1,0:T(8,128)(2,1)} %param.5, pred[8192]{0:T(1024)(128)(4,1)S(1)} %lt.71, pred[256]{0:T(512)(128)(4,1)S(1)} %iota_compare_fusion.2, bf16[2,256,256]{2,1,0:T(8,128)(2,1)} %param.6), kind=kOutput, calls=%fused_computation.3 | convolution fusion | flops 1080033280 | bytes 8528128 | tf_op jit(solution)/shard_map/dot_general | solution.py:26
  13.6 0.0 copy-done.3
  13.6 0.0 copy-done.4
  13.6 4.1 %fusion.1 = bf16[1,256,8192]{1,2,0:T(8,128)(2,1)} fusion(bf16[256,8192]{1,0:T(8,128)(2,1)S(1)} %copy-done.3, pred[8192]{0:T(1024)(128)(4,1)S(1)} %lt.71, pred[256]{0:T(512)(128)(4,1)S(1)} %iota_compare_fusion.2, bf16[2,256,256]{2,1,0:T(8,128)(2,1)S(1)} %copy-done.4), kind=kOutput, calls=%fused_computation.4 | convolution fusion | flops 1080033280 | bytes 8528384 | tf_op jit(solution)/shard_map/dot_general | solution.py:26
  17.7 6.2 %pad_maximum_fusion = bf16[2,256,8192]{1,2,0:T(8,128)(2,1)} fusion(bf16[1,256,8192]{1,2,0:T(8,128)(2,1)} %fusion.1, bf16[1,256,8192]{1,2,0:T(8,128)(2,1)S(1)} %fusion), kind=kLoop, calls=%fused_computation.6 | loop fusion | flops 4194304 | bytes 16777216 | tf_op jit(solution)/shard_map/stack | solution.py:24
  23.9 16.4 %copy.7 = bf16[2,256,8192]{1,0,2:T(2,128)(2,1)} copy(bf16[2,256,8192]{1,2,0:T(8,128)(2,1)} %pad_maximum_fusion) | data formatting | bytes 16777216 | tf_op jit(solution)/shard_map/stack | solution.py:24
  40.3 0.0 copy-start.1
  40.3 0.0 copy-start.2
  40.3 8.8 %all-to-all-start = ((bf16[2,256,8192]{1,0,2:T(2,128)(2,1)}), bf16[2,256,8192]{1,0,2:T(2,128)(2,1)}, u32[]{:S(2)}, u32[]{:S(2)}) async-start(bf16[2,256,8192]{1,0,2:T(2,128)(2,1)} %copy.7), calls=%async_computation | async-start | bytes 16777216 | tf_op jit(solution)/shard_map/all_to_all | solution.py:32
  49.1 0.0 reduce-scatter.2.cloned.1.call-start
  49.1 0.0 copy-done.1
  49.2 0.1 iota_compare_fusion.1
  49.2 0.0 copy-done.2
  49.3 0.6 fusion.7
  49.9 0.6 iota_compare_fusion.3
  50.6 98.3 %all-to-all-done = bf16[2,256,8192]{1,0,2:T(2,128)(2,1)} async-done(((bf16[2,256,8192]{1,0,2:T(2,128)(2,1)}), bf16[2,256,8192]{1,0,2:T(2,128)(2,1)}, u32[]{:S(2)}, u32[]{:S(2)}) %all-to-all-start) | async-done | bytes 8388640 | tf_op jit(solution)/shard_map/all_to_all | solution.py:32
  148.8 20.9 %copy.8 = bf16[2,256,32,256]{3,1,2,0:T(8,128)(2,1)} copy(bf16[2,256,32,256]{1,0,3,2:T(2,128)(2,1)} %bitcast.6) | data formatting | bytes 16777216 | tf_op jit(solution)/shard_map/all_to_all | solution.py:32
  169.7 0.0 copy-done
  169.7 6.7 %fusion.2 = f32[8192,256]{1,0:T(8,128)} fusion(bf16[2,8192,256]{2,1,0:T(8,128)(2,1)} %bitcast.26, bf16[2,256,256]{2,1,0:T(8,128)(2,1)S(1)} %copy-done, pred[256]{0:T(512)(128)(4,1)S(1)} %iota_compare_fusion.3, pred[8192]{0:T(1024)(128)(4,1)S(1)} %lt.63), kind=kOutput, calls=%fused_computation.5 | convolution fusion | flops 2151677952 | bytes 17047808 | tf_op jit(solution)/shard_map/wir,wrc->ic/dot_general | solution.py:33
  176.4 0.0 reduce-scatter.2.cloned.1.call-update
  176.4 99.2 %reduce-scatter.2.cloned.1.call-done = f32[32,32,256]{2,1,0:T(8,128)} async-done(((f32[32,256,256]{2,1,0:T(8,128)}), f32[32,32,256]{2,1,0:T(8,128)}) %reduce-scatter.2.cloned.1.call-update) | async-done | bytes 1048592 | tf_op jit(solution)/shard_map/reduce_scatter | solution.py:40
  275.6 2.1 convert_element_type.19
  (2 shorter events, 0.0 us)
Async XLA Ops:
  6.5 163.2 %copy-start = (bf16[2,256,256]{2,1,0:T(8,128)(2,1)S(1)}, bf16[2,256,256]{2,1,0:T(8,128)(2,1)}, u32[]{:S(2)}) copy-start(bf16[2,256,256]{2,1,0:T(8,128)(2,1)} %param.7) | copy-start | bytes 786436
  9.3 4.3 %copy-start.3 = (bf16[256,8192]{1,0:T(8,128)(2,1)S(1)}, bf16[256,8192]{1,0:T(8,128)(2,1)}, u32[]{:S(2)}) copy-start(bf16[256,8192]{1,0:T(8,128)(2,1)} %param.5) | copy-start | bytes 12582916
  9.3 4.3 %copy-start.4 = (bf16[2,256,256]{2,1,0:T(8,128)(2,1)S(1)}, bf16[2,256,256]{2,1,0:T(8,128)(2,1)}, u32[]{:S(2)}) copy-start(bf16[2,256,256]{2,1,0:T(8,128)(2,1)} %param.6) | copy-start | bytes 786436
  40.3 8.9 %copy-start.1 = (s32[32]{0:T(128)S(1)}, s32[32]{0:T(128)}, u32[]{:S(2)}) copy-start(s32[32]{0:T(128)} %param.8) | copy-start | bytes 388
  40.3 9.0 %copy-start.2 = (s32[32]{0:T(128)S(1)}, s32[32]{0:T(128)}, u32[]{:S(2)}) copy-start(s32[32]{0:T(128)} %param.9) | copy-start | bytes 388
  40.3 108.5 %all-to-all-start = ((bf16[2,256,8192]{1,0,2:T(2,128)(2,1)}), bf16[2,256,8192]{1,0,2:T(2,128)(2,1)}, u32[]{:S(2)}, u32[]{:S(2)}) async-start(bf16[2,256,8192]{1,0,2:T(2,128)(2,1)} %copy.7), calls=%async_computation | async-start | bytes 16777216 | tf_op jit(solution)/shard_map/all_to_all | solution.py:32
  49.1 226.5 %reduce-scatter.2.cloned.1.call-start = ((), (), s32[]{:S(2)}) async-start(), calls=%async_computation.2 | async-start | bytes 9437184 | tf_op jit(solution)/shard_map/reduce_scatter | solution.py:40
Sparse Core Ops, SparseCore 0:
  176.6 99.0 reduce-scatter.1
where the time goes:
time: 285 us
  waiting for transfers between devices  197 us (69%)
  local copies, waits for them, and re-layouts  37.3 us (13%)
  matrix products  15.1 us (5%)
  between operations  13.5 us (5%)
  other arithmetic  12.3 us (4%)
  starting transfers between devices  8.84 us (3%)
    reduce_scatter x1, waiting for transfers between devices, local(): lax.psum_scatter(summed_terms, 'mpo', scatter_dimension=1, tiled=True)  99.2 us
    all_to_all x1, waiting for transfers between devices, local(): lax.all_to_all(products, 'blk', split_axis=2, concat_axis=1, tiled=True)  98.3 us
    all_to_all x1, local copies, waits for them, and re-layouts, local(): lax.all_to_all(products, 'blk', split_axis=2, concat_axis=1, tiled=True)  20.9 us
    another operation x1, local copies, waits for them, and re-layouts, local(): jnp.stack([jnp.dot(left_env[mpo_index], masked, preferred_element_type=jn...  16.4 us
    all_to_all x1, starting transfers between devices, local(): lax.all_to_all(products, 'blk', split_axis=2, concat_axis=1, tiled=True)  8.79 us
    dot_general x2, matrix products, local(): jnp.dot(left_env[mpo_index], masked, preferred_element_type=jnp.float32)  8.4 us
    dot_general x1, matrix products, local(): jnp.einsum('wir,wrc->ic', relayed, right_env, preferred_element_type=jnp....  6.69 us
    another operation x1, other arithmetic, local(): jnp.stack([jnp.dot(left_env[mpo_index], masked, preferred_element_type=jn...  6.16 us
  transfers between devices with their start and end apart: 2, of which 2 were waited for; matrix products, arithmetic and copies ran while one was open for 0% of the time, Pallas kernels for 0%

commit v1 on v0

v1 whole, which is shorter than its diff:
```python
import jax
import jax.numpy as jnp
from jax import lax
from jax.sharding import PartitionSpec as P


def ring_gather(block, axis, n):
    up = [(i, (i + 1) % n) for i in range(n)]
    down = [(i, (i + n - 1) % n) for i in range(n)]
    pieces = {0: block}
    from_below = from_above = block
    for hop in range(1, n // 2 + 1):
        from_below = lax.ppermute(from_below, axis, up)
        pieces[-hop] = from_below
        if 2 * hop < n:
            from_above = lax.ppermute(from_above, axis, down)
            pieces[hop] = from_above
    hops = sorted(pieces)
    stacked = jnp.stack([pieces[hop] for hop in hops])
    owners = jnp.arange(n, dtype=jnp.int32)
    places = jnp.remainder(owners - lax.axis_index(axis) - hops[0], n)
    return jnp.take(stacked, places, axis=0)


def local(wavefunction, left_env, right_env, left_sizes, right_sizes):
    sector = lax.axis_index("blk")
    rank = lax.axis_index("mpo")
    ranks = lax.axis_size("mpo")
    own_w, left_dim, _ = left_env.shape
    right_dim = right_env.shape[2]
    sectors = wavefunction.shape[1] // right_dim
    rows = left_dim // ranks
    own_left = left_sizes[sector]
    own_right = right_sizes[sector]

    split = left_env.reshape(own_w, ranks, rows, left_dim).transpose(1, 0, 2, 3)
    mine = lax.all_to_all(split, "mpo", 0, 0)
    lefts = lax.all_gather(mine, "blk")

    row_own = jnp.arange(left_dim, dtype=jnp.int32) < own_left
    masked = jnp.where(row_own[:, None], wavefunction, jnp.zeros_like(wavefunction))
    by_right = masked.reshape(left_dim, sectors, right_dim).transpose(1, 0, 2)
    psi = lax.all_to_all(by_right, "blk", 0, 0)
    col_own = jnp.arange(right_dim, dtype=jnp.int32) < own_right
    psi = jnp.where(col_own, psi, jnp.zeros_like(psi))

    rights = ring_gather(right_env, "mpo", ranks)

    contracted = jnp.einsum(
        "apwij,ajr->apwir", lefts, psi, preferred_element_type=jnp.float32
    ).astype(jnp.bfloat16)
    summed = jnp.einsum(
        "apwir,pwrc->aic", contracted, rights, preferred_element_type=jnp.float32
    )
    row_ids = rank * rows + jnp.arange(rows, dtype=jnp.int32)
    keep = (row_ids[None, :] < left_sizes[:, None])[:, :, None] & col_own
    return jnp.where(keep, summed, 0.0).astype(jnp.bfloat16)


def solution(mesh):
    placed = (P("blk", None), P("mpo", "blk", None), P("mpo", "blk", None), P(), P())
    return jax.shard_map(
        local, mesh=mesh, in_specs=placed, out_specs=P(None, "mpo", "blk"), check_vma=False
    )
```

time: 285 us -> 143 us (0.50)
  waiting for transfers between devices: 197 us -> 54.4 us
  local copies, waits for them, and re-layouts: 37.3 us -> 17.2 us
  blocking collectives: 0 us -> 19.3 us
  starting transfers between devices: 8.84 us -> 19.2 us
  other arithmetic: 12.3 us -> 5.84 us
    reduce_scatter x1 -> x0, waiting for transfers between devices: 99.2 us -> none  [local(): lax.psum_scatter(summed_terms, 'mpo', scatter_dimension=1, tiled=True)]
    all_to_all x1, waiting for transfers between devices: 98.3 us -> 33.9 us  [local(): psi = lax.all_to_all(by_right, 'blk', 0, 0)]
    all_to_all x1 -> x0, local copies, waits for them, and re-layouts: 20.9 us -> none  [local(): lax.all_to_all(products, 'blk', split_axis=2, concat_axis=1, tiled=True)]
    ppermute x0 -> x7, waiting for transfers between devices: none -> 20.5 us  [the longest x4 20.3 us: ring_gather(): from_below = lax.ppermute(from_below, axis, up)]
    all_to_all x0 -> x1, blocking collectives: none -> 19.3 us  [local(): mine = lax.all_to_all(split, 'mpo', 0, 0)]
    another operation x1, local copies, waits for them, and re-layouts: 16.4 us -> 0.02 us  [ring_gather(): stacked = jnp.stack([pieces[hop] for hop in hops])]
    ppermute x0 -> x7, starting transfers between devices: none -> 9.34 us  [the longest x3 9.02 us: ring_gather(): from_above = lax.ppermute(from_above, axis, down)]
    transpose x0 -> x2, local copies, waits for them, and re-layouts: none -> 7.42 us  [the longest x1 6.46 us: local(): by_right = masked.reshape(left_dim, sectors, right_dim).transpose(1, 0, 2)]
  transfers between devices with their start and end apart: 2 -> 9, of which waited for: 2 -> 7; matrix products, arithmetic and copies ran while one was open for 0% -> 15% of each run, Pallas kernels for 0% -> 0%
where the time goes in v1:
time: 143 us; the launch traced here: 142 us
  waiting for transfers between devices  54.4 us (38%)
  blocking collectives  19.3 us (13%)
  starting transfers between devices  19.2 us (13%)
  local copies, waits for them, and re-layouts  17.2 us (12%)
  between operations  13.5 us (9%)
  matrix products  12.9 us (9%)
  other arithmetic  5.84 us (4%)
    all_to_all x1, waiting for transfers between devices, local(): psi = lax.all_to_all(by_right, 'blk', 0, 0)  33.9 us
    ppermute x4, waiting for transfers between devices, ring_gather(): from_below = lax.ppermute(from_below, axis, up)  20.3 us
    all_to_all x1, blocking collectives, local(): mine = lax.all_to_all(split, 'mpo', 0, 0)  19.3 us
    dot_general x1, matrix products, local(): jnp.einsum('apwir,pwrc->aic', contracted, rights, preferred_element_type=...  12.9 us
    all_to_all x1, starting transfers between devices, local(): psi = lax.all_to_all(by_right, 'blk', 0, 0)  9.88 us
    ppermute x3, starting transfers between devices, ring_gather(): from_above = lax.ppermute(from_above, axis, down)  9.02 us
    unnamed x14, local copies, waits for them, and re-layouts  6.53 us
    transpose x1, local copies, waits for them, and re-layouts, local(): by_right = masked.reshape(left_dim, sectors, right_dim).transpose(1, 0, 2)  6.46 us
  transfers between devices with their start and end apart: 9, of which 7 were waited for; matrix products, arithmetic and copies ran while one was open for 15% of the time, Pallas kernels for 0%

profile of v1, /device:TPU:1, one launch (start us, length us, event | category | flops | bytes accessed | tf_op | source)
XLA Modules:
  0.0 142.3 jit_solution(17633174673429035377)
XLA Ops:
  6.5 0.0 all-gather.3.cloned.1.call-start
  6.5 1.0 copy.12
  7.5 19.3 %all_to_all.10 = bf16[8,2,32,256]{3,2,1,0:T(8,128)(2,1)} all-to-all(bf16[8,2,32,256]{3,2,1,0:T(8,128)(2,1)S(1)} %copy.12), channel_id=1, replica_groups=mesh['blk'=32,'mpo'=8] {'mpo'}, dimensions={0} | all-to-all | bytes 524288 | tf_op jit(solution)/shard_map/all_to_all | solution.py:37
  26.8 0.0 all-gather.3.cloned.1.call-update
  26.8 0.0 copy-start.1
  26.8 6.4 %copy.10 = bf16[256,8192]{0,1:T(8,128)(2,1)} copy(bf16[256,8192]{1,0:T(8,128)(2,1)} %param.5) | data formatting | bytes 8388608 | tf_op args[0]
  33.2 0.0 copy-done.1
  33.2 0.6 dynamic_slice.7
  33.8 0.6 iota_compare_fusion
  34.5 4.4 %broadcast_select_fusion = bf16[256,8192]{0,1:T(8,128)(2,1)} fusion(bf16[256,8192]{0,1:T(8,128)(2,1)} %copy.10, pred[256]{0:T(512)(128)(4,1)S(1)} %iota_compare_fusion), kind=kLoop, calls=%fused_computation.7 | loop fusion | flops 2097152 | bytes 8388864 | tf_op jit(solution)/shard_map/jit(_where)/select_n | solution.py:41
  38.9 6.5 %copy.11 = bf16[32,256,256]{2,1,0:T(8,128)(2,1)} copy(bf16[32,256,256]{1,2,0:T(8,128)(2,1)} %bitcast.72) | data formatting | bytes 8388608 | tf_op jit(solution)/shard_map/transpose | solution.py:42
  45.3 0.0 copy-start
  45.3 0.0 copy-start.2
  45.4 9.9 %all-to-all-start = ((bf16[32,256,256]{2,1,0:T(8,128)(2,1)}), bf16[32,256,256]{2,1,0:T(8,128)(2,1)}, u32[]{:S(2)}, u32[]{:S(2)}) async-start(bf16[32,256,256]{2,1,0:T(8,128)(2,1)} %copy.11), calls=%async_computation | async-start | bytes 8388608 | tf_op jit(solution)/shard_map/all_to_all | solution.py:43
  55.2 0.0 copy-done
  55.2 0.3 collective-permute-start
  55.6 8.7 %collective-permute-done = bf16[2,256,256]{2,1,0:T(8,128)(2,1)S(1)} collective-permute-done((bf16[2,256,256]{2,1,0:T(8,128)(2,1)S(1)}, bf16[2,256,256]{2,1,0:T(8,128)(2,1)S(1)}, u32[]{:S(2)}, u32[]{:S(2)}) %collective-permute-start) | collective-permute-done | bytes 262176 | tf_op jit(solution)/shard_map/ppermute | solution.py:13
  64.2 0.0 collective-permute-start.1
  64.2 2.7 %collective-permute-start.4 = (bf16[2,256,256]{2,1,0:T(8,128)(2,1)S(1)}, bf16[2,256,256]{2,1,0:T(8,128)(2,1)S(1)}, u32[]{:S(2)}, u32[]{:S(2)}) collective-permute-start(bf16[2,256,256]{2,1,0:T(8,128)(2,1)S(1)} %copy-done), channel_id=1, source_target_pairs={{0,7},{1,0},{2,1},{3,2},{4,3},{5,4},{6,5},{7,6},{8,15},{9,8},{10,9... | collective-permute-start | bytes 786440 | tf_op jit(solution)/shard_map/ppermute | solution.py:16
  66.9 5.4 %collective-permute-done.1 = bf16[2,256,256]{2,1,0:T(8,128)(2,1)S(1)} collective-permute-done((bf16[2,256,256]{2,1,0:T(8,128)(2,1)S(1)}, bf16[2,256,256]{2,1,0:T(8,128)(2,1)S(1)}, u32[]{:S(2)}, u32[]{:S(2)}) %collective-permute-start.1) | collective-permute-done | bytes 262176 | tf_op jit(solution)/shard_map/ppermute | solution.py:13
  72.3 0.0 collective-permute-start.2
  72.3 0.0 copy-done.2
  72.3 0.6 dynamic_slice.6
  72.9 0.6 iota_compare_fusion.1
  73.6 0.0 collective-permute-done.4
  73.6 2.7 %collective-permute-start.5 = (bf16[2,256,256]{2,1,0:T(8,128)(2,1)S(1)}, bf16[2,256,256]{2,1,0:T(8,128)(2,1)S(1)}, u32[]{:S(2)}, u32[]{:S(2)}) collective-permute-start(bf16[2,256,256]{2,1,0:T(8,128)(2,1)S(1)} %collective-permute-done.4), channel_id=1, source_target_pairs={{0,7},{1,0},{2,1},{3,2},{4,3},{5,4},{6,5},{7,6},{8,15},{9,8},{10,9... | collective-permute-start | bytes 786440 | tf_op jit(solution)/shard_map/ppermute | solution.py:16
  76.4 3.2 %collective-permute-done.2 = bf16[2,256,256]{2,1,0:T(8,128)(2,1)S(1)} collective-permute-done((bf16[2,256,256]{2,1,0:T(8,128)(2,1)S(1)}, bf16[2,256,256]{2,1,0:T(8,128)(2,1)S(1)}, u32[]{:S(2)}, u32[]{:S(2)}) %collective-permute-start.2) | collective-permute-done | bytes 262176 | tf_op jit(solution)/shard_map/ppermute | solution.py:13
  79.6 0.0 collective-permute-start.3
  79.6 0.1 broadcast_compare_fusion
  79.7 0.1 collective-permute-done.5
  79.7 3.6 %collective-permute-start.6 = (bf16[2,256,256]{2,1,0:T(8,128)(2,1)S(1)}, bf16[2,256,256]{2,1,0:T(8,128)(2,1)S(1)}, u32[]{:S(2)}, u32[]{:S(2)}) collective-permute-start(bf16[2,256,256]{2,1,0:T(8,128)(2,1)S(1)} %collective-permute-done.5), channel_id=1, source_target_pairs={{0,7},{1,0},{2,1},{3,2},{4,3},{5,4},{6,5},{7,6},{8,15},{9,8},{10,9... | collective-permute-start | bytes 786440 | tf_op jit(solution)/shard_map/ppermute | solution.py:16
  83.3 3.1 %collective-permute-done.3 = bf16[2,256,256]{2,1,0:T(8,128)(2,1)S(1)} collective-permute-done((bf16[2,256,256]{2,1,0:T(8,128)(2,1)S(1)}, bf16[2,256,256]{2,1,0:T(8,128)(2,1)S(1)}, u32[]{:S(2)}, u32[]{:S(2)}) %collective-permute-start.3) | collective-permute-done | bytes 262176 | tf_op jit(solution)/shard_map/ppermute | solution.py:13
  86.6 0.1 collective-permute-done.6
  86.7 2.0 %gather_fusion = bf16[8,2,256,256]{3,2,1,0:T(8,128)(2,1)} fusion(bf16[8,2,256,256]{3,2,1,0:T(8,128)(2,1)S(1)} %bitcast_dynamic-update-slice_fusion, s32[1024]{0:T(1024)S(1)} %pad_clamp_fusion), kind=kCustom, calls=%fused_computation | custom fusion | bytes 4194336 | tf_op jit(solution)/shard_map/jit(_take)/gather | solution.py:22
  88.7 33.9 %all-to-all-done = bf16[32,256,256]{2,1,0:T(8,128)(2,1)} async-done(((bf16[32,256,256]{2,1,0:T(8,128)(2,1)}), bf16[32,256,256]{2,1,0:T(8,128)(2,1)}, u32[]{:S(2)}, u32[]{:S(2)}) %all-to-all-start) | async-done | bytes 4194336 | tf_op jit(solution)/shard_map/all_to_all | solution.py:43
  122.6 0.0 all-gather.3.cloned.1.call-done
  122.6 12.9 %fusion.30 = bf16[32,32,256]{2,1,0:T(8,128)(2,1)} fusion(bf16[8,2,256,256]{3,2,1,0:T(8,128)(2,1)} %gather_fusion, pred[8]{0:T(512)(128)(4,1)S(1)} %compare_and_fusion, bf16[32,8,2,32,256]{4,3,2,1,0:T(8,128)(2,1)} %bitcast.74, bf16[32,256,256]{2,1,0:T(8,128)(2,1)} %all-to-all-done, pred[256]{0:T(512)(128)(4,1)S(1)} %iota_compare_fusion.1, ...), kind=kOutput, calls=%fused_computation.15 | convolution fusion | flops 4303093760 | bytes 15205640 | tf_op jit(solution)/shard_map/apwir,pwrc->aic/dot_general | solution.py:52
  (12 shorter events, 0.2 us)
Async XLA Ops:
  6.5 116.1 %all-gather.3.cloned.1.call-start = ((), (), s32[]{:S(2)}) async-start(), calls=%async_computation.2 | async-start | bytes 8650752 | tf_op jit(solution)/shard_map/all_gather | solution.py:38
  26.8 6.4 %copy-start.1 = (s32[32]{0:T(128)S(1)}, s32[32]{0:T(128)}, u32[]{:S(2)}) copy-start(s32[32]{0:T(128)} %param.8) | copy-start | bytes 388
  45.3 9.9 %copy-start = (bf16[2,256,256]{2,1,0:T(8,128)(2,1)S(1)}, bf16[2,256,256]{2,1,0:T(8,128)(2,1)}, u32[]{:S(2)}) copy-start(bf16[2,256,256]{2,1,0:T(8,128)(2,1)} %param.7) | copy-start | bytes 786436
  45.3 27.0 %copy-start.2 = (s32[32]{0:T(128)S(1)}, s32[32]{0:T(128)}, u32[]{:S(2)}) copy-start(s32[32]{0:T(128)} %param.9) | copy-start | bytes 388
  45.4 77.2 %all-to-all-start = ((bf16[32,256,256]{2,1,0:T(8,128)(2,1)}), bf16[32,256,256]{2,1,0:T(8,128)(2,1)}, u32[]{:S(2)}, u32[]{:S(2)}) async-start(bf16[32,256,256]{2,1,0:T(8,128)(2,1)} %copy.11), calls=%async_computation | async-start | bytes 8388608 | tf_op jit(solution)/shard_map/all_to_all | solution.py:43
  55.2 9.0 %collective-permute-start = (bf16[2,256,256]{2,1,0:T(8,128)(2,1)S(1)}, bf16[2,256,256]{2,1,0:T(8,128)(2,1)S(1)}, u32[]{:S(2)}, u32[]{:S(2)}) collective-permute-start(bf16[2,256,256]{2,1,0:T(8,128)(2,1)S(1)} %copy-done), channel_id=1, source_target_pairs={{0,1},{1,2},{2,3},{3,4},{4,5},{5,6},{6,7},{7,0},{8,9},{9,10},{10,1... | collective-permute-start | bytes 786440 | tf_op jit(solution)/shard_map/ppermute | solution.py:13
  64.2 8.1 %collective-permute-start.1 = (bf16[2,256,256]{2,1,0:T(8,128)(2,1)S(1)}, bf16[2,256,256]{2,1,0:T(8,128)(2,1)S(1)}, u32[]{:S(2)}, u32[]{:S(2)}) collective-permute-start(bf16[2,256,256]{2,1,0:T(8,128)(2,1)S(1)} %collective-permute-done), channel_id=1, source_target_pairs={{0,1},{1,2},{2,3},{3,4},{4,5},{5,6},{6,7},{7,0},{8,9},{9,10},{10,1... | collective-permute-start | bytes 786440 | tf_op jit(solution)/shard_map/ppermute | solution.py:13
  64.2 9.4 %collective-permute-start.4 = (bf16[2,256,256]{2,1,0:T(8,128)(2,1)S(1)}, bf16[2,256,256]{2,1,0:T(8,128)(2,1)S(1)}, u32[]{:S(2)}, u32[]{:S(2)}) collective-permute-start(bf16[2,256,256]{2,1,0:T(8,128)(2,1)S(1)} %copy-done), channel_id=1, source_target_pairs={{0,7},{1,0},{2,1},{3,2},{4,3},{5,4},{6,5},{7,6},{8,15},{9,8},{10,9... | collective-permute-start | bytes 786440 | tf_op jit(solution)/shard_map/ppermute | solution.py:16
  72.3 7.3 %collective-permute-start.2 = (bf16[2,256,256]{2,1,0:T(8,128)(2,1)S(1)}, bf16[2,256,256]{2,1,0:T(8,128)(2,1)S(1)}, u32[]{:S(2)}, u32[]{:S(2)}) collective-permute-start(bf16[2,256,256]{2,1,0:T(8,128)(2,1)S(1)} %collective-permute-done.1), channel_id=1, source_target_pairs={{0,1},{1,2},{2,3},{3,4},{4,5},{5,6},{6,7},{7,0},{8,9},{9,10},{10,1... | collective-permute-start | bytes 786440 | tf_op jit(solution)/shard_map/ppermute | solution.py:13
  73.6 6.1 %collective-permute-start.5 = (bf16[2,256,256]{2,1,0:T(8,128)(2,1)S(1)}, bf16[2,256,256]{2,1,0:T(8,128)(2,1)S(1)}, u32[]{:S(2)}, u32[]{:S(2)}) collective-permute-start(bf16[2,256,256]{2,1,0:T(8,128)(2,1)S(1)} %collective-permute-done.4), channel_id=1, source_target_pairs={{0,7},{1,0},{2,1},{3,2},{4,3},{5,4},{6,5},{7,6},{8,15},{9,8},{10,9... | collective-permute-start | bytes 786440 | tf_op jit(solution)/shard_map/ppermute | solution.py:16
  79.6 6.8 %collective-permute-start.3 = (bf16[2,256,256]{2,1,0:T(8,128)(2,1)S(1)}, bf16[2,256,256]{2,1,0:T(8,128)(2,1)S(1)}, u32[]{:S(2)}, u32[]{:S(2)}) collective-permute-start(bf16[2,256,256]{2,1,0:T(8,128)(2,1)S(1)} %collective-permute-done.2), channel_id=1, source_target_pairs={{0,1},{1,2},{2,3},{3,4},{4,5},{5,6},{6,7},{7,0},{8,9},{9,10},{10,1... | collective-permute-start | bytes 786440 | tf_op jit(solution)/shard_map/ppermute | solution.py:13
  79.7 6.9 %collective-permute-start.6 = (bf16[2,256,256]{2,1,0:T(8,128)(2,1)S(1)}, bf16[2,256,256]{2,1,0:T(8,128)(2,1)S(1)}, u32[]{:S(2)}, u32[]{:S(2)}) collective-permute-start(bf16[2,256,256]{2,1,0:T(8,128)(2,1)S(1)} %collective-permute-done.5), channel_id=1, source_target_pairs={{0,7},{1,0},{2,1},{3,2},{4,3},{5,4},{6,5},{7,6},{8,15},{9,8},{10,9... | collective-permute-start | bytes 786440 | tf_op jit(solution)/shard_map/ppermute | solution.py:16
Sparse Core Ops, SparseCore 0:
  26.9 93.6 all-gather.2

commit v2 on v1

v2 whole, which is shorter than its diff:
```python
import jax
import jax.numpy as jnp
from jax import lax
from jax.experimental import pallas as pl
from jax.experimental.pallas import tpu as pltpu
from jax.sharding import PartitionSpec as P

MIB = 1024 * 1024


def ring_gather(block, axis, n):
    up = [(i, (i + 1) % n) for i in range(n)]
    down = [(i, (i + n - 1) % n) for i in range(n)]
    pieces = {0: block}
    from_below = from_above = block
    for hop in range(1, n // 2 + 1):
        from_below = lax.ppermute(from_below, axis, up)
        pieces[-hop] = from_below
        if 2 * hop < n:
            from_above = lax.ppermute(from_above, axis, down)
            pieces[hop] = from_above
    hops = sorted(pieces)
    stacked = jnp.stack([pieces[hop] for hop in hops])
    owners = jnp.arange(n, dtype=jnp.int32)
    places = jnp.remainder(owners - lax.axis_index(axis) - hops[0], n)
    return jnp.take(stacked, places, axis=0)


def split_kernel(scalars, psi_ref, keep_ref, send_ref):
    step = pl.program_id(0)
    core, own_left = scalars[0], scalars[1]
    left_dim, both = psi_ref.shape
    right_dim = both // 2
    row = lax.broadcasted_iota(jnp.int32, (left_dim, right_dim), 0)
    col = lax.broadcasted_iota(jnp.int32, (left_dim, right_dim), 1)

    def masked(at):
        size = scalars[2 + 2 * step + at]
        block = psi_ref[:, at * right_dim : (at + 1) * right_dim]
        inside = jnp.logical_and(row < own_left, col < size)
        return jnp.where(inside, block.astype(jnp.float32), 0.0).astype(block.dtype)

    first, second = masked(0), masked(1)

    @pl.when(core == 0)
    def _():
        keep_ref[0], send_ref[0] = first, second

    @pl.when(core != 0)
    def _():
        keep_ref[0], send_ref[0] = second, first


def split_psi(wavefunction, scalars, sectors):
    left_dim, columns = wavefunction.shape
    right_dim = columns // sectors
    block = pl.BlockSpec((1, left_dim, right_dim), lambda i, s: (i, 0, 0))
    shape = jax.ShapeDtypeStruct((sectors // 2, left_dim, right_dim), wavefunction.dtype)
    return pl.pallas_call(
        split_kernel,
        out_shape=(shape, shape),
        grid_spec=pltpu.PrefetchScalarGridSpec(
            num_scalar_prefetch=1,
            grid=(sectors // 2,),
            in_specs=[pl.BlockSpec((left_dim, 2 * right_dim), lambda i, s: (0, i))],
            out_specs=(block, block),
        ),
        compiler_params=pltpu.CompilerParams(vmem_limit_bytes=32 * MIB),
    )(scalars, wavefunction)


def apply_kernel(scalars, left_ref, psi_ref, right_ref, keep_ref, send_ref, middle):
    step = pl.program_id(0)
    parity, first_row, own_right = scalars[0], scalars[1], scalars[2]
    chips, halves, pairs, rows, left_dim = left_ref.shape
    right_dim = psi_ref.shape[2]
    indices = halves * pairs
    for a in range(chips):
        block = left_ref[a].reshape(indices * rows, left_dim)
        out = jnp.dot(block, psi_ref[a], preferred_element_type=jnp.float32)
        middle[:, a] = out.astype(middle.dtype).reshape(indices, rows, right_dim)
    total = jnp.zeros((chips * rows, right_dim), jnp.float32)
    for half in range(halves):
        for pair in range(pairs):
            block = middle[half * pairs + pair].reshape(chips * rows, right_dim)
            total += jnp.dot(block, right_ref[pair, half], preferred_element_type=jnp.float32)
    row = first_row + lax.broadcasted_iota(jnp.int32, (rows, right_dim), 0)
    col = lax.broadcasted_iota(jnp.int32, (rows, right_dim), 1)
    for a in range(chips):
        size = scalars[3 + step * chips + a]
        inside = jnp.logical_and(row < size, col < own_right)
        block = jnp.where(inside, total[a * rows : (a + 1) * rows], 0.0)
        low, high = block[: rows // 2], block[rows // 2 :]
        keep_ref[a] = jnp.where(parity == 0, low, high).astype(keep_ref.dtype)
        send_ref[a] = jnp.where(parity == 0, high, low).astype(send_ref.dtype)


def apply(scalars, lefts, psi, rights, steps):
    chips, halves, pairs, rows, left_dim = lefts.shape
    right_dim = psi.shape[2]
    some = chips // steps
    out = pl.BlockSpec((some, rows // 2, right_dim), lambda i, s: (i, 0, 0))
    shape = jax.ShapeDtypeStruct((chips, rows // 2, right_dim), psi.dtype)
    return pl.pallas_call(
        apply_kernel,
        out_shape=(shape, shape),
        grid_spec=pltpu.PrefetchScalarGridSpec(
            num_scalar_prefetch=1,
            grid=(steps,),
            in_specs=[
                pl.BlockSpec((some, halves, pairs, rows, left_dim), lambda i, s: (i, 0, 0, 0, 0)),
                pl.BlockSpec((some, left_dim, right_dim), lambda i, s: (i, 0, 0)),
                pl.BlockSpec(rights.shape, lambda i, s: (0, 0, 0, 0)),
            ],
            out_specs=(out, out),
            scratch_shapes=[pltpu.VMEM((halves * pairs, some, rows, right_dim), psi.dtype)],
        ),
        compiler_params=pltpu.CompilerParams(vmem_limit_bytes=48 * MIB),
    )(scalars, lefts, psi, rights)


def local(wavefunction, left_env, right_env, left_sizes, right_sizes):
    sector = lax.axis_index("blk")
    rank = lax.axis_index("mpo")
    sectors, ranks = lax.axis_size("blk"), lax.axis_size("mpo")
    core, parity = sector % 2, rank % 2
    _, left_dim, _ = left_env.shape
    right_dim = right_env.shape[2]
    chips = sectors // 2
    rows = 2 * left_dim // ranks
    own_left = left_sizes[sector]
    own_right = right_sizes[sector]

    swap = [(i, i ^ 1) for i in range(sectors)]
    own_w = lax.dynamic_index_in_dim(left_env, core, 0, keepdims=False)
    other_w = lax.dynamic_index_in_dim(left_env, 1 - core, 0, keepdims=False)
    got = lax.ppermute(other_w, "blk", swap)
    both = jnp.where(core == 0, jnp.stack([own_w, got]), jnp.stack([got, own_w]))
    pieces = both.reshape(2, ranks // 2, rows, left_dim).transpose(1, 0, 2, 3)
    mine = lax.all_to_all(pieces.reshape(ranks, rows, left_dim), "mpo", 0, 0)
    lefts = lax.all_gather(mine, "blk").reshape(chips, 2, ranks, rows, left_dim)

    scalars = jnp.concatenate([jnp.stack([core, own_left]), right_sizes]).astype(jnp.int32)
    keep, send = split_psi(wavefunction, scalars, sectors)
    give = [
        ((2 * chip + z % 2) * ranks + z, (2 * chip + 1 - z % 2) * ranks + z)
        for chip in range(chips)
        for z in range(ranks)
    ]
    given = lax.ppermute(send, ("blk", "mpo"), give)
    columns = jnp.where(core == parity, keep, given)
    groups = [[2 * chip + c for chip in range(chips)] for c in range(2)]
    psi = lax.all_to_all(columns, "blk", 0, 0, axis_index_groups=groups)

    rights = ring_gather(right_env, "mpo", ranks)

    sizes = lax.dynamic_index_in_dim(left_sizes.reshape(chips, 2), parity, 1, keepdims=False)
    first_row = (rank // 2) * rows
    scalars = jnp.concatenate([jnp.stack([parity, first_row, own_right]), sizes])
    kept, sent = apply(scalars.astype(jnp.int32), lefts, psi, rights, 4)

    came = lax.ppermute(sent, "mpo", [(z, z ^ 1) for z in range(ranks)])
    even = jnp.where(parity == 0, kept, came)
    odd = jnp.where(parity == 0, came, kept)
    return jnp.stack([even, odd], axis=1).reshape(sectors, rows // 2, right_dim)


def solution(mesh):
    placed = (P("blk", None), P("mpo", "blk", None), P("mpo", "blk", None), P(), P())
    return jax.shard_map(
        local, mesh=mesh, in_specs=placed, out_specs=P(None, "mpo", "blk"), check_vma=False
    )
```

time: 143 us -> 142 us (level)
  the two profiles are of different devices: /device:TPU:1 before, /device:TPU:64 now
where the time goes in v2:
time: 142 us; the launch traced here: 141 us
  waiting for transfers between devices  50.7 us (36%)
  local copies, waits for them, and re-layouts  20 us (14%)
  Pallas kernels  17.8 us (13%)
  blocking collectives  17.2 us (12%)
  starting transfers between devices  15 us (11%)
  between operations  13.5 us (10%)
  other arithmetic  7.02 us (5%)
    ppermute x4, waiting for transfers between devices, ring_gather(): from_below = lax.ppermute(from_below, axis, up)  25.7 us
    all_to_all x1, waiting for transfers between devices, local(): psi = lax.all_to_all(columns, 'blk', 0, 0, axis_index_groups=groups)  17.3 us
    all_to_all x1, blocking collectives, local(): mine = lax.all_to_all(pieces.reshape(ranks, rows, left_dim), 'mpo', 0, 0)  17.2 us
    pallas_call x1, Pallas kernels, apply(): pl.pallas_call(apply_kernel, out_shape=(shape, shape), grid_spec=pltpu.Pr...  10.9 us
    unnamed x17, local copies, waits for them, and re-layouts  10.8 us
    pallas_call x1, Pallas kernels, split_psi(): pl.pallas_call(split_kernel, out_shape=(shape, shape), grid_spec=pltpu.Pr...  6.85 us
    ppermute x1, waiting for transfers between devices, local(): came = lax.ppermute(sent, 'mpo', [(z, z ^ 1) for z in range(ranks)])  6.36 us
    all_to_all x1, starting transfers between devices, local(): psi = lax.all_to_all(columns, 'blk', 0, 0, axis_index_groups=groups)  5.94 us
  transfers between devices with their start and end apart: 12, of which 7 were waited for; matrix products, arithmetic and copies ran while one was open for 15% of the time, Pallas kernels for 5%

profile of v2, /device:TPU:64, one launch (start us, length us, event | category | flops | bytes accessed | tf_op | source)
XLA Modules:
  0.0 141.2 jit_solution(2056160433108582982)
XLA Ops:
  6.5 0.0 all-gather.3.cloned.1.call-start
  6.5 1.0 constant_dynamic-slice_fusion
  7.5 0.1 collective-permute-start
  7.6 1.3 collective-permute-done
  9.0 17.2 %all_to_all.10 = bf16[8,64,256]{2,1,0:T(8,128)(2,1)} all-to-all(bf16[8,64,256]{2,1,0:T(8,128)(2,1)S(1)} %bitcast.35), channel_id=1, replica_groups=mesh['blk'=32,'mpo'=8] {'mpo'}, dimensions={0} | all-to-all | bytes 524288 | tf_op jit(solution)/shard_map/all_to_all | solution.py:140
  26.1 0.0 all-gather.3.cloned.1.call-update
  26.2 1.2 dynamic_slice.21
  27.4 1.4 pad_add_fusion.1.scalars
  28.8 0.0 copy-start.1
  28.8 2.2 %copy-done.1 = bf16[256,8192]{1,0:T(8,128)(2,1)S(1)} copy-done((bf16[256,8192]{1,0:T(8,128)(2,1)S(1)}, bf16[256,8192]{1,0:T(8,128)(2,1)}, u32[]{:S(2)}) %copy-start.1) | copy-done | bytes 4194328
  31.0 0.0 copy-start.2
  31.0 0.0 copy-start.3
  31.0 0.0 copy-start.4
  31.0 6.8 %shard_map.55 = (bf16[16,256,256]{2,1,0:T(8,128)(2,1)S(1)}, bf16[16,256,256]{2,1,0:T(8,128)(2,1)}) custom-call(s32[34]{0:T(128)S(1)} %pad_add_fusion.1.scalars, bf16[256,8192]{1,0:T(8,128)(2,1)S(1)} %copy-done.1), custom_call_target="tpu_custom_call" | custom-call | tf_op jit(solution)/shard_map/pallas_call | solution.py:59
  37.8 2.6 %collective-permute-start.1 = (bf16[16,256,256]{2,1,0:T(8,128)(2,1)}, bf16[16,256,256]{2,1,0:T(8,128)(2,1)}, u32[]{:S(2)}, u32[]{:S(2)}) collective-permute-start(bf16[16,256,256]{2,1,0:T(8,128)(2,1)} %get-tuple-element.10), channel_id=1, source_target_pairs={{0,8},{9,1},{2,10},{11,3},{4,12},{13,5},{6,14},{15,7},{16,24},{25,... | collective-permute-start | bytes 6291464 | tf_op jit(solution)/shard_map/ppermute | solution.py:150
  40.4 0.0 copy-done.2
  40.5 0.0 collective-permute-start.2
  40.5 8.7 %collective-permute-done.2 = bf16[2,256,256]{2,1,0:T(8,128)(2,1)S(1)} collective-permute-done((bf16[2,256,256]{2,1,0:T(8,128)(2,1)S(1)}, bf16[2,256,256]{2,1,0:T(8,128)(2,1)S(1)}, u32[]{:S(2)}, u32[]{:S(2)}) %collective-permute-start.2) | collective-permute-done | bytes 262176 | tf_op jit(solution)/shard_map/ppermute | solution.py:17
  49.1 0.0 collective-permute-start.3
  49.1 2.0 %collective-permute-start.6 = (bf16[2,256,256]{2,1,0:T(8,128)(2,1)S(1)}, bf16[2,256,256]{2,1,0:T(8,128)(2,1)S(1)}, u32[]{:S(2)}, u32[]{:S(2)}) collective-permute-start(bf16[2,256,256]{2,1,0:T(8,128)(2,1)S(1)} %copy-done.2), channel_id=1, source_target_pairs={{0,7},{1,0},{2,1},{3,2},{4,3},{5,4},{6,5},{7,6},{8,15},{9,8},{10,9... | collective-permute-start | bytes 786440 | tf_op jit(solution)/shard_map/ppermute | solution.py:20
  51.1 6.9 %collective-permute-done.3 = bf16[2,256,256]{2,1,0:T(8,128)(2,1)S(1)} collective-permute-done((bf16[2,256,256]{2,1,0:T(8,128)(2,1)S(1)}, bf16[2,256,256]{2,1,0:T(8,128)(2,1)S(1)}, u32[]{:S(2)}, u32[]{:S(2)}) %collective-permute-start.3) | collective-permute-done | bytes 262176 | tf_op jit(solution)/shard_map/ppermute | solution.py:17
  58.1 0.2 collective-permute-start.4
  58.3 0.0 collective-permute-done.6
  58.3 1.9 %collective-permute-start.7 = (bf16[2,256,256]{2,1,0:T(8,128)(2,1)S(1)}, bf16[2,256,256]{2,1,0:T(8,128)(2,1)S(1)}, u32[]{:S(2)}, u32[]{:S(2)}) collective-permute-start(bf16[2,256,256]{2,1,0:T(8,128)(2,1)S(1)} %collective-permute-done.6), channel_id=1, source_target_pairs={{0,7},{1,0},{2,1},{3,2},{4,3},{5,4},{6,5},{7,6},{8,15},{9,8},{10,9... | collective-permute-start | bytes 786440 | tf_op jit(solution)/shard_map/ppermute | solution.py:20
  60.2 6.1 %collective-permute-done.4 = bf16[2,256,256]{2,1,0:T(8,128)(2,1)} collective-permute-done((bf16[2,256,256]{2,1,0:T(8,128)(2,1)S(1)}, bf16[2,256,256]{2,1,0:T(8,128)(2,1)}, u32[]{:S(2)}, u32[]{:S(2)}) %collective-permute-start.4) | collective-permute-done | bytes 262176 | tf_op jit(solution)/shard_map/ppermute | solution.py:17
  66.3 0.5 collective-permute-start.5
  66.8 0.0 copy-done.3
  66.8 0.1 reshape.76
  66.9 0.0 copy-done.4
  66.9 0.6 dynamic_slice.17
  67.5 0.2 dynamic-slice_reduce_fusion
  67.6 0.7 pad_add_fusion.scalars
  68.3 0.0 collective-permute-done.7
  68.4 1.6 %collective-permute-start.8 = (bf16[2,256,256]{2,1,0:T(8,128)(2,1)S(1)}, bf16[2,256,256]{2,1,0:T(8,128)(2,1)}, u32[]{:S(2)}, u32[]{:S(2)}) collective-permute-start(bf16[2,256,256]{2,1,0:T(8,128)(2,1)S(1)} %collective-permute-done.7), channel_id=1, source_target_pairs={{0,7},{1,0},{2,1},{3,2},{4,3},{5,4},{6,5},{7,6},{8,15},{9,8},{10,9... | collective-permute-start | bytes 786440 | tf_op jit(solution)/shard_map/ppermute | solution.py:20
  70.0 4.0 %collective-permute-done.5 = bf16[2,256,256]{2,1,0:T(8,128)(2,1)} collective-permute-done((bf16[2,256,256]{2,1,0:T(8,128)(2,1)}, bf16[2,256,256]{2,1,0:T(8,128)(2,1)}, u32[]{:S(2)}, u32[]{:S(2)}) %collective-permute-start.5) | collective-permute-done | bytes 262176 | tf_op jit(solution)/shard_map/ppermute | solution.py:17
  74.0 1.7 %bitcast_dynamic-update-slice_fusion.7 = bf16[8,2,256,256]{3,2,1,0:T(8,128)(2,1)} fusion(bf16[2,256,256]{2,1,0:T(8,128)(2,1)} %collective-permute-done.5), kind=kLoop, calls=%fused_computation.12 | loop fusion | bytes 524288
  75.7 0.0 collective-permute-done.1
  75.7 1.6 %broadcast_select_fusion.1 = bf16[16,256,256]{2,1,0:T(8,128)(2,1)} fusion(bf16[16,256,256]{2,1,0:T(8,128)(2,1)S(1)} %get-tuple-element.9, bf16[16,256,256]{2,1,0:T(8,128)(2,1)} %collective-permute-done.1, pred[]{:T(512)S(6)} %eq.17), kind=kLoop, calls=%fused_computation.2 | loop fusion | flops 1048576 | bytes 6291457 | tf_op jit(solution)/shard_map/jit(_where)/select_n | solution.py:151
  77.3 5.9 %all-to-all-start.1 = ((bf16[16,256,256]{2,1,0:T(8,128)(2,1)}), bf16[16,256,256]{2,1,0:T(8,128)(2,1)S(1)}, u32[]{:S(2)}, u32[]{:S(2)}) async-start(bf16[16,256,256]{2,1,0:T(8,128)(2,1)} %broadcast_select_fusion.1), calls=%async_computation.1 | async-start | bytes 4194304 | tf_op jit(solution)/shard_map/all_to_all | solution.py:153
  83.3 1.7 %bitcast_dynamic-update-slice_fusion.6 = bf16[8,2,256,256]{3,2,1,0:T(8,128)(2,1)} fusion(bf16[8,2,256,256]{3,2,1,0:T(8,128)(2,1)} %bitcast_dynamic-update-slice_fusion.7, bf16[2,256,256]{2,1,0:T(8,128)(2,1)} %collective-permute-done.4), kind=kLoop, calls=%fused_computation.11 | loop fusion | bytes 524288
  85.0 0.7 bitcast_dynamic-update-slice_fusion.5
  85.7 0.7 bitcast_dynamic-update-slice_fusion.4
  86.4 0.7 bitcast_dynamic-update-slice_fusion.3
  87.1 0.7 bitcast_dynamic-update-slice_fusion.2
  87.8 0.7 bitcast_dynamic-update-slice_fusion.1
  88.5 0.0 collective-permute-done.8
  88.5 1.7 %bitcast_dynamic-update-slice_fusion = bf16[8,2,256,256]{3,2,1,0:T(8,128)(2,1)} fusion(bf16[8,2,256,256]{3,2,1,0:T(8,128)(2,1)} %bitcast_dynamic-update-slice_fusion.1, bf16[2,256,256]{2,1,0:T(8,128)(2,1)} %collective-permute-done.8), kind=kLoop, calls=%fused_computation.5 | loop fusion | bytes 524288 | tf_op jit(solution)/shard_map/stack | solution.py:23
  90.2 3.6 %gather_fusion = bf16[8,2,256,256]{3,2,1,0:T(8,128)(2,1)} fusion(bf16[8,2,256,256]{3,2,1,0:T(8,128)(2,1)} %bitcast_dynamic-update-slice_fusion, s32[1024]{0:T(1024)S(1)} %pad_clamp_fusion), kind=kCustom, calls=%fused_computation | custom fusion | bytes 4194336 | tf_op jit(solution)/shard_map/jit(_take)/gather | solution.py:26
  93.8 3.2 %broadcast_select_fusion.right_ref = bf16[8,2,256,256]{3,2,1,0:T(8,128)(2,1)} fusion(bf16[8,2,256,256]{3,2,1,0:T(8,128)(2,1)} %gather_fusion, pred[8]{0:T(512)(128)(4,1)S(1)} %compare_and_fusion), kind=kLoop, calls=%fused_computation.1 | loop fusion | flops 1048576 | bytes 4194312 | tf_op jit(solution)/shard_map/jit(_take)/select_n | solution.py:26
  97.0 17.3 %all-to-all-done.1.psi_ref = bf16[16,256,256]{2,1,0:T(8,128)(2,1)S(1)} async-done(((bf16[16,256,256]{2,1,0:T(8,128)(2,1)}), bf16[16,256,256]{2,1,0:T(8,128)(2,1)S(1)}, u32[]{:S(2)}, u32[]{:S(2)}) %all-to-all-start.1) | async-done | bytes 2097184 | tf_op jit(solution)/shard_map/all_to_all | solution.py:153
  114.4 0.0 all-gather.3.cloned.1.call-done
  114.4 0.0 copy-start
  114.4 1.6 %copy-done = bf16[8,2,256,256]{3,2,1,0:T(8,128)(2,1)S(1)} copy-done((bf16[8,2,256,256]{3,2,1,0:T(8,128)(2,1)S(1)}, bf16[8,2,256,256]{3,2,1,0:T(8,128)(2,1)}, u32[]{:S(2)}) %copy-start) | copy-done | bytes 2097176
  115.9 10.9 %shard_map.56 = (bf16[16,32,256]{2,1,0:T(8,128)(2,1)S(1)}, bf16[16,32,256]{2,1,0:T(8,128)(2,1)S(1)}) custom-call(s32[19]{0:T(128)S(1)} %pad_add_fusion.scalars, bf16[16,2,8,64,256]{4,3,2,1,0:T(8,128)(2,1)} %bitcast.34, bf16[16,256,256]{2,1,0:T(8,128)(2,1)S(1)} %all-to-all-done.1.psi_ref, bf16[8,2,256,256]{3,2,1,0:T(8,128)(2,1)S(1)} %copy-done), custom_call_target="tpu_custom_call" | custom-call | tf_op jit(solution)/shard_map/pallas_call | solution.py:104
  126.9 0.1 collective-permute-start.9
  127.0 6.4 %collective-permute-done.9 = bf16[16,32,256]{2,1,0:T(8,128)(2,1)S(1)} collective-permute-done((bf16[16,32,256]{2,1,0:T(8,128)(2,1)S(1)}, bf16[16,32,256]{2,1,0:T(8,128)(2,1)S(1)}, u32[]{:S(2)}, u32[]{:S(2)}) %collective-permute-start.9) | collective-permute-done | bytes 262176 | tf_op jit(solution)/shard_map/ppermute | solution.py:162
  133.4 0.1 pad_maximum_fusion
  133.5 0.8 copy.7
  (5 shorter events, 0.1 us)
Async XLA Ops:
  6.5 107.8 %all-gather.3.cloned.1.call-start = ((), (), s32[]{:S(2)}) async-start(), calls=%async_computation.2 | async-start | bytes 8650752 | tf_op jit(solution)/shard_map/all_gather | solution.py:141
  7.5 1.4 %collective-permute-start = (bf16[256,256]{1,0:T(8,128)(2,1)S(1)}, bf16[256,256]{1,0:T(8,128)(2,1)S(1)}, u32[]{:S(2)}, u32[]{:S(2)}) collective-permute-start(bf16[256,256]{1,0:T(8,128)(2,1)S(1)} %get-tuple-element.16), channel_id=1, source_target_pairs={{0,8},{8,0},{16,24},{24,16},{32,40},{40,32},{48,56},{56,48},{64,72... | collective-permute-start | bytes 393224 | tf_op jit(solution)/shard_map/ppermute | solution.py:137
  28.8 2.2 %copy-start.1 = (bf16[256,8192]{1,0:T(8,128)(2,1)S(1)}, bf16[256,8192]{1,0:T(8,128)(2,1)}, u32[]{:S(2)}) copy-start(bf16[256,8192]{1,0:T(8,128)(2,1)} %psi_ref.1) | copy-start | bytes 12582916
  31.0 9.5 %copy-start.2 = (bf16[2,256,256]{2,1,0:T(8,128)(2,1)S(1)}, bf16[2,256,256]{2,1,0:T(8,128)(2,1)}, u32[]{:S(2)}) copy-start(bf16[2,256,256]{2,1,0:T(8,128)(2,1)} %param.7) | copy-start | bytes 786436
  31.0 35.8 %copy-start.3 = (s32[32]{0:T(128)S(1)}, s32[32]{0:T(128)}, u32[]{:S(2)}) copy-start(s32[32]{0:T(128)} %param.8) | copy-start | bytes 388
  31.0 35.9 %copy-start.4 = (s32[32]{0:T(128)S(1)}, s32[32]{0:T(128)}, u32[]{:S(2)}) copy-start(s32[32]{0:T(128)} %param.9) | copy-start | bytes 388
  37.8 37.9 %collective-permute-start.1 = (bf16[16,256,256]{2,1,0:T(8,128)(2,1)}, bf16[16,256,256]{2,1,0:T(8,128)(2,1)}, u32[]{:S(2)}, u32[]{:S(2)}) collective-permute-start(bf16[16,256,256]{2,1,0:T(8,128)(2,1)} %get-tuple-element.10), channel_id=1, source_target_pairs={{0,8},{9,1},{2,10},{11,3},{4,12},{13,5},{6,14},{15,7},{16,24},{25,... | collective-permute-start | bytes 6291464 | tf_op jit(solution)/shard_map/ppermute | solution.py:150
  40.5 8.7 %collective-permute-start.2 = (bf16[2,256,256]{2,1,0:T(8,128)(2,1)S(1)}, bf16[2,256,256]{2,1,0:T(8,128)(2,1)S(1)}, u32[]{:S(2)}, u32[]{:S(2)}) collective-permute-start(bf16[2,256,256]{2,1,0:T(8,128)(2,1)S(1)} %copy-done.2), channel_id=1, source_target_pairs={{0,1},{1,2},{2,3},{3,4},{4,5},{5,6},{6,7},{7,0},{8,9},{9,10},{10,1... | collective-permute-start | bytes 786440 | tf_op jit(solution)/shard_map/ppermute | solution.py:17
  49.1 8.9 %collective-permute-start.3 = (bf16[2,256,256]{2,1,0:T(8,128)(2,1)S(1)}, bf16[2,256,256]{2,1,0:T(8,128)(2,1)S(1)}, u32[]{:S(2)}, u32[]{:S(2)}) collective-permute-start(bf16[2,256,256]{2,1,0:T(8,128)(2,1)S(1)} %collective-permute-done.2), channel_id=1, source_target_pairs={{0,1},{1,2},{2,3},{3,4},{4,5},{5,6},{6,7},{7,0},{8,9},{9,10},{10,1... | collective-permute-start | bytes 786440 | tf_op jit(solution)/shard_map/ppermute | solution.py:17
  49.1 9.1 %collective-permute-start.6 = (bf16[2,256,256]{2,1,0:T(8,128)(2,1)S(1)}, bf16[2,256,256]{2,1,0:T(8,128)(2,1)S(1)}, u32[]{:S(2)}, u32[]{:S(2)}) collective-permute-start(bf16[2,256,256]{2,1,0:T(8,128)(2,1)S(1)} %copy-done.2), channel_id=1, source_target_pairs={{0,7},{1,0},{2,1},{3,2},{4,3},{5,4},{6,5},{7,6},{8,15},{9,8},{10,9... | collective-permute-start | bytes 786440 | tf_op jit(solution)/shard_map/ppermute | solution.py:20
  58.1 8.2 %collective-permute-start.4 = (bf16[2,256,256]{2,1,0:T(8,128)(2,1)S(1)}, bf16[2,256,256]{2,1,0:T(8,128)(2,1)}, u32[]{:S(2)}, u32[]{:S(2)}) collective-permute-start(bf16[2,256,256]{2,1,0:T(8,128)(2,1)S(1)} %collective-permute-done.3), channel_id=1, source_target_pairs={{0,1},{1,2},{2,3},{3,4},{4,5},{5,6},{6,7},{7,0},{8,9},{9,10},{10,1... | collective-permute-start | bytes 786440 | tf_op jit(solution)/shard_map/ppermute | solution.py:17
  58.3 10.1 %collective-permute-start.7 = (bf16[2,256,256]{2,1,0:T(8,128)(2,1)S(1)}, bf16[2,256,256]{2,1,0:T(8,128)(2,1)S(1)}, u32[]{:S(2)}, u32[]{:S(2)}) collective-permute-start(bf16[2,256,256]{2,1,0:T(8,128)(2,1)S(1)} %collective-permute-done.6), channel_id=1, source_target_pairs={{0,7},{1,0},{2,1},{3,2},{4,3},{5,4},{6,5},{7,6},{8,15},{9,8},{10,9... | collective-permute-start | bytes 786440 | tf_op jit(solution)/shard_map/ppermute | solution.py:20
  66.3 7.7 %collective-permute-start.5 = (bf16[2,256,256]{2,1,0:T(8,128)(2,1)}, bf16[2,256,256]{2,1,0:T(8,128)(2,1)}, u32[]{:S(2)}, u32[]{:S(2)}) collective-permute-start(bf16[2,256,256]{2,1,0:T(8,128)(2,1)} %collective-permute-done.4), channel_id=1, source_target_pairs={{0,1},{1,2},{2,3},{3,4},{4,5},{5,6},{6,7},{7,0},{8,9},{9,10},{10,1... | collective-permute-start | bytes 786440 | tf_op jit(solution)/shard_map/ppermute | solution.py:17
  68.4 20.2 %collective-permute-start.8 = (bf16[2,256,256]{2,1,0:T(8,128)(2,1)S(1)}, bf16[2,256,256]{2,1,0:T(8,128)(2,1)}, u32[]{:S(2)}, u32[]{:S(2)}) collective-permute-start(bf16[2,256,256]{2,1,0:T(8,128)(2,1)S(1)} %collective-permute-done.7), channel_id=1, source_target_pairs={{0,7},{1,0},{2,1},{3,2},{4,3},{5,4},{6,5},{7,6},{8,15},{9,8},{10,9... | collective-permute-start | bytes 786440 | tf_op jit(solution)/shard_map/ppermute | solution.py:20
  77.3 37.0 %all-to-all-start.1 = ((bf16[16,256,256]{2,1,0:T(8,128)(2,1)}), bf16[16,256,256]{2,1,0:T(8,128)(2,1)S(1)}, u32[]{:S(2)}, u32[]{:S(2)}) async-start(bf16[16,256,256]{2,1,0:T(8,128)(2,1)} %broadcast_select_fusion.1), calls=%async_computation.1 | async-start | bytes 4194304 | tf_op jit(solution)/shard_map/all_to_all | solution.py:153
  114.4 1.6 %copy-start = (bf16[8,2,256,256]{3,2,1,0:T(8,128)(2,1)S(1)}, bf16[8,2,256,256]{3,2,1,0:T(8,128)(2,1)}, u32[]{:S(2)}) copy-start(bf16[8,2,256,256]{3,2,1,0:T(8,128)(2,1)} %broadcast_select_fusion.right_ref) | copy-start | bytes 6291460
  126.9 6.5 %collective-permute-start.9 = (bf16[16,32,256]{2,1,0:T(8,128)(2,1)S(1)}, bf16[16,32,256]{2,1,0:T(8,128)(2,1)S(1)}, u32[]{:S(2)}, u32[]{:S(2)}) collective-permute-start(bf16[16,32,256]{2,1,0:T(8,128)(2,1)S(1)} %get-tuple-element.12), channel_id=1, source_target_pairs={{0,1},{1,0},{2,3},{3,2},{4,5},{5,4},{6,7},{7,6},{8,9},{9,8},{10,11... | collective-permute-start | bytes 786440 | tf_op jit(solution)/shard_map/ppermute | solution.py:162
Sparse Core Ops, SparseCore 0:
  26.3 56.9 all-gather.2

commit v3 on v0

v3 whole, which is shorter than its diff:
```python
import functools

import jax
import jax.numpy as jnp
from jax import lax
from jax.experimental import pallas as pl
from jax.experimental.pallas import tpu as pltpu
from jax.sharding import PartitionSpec as P

MIB = 1024 * 1024
SIDE = 4
OFFSETS = (0, SIDE - 1, 1, 2)


def place(y, x, core):
    return ((y % SIDE) * SIDE + x % SIDE) * 2 + core


def stack_kernel(places, *refs):
    inputs, out, sems = refs[: len(places)], refs[-2], refs[-1]
    copies = []
    for i, (ref, (at, lo, hi)) in enumerate(zip(inputs, places)):
        copies.append(pltpu.make_async_copy(ref, out.at[at, lo:hi], sems.at[i]))
    for copy in copies:
        copy.start()
    for copy in copies:
        copy.wait()


def stack(pieces, places, shape):
    return pl.pallas_call(
        functools.partial(stack_kernel, places),
        out_shape=jax.ShapeDtypeStruct(shape, pieces[0].dtype),
        in_specs=[pl.BlockSpec(memory_space=pl.ANY)] * len(pieces),
        out_specs=pl.BlockSpec(memory_space=pl.ANY),
        scratch_shapes=[pltpu.SemaphoreType.DMA((len(pieces),))],
        compiler_params=pltpu.CompilerParams(vmem_limit_bytes=MIB),
    )(*pieces)


def rows_kernel(scalars, psi_ref, out_ref):
    first, own_left = scalars[0], scalars[1]
    sectors, rows, right_dim = out_ref.shape
    row = first + lax.broadcasted_iota(jnp.int32, (rows, right_dim), 0)
    col = lax.broadcasted_iota(jnp.int32, (rows, right_dim), 1)
    for at in range(sectors):
        g, y = at // SIDE, at % SIDE
        b = place(y, g % SIDE, g // SIDE)
        block = psi_ref[:, b * right_dim : (b + 1) * right_dim].astype(jnp.float32)
        inside = jnp.logical_and(row < own_left, col < scalars[2 + b])
        out_ref[at] = jnp.where(inside, block, 0.0).astype(out_ref.dtype)


def split_rows(wavefunction, scalars, sectors, ranks):
    left_dim, columns = wavefunction.shape
    rows, right_dim = left_dim // ranks, columns // sectors
    return pl.pallas_call(
        rows_kernel,
        out_shape=jax.ShapeDtypeStruct((sectors, rows, right_dim), wavefunction.dtype),
        grid_spec=pltpu.PrefetchScalarGridSpec(
            num_scalar_prefetch=1,
            grid=(1,),
            in_specs=[pl.BlockSpec((rows, columns), lambda i, s: (s[0] // rows, 0))],
            out_specs=pl.BlockSpec((sectors, rows, right_dim), lambda i, s: (0, 0, 0)),
        ),
        compiler_params=pltpu.CompilerParams(vmem_limit_bytes=60 * MIB),
    )(scalars, wavefunction)


def add_blocks(scalars, pieces, refs, psi_ref, right_ref, total):
    core, x0, y0, rank = scalars[0], scalars[1], scalars[2], scalars[3]
    ranks, parts, rows, right_dim = psi_ref.shape
    for ref, (sibling, far, first) in zip(refs, pieces):
        tree = 1 - core if sibling else core
        for k in range(ref.shape[0]):
            near = OFFSETS[first + k]
            y = jnp.where(tree == 0, y0 + far, y0 + near) & (SIDE - 1)
            x = jnp.where(tree == 0, x0 + near, x0 + far) & (SIDE - 1)
            at = (2 * x + tree - rank) & (ranks - 1)
            psi = psi_ref[:, pl.ds(y, 1)].reshape(ranks * rows, right_dim)
            _, left_dim, inner = ref.shape[1:]
            block = ref[k].reshape(2 * left_dim, inner)
            both = jnp.dot(block, psi, preferred_element_type=jnp.float32).astype(psi.dtype)
            term = jnp.dot(both[:left_dim], right_ref[at, 0], preferred_element_type=jnp.float32)
            term += jnp.dot(both[left_dim:], right_ref[at, 1], preferred_element_type=jnp.float32)
            total[y] += term


def first_kernel(pieces, scalars, *refs):
    blocks, (psi_ref, right_ref, total) = refs[: len(pieces)], refs[len(pieces) :]
    total[...] = jnp.zeros_like(total)
    add_blocks(scalars, pieces, blocks, psi_ref, right_ref, total)


def last_kernel(pieces, scalars, *refs):
    blocks, (psi_ref, right_ref, total_in, out_ref, total) = refs[: len(pieces)], refs[len(pieces) :]
    total[...] = total_in[...]
    add_blocks(scalars, pieces, blocks, psi_ref, right_ref, total)
    ranks, parts, rows, right_dim = out_ref.shape
    row = lax.broadcasted_iota(jnp.int32, (ranks * rows, right_dim), 0)
    col = lax.broadcasted_iota(jnp.int32, (ranks * rows, right_dim), 1)
    for y in range(parts):
        inside = jnp.logical_and(row < scalars[5 + y], col < scalars[4])
        block = jnp.where(inside, total[y], 0.0).astype(out_ref.dtype)
        out_ref[:, y] = block.reshape(ranks, rows, right_dim)


def call(kernel, pieces, scalars, arrays, shape, scratch):
    smem = pl.BlockSpec(memory_space=pltpu.SMEM)
    vmem = pl.BlockSpec(memory_space=pltpu.VMEM)
    return pl.pallas_call(
        functools.partial(kernel, pieces),
        out_shape=shape,
        in_specs=[smem] + [vmem] * len(arrays),
        out_specs=vmem,
        scratch_shapes=scratch,
        compiler_params=pltpu.CompilerParams(vmem_limit_bytes=28 * MIB),
    )(scalars, *arrays)


def local(wavefunction, left_env, right_env, left_sizes, right_sizes):
    sector = lax.axis_index("blk")
    rank = lax.axis_index("mpo")
    sectors, ranks = lax.axis_size("blk"), lax.axis_size("mpo")
    left_dim, right_dim = left_env.shape[2], right_env.shape[2]
    rows = left_dim // ranks
    core, x0, y0 = sector % 2, sector // 2 % SIDE, sector // (2 * SIDE)
    spots = [(y, x, c) for y in range(SIDE) for x in range(SIDE) for c in range(2)]

    def axis_step(second, by):
        pairs = []
        for y, x, c in spots:
            along_x = (c == 0) != second
            to = place(y, x + by, c) if along_x else place(y + by, x, c)
            pairs.append((place(y, x, c), to))
        return pairs

    turn = [
        (place(y, x, c) * ranks + z, place(y, z // 2, z % 2) * ranks + x + SIDE * c)
        for y, x, c in spots
        for z in range(ranks)
    ]
    own = lax.ppermute(left_env, ("blk", "mpo"), turn)

    scalars = jnp.concatenate([jnp.stack([rank * rows, left_sizes[sector]]), right_sizes])
    mine = split_rows(wavefunction, scalars.astype(jnp.int32), sectors, ranks)
    order = [place(y, g % SIDE, g // SIDE) for g in range(ranks) for y in range(SIDE)]
    spread = lax.all_to_all(mine, "blk", 0, 0, axis_index_groups=[order])
    spread = spread.reshape(ranks, SIDE, rows, right_dim)
    own, spread = lax.optimization_barrier((own, spread))

    below = lax.ppermute(own, "blk", axis_step(False, 1))
    above = lax.ppermute(own, "blk", axis_step(False, -1))
    below2 = lax.ppermute(below[:1], "blk", axis_step(False, 1))
    above2 = lax.ppermute(above[1:], "blk", axis_step(False, -1))
    line = stack(
        (own, below, above, below2, above2),
        ((0, 0, 2), (1, 0, 2), (2, 0, 2), (3, 0, 1), (3, 1, 2)),
        (SIDE, *left_env.shape),
    )
    line, spread = lax.optimization_barrier((line, spread))
    line_below = lax.ppermute(line, "blk", axis_step(True, 1))
    line_above = lax.ppermute(line, "blk", axis_step(True, -1))
    far_below = lax.ppermute(line_below[: SIDE // 2], "blk", axis_step(True, 1))
    far_above = lax.ppermute(line_above[SIDE // 2 :], "blk", axis_step(True, -1))
    psi = lax.all_to_all(spread, "mpo", 0, 0)

    swap = [(i, i ^ 1) for i in range(sectors)]
    near = [line, line_below, line_above]
    near += [lax.ppermute(block, "blk", swap) for block in near]
    distant = [far_below, far_above]
    distant += [lax.ppermute(block, "blk", swap) for block in distant]

    up = [(z, (z + 1) % ranks) for z in range(ranks)]
    down = [(z, (z - 1) % ranks) for z in range(ranks)]
    ring = {0: right_env}
    for hop in range(1, ranks // 2 + 1):
        ring[ranks - hop] = lax.ppermute(ring[(ranks + 1 - hop) % ranks], "mpo", up)
        if 2 * hop < ranks:
            ring[hop] = lax.ppermute(ring[hop - 1], "mpo", down)
    rights = stack(
        [ring[i] for i in range(ranks)],
        [(i, 0, 2) for i in range(ranks)],
        (ranks, *right_env.shape),
    )

    group = jnp.stack([left_sizes[place(y, 0, 0) + rank % SIDE * 2 + rank // SIDE] for y in range(SIDE)])
    scalars = jnp.concatenate([jnp.stack([core, x0, y0, rank, right_sizes[sector]]), group])
    scalars = scalars.astype(jnp.int32)
    total = jax.ShapeDtypeStruct((SIDE, left_dim, right_dim), jnp.float32)
    pieces = tuple((s, d, 0) for s in (False, True) for d in (0, SIDE - 1, 1))
    begun = call(first_kernel, pieces, scalars, (*near, psi, rights), total, [])
    pieces = tuple((s, 2, k) for s in (False, True) for k in (0, SIDE // 2))
    done = call(
        last_kernel,
        pieces,
        scalars,
        (*distant, psi, rights, begun),
        jax.ShapeDtypeStruct((ranks, SIDE, rows, right_dim), wavefunction.dtype),
        [pltpu.VMEM(total.shape, total.dtype)],
    )

    out = lax.all_to_all(done, "mpo", 0, 0).reshape(2, SIDE, SIDE, rows, right_dim)
    return out.transpose(2, 1, 0, 3, 4).reshape(sectors, rows, right_dim)


def solution(mesh):
    placed = (P("blk", None), P("mpo", "blk", None), P("mpo", "blk", None), P(), P())
    return jax.shard_map(
        local, mesh=mesh, in_specs=placed, out_specs=P(None, "mpo", "blk"), check_vma=False
    )
```

time: 285 us -> 147 us (0.52)
  waiting for transfers between devices: 197 us -> 25.4 us
  starting transfers between devices: 8.84 us -> 65 us
  blocking collectives: 0 us -> 20.9 us
  local copies, waits for them, and re-layouts: 37.3 us -> 19.1 us
  matrix products: 15.1 us -> 0 us
  Pallas kernels: 0 us -> 13.5 us
  between operations: 13.5 us -> 0.16 us
  other arithmetic: 12.3 us -> 1.92 us
    reduce_scatter x1 -> x0, waiting for transfers between devices: 99.2 us -> none  [local(): lax.psum_scatter(summed_terms, 'mpo', scatter_dimension=1, tiled=True)]
    all_to_all x1 -> x2, waiting for transfers between devices: 98.3 us -> 1.1 us  [the longest x1 1.1 us: local(): psi = lax.all_to_all(spread, 'mpo', 0, 0)]
    ppermute x0 -> x21, starting transfers between devices: none -> 52 us  [the longest x3 10.9 us: local(): ring[hop] = lax.ppermute(ring[hop - 1], 'mpo', down)]
    ppermute x0 -> x21, waiting for transfers between devices: none -> 24.3 us  [the longest x4 9.42 us: local(): ring[ranks - hop] = lax.ppermute(ring[(ranks + 1 - hop) % ranks], 'mpo', up)]
    all_to_all x0 -> x1, blocking collectives: none -> 20.9 us  [local(): lax.all_to_all(done, 'mpo', 0, 0).reshape(2, SIDE, SIDE, rows, right_dim)]
    all_to_all x1 -> x0, local copies, waits for them, and re-layouts: 20.9 us -> none  [local(): lax.all_to_all(products, 'blk', split_axis=2, concat_axis=1, tiled=True)]
    another operation x1 -> x0, local copies, waits for them, and re-layouts: 16.4 us -> none  [local(): jnp.stack([jnp.dot(left_env[mpo_index], masked, preferred_element_type=jn...]
    dot_general x3 -> x0, matrix products: 15.1 us -> none  [the longest x2 8.4 us: local(): jnp.dot(left_env[mpo_index], masked, preferred_element_type=jnp.float32)]
  transfers between devices with their start and end apart: 2 -> 23, of which waited for: 2 -> 8; matrix products, arithmetic and copies ran while one was open for 0% -> 4% of each run, Pallas kernels for 0% -> 5%
where the time goes in v3:
time: 147 us; the launch traced here: 146 us
  starting transfers between devices  65 us (44%)
  waiting for transfers between devices  25.4 us (17%)
  blocking collectives  20.9 us (14%)
  local copies, waits for them, and re-layouts  19.1 us (13%)
  Pallas kernels  13.5 us (9%)
  other arithmetic  1.92 us (1%)
    all_to_all x1, blocking collectives, local(): lax.all_to_all(done, 'mpo', 0, 0).reshape(2, SIDE, SIDE, rows, right_dim)  20.9 us
    unnamed x34, local copies, waits for them, and re-layouts  10.9 us
    ppermute x3, starting transfers between devices, local(): ring[hop] = lax.ppermute(ring[hop - 1], 'mpo', down)  10.9 us
    ppermute x1, starting transfers between devices, local(): line_above = lax.ppermute(line, 'blk', axis_step(True, -1))  9.64 us
    pallas_call x2, Pallas kernels, call(): pl.pallas_call(functools.partial(kernel, pieces), out_shape=shape, in_spe...  9.48 us
    ppermute x4, waiting for transfers between devices, local(): ring[ranks - hop] = lax.ppermute(ring[(ranks + 1 - hop) % ranks], 'mpo', up)  9.42 us
    ppermute x1, starting transfers between devices, local(): own = lax.ppermute(left_env, ('blk', 'mpo'), turn)  9 us
    ppermute x3, starting transfers between devices, local(): near += [lax.ppermute(block, 'blk', swap) for block in near]  8.89 us
  transfers between devices with their start and end apart: 23, of which 8 were waited for; matrix products, arithmetic and copies ran while one was open for 4% of the time, Pallas kernels for 5%

profile of v3, /device:TPU:1, one launch (start us, length us, event | category | flops | bytes accessed | tf_op | source)
XLA Modules:
  0.0 146.0 jit_solution(2171517086991381478)
XLA Ops:
  0.0 1.5 %fusion = (s32[1]{0:T(128)}, s32[1]{0:T(128)}, s32[1]{0:T(128)}, s32[1]{0:T(128)}, s32[1]{0:T(128)}) fusion(s32[32]{0:T(128)} %param.8, s32[]{:T(128)S(6)} %select_n.54, s32[]{:T(128)S(6)} %select_n.59, s32[]{:T(128)S(6)} %select_n.58, s32[]{:T(128)S(6)} %select_n.57, s32[]{:T(128)S(6)} %select_n.60), kind=kLoop, calls=%fused_computation.1 | loop fusion | bytes 60 | tf_op jit(solution)/shard_map/dynamic_slice | solution.py:145
  1.5 1.9 %pad_add_fusion.scalars = s32[34]{0:T(128)} fusion(s32[32]{0:T(128)} %param.9, s32[1]{0:T(128)} %get-tuple-element.13, s32[1]{0:T(128)} %bitcast.4), kind=kLoop, calls=%fused_computation | loop fusion | flops 68 | bytes 272 | tf_op jit(solution)/shard_map/concatenate | solution.py:145
  3.4 2.8 %shard_map.55 = bf16[32,32,256]{2,1,0:T(8,128)(2,1)} custom-call(s32[34]{0:T(128)} %pad_add_fusion.scalars, bf16[256,8192]{1,0:T(8,128)(2,1)} %psi_ref.1), custom_call_target="tpu_custom_call" | custom-call | tf_op jit(solution)/shard_map/pallas_call | solution.py:57
  6.2 8.8 %all-to-all-start = ((bf16[32,32,256]{2,1,0:T(8,128)(2,1)}), bf16[32,32,256]{2,1,0:T(8,128)(2,1)}, u32[]{:S(2)}, u32[]{:S(2)}) async-start(bf16[32,32,256]{2,1,0:T(8,128)(2,1)} %shard_map.55), calls=%async_computation | async-start | bytes 1048576 | tf_op jit(solution)/shard_map/all_to_all | solution.py:148
  15.0 9.0 %collective-permute-start = (bf16[2,256,256]{2,1,0:T(8,128)(2,1)S(1)}, bf16[2,256,256]{2,1,0:T(8,128)(2,1)S(1)}, u32[]{:S(2)}, u32[]{:S(2)}) collective-permute-start(bf16[2,256,256]{2,1,0:T(8,128)(2,1)S(1)} %copy-done.16), channel_id=1, source_target_pairs={{0,0},{1,8},{2,16},{3,24},{4,32},{5,40},{6,48},{7,56},{8,4},{9,12}... | collective-permute-start | bytes 786440 | tf_op jit(solution)/shard_map/ppermute | solution.py:143
  24.0 3.7 %collective-permute-done.refs_0_ = bf16[2,256,256]{2,1,0:T(8,128)(2,1)S(1)} collective-permute-done((bf16[2,256,256]{2,1,0:T(8,128)(2,1)S(1)}, bf16[2,256,256]{2,1,0:T(8,128)(2,1)S(1)}, u32[]{:S(2)}, u32[]{:S(2)}) %collective-permute-start) | collective-permute-done | bytes 262176 | tf_op jit(solution)/shard_map/ppermute | solution.py:143
  27.7 1.7 %collective-permute-start.1 = (bf16[2,256,256]{2,1,0:T(8,128)(2,1)S(1)}, bf16[2,256,256]{2,1,0:T(8,128)(2,1)S(1)}, u32[]{:S(2)}, u32[]{:S(2)}) collective-permute-start(bf16[2,256,256]{2,1,0:T(8,128)(2,1)S(1)} %collective-permute-done.refs_0_), channel_id=1, source_target_pairs={{0,16},{8,72},{16,32},{24,88},{32,48},{40,104},{48,0},{56,120},{64... | collective-permute-start | bytes 786440 | tf_op jit(solution)/shard_map/ppermute | solution.py:152
  29.4 1.2 collective-permute-start.2
  30.6 3.8 %collective-permute-done.1.refs_1_ = bf16[2,256,256]{2,1,0:T(8,128)(2,1)S(1)} collective-permute-done((bf16[2,256,256]{2,1,0:T(8,128)(2,1)S(1)}, bf16[2,256,256]{2,1,0:T(8,128)(2,1)S(1)}, u32[]{:S(2)}, u32[]{:S(2)}) %collective-permute-start.1) | collective-permute-done | bytes 262176 | tf_op jit(solution)/shard_map/ppermute | solution.py:152
  34.4 0.3 collective-permute-start.3
  34.7 2.5 %collective-permute-start.4 = (bf16[1,256,256]{2,1,0:T(8,128)(2,1)S(1)}, bf16[1,256,256]{2,1,0:T(8,128)(2,1)S(1)}, u32[]{:S(2)}, u32[]{:S(2)}) collective-permute-start(bf16[1,256,256]{2,1,0:T(8,128)(2,1)S(1)} %slice.17), channel_id=1, source_target_pairs={{0,48},{8,200},{16,0},{24,216},{32,16},{40,232},{48,32},{56,248},{... | collective-permute-start | bytes 393224 | tf_op jit(solution)/shard_map/ppermute | solution.py:155
  37.3 2.6 %collective-permute-done.3.refs_3_ = bf16[1,256,256]{2,1,0:T(8,128)(2,1)S(1)} collective-permute-done((bf16[1,256,256]{2,1,0:T(8,128)(2,1)S(1)}, bf16[1,256,256]{2,1,0:T(8,128)(2,1)S(1)}, u32[]{:S(2)}, u32[]{:S(2)}) %collective-permute-start.3) | collective-permute-done | bytes 131104 | tf_op jit(solution)/shard_map/ppermute | solution.py:154
  39.8 0.0 collective-permute-done.4.refs_4_
  39.8 1.0 shard_map.56.refs_0_
  40.9 9.6 %collective-permute-start.7 = (bf16[4,2,256,256]{3,2,1,0:T(8,128)(2,1)}, bf16[4,2,256,256]{3,2,1,0:T(8,128)(2,1)}, u32[]{:S(2)}, u32[]{:S(2)}) collective-permute-start(bf16[4,2,256,256]{3,2,1,0:T(8,128)(2,1)} %shard_map.56.refs_0_), channel_id=1, source_target_pairs={{0,192},{8,56},{16,208},{24,8},{32,224},{40,24},{48,240},{56,40},{... | collective-permute-start | bytes 3145736 | tf_op jit(solution)/shard_map/ppermute | solution.py:163
  50.5 0.0 collective-permute-start.5
  50.5 0.1 collective-permute-start.14
  50.6 5.6 %collective-permute-start.11 = (bf16[2,256,256]{2,1,0:T(8,128)(2,1)S(1)}, bf16[2,256,256]{2,1,0:T(8,128)(2,1)S(1)}, u32[]{:S(2)}, u32[]{:S(2)}) collective-permute-start(bf16[2,256,256]{2,1,0:T(8,128)(2,1)S(1)} %copy-done), channel_id=1, source_target_pairs={{0,7},{1,0},{2,1},{3,2},{4,3},{5,4},{6,5},{7,6},{8,15},{9,8},{10,9... | collective-permute-start | bytes 786440 | tf_op jit(solution)/shard_map/ppermute | solution.py:180
  56.2 4.2 %collective-permute-done.14.refs_7_ = bf16[2,256,256]{2,1,0:T(8,128)(2,1)S(1)} collective-permute-done((bf16[2,256,256]{2,1,0:T(8,128)(2,1)S(1)}, bf16[2,256,256]{2,1,0:T(8,128)(2,1)S(1)}, u32[]{:S(2)}, u32[]{:S(2)}) %collective-permute-start.14) | collective-permute-done | bytes 262176 | tf_op jit(solution)/shard_map/ppermute | solution.py:178
  60.3 0.0 collective-permute-start.15
  60.3 0.7 copy-done.1
  61.0 0.0 collective-permute-done.11.refs_1_
  61.0 2.7 %collective-permute-start.12 = (bf16[2,256,256]{2,1,0:T(8,128)(2,1)S(1)}, bf16[2,256,256]{2,1,0:T(8,128)(2,1)S(1)}, u32[]{:S(2)}, u32[]{:S(2)}) collective-permute-start(bf16[2,256,256]{2,1,0:T(8,128)(2,1)S(1)} %collective-permute-done.11.refs_1_), channel_id=1, source_target_pairs={{0,7},{1,0},{2,1},{3,2},{4,3},{5,4},{6,5},{7,6},{8,15},{9,8},{10,9... | collective-permute-start | bytes 786440 | tf_op jit(solution)/shard_map/ppermute | solution.py:180
  63.7 0.7 copy-done.3
  64.4 2.7 %collective-permute-done.15.refs_6_ = bf16[2,256,256]{2,1,0:T(8,128)(2,1)S(1)} collective-permute-done((bf16[2,256,256]{2,1,0:T(8,128)(2,1)S(1)}, bf16[2,256,256]{2,1,0:T(8,128)(2,1)S(1)}, u32[]{:S(2)}, u32[]{:S(2)}) %collective-permute-start.15) | collective-permute-done | bytes 262176 | tf_op jit(solution)/shard_map/ppermute | solution.py:178
  67.2 0.0 collective-permute-start.16
  67.2 0.7 copy-done.5
  67.9 2.7 %collective-permute-start.13 = (bf16[2,256,256]{2,1,0:T(8,128)(2,1)S(1)}, bf16[2,256,256]{2,1,0:T(8,128)(2,1)S(1)}, u32[]{:S(2)}, u32[]{:S(2)}) collective-permute-start(bf16[2,256,256]{2,1,0:T(8,128)(2,1)S(1)} %collective-permute-done.12.refs_2_), channel_id=1, source_target_pairs={{0,7},{1,0},{2,1},{3,2},{4,3},{5,4},{6,5},{7,6},{8,15},{9,8},{10,9... | collective-permute-start | bytes 786440 | tf_op jit(solution)/shard_map/ppermute | solution.py:180
  70.5 0.7 copy-done.7
  71.3 2.5 %collective-permute-done.16.refs_5_ = bf16[2,256,256]{2,1,0:T(8,128)(2,1)S(1)} collective-permute-done((bf16[2,256,256]{2,1,0:T(8,128)(2,1)S(1)}, bf16[2,256,256]{2,1,0:T(8,128)(2,1)S(1)}, u32[]{:S(2)}, u32[]{:S(2)}) %collective-permute-start.16) | collective-permute-done | bytes 262176 | tf_op jit(solution)/shard_map/ppermute | solution.py:178
  73.8 0.0 collective-permute-start.17
  73.8 8.4 %collective-permute-start.18 = (bf16[4,2,256,256]{3,2,1,0:T(8,128)(2,1)}, bf16[4,2,256,256]{3,2,1,0:T(8,128)(2,1)}, u32[]{:S(2)}, u32[]{:S(2)}) collective-permute-start(bf16[4,2,256,256]{3,2,1,0:T(8,128)(2,1)} %shard_map.56.refs_0_), channel_id=1, source_target_pairs={{0,8},{8,0},{16,24},{24,16},{32,40},{40,32},{48,56},{56,48},{64,72... | collective-permute-start | bytes 3145736 | tf_op jit(solution)/shard_map/ppermute | solution.py:170
  82.2 1.1 slice.19
  83.3 6.2 %collective-permute-start.8 = (bf16[2,2,256,256]{3,2,1,0:T(8,128)(2,1)S(1)}, bf16[2,2,256,256]{3,2,1,0:T(8,128)(2,1)S(1)}, u32[]{:S(2)}, u32[]{:S(2)}) collective-permute-start(bf16[2,2,256,256]{3,2,1,0:T(8,128)(2,1)S(1)} %slice.19), channel_id=1, source_target_pairs={{0,192},{8,56},{16,208},{24,8},{32,224},{40,24},{48,240},{56,40},{... | collective-permute-start | bytes 1572872 | tf_op jit(solution)/shard_map/ppermute | solution.py:165
  89.4 0.0 collective-permute-done.5.refs_1_
  89.5 0.0 collective-permute-start.19
  89.5 1.1 slice.18
  90.5 0.0 collective-permute-done.13.refs_3_
  90.6 0.7 copy-done.11
  91.3 0.5 collective-permute-start.20
  91.8 0.0 collective-permute-done.17.refs_4_
  91.8 0.7 copy-done.13
  92.5 0.0 collective-permute-start.6
  92.5 4.2 %all-to-all-start.1 = ((bf16[8,4,32,256]{3,2,1,0:T(8,128)(2,1)}), bf16[8,4,32,256]{3,2,1,0:T(8,128)(2,1)S(1)}, u32[]{:S(2)}, u32[]{:S(2)}) async-start(bf16[8,4,32,256]{3,2,1,0:T(8,128)(2,1)} %bitcast.5), calls=%async_computation.1 | async-start | bytes 1048576 | tf_op jit(solution)/shard_map/all_to_all | solution.py:166
  96.7 0.0 collective-permute-done.8.refs_1_
  96.7 0.6 collective-permute-start.10
  97.4 4.8 %collective-permute-done.6.refs_0_ = bf16[2,2,256,256]{3,2,1,0:T(8,128)(2,1)} collective-permute-done((bf16[2,2,256,256]{3,2,1,0:T(8,128)(2,1)S(1)}, bf16[2,2,256,256]{3,2,1,0:T(8,128)(2,1)}, u32[]{:S(2)}, u32[]{:S(2)}) %collective-permute-start.6) | collective-permute-done | bytes 524320 | tf_op jit(solution)/shard_map/ppermute | solution.py:164
  102.1 0.9 collective-permute-start.9
  103.0 0.6 dynamic_slice.18
  103.6 3.1 %concatenate.6.scalars = s32[9]{0:T(128)S(1)} concatenate(s32[1]{0:T(128)} %bitcast, s32[1]{0:T(128)} %bitcast.1, s32[1]{0:T(128)} %bitcast.2, s32[1]{0:T(128)} %bitcast.3, s32[1]{0:T(128)} %dynamic_slice.18, s32[1]{0:T(128)} %get-tuple-element.16, s32[1]{0:T(128)} %get-tuple-element.15, s32[1]{0:T(128)} %get-tuple-element.14, s32[1]{0:T(128)} %get-tuple-element.17), dimensions={0} | concatenate | bytes 72 | tf_op jit(solution)/shard_map/concatenate | solution.py:188
  106.7 1.0 copy-done.2
  107.6 0.9 copy-done.4
  108.6 0.9 copy-done.6
  109.5 0.9 copy-done.8
  110.5 0.9 copy-done.10
  111.5 0.9 copy-done.12
  112.4 0.9 copy-done.14
  113.3 0.2 shard_map.57.refs_7_.refs_5_
  113.6 1.1 all-to-all-done.1.refs_6_.refs_4_
  114.7 0.0 collective-permute-done.18.refs_3_
  114.7 6.6 %shard_map.58.refs_6_ = f32[4,256,256]{2,1,0:T(8,128)S(1)} custom-call(s32[9]{0:T(128)S(1)} %concatenate.6.scalars, bf16[4,2,256,256]{3,2,1,0:T(8,128)(2,1)} %shard_map.56.refs_0_, bf16[4,2,256,256]{3,2,1,0:T(8,128)(2,1)} %collective-permute-done.5.refs_1_, bf16[4,2,256,256]{3,2,1,0:T(8,128)(2,1)} %collective-permute-done.7.refs_2_, ...), custom_call_target="tpu_custom_call" | custom-call | tf_op jit(solution)/shard_map/pallas_call | solution.py:111
  121.3 2.9 %shard_map.59 = bf16[8,4,32,256]{3,2,1,0:T(8,128)(2,1)S(1)} custom-call(s32[9]{0:T(128)S(1)} %concatenate.6.scalars, bf16[2,2,256,256]{3,2,1,0:T(8,128)(2,1)} %collective-permute-done.6.refs_0_, bf16[2,2,256,256]{3,2,1,0:T(8,128)(2,1)S(1)} %collective-permute-done.8.refs_1_, bf16[2,2,256,256]{3,2,1,0:T(8,128)(2,1)} %collective-permute-done.9.refs_2_, ...), custom_call_target="tpu_custom_call" | custom-call | tf_op jit(solution)/shard_map/pallas_call | solution.py:111
  124.2 20.9 %all_to_all.15 = bf16[8,4,32,256]{3,2,1,0:T(8,128)(2,1)S(1)} all-to-all(bf16[8,4,32,256]{3,2,1,0:T(8,128)(2,1)S(1)} %shard_map.59), channel_id=1, replica_groups=mesh['blk'=32,'mpo'=8] {'mpo'}, dimensions={0} | all-to-all | bytes 1048576 | tf_op jit(solution)/shard_map/all_to_all | solution.py:203
  145.1 0.8 copy.6
  (31 shorter events, 0.1 us)
Async XLA Ops:
  0.0 15.0 %copy-start.16 = (bf16[2,256,256]{2,1,0:T(8,128)(2,1)S(1)}, bf16[2,256,256]{2,1,0:T(8,128)(2,1)}, u32[]{:S(2)}) copy-start(bf16[2,256,256]{2,1,0:T(8,128)(2,1)} %param.6) | copy-start | bytes 786436
  3.4 47.1 %copy-start = (bf16[2,256,256]{2,1,0:T(8,128)(2,1)S(1)}, bf16[2,256,256]{2,1,0:T(8,128)(2,1)}, u32[]{:S(2)}) copy-start(bf16[2,256,256]{2,1,0:T(8,128)(2,1)} %refs_0_.1) | copy-start | bytes 786436
  6.2 96.8 %copy-start.15 = (s32[32]{0:T(128)S(1)}, s32[32]{0:T(128)}, u32[]{:S(2)}) copy-start(s32[32]{0:T(128)} %param.9) | copy-start | bytes 388
  6.2 21.6 %all-to-all-start = ((bf16[32,32,256]{2,1,0:T(8,128)(2,1)}), bf16[32,32,256]{2,1,0:T(8,128)(2,1)}, u32[]{:S(2)}, u32[]{:S(2)}) async-start(bf16[32,32,256]{2,1,0:T(8,128)(2,1)} %shard_map.55), calls=%async_computation | async-start | bytes 1048576 | tf_op jit(solution)/shard_map/all_to_all | solution.py:148
  15.0 12.8 %collective-permute-start = (bf16[2,256,256]{2,1,0:T(8,128)(2,1)S(1)}, bf16[2,256,256]{2,1,0:T(8,128)(2,1)S(1)}, u32[]{:S(2)}, u32[]{:S(2)}) collective-permute-start(bf16[2,256,256]{2,1,0:T(8,128)(2,1)S(1)} %copy-done.16), channel_id=1, source_target_pairs={{0,0},{1,8},{2,16},{3,24},{4,32},{5,40},{6,48},{7,56},{8,4},{9,12}... | collective-permute-start | bytes 786440 | tf_op jit(solution)/shard_map/ppermute | solution.py:143
  27.7 6.7 %collective-permute-start.1 = (bf16[2,256,256]{2,1,0:T(8,128)(2,1)S(1)}, bf16[2,256,256]{2,1,0:T(8,128)(2,1)S(1)}, u32[]{:S(2)}, u32[]{:S(2)}) collective-permute-start(bf16[2,256,256]{2,1,0:T(8,128)(2,1)S(1)} %collective-permute-done.refs_0_), channel_id=1, source_target_pairs={{0,16},{8,72},{16,32},{24,88},{32,48},{40,104},{48,0},{56,120},{64... | collective-permute-start | bytes 786440 | tf_op jit(solution)/shard_map/ppermute | solution.py:152
  29.4 5.3 %collective-permute-start.2 = (bf16[2,256,256]{2,1,0:T(8,128)(2,1)S(1)}, bf16[2,256,256]{2,1,0:T(8,128)(2,1)S(1)}, u32[]{:S(2)}, u32[]{:S(2)}) collective-permute-start(bf16[2,256,256]{2,1,0:T(8,128)(2,1)S(1)} %collective-permute-done.refs_0_), channel_id=1, source_target_pairs={{0,48},{8,200},{16,0},{24,216},{32,16},{40,232},{48,32},{56,248},{... | collective-permute-start | bytes 786440 | tf_op jit(solution)/shard_map/ppermute | solution.py:153
  34.4 5.4 %collective-permute-start.3 = (bf16[1,256,256]{2,1,0:T(8,128)(2,1)S(1)}, bf16[1,256,256]{2,1,0:T(8,128)(2,1)S(1)}, u32[]{:S(2)}, u32[]{:S(2)}) collective-permute-start(bf16[1,256,256]{2,1,0:T(8,128)(2,1)S(1)} %slice.16), channel_id=1, source_target_pairs={{0,16},{8,72},{16,32},{24,88},{32,48},{40,104},{48,0},{56,120},{64... | collective-permute-start | bytes 393224 | tf_op jit(solution)/shard_map/ppermute | solution.py:154
  34.7 5.1 %collective-permute-start.4 = (bf16[1,256,256]{2,1,0:T(8,128)(2,1)S(1)}, bf16[1,256,256]{2,1,0:T(8,128)(2,1)S(1)}, u32[]{:S(2)}, u32[]{:S(2)}) collective-permute-start(bf16[1,256,256]{2,1,0:T(8,128)(2,1)S(1)} %slice.17), channel_id=1, source_target_pairs={{0,48},{8,200},{16,0},{24,216},{32,16},{40,232},{48,32},{56,248},{... | collective-permute-start | bytes 393224 | tf_op jit(solution)/shard_map/ppermute | solution.py:155
  40.9 41.3 %collective-permute-start.7 = (bf16[4,2,256,256]{3,2,1,0:T(8,128)(2,1)}, bf16[4,2,256,256]{3,2,1,0:T(8,128)(2,1)}, u32[]{:S(2)}, u32[]{:S(2)}) collective-permute-start(bf16[4,2,256,256]{3,2,1,0:T(8,128)(2,1)} %shard_map.56.refs_0_), channel_id=1, source_target_pairs={{0,192},{8,56},{16,208},{24,8},{32,224},{40,24},{48,240},{56,40},{... | collective-permute-start | bytes 3145736 | tf_op jit(solution)/shard_map/ppermute | solution.py:163
  50.5 38.9 %collective-permute-start.5 = (bf16[4,2,256,256]{3,2,1,0:T(8,128)(2,1)}, bf16[4,2,256,256]{3,2,1,0:T(8,128)(2,1)}, u32[]{:S(2)}, u32[]{:S(2)}) collective-permute-start(bf16[4,2,256,256]{3,2,1,0:T(8,128)(2,1)} %shard_map.56.refs_0_), channel_id=1, source_target_pairs={{0,64},{8,24},{16,80},{24,40},{32,96},{40,56},{48,112},{56,8},{64,... | collective-permute-start | bytes 3145736 | tf_op jit(solution)/shard_map/ppermute | solution.py:162
  50.5 9.8 %collective-permute-start.14 = (bf16[2,256,256]{2,1,0:T(8,128)(2,1)S(1)}, bf16[2,256,256]{2,1,0:T(8,128)(2,1)S(1)}, u32[]{:S(2)}, u32[]{:S(2)}) collective-permute-start(bf16[2,256,256]{2,1,0:T(8,128)(2,1)S(1)} %copy-done), channel_id=1, source_target_pairs={{0,1},{1,2},{2,3},{3,4},{4,5},{5,6},{6,7},{7,0},{8,9},{9,10},{10,1... | collective-permute-start | bytes 786440 | tf_op jit(solution)/shard_map/ppermute | solution.py:178
  50.6 10.4 %collective-permute-start.11 = (bf16[2,256,256]{2,1,0:T(8,128)(2,1)S(1)}, bf16[2,256,256]{2,1,0:T(8,128)(2,1)S(1)}, u32[]{:S(2)}, u32[]{:S(2)}) collective-permute-start(bf16[2,256,256]{2,1,0:T(8,128)(2,1)S(1)} %copy-done), channel_id=1, source_target_pairs={{0,7},{1,0},{2,1},{3,2},{4,3},{5,4},{6,5},{7,6},{8,15},{9,8},{10,9... | collective-permute-start | bytes 786440 | tf_op jit(solution)/shard_map/ppermute | solution.py:180
  60.3 6.8 %collective-permute-start.15 = (bf16[2,256,256]{2,1,0:T(8,128)(2,1)S(1)}, bf16[2,256,256]{2,1,0:T(8,128)(2,1)S(1)}, u32[]{:S(2)}, u32[]{:S(2)}) collective-permute-start(bf16[2,256,256]{2,1,0:T(8,128)(2,1)S(1)} %collective-permute-done.14.refs_7_), channel_id=1, source_target_pairs={{0,1},{1,2},{2,3},{3,4},{4,5},{5,6},{6,7},{7,0},{8,9},{9,10},{10,1... | collective-permute-start | bytes 786440 | tf_op jit(solution)/shard_map/ppermute | solution.py:178
  60.3 0.7 copy-start.1
  61.0 6.8 %collective-permute-start.12 = (bf16[2,256,256]{2,1,0:T(8,128)(2,1)S(1)}, bf16[2,256,256]{2,1,0:T(8,128)(2,1)S(1)}, u32[]{:S(2)}, u32[]{:S(2)}) collective-permute-start(bf16[2,256,256]{2,1,0:T(8,128)(2,1)S(1)} %collective-permute-done.11.refs_1_), channel_id=1, source_target_pairs={{0,7},{1,0},{2,1},{3,2},{4,3},{5,4},{6,5},{7,6},{8,15},{9,8},{10,9... | collective-permute-start | bytes 786440 | tf_op jit(solution)/shard_map/ppermute | solution.py:180
  63.7 0.7 copy-start.3
  67.2 6.6 %collective-permute-start.16 = (bf16[2,256,256]{2,1,0:T(8,128)(2,1)S(1)}, bf16[2,256,256]{2,1,0:T(8,128)(2,1)S(1)}, u32[]{:S(2)}, u32[]{:S(2)}) collective-permute-start(bf16[2,256,256]{2,1,0:T(8,128)(2,1)S(1)} %collective-permute-done.15.refs_6_), channel_id=1, source_target_pairs={{0,1},{1,2},{2,3},{3,4},{4,5},{5,6},{6,7},{7,0},{8,9},{9,10},{10,1... | collective-permute-start | bytes 786440 | tf_op jit(solution)/shard_map/ppermute | solution.py:178
  67.2 0.7 copy-start.5
  67.9 22.7 %collective-permute-start.13 = (bf16[2,256,256]{2,1,0:T(8,128)(2,1)S(1)}, bf16[2,256,256]{2,1,0:T(8,128)(2,1)S(1)}, u32[]{:S(2)}, u32[]{:S(2)}) collective-permute-start(bf16[2,256,256]{2,1,0:T(8,128)(2,1)S(1)} %collective-permute-done.12.refs_2_), channel_id=1, source_target_pairs={{0,7},{1,0},{2,1},{3,2},{4,3},{5,4},{6,5},{7,6},{8,15},{9,8},{10,9... | collective-permute-start | bytes 786440 | tf_op jit(solution)/shard_map/ppermute | solution.py:180
  70.5 0.7 copy-start.7
  73.8 16.8 %copy-start.9 = (bf16[2,256,256]{2,1,0:T(8,128)(2,1)}, bf16[2,256,256]{2,1,0:T(8,128)(2,1)S(1)}, u32[]{:S(2)}) copy-start(bf16[2,256,256]{2,1,0:T(8,128)(2,1)S(1)} %collective-permute-done.16.refs_5_) | copy-start | bytes 786436
  73.8 18.0 %collective-permute-start.17 = (bf16[2,256,256]{2,1,0:T(8,128)(2,1)S(1)}, bf16[2,256,256]{2,1,0:T(8,128)(2,1)S(1)}, u32[]{:S(2)}, u32[]{:S(2)}) collective-permute-start(bf16[2,256,256]{2,1,0:T(8,128)(2,1)S(1)} %collective-permute-done.16.refs_5_), channel_id=1, source_target_pairs={{0,1},{1,2},{2,3},{3,4},{4,5},{5,6},{6,7},{7,0},{8,9},{9,10},{10,1... | collective-permute-start | bytes 786440 | tf_op jit(solution)/shard_map/ppermute | solution.py:178
  73.8 40.9 %collective-permute-start.18 = (bf16[4,2,256,256]{3,2,1,0:T(8,128)(2,1)}, bf16[4,2,256,256]{3,2,1,0:T(8,128)(2,1)}, u32[]{:S(2)}, u32[]{:S(2)}) collective-permute-start(bf16[4,2,256,256]{3,2,1,0:T(8,128)(2,1)} %shard_map.56.refs_0_), channel_id=1, source_target_pairs={{0,8},{8,0},{16,24},{24,16},{32,40},{40,32},{48,56},{56,48},{64,72... | collective-permute-start | bytes 3145736 | tf_op jit(solution)/shard_map/ppermute | solution.py:170
  83.3 13.5 %collective-permute-start.8 = (bf16[2,2,256,256]{3,2,1,0:T(8,128)(2,1)S(1)}, bf16[2,2,256,256]{3,2,1,0:T(8,128)(2,1)S(1)}, u32[]{:S(2)}, u32[]{:S(2)}) collective-permute-start(bf16[2,2,256,256]{3,2,1,0:T(8,128)(2,1)S(1)} %slice.19), channel_id=1, source_target_pairs={{0,192},{8,56},{16,208},{24,8},{32,224},{40,24},{48,240},{56,40},{... | collective-permute-start | bytes 1572872 | tf_op jit(solution)/shard_map/ppermute | solution.py:165
  89.5 25.2 %collective-permute-start.19 = (bf16[4,2,256,256]{3,2,1,0:T(8,128)(2,1)}, bf16[4,2,256,256]{3,2,1,0:T(8,128)(2,1)}, u32[]{:S(2)}, u32[]{:S(2)}) collective-permute-start(bf16[4,2,256,256]{3,2,1,0:T(8,128)(2,1)} %collective-permute-done.5.refs_1_), channel_id=1, source_target_pairs={{0,8},{8,0},{16,24},{24,16},{32,40},{40,32},{48,56},{56,48},{64,72... | collective-permute-start | bytes 3145736 | tf_op jit(solution)/shard_map/ppermute | solution.py:170
  90.6 0.7 copy-start.11
  91.3 23.4 %collective-permute-start.20 = (bf16[4,2,256,256]{3,2,1,0:T(8,128)(2,1)}, bf16[4,2,256,256]{3,2,1,0:T(8,128)(2,1)}, u32[]{:S(2)}, u32[]{:S(2)}) collective-permute-start(bf16[4,2,256,256]{3,2,1,0:T(8,128)(2,1)} %collective-permute-done.7.refs_2_), channel_id=1, source_target_pairs={{0,8},{8,0},{16,24},{24,16},{32,40},{40,32},{48,56},{56,48},{64,72... | collective-permute-start | bytes 3145736 | tf_op jit(solution)/shard_map/ppermute | solution.py:170
  91.8 0.7 copy-start.13
  92.5 9.6 %collective-permute-start.6 = (bf16[2,2,256,256]{3,2,1,0:T(8,128)(2,1)S(1)}, bf16[2,2,256,256]{3,2,1,0:T(8,128)(2,1)}, u32[]{:S(2)}, u32[]{:S(2)}) collective-permute-start(bf16[2,2,256,256]{3,2,1,0:T(8,128)(2,1)S(1)} %slice.18), channel_id=1, source_target_pairs={{0,64},{8,24},{16,80},{24,40},{32,96},{40,56},{48,112},{56,8},{64,... | collective-permute-start | bytes 1572872 | tf_op jit(solution)/shard_map/ppermute | solution.py:164
  92.5 22.2 %all-to-all-start.1 = ((bf16[8,4,32,256]{3,2,1,0:T(8,128)(2,1)}), bf16[8,4,32,256]{3,2,1,0:T(8,128)(2,1)S(1)}, u32[]{:S(2)}, u32[]{:S(2)}) async-start(bf16[8,4,32,256]{3,2,1,0:T(8,128)(2,1)} %bitcast.5), calls=%async_computation.1 | async-start | bytes 1048576 | tf_op jit(solution)/shard_map/all_to_all | solution.py:166
  96.7 24.5 %collective-permute-start.10 = (bf16[2,2,256,256]{3,2,1,0:T(8,128)(2,1)S(1)}, bf16[2,2,256,256]{3,2,1,0:T(8,128)(2,1)}, u32[]{:S(2)}, u32[]{:S(2)}) collective-permute-start(bf16[2,2,256,256]{3,2,1,0:T(8,128)(2,1)S(1)} %collective-permute-done.8.refs_1_), channel_id=1, source_target_pairs={{0,8},{8,0},{16,24},{24,16},{32,40},{40,32},{48,56},{56,48},{64,72... | collective-permute-start | bytes 1572872 | tf_op jit(solution)/shard_map/ppermute | solution.py:172
  102.1 19.1 %collective-permute-start.9 = (bf16[2,2,256,256]{3,2,1,0:T(8,128)(2,1)}, bf16[2,2,256,256]{3,2,1,0:T(8,128)(2,1)}, u32[]{:S(2)}, u32[]{:S(2)}) collective-permute-start(bf16[2,2,256,256]{3,2,1,0:T(8,128)(2,1)} %collective-permute-done.6.refs_0_), channel_id=1, source_target_pairs={{0,8},{8,0},{16,24},{24,16},{32,40},{40,32},{48,56},{56,48},{64,72... | collective-permute-start | bytes 1572872 | tf_op jit(solution)/shard_map/ppermute | solution.py:172
  106.7 1.0 copy-start.2
  107.6 0.9 copy-start.4
  108.6 0.9 copy-start.6
  109.5 0.9 copy-start.8
  110.5 0.9 copy-start.10
  111.4 0.9 copy-start.12
  112.4 0.9 copy-start.14

commit v4 on v3

v4 whole, which is shorter than its diff:
```python
import functools

import jax
import jax.numpy as jnp
from jax import lax
from jax.experimental import pallas as pl
from jax.experimental.pallas import tpu as pltpu
from jax.sharding import PartitionSpec as P

MIB = 1024 * 1024
VMEM_LIMIT = 60
SIDE = 4
OFFSETS = (0, SIDE - 1, 1, 2)


def place(y, x, core):
    return ((y % SIDE) * SIDE + x % SIDE) * 2 + core


def stack_kernel(places, *refs):
    inputs, out, sems = refs[: len(places)], refs[-2], refs[-1]
    copies = []
    for i, (ref, (at, lo, hi)) in enumerate(zip(inputs, places)):
        copies.append(pltpu.make_async_copy(ref, out.at[at, lo:hi], sems.at[i]))
    for copy in copies:
        copy.start()
    for copy in copies:
        copy.wait()


def stack(pieces, places, shape):
    return pl.pallas_call(
        functools.partial(stack_kernel, places),
        out_shape=jax.ShapeDtypeStruct(shape, pieces[0].dtype),
        in_specs=[pl.BlockSpec(memory_space=pl.ANY)] * len(pieces),
        out_specs=pl.BlockSpec(memory_space=pl.ANY),
        scratch_shapes=[pltpu.SemaphoreType.DMA((len(pieces),))],
        compiler_params=pltpu.CompilerParams(vmem_limit_bytes=MIB),
    )(*pieces)


def coordinates():
    sector, rank = lax.axis_index("blk"), lax.axis_index("mpo")
    return sector, rank, sector % 2, sector // 2 % SIDE, sector // (2 * SIDE)


def rows_kernel(left_sizes, right_sizes, psi_ref, out_ref, held, sem):
    sector, rank, _, _, _ = coordinates()
    sectors, rows, right_dim = out_ref.shape
    first = pl.multiple_of(rank * rows, rows)
    copy = pltpu.make_async_copy(psi_ref.at[pl.ds(first, rows)], held, sem)
    copy.start()
    copy.wait()
    row = first + lax.broadcasted_iota(jnp.int32, (rows, right_dim), 0)
    col = lax.broadcasted_iota(jnp.int32, (rows, right_dim), 1)
    own_left = left_sizes[sector]
    for at in range(sectors):
        g, y = at // SIDE, at % SIDE
        b = place(y, g % SIDE, g // SIDE)
        block = held[:, b * right_dim : (b + 1) * right_dim].astype(jnp.float32)
        inside = jnp.logical_and(row < own_left, col < right_sizes[b])
        out_ref[at] = jnp.where(inside, block, 0.0).astype(out_ref.dtype)


SMEM = pl.BlockSpec(memory_space=pltpu.SMEM)
VMEM = pl.BlockSpec(memory_space=pltpu.VMEM)


def split_rows(wavefunction, left_sizes, right_sizes, ranks):
    left_dim, columns = wavefunction.shape
    sectors = left_sizes.shape[0]
    rows, right_dim = left_dim // ranks, columns // sectors
    return pl.pallas_call(
        rows_kernel,
        out_shape=jax.ShapeDtypeStruct((sectors, rows, right_dim), wavefunction.dtype),
        in_specs=[SMEM, SMEM, pl.BlockSpec(memory_space=pl.ANY)],
        out_specs=VMEM,
        scratch_shapes=[pltpu.VMEM((rows, columns), wavefunction.dtype), pltpu.SemaphoreType.DMA],
        compiler_params=pltpu.CompilerParams(vmem_limit_bytes=60 * MIB),
    )(left_sizes, right_sizes, wavefunction)


def fetch(refs, held, sems, first):
    copies = [pltpu.make_async_copy(r, h, sems.at[first + i]) for i, (r, h) in enumerate(zip(refs, held))]
    for copy in copies:
        copy.start()
    return copies


def add_blocks(pieces, refs, total_in, total, held, psi_held, right_held, sems):
    _, rank, core, x0, y0 = coordinates()
    ranks, parts, rows, right_dim = psi_held.shape
    blocks, psi_ref, rights = refs[: len(pieces)], refs[len(pieces)], refs[len(pieces) + 1 :]
    needed = fetch((psi_ref, *rights), (psi_held, *(right_held.at[i] for i in range(ranks))), sems, 0)
    if total_in is not None:
        needed += fetch((total_in,), (total,), sems, len(needed))
    coming = fetch(blocks, [held.at[i] for i in range(len(pieces))], sems, len(needed))
    if total_in is None:
        total[...] = jnp.zeros_like(total)
    for copy in needed:
        copy.wait()
    for i, (sibling, far, first) in enumerate(pieces):
        tree = 1 - core if sibling else core
        coming[i].wait()
        _, count, _, left_dim, inner = held.shape
        for k in range(count):
            near = OFFSETS[first + k]
            y = jnp.where(tree == 0, y0 + far, y0 + near) & (SIDE - 1)
            x = jnp.where(tree == 0, x0 + near, x0 + far) & (SIDE - 1)
            at = (2 * x + tree - rank) & (ranks - 1)
            psi = psi_held[:, pl.ds(y, 1)].reshape(ranks * rows, right_dim)
            block = held[i, k].reshape(2 * left_dim, inner)
            both = jnp.dot(block, psi, preferred_element_type=jnp.float32).astype(psi.dtype)
            term = jnp.dot(both[:left_dim], right_held[at, 0], preferred_element_type=jnp.float32)
            term += jnp.dot(both[left_dim:], right_held[at, 1], preferred_element_type=jnp.float32)
            total[y] += term


def first_kernel(pieces, *refs):
    refs, (total, held, psi_held, right_held, sems) = refs[:-5], refs[-5:]
    add_blocks(pieces, refs, None, total, held, psi_held, right_held, sems)


def last_kernel(pieces, left_sizes, right_sizes, total_in, *refs):
    refs, (out_ref, total, held, psi_held, right_held, sems) = refs[:-6], refs[-6:]
    add_blocks(pieces, refs, total_in, total, held, psi_held, right_held, sems)
    sector, rank, _, _, _ = coordinates()
    own_right = right_sizes[sector]
    ranks, parts, rows, right_dim = out_ref.shape
    row = lax.broadcasted_iota(jnp.int32, (ranks * rows, right_dim), 0)
    col = lax.broadcasted_iota(jnp.int32, (ranks * rows, right_dim), 1)
    for y in range(parts):
        own_left = left_sizes[2 * SIDE * y + rank % SIDE * 2 + rank // SIDE]
        inside = jnp.logical_and(row < own_left, col < own_right)
        block = jnp.where(inside, total[y], 0.0).astype(out_ref.dtype)
        out_ref[:, y] = block.reshape(ranks, rows, right_dim)


def call(kernel, pieces, ready, blocks, psi, rights, shape, scratch):
    dtype = psi.dtype
    scratch = scratch + [
        pltpu.VMEM((len(pieces), *blocks[0].shape), dtype),
        pltpu.VMEM(psi.shape, dtype),
        pltpu.VMEM((len(rights), *rights[0].shape), dtype),
        pltpu.SemaphoreType.DMA((len(pieces) + len(rights) + 2,)),
    ]
    anywhere = pl.BlockSpec(memory_space=pl.ANY)
    others = (*blocks, psi, *rights)
    return pl.pallas_call(
        functools.partial(kernel, pieces),
        out_shape=shape,
        in_specs=[SMEM, SMEM, anywhere][: len(ready)] + [anywhere] * len(others),
        out_specs=VMEM,
        scratch_shapes=scratch,
        compiler_params=pltpu.CompilerParams(vmem_limit_bytes=VMEM_LIMIT * MIB),
    )(*ready, *others)


def together(*values):
    return lax.optimization_barrier(values)


def local(wavefunction, left_env, right_env, left_sizes, right_sizes):
    sectors, ranks = lax.axis_size("blk"), lax.axis_size("mpo")
    left_dim, right_dim = left_env.shape[2], right_env.shape[2]
    rows = left_dim // ranks
    spots = [(y, x, c) for y in range(SIDE) for x in range(SIDE) for c in range(2)]

    def step(second, by):
        pairs = []
        for y, x, c in spots:
            along_x = (c == 0) != second
            to = place(y, x + by, c) if along_x else place(y + by, x, c)
            pairs.append((place(y, x, c), to))
        return pairs

    def near_step(block, by):
        return lax.ppermute(block, "blk", step(False, by))

    def far_step(block, by):
        return lax.ppermute(block, "blk", step(True, by))

    def swap(block):
        return lax.ppermute(block, "blk", [(i, i ^ 1) for i in range(sectors)])

    def up(block):
        return lax.ppermute(block, "mpo", [(z, (z + 1) % ranks) for z in range(ranks)])

    def down(block):
        return lax.ppermute(block, "mpo", [(z, (z - 1) % ranks) for z in range(ranks)])

    turn = [
        (place(y, x, c) * ranks + z, place(y, z // 2, z % 2) * ranks + x + SIDE * c)
        for y, x, c in spots
        for z in range(ranks)
    ]
    own = lax.ppermute(left_env, ("blk", "mpo"), turn)
    up1, down1 = up(right_env), down(right_env)
    mine = split_rows(wavefunction, left_sizes, right_sizes, ranks)
    order = [place(y, g % SIDE, g // SIDE) for g in range(ranks) for y in range(SIDE)]
    own, up1, down1, mine = together(own, up1, down1, mine)
    spread = lax.all_to_all(mine, "blk", 0, 0, axis_index_groups=[order])
    spread = spread.reshape(ranks, SIDE, rows, right_dim)

    below, above = near_step(own, 1), near_step(own, -1)
    up2, down2 = up(up1), down(down1)
    below, above, up2, down2 = together(below, above, up2, down2)

    two = near_step(below, 1)
    line_a = stack((own, below), ((0, 0, 2), (1, 0, 2)), (2, *left_env.shape))
    a_below, a_above = far_step(line_a, 1), far_step(line_a, -1)
    up3, down3 = up(up2), down(down2)
    two, up3, down3 = together(two, up3, down3)

    line_b = stack((above, two), ((0, 0, 2), (1, 0, 2)), (2, *left_env.shape))
    b_below, b_above = far_step(line_b, 1), far_step(line_b, -1)
    up4 = up(up3)
    line_b, a_below, a_above, spread = together(line_b, a_below, a_above, spread)
    a_two = far_step(a_below, 1)
    psi = lax.all_to_all(spread, "mpo", 0, 0)
    b_two = far_step(b_above, -1)

    rights = (right_env, down1, down2, down3, up4, up3, up2, up1)
    early = (line_a, line_b, a_below, a_above, b_below, b_above)
    early += tuple(swap(block) for block in early)
    late = (a_two, b_two)
    late += tuple(swap(block) for block in late)
    total = jax.ShapeDtypeStruct((SIDE, left_dim, right_dim), jnp.float32)
    places = ((0, 0), (0, 2), (SIDE - 1, 0), (1, 0), (SIDE - 1, 2), (1, 2))
    pieces = tuple((s, *p) for s in (False, True) for p in places)
    begun = call(first_kernel, pieces, (), early, psi, rights, total, [])
    pieces = tuple((s, 2, k) for s in (False, True) for k in (0, 2))
    done = call(
        last_kernel,
        pieces,
        (left_sizes, right_sizes, begun),
        late,
        psi,
        rights,
        jax.ShapeDtypeStruct((ranks, SIDE, rows, right_dim), wavefunction.dtype),
        [pltpu.VMEM(total.shape, total.dtype)],
    )

    out = lax.all_to_all(done, "mpo", 0, 0).reshape(2, SIDE, SIDE, rows, right_dim)
    return out.transpose(2, 1, 0, 3, 4).reshape(sectors, rows, right_dim)


def solution(mesh):
    placed = (P("blk", None), P("mpo", "blk", None), P("mpo", "blk", None), P(), P())
    return jax.shard_map(
        local, mesh=mesh, in_specs=placed, out_specs=P(None, "mpo", "blk"), check_vma=False
    )
```

time: 147 us -> 136 us (0.925)
  local copies, waits for them, and re-layouts: 19.1 us -> 2.79 us
  waiting for transfers between devices: 25.4 us -> 37.4 us
  starting transfers between devices: 65 us -> 56.1 us
  Pallas kernels: 13.5 us -> 19.4 us
  blocking collectives: 20.9 us -> 18.8 us
  other arithmetic: 1.92 us -> 0 us
    ppermute x20 -> x24, starting transfers between devices: 43 us -> 31.8 us  [the longest x6 13.8 us: far_step(): return lax.ppermute(block, 'blk', step(True, by))]
    all_to_all x1, waiting for transfers between devices: 1.1 us -> 11.3 us  [local(): psi = lax.all_to_all(spread, 'mpo', 0, 0)]
    all_to_all x1, waiting for transfers between devices: 0.01 us -> 9.75 us  [local(): spread = lax.all_to_all(mine, 'blk', 0, 0, axis_index_groups=[order])]
    unnamed x34 -> x26, local copies, waits for them, and re-layouts: 10.9 us -> 1.96 us
    pallas_call x2, Pallas kernels: 9.48 us -> 16.6 us  [call(): pl.pallas_call(functools.partial(kernel, pieces), out_shape=shape, in_spe...]
    ppermute x20 -> x24, waiting for transfers between devices: 20.5 us -> 16.3 us  [the longest x4 12.5 us: up(): lax.ppermute(block, 'mpo', [(z, (z + 1) % ranks) for z in range(ranks)])]
    ppermute x1, waiting for transfers between devices: 3.74 us -> 0.01 us  [local(): own = lax.ppermute(left_env, ('blk', 'mpo'), turn)]
    concatenate x1 -> x0, local copies, waits for them, and re-layouts: 3.06 us -> none  [local(): jnp.concatenate([jnp.stack([core, x0, y0, rank, right_sizes[sector]]), gr...]
  transfers between devices with their start and end apart: 23 -> 27, of which waited for: 8 -> 9; matrix products, arithmetic and copies ran while one was open for 4% -> 0% of each run, Pallas kernels for 5% -> 10%
where the time goes in v4:
time: 136 us; the launch traced here: 135 us
  starting transfers between devices  56.1 us (41%)
  waiting for transfers between devices  37.4 us (28%)
  Pallas kernels  19.4 us (14%)
  blocking collectives  18.8 us (14%)
  local copies, waits for them, and re-layouts  2.79 us (2%)
    all_to_all x1, blocking collectives, local(): lax.all_to_all(done, 'mpo', 0, 0).reshape(2, SIDE, SIDE, rows, right_dim)  18.8 us
    pallas_call x2, Pallas kernels, call(): pl.pallas_call(functools.partial(kernel, pieces), out_shape=shape, in_spe...  16.6 us
    ppermute x6, starting transfers between devices, far_step(): return lax.ppermute(block, 'blk', step(True, by))  13.8 us
    ppermute x4, waiting for transfers between devices, up(): lax.ppermute(block, 'mpo', [(z, (z + 1) % ranks) for z in range(ranks)])  12.5 us
    all_to_all x1, waiting for transfers between devices, local(): psi = lax.all_to_all(spread, 'mpo', 0, 0)  11.3 us
    ppermute x1, starting transfers between devices, local(): own = lax.ppermute(left_env, ('blk', 'mpo'), turn)  10.2 us
    all_to_all x1, starting transfers between devices, local(): spread = lax.all_to_all(mine, 'blk', 0, 0, axis_index_groups=[order])  9.8 us
    all_to_all x1, waiting for transfers between devices, local(): spread = lax.all_to_all(mine, 'blk', 0, 0, axis_index_groups=[order])  9.75 us
  transfers between devices with their start and end apart: 27, of which 9 were waited for; matrix products, arithmetic and copies ran while one was open for 0% of the time, Pallas kernels for 10%

profile of v4, /device:TPU:1, one launch (start us, length us, event | category | flops | bytes accessed | tf_op | source)
XLA Modules:
  0.0 134.7 jit_solution(10200818790085005321)
XLA Ops:
  0.0 10.2 %collective-permute-start = (bf16[2,256,256]{2,1,0:T(8,128)(2,1)}, bf16[2,256,256]{2,1,0:T(8,128)(2,1)S(1)}, u32[]{:S(2)}, u32[]{:S(2)}) collective-permute-start(bf16[2,256,256]{2,1,0:T(8,128)(2,1)} %param.6), channel_id=1, source_target_pairs={{0,0},{1,8},{2,16},{3,24},{4,32},{5,40},{6,48},{7,56},{8,4},{9,12}... | collective-permute-start | bytes 786440 | tf_op jit(solution)/shard_map/ppermute | solution.py:197
  10.2 0.1 collective-permute-start.1
  10.3 2.7 %collective-permute-start.2 = (bf16[2,256,256]{2,1,0:T(8,128)(2,1)}, bf16[2,256,256]{2,1,0:T(8,128)(2,1)S(1)}, u32[]{:S(2)}, u32[]{:S(2)}) collective-permute-start(bf16[2,256,256]{2,1,0:T(8,128)(2,1)} %refs_5_.1), channel_id=1, source_target_pairs={{0,7},{1,0},{2,1},{3,2},{4,3},{5,4},{6,5},{7,6},{8,15},{9,8},{10,9... | collective-permute-start | bytes 786440 | tf_op jit(solution)/shard_map/ppermute | solution.py:190
  13.0 2.6 %shard_map.55 = bf16[32,32,256]{2,1,0:T(8,128)(2,1)} custom-call(s32[32]{0:T(128)} %left_sizes.3, s32[32]{0:T(128)} %right_sizes.3, bf16[256,8192]{1,0:T(8,128)(2,1)} %psi_ref.1), custom_call_target="tpu_custom_call" | custom-call | tf_op jit(solution)/shard_map/pallas_call | solution.py:73
  15.6 0.0 collective-permute-done.refs_0_
  15.6 9.8 %collective-permute-done.1.refs_20_.refs_12_ = bf16[2,256,256]{2,1,0:T(8,128)(2,1)S(1)} collective-permute-done((bf16[2,256,256]{2,1,0:T(8,128)(2,1)}, bf16[2,256,256]{2,1,0:T(8,128)(2,1)S(1)}, u32[]{:S(2)}, u32[]{:S(2)}) %collective-permute-start.1) | collective-permute-done | bytes 262176 | tf_op jit(solution)/shard_map/ppermute | solution.py:187
  25.4 0.0 collective-permute-done.2.refs_14_.refs_6_
  25.4 1.4 %collective-permute-start.3 = (bf16[2,256,256]{2,1,0:T(8,128)(2,1)S(1)}, bf16[2,256,256]{2,1,0:T(8,128)(2,1)S(1)}, u32[]{:S(2)}, u32[]{:S(2)}) collective-permute-start(bf16[2,256,256]{2,1,0:T(8,128)(2,1)S(1)} %collective-permute-done.refs_0_), channel_id=1, source_target_pairs={{0,16},{8,72},{16,32},{24,88},{32,48},{40,104},{48,0},{56,120},{64... | collective-permute-start | bytes 786440 | tf_op jit(solution)/shard_map/ppermute | solution.py:178
  26.8 1.5 %collective-permute-start.4 = (bf16[2,256,256]{2,1,0:T(8,128)(2,1)S(1)}, bf16[2,256,256]{2,1,0:T(8,128)(2,1)S(1)}, u32[]{:S(2)}, u32[]{:S(2)}) collective-permute-start(bf16[2,256,256]{2,1,0:T(8,128)(2,1)S(1)} %collective-permute-done.refs_0_), channel_id=1, source_target_pairs={{0,48},{8,200},{16,0},{24,216},{32,16},{40,232},{48,32},{56,248},{... | collective-permute-start | bytes 786440 | tf_op jit(solution)/shard_map/ppermute | solution.py:178
  28.3 0.0 collective-permute-start.5
  28.3 2.7 %collective-permute-start.6 = (bf16[2,256,256]{2,1,0:T(8,128)(2,1)S(1)}, bf16[2,256,256]{2,1,0:T(8,128)(2,1)S(1)}, u32[]{:S(2)}, u32[]{:S(2)}) collective-permute-start(bf16[2,256,256]{2,1,0:T(8,128)(2,1)S(1)} %collective-permute-done.2.refs_14_.refs_6_), channel_id=1, source_target_pairs={{0,7},{1,0},{2,1},{3,2},{4,3},{5,4},{6,5},{7,6},{8,15},{9,8},{10,9... | collective-permute-start | bytes 786440 | tf_op jit(solution)/shard_map/ppermute | solution.py:190
  31.0 1.0 collective-permute-done.3.refs_1_
  32.0 0.3 collective-permute-done.4.refs_0_
  32.3 2.7 %collective-permute-done.5.refs_19_.refs_11_ = bf16[2,256,256]{2,1,0:T(8,128)(2,1)S(1)} collective-permute-done((bf16[2,256,256]{2,1,0:T(8,128)(2,1)S(1)}, bf16[2,256,256]{2,1,0:T(8,128)(2,1)S(1)}, u32[]{:S(2)}, u32[]{:S(2)}) %collective-permute-start.5) | collective-permute-done | bytes 262176 | tf_op jit(solution)/shard_map/ppermute | solution.py:187
  35.0 0.0 collective-permute-done.6.refs_15_.refs_7_
  35.1 1.9 %collective-permute-start.8 = (bf16[2,256,256]{2,1,0:T(8,128)(2,1)S(1)}, bf16[2,256,256]{2,1,0:T(8,128)(2,1)S(1)}, u32[]{:S(2)}, u32[]{:S(2)}) collective-permute-start(bf16[2,256,256]{2,1,0:T(8,128)(2,1)S(1)} %collective-permute-done.5.refs_19_.refs_11_), channel_id=1, source_target_pairs={{0,1},{1,2},{2,3},{3,4},{4,5},{5,6},{6,7},{7,0},{8,9},{9,10},{10,1... | collective-permute-start | bytes 786440 | tf_op jit(solution)/shard_map/ppermute | solution.py:187
  37.0 0.8 collective-permute-start.9
  37.8 0.0 collective-permute-start.7
  37.8 0.1 shard_map.56.refs_0_
  37.9 0.0 copy-start
  37.9 2.7 %collective-permute-start.10 = (bf16[2,2,256,256]{3,2,1,0:T(8,128)(2,1)S(1)}, bf16[2,2,256,256]{3,2,1,0:T(8,128)(2,1)}, u32[]{:S(2)}, u32[]{:S(2)}) collective-permute-start(bf16[2,2,256,256]{3,2,1,0:T(8,128)(2,1)S(1)} %shard_map.56.refs_0_), channel_id=1, source_target_pairs={{0,64},{8,24},{16,80},{24,40},{32,96},{40,56},{48,112},{56,8},{64,... | collective-permute-start | bytes 1572872 | tf_op jit(solution)/shard_map/ppermute | solution.py:181
  40.6 3.4 %collective-permute-start.11 = (bf16[2,2,256,256]{3,2,1,0:T(8,128)(2,1)S(1)}, bf16[2,2,256,256]{3,2,1,0:T(8,128)(2,1)S(1)}, u32[]{:S(2)}, u32[]{:S(2)}) collective-permute-start(bf16[2,2,256,256]{3,2,1,0:T(8,128)(2,1)S(1)} %shard_map.56.refs_0_), channel_id=1, source_target_pairs={{0,192},{8,56},{16,208},{24,8},{32,224},{40,24},{48,240},{56,40},{... | collective-permute-start | bytes 1572872 | tf_op jit(solution)/shard_map/ppermute | solution.py:181
  44.0 0.0 collective-permute-done.8.refs_18_.refs_10_
  44.0 2.4 %collective-permute-start.14 = (bf16[2,2,256,256]{3,2,1,0:T(8,128)(2,1)S(1)}, bf16[2,2,256,256]{3,2,1,0:T(8,128)(2,1)}, u32[]{:S(2)}, u32[]{:S(2)}) collective-permute-start(bf16[2,2,256,256]{3,2,1,0:T(8,128)(2,1)S(1)} %shard_map.56.refs_0_), channel_id=1, source_target_pairs={{0,8},{8,0},{16,24},{24,16},{32,40},{40,32},{48,56},{56,48},{64,72... | collective-permute-start | bytes 1572872 | tf_op jit(solution)/shard_map/ppermute | solution.py:184
  46.4 1.0 collective-permute-done.9.refs_16_.refs_8_
  47.4 0.0 collective-permute-done.7.refs_1_
  47.4 0.1 shard_map.57.refs_1_
  47.5 3.6 %collective-permute-start.13 = (bf16[2,2,256,256]{3,2,1,0:T(8,128)(2,1)S(1)}, bf16[2,2,256,256]{3,2,1,0:T(8,128)(2,1)}, u32[]{:S(2)}, u32[]{:S(2)}) collective-permute-start(bf16[2,2,256,256]{3,2,1,0:T(8,128)(2,1)S(1)} %shard_map.57.refs_1_), channel_id=1, source_target_pairs={{0,192},{8,56},{16,208},{24,8},{32,224},{40,24},{48,240},{56,40},{... | collective-permute-start | bytes 1572872 | tf_op jit(solution)/shard_map/ppermute | solution.py:181
  51.0 9.8 %all-to-all-start = ((bf16[32,32,256]{2,1,0:T(8,128)(2,1)}), bf16[32,32,256]{2,1,0:T(8,128)(2,1)}, u32[]{:S(2)}, u32[]{:S(2)}) async-start(bf16[32,32,256]{2,1,0:T(8,128)(2,1)} %shard_map.55), calls=%async_computation | async-start | bytes 1048576 | tf_op jit(solution)/shard_map/all_to_all | solution.py:202
  60.8 0.1 collective-permute-start.20
  60.9 0.0 collective-permute-done.10.refs_2_
  60.9 1.5 %collective-permute-start.12 = (bf16[2,2,256,256]{3,2,1,0:T(8,128)(2,1)S(1)}, bf16[2,2,256,256]{3,2,1,0:T(8,128)(2,1)}, u32[]{:S(2)}, u32[]{:S(2)}) collective-permute-start(bf16[2,2,256,256]{3,2,1,0:T(8,128)(2,1)S(1)} %shard_map.57.refs_1_), channel_id=1, source_target_pairs={{0,64},{8,24},{16,80},{24,40},{32,96},{40,56},{48,112},{56,8},{64,... | collective-permute-start | bytes 1572872 | tf_op jit(solution)/shard_map/ppermute | solution.py:181
  62.4 9.7 %all-to-all-done = bf16[32,32,256]{2,1,0:T(8,128)(2,1)} async-done(((bf16[32,32,256]{2,1,0:T(8,128)(2,1)}), bf16[32,32,256]{2,1,0:T(8,128)(2,1)}, u32[]{:S(2)}, u32[]{:S(2)}) %all-to-all-start) | async-done | bytes 524320 | tf_op jit(solution)/shard_map/all_to_all | solution.py:202
  72.1 0.0 collective-permute-done.11.refs_3_
  72.1 1.2 collective-permute-start.15
  73.3 0.0 collective-permute-done.20.refs_17_.refs_9_
  73.3 0.1 collective-permute-start.16
  73.4 0.0 collective-permute-done.14.refs_6_
  73.4 0.3 collective-permute-start.21
  73.7 0.0 collective-permute-done.13.refs_5_
  73.7 2.4 %collective-permute-start.22 = (bf16[2,2,256,256]{3,2,1,0:T(8,128)(2,1)}, bf16[2,2,256,256]{3,2,1,0:T(8,128)(2,1)}, u32[]{:S(2)}, u32[]{:S(2)}) collective-permute-start(bf16[2,2,256,256]{3,2,1,0:T(8,128)(2,1)} %collective-permute-done.13.refs_5_), channel_id=1, source_target_pairs={{0,192},{8,56},{16,208},{24,8},{32,224},{40,24},{48,240},{56,40},{... | collective-permute-start | bytes 1572872 | tf_op jit(solution)/shard_map/ppermute | solution.py:181
  76.1 4.4 %all-to-all-start.1 = ((bf16[8,4,32,256]{3,2,1,0:T(8,128)(2,1)}), bf16[8,4,32,256]{3,2,1,0:T(8,128)(2,1)S(1)}, u32[]{:S(2)}, u32[]{:S(2)}) async-start(bf16[8,4,32,256]{3,2,1,0:T(8,128)(2,1)} %bitcast), calls=%async_computation.1 | async-start | bytes 1048576 | tf_op jit(solution)/shard_map/all_to_all | solution.py:220
  80.5 0.0 collective-permute-done.12.refs_4_
  80.5 1.3 collective-permute-start.17
  81.8 0.0 collective-permute-done.15.refs_7_
  81.8 0.1 collective-permute-start.18
  81.9 0.0 collective-permute-done.16.refs_8_
  81.9 0.4 collective-permute-start.19
  82.3 1.0 collective-permute-done.21.refs_0_
  83.3 1.3 collective-permute-start.23
  84.5 0.0 collective-permute-done.22.refs_1_
  84.5 0.0 collective-permute-start.24
  84.5 0.0 collective-permute-done.17.refs_9_
  84.6 0.5 collective-permute-done.18.refs_10_
  85.1 0.3 copy-done.11
  85.4 0.8 copy-done.12
  86.2 0.0 collective-permute-done.19.refs_11_
  86.2 11.3 %all-to-all-done.1.refs_12_.refs_4_ = bf16[8,4,32,256]{3,2,1,0:T(8,128)(2,1)S(1)} async-done(((bf16[8,4,32,256]{3,2,1,0:T(8,128)(2,1)}), bf16[8,4,32,256]{3,2,1,0:T(8,128)(2,1)S(1)}, u32[]{:S(2)}, u32[]{:S(2)}) %all-to-all-start.1) | async-done | bytes 524320 | tf_op jit(solution)/shard_map/all_to_all | solution.py:220
  97.6 0.8 copy-done.2
  98.4 10.4 %shard_map.58.total_in = f32[4,256,256]{2,1,0:T(8,128)} custom-call(bf16[2,2,256,256]{3,2,1,0:T(8,128)(2,1)} %copy-done, bf16[2,2,256,256]{3,2,1,0:T(8,128)(2,1)} %copy-done.1, bf16[2,2,256,256]{3,2,1,0:T(8,128)(2,1)} %collective-permute-done.10.refs_2_, bf16[2,2,256,256]{3,2,1,0:T(8,128)(2,1)} %copy-done.10, ...), custom_call_target="tpu_custom_call" | custom-call | tf_op jit(solution)/shard_map/pallas_call | solution.py:149
  108.7 0.0 collective-permute-done.23.refs_2_
  108.8 6.3 %shard_map.59 = bf16[8,4,32,256]{3,2,1,0:T(8,128)(2,1)} custom-call(s32[32]{0:T(128)} %left_sizes.3, s32[32]{0:T(128)} %right_sizes.3, f32[4,256,256]{2,1,0:T(8,128)} %shard_map.58.total_in, bf16[2,2,256,256]{3,2,1,0:T(8,128)(2,1)} %collective-permute-done.21.refs_0_, bf16[2,2,256,256]{3,2,1,0:T(8,128)(2,1)} %collective-permute-done.22.refs_1_, ...), custom_call_target="tpu_custom_call" | custom-call | tf_op jit(solution)/shard_map/pallas_call | solution.py:149
  115.1 18.8 %all_to_all.15 = bf16[8,4,32,256]{3,2,1,0:T(8,128)(2,1)S(1)} all-to-all(bf16[8,4,32,256]{3,2,1,0:T(8,128)(2,1)} %shard_map.59), channel_id=1, replica_groups=mesh['blk'=32,'mpo'=8] {'mpo'}, dimensions={0} | all-to-all | bytes 1048576 | tf_op jit(solution)/shard_map/all_to_all | solution.py:244
  133.8 0.8 copy.6
  (23 shorter events, 0.0 us)
Async XLA Ops:
  0.0 15.6 %collective-permute-start = (bf16[2,256,256]{2,1,0:T(8,128)(2,1)}, bf16[2,256,256]{2,1,0:T(8,128)(2,1)S(1)}, u32[]{:S(2)}, u32[]{:S(2)}) collective-permute-start(bf16[2,256,256]{2,1,0:T(8,128)(2,1)} %param.6), channel_id=1, source_target_pairs={{0,0},{1,8},{2,16},{3,24},{4,32},{5,40},{6,48},{7,56},{8,4},{9,12}... | collective-permute-start | bytes 786440 | tf_op jit(solution)/shard_map/ppermute | solution.py:197
  10.2 15.2 %collective-permute-start.1 = (bf16[2,256,256]{2,1,0:T(8,128)(2,1)}, bf16[2,256,256]{2,1,0:T(8,128)(2,1)S(1)}, u32[]{:S(2)}, u32[]{:S(2)}) collective-permute-start(bf16[2,256,256]{2,1,0:T(8,128)(2,1)} %refs_5_.1), channel_id=1, source_target_pairs={{0,1},{1,2},{2,3},{3,4},{4,5},{5,6},{6,7},{7,0},{8,9},{9,10},{10,1... | collective-permute-start | bytes 786440 | tf_op jit(solution)/shard_map/ppermute | solution.py:187
  10.3 15.1 %collective-permute-start.2 = (bf16[2,256,256]{2,1,0:T(8,128)(2,1)}, bf16[2,256,256]{2,1,0:T(8,128)(2,1)S(1)}, u32[]{:S(2)}, u32[]{:S(2)}) collective-permute-start(bf16[2,256,256]{2,1,0:T(8,128)(2,1)} %refs_5_.1), channel_id=1, source_target_pairs={{0,7},{1,0},{2,1},{3,2},{4,3},{5,4},{6,5},{7,6},{8,15},{9,8},{10,9... | collective-permute-start | bytes 786440 | tf_op jit(solution)/shard_map/ppermute | solution.py:190
  25.4 72.1 %copy-start.3 = (bf16[2,256,256]{2,1,0:T(8,128)(2,1)}, bf16[2,256,256]{2,1,0:T(8,128)(2,1)S(1)}, u32[]{:S(2)}) copy-start(bf16[2,256,256]{2,1,0:T(8,128)(2,1)S(1)} %collective-permute-done.1.refs_20_.refs_12_) | copy-start | bytes 786436
  25.4 72.1 %copy-start.4 = (bf16[2,256,256]{2,1,0:T(8,128)(2,1)}, bf16[2,256,256]{2,1,0:T(8,128)(2,1)S(1)}, u32[]{:S(2)}) copy-start(bf16[2,256,256]{2,1,0:T(8,128)(2,1)S(1)} %collective-permute-done.2.refs_14_.refs_6_) | copy-start | bytes 786436
  25.4 6.6 %collective-permute-start.3 = (bf16[2,256,256]{2,1,0:T(8,128)(2,1)S(1)}, bf16[2,256,256]{2,1,0:T(8,128)(2,1)S(1)}, u32[]{:S(2)}, u32[]{:S(2)}) collective-permute-start(bf16[2,256,256]{2,1,0:T(8,128)(2,1)S(1)} %collective-permute-done.refs_0_), channel_id=1, source_target_pairs={{0,16},{8,72},{16,32},{24,88},{32,48},{40,104},{48,0},{56,120},{64... | collective-permute-start | bytes 786440 | tf_op jit(solution)/shard_map/ppermute | solution.py:178
  26.8 5.5 %collective-permute-start.4 = (bf16[2,256,256]{2,1,0:T(8,128)(2,1)S(1)}, bf16[2,256,256]{2,1,0:T(8,128)(2,1)S(1)}, u32[]{:S(2)}, u32[]{:S(2)}) collective-permute-start(bf16[2,256,256]{2,1,0:T(8,128)(2,1)S(1)} %collective-permute-done.refs_0_), channel_id=1, source_target_pairs={{0,48},{8,200},{16,0},{24,216},{32,16},{40,232},{48,32},{56,248},{... | collective-permute-start | bytes 786440 | tf_op jit(solution)/shard_map/ppermute | solution.py:178
  28.3 6.7 %collective-permute-start.5 = (bf16[2,256,256]{2,1,0:T(8,128)(2,1)S(1)}, bf16[2,256,256]{2,1,0:T(8,128)(2,1)S(1)}, u32[]{:S(2)}, u32[]{:S(2)}) collective-permute-start(bf16[2,256,256]{2,1,0:T(8,128)(2,1)S(1)} %collective-permute-done.1.refs_20_.refs_12_), channel_id=1, source_target_pairs={{0,1},{1,2},{2,3},{3,4},{4,5},{5,6},{6,7},{7,0},{8,9},{9,10},{10,1... | collective-permute-start | bytes 786440 | tf_op jit(solution)/shard_map/ppermute | solution.py:187
  28.3 6.7 %collective-permute-start.6 = (bf16[2,256,256]{2,1,0:T(8,128)(2,1)S(1)}, bf16[2,256,256]{2,1,0:T(8,128)(2,1)S(1)}, u32[]{:S(2)}, u32[]{:S(2)}) collective-permute-start(bf16[2,256,256]{2,1,0:T(8,128)(2,1)S(1)} %collective-permute-done.2.refs_14_.refs_6_), channel_id=1, source_target_pairs={{0,7},{1,0},{2,1},{3,2},{4,3},{5,4},{6,5},{7,6},{8,15},{9,8},{10,9... | collective-permute-start | bytes 786440 | tf_op jit(solution)/shard_map/ppermute | solution.py:190
  35.0 62.5 %copy-start.5 = (bf16[2,256,256]{2,1,0:T(8,128)(2,1)}, bf16[2,256,256]{2,1,0:T(8,128)(2,1)S(1)}, u32[]{:S(2)}) copy-start(bf16[2,256,256]{2,1,0:T(8,128)(2,1)S(1)} %collective-permute-done.5.refs_19_.refs_11_) | copy-start | bytes 786436
  35.0 62.5 %copy-start.6 = (bf16[2,256,256]{2,1,0:T(8,128)(2,1)}, bf16[2,256,256]{2,1,0:T(8,128)(2,1)S(1)}, u32[]{:S(2)}) copy-start(bf16[2,256,256]{2,1,0:T(8,128)(2,1)S(1)} %collective-permute-done.6.refs_15_.refs_7_) | copy-start | bytes 786436
  35.1 8.9 %collective-permute-start.8 = (bf16[2,256,256]{2,1,0:T(8,128)(2,1)S(1)}, bf16[2,256,256]{2,1,0:T(8,128)(2,1)S(1)}, u32[]{:S(2)}, u32[]{:S(2)}) collective-permute-start(bf16[2,256,256]{2,1,0:T(8,128)(2,1)S(1)} %collective-permute-done.5.refs_19_.refs_11_), channel_id=1, source_target_pairs={{0,1},{1,2},{2,3},{3,4},{4,5},{5,6},{6,7},{7,0},{8,9},{9,10},{10,1... | collective-permute-start | bytes 786440 | tf_op jit(solution)/shard_map/ppermute | solution.py:187
  37.0 10.4 %collective-permute-start.9 = (bf16[2,256,256]{2,1,0:T(8,128)(2,1)S(1)}, bf16[2,256,256]{2,1,0:T(8,128)(2,1)S(1)}, u32[]{:S(2)}, u32[]{:S(2)}) collective-permute-start(bf16[2,256,256]{2,1,0:T(8,128)(2,1)S(1)} %collective-permute-done.6.refs_15_.refs_7_), channel_id=1, source_target_pairs={{0,7},{1,0},{2,1},{3,2},{4,3},{5,4},{6,5},{7,6},{8,15},{9,8},{10,9... | collective-permute-start | bytes 786440 | tf_op jit(solution)/shard_map/ppermute | solution.py:190
  37.8 9.6 %collective-permute-start.7 = (bf16[2,256,256]{2,1,0:T(8,128)(2,1)S(1)}, bf16[2,256,256]{2,1,0:T(8,128)(2,1)S(1)}, u32[]{:S(2)}, u32[]{:S(2)}) collective-permute-start(bf16[2,256,256]{2,1,0:T(8,128)(2,1)S(1)} %collective-permute-done.3.refs_1_), channel_id=1, source_target_pairs={{0,16},{8,72},{16,32},{24,88},{32,48},{40,104},{48,0},{56,120},{64... | collective-permute-start | bytes 786440 | tf_op jit(solution)/shard_map/ppermute | solution.py:178
  37.9 59.7 %copy-start = (bf16[2,2,256,256]{3,2,1,0:T(8,128)(2,1)}, bf16[2,2,256,256]{3,2,1,0:T(8,128)(2,1)S(1)}, u32[]{:S(2)}) copy-start(bf16[2,2,256,256]{3,2,1,0:T(8,128)(2,1)S(1)} %shard_map.56.refs_0_) | copy-start | bytes 1572868
  37.9 23.0 %collective-permute-start.10 = (bf16[2,2,256,256]{3,2,1,0:T(8,128)(2,1)S(1)}, bf16[2,2,256,256]{3,2,1,0:T(8,128)(2,1)}, u32[]{:S(2)}, u32[]{:S(2)}) collective-permute-start(bf16[2,2,256,256]{3,2,1,0:T(8,128)(2,1)S(1)} %shard_map.56.refs_0_), channel_id=1, source_target_pairs={{0,64},{8,24},{16,80},{24,40},{32,96},{40,56},{48,112},{56,8},{64,... | collective-permute-start | bytes 1572872 | tf_op jit(solution)/shard_map/ppermute | solution.py:181
  40.6 31.5 %collective-permute-start.11 = (bf16[2,2,256,256]{3,2,1,0:T(8,128)(2,1)S(1)}, bf16[2,2,256,256]{3,2,1,0:T(8,128)(2,1)S(1)}, u32[]{:S(2)}, u32[]{:S(2)}) collective-permute-start(bf16[2,2,256,256]{3,2,1,0:T(8,128)(2,1)S(1)} %shard_map.56.refs_0_), channel_id=1, source_target_pairs={{0,192},{8,56},{16,208},{24,8},{32,224},{40,24},{48,240},{56,40},{... | collective-permute-start | bytes 1572872 | tf_op jit(solution)/shard_map/ppermute | solution.py:181
  44.0 53.6 %copy-start.7 = (bf16[2,256,256]{2,1,0:T(8,128)(2,1)}, bf16[2,256,256]{2,1,0:T(8,128)(2,1)S(1)}, u32[]{:S(2)}) copy-start(bf16[2,256,256]{2,1,0:T(8,128)(2,1)S(1)} %collective-permute-done.8.refs_18_.refs_10_) | copy-start | bytes 786436
  44.0 29.4 %collective-permute-start.14 = (bf16[2,2,256,256]{3,2,1,0:T(8,128)(2,1)S(1)}, bf16[2,2,256,256]{3,2,1,0:T(8,128)(2,1)}, u32[]{:S(2)}, u32[]{:S(2)}) collective-permute-start(bf16[2,2,256,256]{3,2,1,0:T(8,128)(2,1)S(1)} %shard_map.56.refs_0_), channel_id=1, source_target_pairs={{0,8},{8,0},{16,24},{24,16},{32,40},{40,32},{48,56},{56,48},{64,72... | collective-permute-start | bytes 1572872 | tf_op jit(solution)/shard_map/ppermute | solution.py:184
  47.4 50.2 %copy-start.8 = (bf16[2,256,256]{2,1,0:T(8,128)(2,1)}, bf16[2,256,256]{2,1,0:T(8,128)(2,1)S(1)}, u32[]{:S(2)}) copy-start(bf16[2,256,256]{2,1,0:T(8,128)(2,1)S(1)} %collective-permute-done.9.refs_16_.refs_8_) | copy-start | bytes 786436
  47.4 50.1 %copy-start.1 = (bf16[2,2,256,256]{3,2,1,0:T(8,128)(2,1)}, bf16[2,2,256,256]{3,2,1,0:T(8,128)(2,1)S(1)}, u32[]{:S(2)}) copy-start(bf16[2,2,256,256]{3,2,1,0:T(8,128)(2,1)S(1)} %shard_map.57.refs_1_) | copy-start | bytes 1572868
  47.5 26.3 %collective-permute-start.13 = (bf16[2,2,256,256]{3,2,1,0:T(8,128)(2,1)S(1)}, bf16[2,2,256,256]{3,2,1,0:T(8,128)(2,1)}, u32[]{:S(2)}, u32[]{:S(2)}) collective-permute-start(bf16[2,2,256,256]{3,2,1,0:T(8,128)(2,1)S(1)} %shard_map.57.refs_1_), channel_id=1, source_target_pairs={{0,192},{8,56},{16,208},{24,8},{32,224},{40,24},{48,240},{56,40},{... | collective-permute-start | bytes 1572872 | tf_op jit(solution)/shard_map/ppermute | solution.py:181
  51.0 21.1 %all-to-all-start = ((bf16[32,32,256]{2,1,0:T(8,128)(2,1)}), bf16[32,32,256]{2,1,0:T(8,128)(2,1)}, u32[]{:S(2)}, u32[]{:S(2)}) async-start(bf16[32,32,256]{2,1,0:T(8,128)(2,1)} %shard_map.55), calls=%async_computation | async-start | bytes 1048576 | tf_op jit(solution)/shard_map/all_to_all | solution.py:202
  60.8 12.5 %collective-permute-start.20 = (bf16[2,256,256]{2,1,0:T(8,128)(2,1)S(1)}, bf16[2,256,256]{2,1,0:T(8,128)(2,1)S(1)}, u32[]{:S(2)}, u32[]{:S(2)}) collective-permute-start(bf16[2,256,256]{2,1,0:T(8,128)(2,1)S(1)} %collective-permute-done.8.refs_18_.refs_10_), channel_id=1, source_target_pairs={{0,1},{1,2},{2,3},{3,4},{4,5},{5,6},{6,7},{7,0},{8,9},{9,10},{10,1... | collective-permute-start | bytes 786440 | tf_op jit(solution)/shard_map/ppermute | solution.py:187
  60.9 19.6 %collective-permute-start.12 = (bf16[2,2,256,256]{3,2,1,0:T(8,128)(2,1)S(1)}, bf16[2,2,256,256]{3,2,1,0:T(8,128)(2,1)}, u32[]{:S(2)}, u32[]{:S(2)}) collective-permute-start(bf16[2,2,256,256]{3,2,1,0:T(8,128)(2,1)S(1)} %shard_map.57.refs_1_), channel_id=1, source_target_pairs={{0,64},{8,24},{16,80},{24,40},{32,96},{40,56},{48,112},{56,8},{64,... | collective-permute-start | bytes 1572872 | tf_op jit(solution)/shard_map/ppermute | solution.py:181
  72.1 4.0 %copy-start.10 = (bf16[2,2,256,256]{3,2,1,0:T(8,128)(2,1)}, bf16[2,2,256,256]{3,2,1,0:T(8,128)(2,1)S(1)}, u32[]{:S(2)}) copy-start(bf16[2,2,256,256]{3,2,1,0:T(8,128)(2,1)S(1)} %collective-permute-done.11.refs_3_) | copy-start | bytes 1572868
  72.1 9.7 %collective-permute-start.15 = (bf16[2,2,256,256]{3,2,1,0:T(8,128)(2,1)S(1)}, bf16[2,2,256,256]{3,2,1,0:T(8,128)(2,1)}, u32[]{:S(2)}, u32[]{:S(2)}) collective-permute-start(bf16[2,2,256,256]{3,2,1,0:T(8,128)(2,1)S(1)} %shard_map.57.refs_1_), channel_id=1, source_target_pairs={{0,8},{8,0},{16,24},{24,16},{32,40},{40,32},{48,56},{56,48},{64,72... | collective-permute-start | bytes 1572872 | tf_op jit(solution)/shard_map/ppermute | solution.py:184
  73.3 24.3 %copy-start.9 = (bf16[2,256,256]{2,1,0:T(8,128)(2,1)}, bf16[2,256,256]{2,1,0:T(8,128)(2,1)S(1)}, u32[]{:S(2)}) copy-start(bf16[2,256,256]{2,1,0:T(8,128)(2,1)S(1)} %collective-permute-done.20.refs_17_.refs_9_) | copy-start | bytes 786436
  73.3 8.6 %collective-permute-start.16 = (bf16[2,2,256,256]{3,2,1,0:T(8,128)(2,1)}, bf16[2,2,256,256]{3,2,1,0:T(8,128)(2,1)}, u32[]{:S(2)}, u32[]{:S(2)}) collective-permute-start(bf16[2,2,256,256]{3,2,1,0:T(8,128)(2,1)} %collective-permute-done.10.refs_2_), channel_id=1, source_target_pairs={{0,8},{8,0},{16,24},{24,16},{32,40},{40,32},{48,56},{56,48},{64,72... | collective-permute-start | bytes 1572872 | tf_op jit(solution)/shard_map/ppermute | solution.py:184
  73.4 9.9 %collective-permute-start.21 = (bf16[2,2,256,256]{3,2,1,0:T(8,128)(2,1)}, bf16[2,2,256,256]{3,2,1,0:T(8,128)(2,1)}, u32[]{:S(2)}, u32[]{:S(2)}) collective-permute-start(bf16[2,2,256,256]{3,2,1,0:T(8,128)(2,1)} %collective-permute-done.10.refs_2_), channel_id=1, source_target_pairs={{0,64},{8,24},{16,80},{24,40},{32,96},{40,56},{48,112},{56,8},{64,... | collective-permute-start | bytes 1572872 | tf_op jit(solution)/shard_map/ppermute | solution.py:181
  73.7 10.8 %collective-permute-start.22 = (bf16[2,2,256,256]{3,2,1,0:T(8,128)(2,1)}, bf16[2,2,256,256]{3,2,1,0:T(8,128)(2,1)}, u32[]{:S(2)}, u32[]{:S(2)}) collective-permute-start(bf16[2,2,256,256]{3,2,1,0:T(8,128)(2,1)} %collective-permute-done.13.refs_5_), channel_id=1, source_target_pairs={{0,192},{8,56},{16,208},{24,8},{32,224},{40,24},{48,240},{56,40},{... | collective-permute-start | bytes 1572872 | tf_op jit(solution)/shard_map/ppermute | solution.py:181
  76.1 21.4 %all-to-all-start.1 = ((bf16[8,4,32,256]{3,2,1,0:T(8,128)(2,1)}), bf16[8,4,32,256]{3,2,1,0:T(8,128)(2,1)S(1)}, u32[]{:S(2)}, u32[]{:S(2)}) async-start(bf16[8,4,32,256]{3,2,1,0:T(8,128)(2,1)} %bitcast), calls=%async_computation.1 | async-start | bytes 1048576 | tf_op jit(solution)/shard_map/all_to_all | solution.py:220
  80.5 4.1 %collective-permute-start.17 = (bf16[2,2,256,256]{3,2,1,0:T(8,128)(2,1)}, bf16[2,2,256,256]{3,2,1,0:T(8,128)(2,1)S(1)}, u32[]{:S(2)}, u32[]{:S(2)}) collective-permute-start(bf16[2,2,256,256]{3,2,1,0:T(8,128)(2,1)} %copy-done.10), channel_id=1, source_target_pairs={{0,8},{8,0},{16,24},{24,16},{32,40},{40,32},{48,56},{56,48},{64,72... | collective-permute-start | bytes 1572872 | tf_op jit(solution)/shard_map/ppermute | solution.py:184
  81.8 3.2 %collective-permute-start.18 = (bf16[2,2,256,256]{3,2,1,0:T(8,128)(2,1)}, bf16[2,2,256,256]{3,2,1,0:T(8,128)(2,1)S(1)}, u32[]{:S(2)}, u32[]{:S(2)}) collective-permute-start(bf16[2,2,256,256]{3,2,1,0:T(8,128)(2,1)} %collective-permute-done.12.refs_4_), channel_id=1, source_target_pairs={{0,8},{8,0},{16,24},{24,16},{32,40},{40,32},{48,56},{56,48},{64,72... | collective-permute-start | bytes 1572872 | tf_op jit(solution)/shard_map/ppermute | solution.py:184
  81.9 4.3 %collective-permute-start.19 = (bf16[2,2,256,256]{3,2,1,0:T(8,128)(2,1)}, bf16[2,2,256,256]{3,2,1,0:T(8,128)(2,1)}, u32[]{:S(2)}, u32[]{:S(2)}) collective-permute-start(bf16[2,2,256,256]{3,2,1,0:T(8,128)(2,1)} %collective-permute-done.13.refs_5_), channel_id=1, source_target_pairs={{0,8},{8,0},{16,24},{24,16},{32,40},{40,32},{48,56},{56,48},{64,72... | collective-permute-start | bytes 1572872 | tf_op jit(solution)/shard_map/ppermute | solution.py:184
  83.3 25.5 %collective-permute-start.23 = (bf16[2,2,256,256]{3,2,1,0:T(8,128)(2,1)}, bf16[2,2,256,256]{3,2,1,0:T(8,128)(2,1)}, u32[]{:S(2)}, u32[]{:S(2)}) collective-permute-start(bf16[2,2,256,256]{3,2,1,0:T(8,128)(2,1)} %collective-permute-done.21.refs_0_), channel_id=1, source_target_pairs={{0,8},{8,0},{16,24},{24,16},{32,40},{40,32},{48,56},{56,48},{64,72... | collective-permute-start | bytes 1572872 | tf_op jit(solution)/shard_map/ppermute | solution.py:184
  84.5 24.2 %collective-permute-start.24 = (bf16[2,2,256,256]{3,2,1,0:T(8,128)(2,1)}, bf16[2,2,256,256]{3,2,1,0:T(8,128)(2,1)}, u32[]{:S(2)}, u32[]{:S(2)}) collective-permute-start(bf16[2,2,256,256]{3,2,1,0:T(8,128)(2,1)} %collective-permute-done.22.refs_1_), channel_id=1, source_target_pairs={{0,8},{8,0},{16,24},{24,16},{32,40},{40,32},{48,56},{56,48},{64,72... | collective-permute-start | bytes 1572872 | tf_op jit(solution)/shard_map/ppermute | solution.py:184
  84.6 0.8 copy-start.11
  85.4 0.8 copy-start.12
  97.6 0.8 copy-start.2

commit v5 on v4

v5 whole, which is shorter than its diff:
```python
import functools

import jax
import jax.numpy as jnp
from jax import lax
from jax.experimental import pallas as pl
from jax.experimental.pallas import tpu as pltpu
from jax.sharding import PartitionSpec as P

MIB = 1024 * 1024
SIDE = 4
OFFSETS = (0, SIDE - 1, 1, 2)


def place(y, x, core):
    return ((y % SIDE) * SIDE + x % SIDE) * 2 + core


def stack_kernel(places, *refs):
    inputs, out, sems = refs[: len(places)], refs[-2], refs[-1]
    copies = []
    for i, (ref, (at, lo, hi)) in enumerate(zip(inputs, places)):
        copies.append(pltpu.make_async_copy(ref, out.at[at, lo:hi], sems.at[i]))
    for copy in copies:
        copy.start()
    for copy in copies:
        copy.wait()


def stack(pieces, places, shape):
    return pl.pallas_call(
        functools.partial(stack_kernel, places),
        out_shape=jax.ShapeDtypeStruct(shape, pieces[0].dtype),
        in_specs=[pl.BlockSpec(memory_space=pl.ANY)] * len(pieces),
        out_specs=pl.BlockSpec(memory_space=pl.ANY),
        scratch_shapes=[pltpu.SemaphoreType.DMA((len(pieces),))],
        compiler_params=pltpu.CompilerParams(vmem_limit_bytes=MIB),
    )(*pieces)


def coordinates():
    sector, rank = lax.axis_index("blk"), lax.axis_index("mpo")
    return sector, rank, sector % 2, sector // 2 % SIDE, sector // (2 * SIDE)


def columns_kernel(left_sizes, right_sizes, psi_ref, *refs):
    outs, (held, sems) = refs[:SIDE], refs[SIDE:]
    sector, rank, _, _, y0 = coordinates()
    _, left_dim, right_dim = outs[0].shape
    at = [2 * SIDE * ((y0 + ahead) & (SIDE - 1)) + rank for ahead in range(SIDE)]
    copies = []
    for ahead in range(SIDE):
        first = pl.multiple_of(at[ahead] * right_dim, right_dim)
        source = psi_ref.at[:, pl.ds(first, right_dim)]
        copies.append(pltpu.make_async_copy(source, held.at[ahead], sems.at[ahead]))
    for copy in copies:
        copy.start()
    row = lax.broadcasted_iota(jnp.int32, (left_dim, right_dim), 0)
    col = lax.broadcasted_iota(jnp.int32, (left_dim, right_dim), 1)
    own_left = left_sizes[sector]
    for ahead in range(SIDE):
        copies[ahead].wait()
        block = held[ahead].astype(jnp.float32)
        inside = jnp.logical_and(row < own_left, col < right_sizes[at[ahead]])
        outs[ahead][0] = jnp.where(inside, block, 0.0).astype(outs[ahead].dtype)


SMEM = pl.BlockSpec(memory_space=pltpu.SMEM)
VMEM = pl.BlockSpec(memory_space=pltpu.VMEM)


def pick_columns(wavefunction, left_sizes, right_sizes):
    left_dim, columns = wavefunction.shape
    shape = (1, left_dim, columns // right_sizes.shape[0])
    return pl.pallas_call(
        columns_kernel,
        out_shape=[jax.ShapeDtypeStruct(shape, wavefunction.dtype)] * SIDE,
        in_specs=[SMEM, SMEM, pl.BlockSpec(memory_space=pl.ANY)],
        out_specs=[VMEM] * SIDE,
        scratch_shapes=[
            pltpu.VMEM((SIDE, *shape[1:]), wavefunction.dtype),
            pltpu.SemaphoreType.DMA((SIDE,)),
        ],
        compiler_params=pltpu.CompilerParams(vmem_limit_bytes=60 * MIB),
    )(left_sizes, right_sizes, wavefunction)


def fetch(refs, held, sems, first):
    copies = [pltpu.make_async_copy(r, h, sems.at[first + i]) for i, (r, h) in enumerate(zip(refs, held))]
    for copy in copies:
        copy.start()
    return copies


def apply_kernel(pieces, left_sizes, right_sizes, *refs):
    refs, (out_ref, total, held, psi_held, right_held, sems) = refs[:-6], refs[-6:]
    sector, rank, core, x0, y0 = coordinates()
    ranks, parts, rows, right_dim = out_ref.shape
    blocks, others = refs[: len(pieces)], refs[len(pieces) :]
    places = [psi_held.at[pl.ds(i, 1)] for i in range(parts)] + [right_held.at[i] for i in range(ranks)]
    needed = fetch(others, places, sems, 0)
    coming = fetch(blocks, [held.at[i] for i in range(len(pieces))], sems, len(needed))
    total[...] = jnp.zeros_like(total)
    for copy in needed:
        copy.wait()
    _, count, _, left_dim, inner = held.shape
    for i, (sibling, far, first) in enumerate(pieces):
        tree = 1 - core if sibling else core
        coming[i].wait()
        for k in range(count):
            near = OFFSETS[first + k]
            y = jnp.where(tree == 0, y0 + far, y0 + near) & (SIDE - 1)
            x = jnp.where(tree == 0, x0 + near, x0 + far) & (SIDE - 1)
            at = (2 * x + tree - rank) & (ranks - 1)
            block = held[i, k].reshape(2 * left_dim, inner)
            both = jnp.dot(block, psi_held[(y0 - y) & (SIDE - 1)], preferred_element_type=jnp.float32).astype(out_ref.dtype)
            term = jnp.dot(both[:left_dim], right_held[at, 0], preferred_element_type=jnp.float32)
            term += jnp.dot(both[left_dim:], right_held[at, 1], preferred_element_type=jnp.float32)
            total[y] += term
    own_right = right_sizes[sector]
    row = lax.broadcasted_iota(jnp.int32, (left_dim, right_dim), 0)
    col = lax.broadcasted_iota(jnp.int32, (left_dim, right_dim), 1)
    for y in range(parts):
        own_left = left_sizes[2 * SIDE * y + rank % SIDE * 2 + rank // SIDE]
        inside = jnp.logical_and(row < own_left, col < own_right)
        block = jnp.where(inside, total[y], 0.0).astype(out_ref.dtype)
        out_ref[:, y] = block.reshape(ranks, rows, right_dim)


def apply(pieces, blocks, psi, rights, left_sizes, right_sizes):
    dtype, ranks, parts = psi[0].dtype, len(rights), len(psi)
    _, left_dim, right_dim = psi[0].shape
    anywhere = pl.BlockSpec(memory_space=pl.ANY)
    others = (*blocks, *psi, *rights)
    return pl.pallas_call(
        functools.partial(apply_kernel, pieces),
        out_shape=jax.ShapeDtypeStruct((ranks, parts, left_dim // ranks, right_dim), dtype),
        in_specs=[SMEM, SMEM] + [anywhere] * len(others),
        out_specs=VMEM,
        scratch_shapes=[
            pltpu.VMEM((parts, left_dim, right_dim), jnp.float32),
            pltpu.VMEM((len(pieces), *blocks[0].shape), dtype),
            pltpu.VMEM((parts, left_dim, right_dim), dtype),
            pltpu.VMEM((ranks, *rights[0].shape), dtype),
            pltpu.SemaphoreType.DMA((len(others),)),
        ],
        compiler_params=pltpu.CompilerParams(vmem_limit_bytes=60 * MIB),
    )(left_sizes, right_sizes, *others)


def together(*values):
    return lax.optimization_barrier(values)


def local(wavefunction, left_env, right_env, left_sizes, right_sizes):
    sectors, ranks = lax.axis_size("blk"), lax.axis_size("mpo")
    rows, right_dim = left_env.shape[1] // ranks, right_env.shape[2]
    spots = [(y, x, c) for y in range(SIDE) for x in range(SIDE) for c in range(2)]

    def step(second, by):
        pairs = []
        for y, x, c in spots:
            along_x = (c == 0) != second
            to = place(y, x + by, c) if along_x else place(y + by, x, c)
            pairs.append((place(y, x, c), to))
        return pairs

    def near_step(block, by):
        return lax.ppermute(block, "blk", step(False, by))

    def far_step(block, by):
        return lax.ppermute(block, "blk", step(True, by))

    def swap(block):
        return lax.ppermute(block, "blk", [(i, i ^ 1) for i in range(sectors)])

    def up(block):
        return lax.ppermute(block, "mpo", [(z, (z + 1) % ranks) for z in range(ranks)])

    def down(block):
        return lax.ppermute(block, "mpo", [(z, (z - 1) % ranks) for z in range(ranks)])

    turn = [
        (place(y, x, c) * ranks + z, place(y, z // 2, z % 2) * ranks + x + SIDE * c)
        for y, x, c in spots
        for z in range(ranks)
    ]
    own = lax.ppermute(left_env, ("blk", "mpo"), turn)
    up1, down1 = up(right_env), down(right_env)
    mine = pick_columns(wavefunction, left_sizes, right_sizes)
    own, *mine = together(own, *mine)

    def turned(block):
        return lax.ppermute(block, ("blk", "mpo"), turn)

    def rows_on(block, by):
        pairs = [(place(y, x, c), place(y + by, x, c)) for y, x, c in spots]
        return lax.ppermute(block, "blk", pairs)

    below, above = near_step(own, 1), near_step(own, -1)
    psi1 = turned(mine[1])
    below, above, up1, down1, psi1 = together(below, above, up1, down1, psi1)

    two = near_step(below, 1)
    line_a = stack((own, below), ((0, 0, 2), (1, 0, 2)), (2, *left_env.shape))
    a_below, a_above = far_step(line_a, 1), far_step(line_a, -1)
    up2, down2 = up(up1), down(down1)
    psi3 = turned(mine[3])
    two, up2, down2, psi3 = together(two, up2, down2, psi3)

    line_b = stack((above, two), ((0, 0, 2), (1, 0, 2)), (2, *left_env.shape))
    b_below, b_above = far_step(line_b, 1), far_step(line_b, -1)
    up3, down3 = up(up2), down(down2)
    psi1, psi2 = rows_on(psi1, 1), turned(mine[2])
    a_below, a_above, up3, psi2 = together(a_below, a_above, up3, psi2)

    a_two = far_step(a_below, 1)
    up4 = up(up3)
    psi3, psi2, psi0 = rows_on(psi3, 3), rows_on(psi2, 2), turned(mine[0])
    b_two = far_step(b_above, -1)
    psi = (psi0, psi1, psi2, psi3)

    rights = (right_env, down1, down2, down3, up4, up3, up2, up1)
    blocks = (line_a, line_b, a_below, a_above, b_below, b_above, a_two, b_two)
    blocks += tuple(swap(block) for block in blocks)
    places = ((0, 0), (0, 2), (SIDE - 1, 0), (1, 0), (SIDE - 1, 2), (1, 2), (2, 0), (2, 2))
    pieces = tuple((s, *p) for s in (False, True) for p in places)
    done = apply(pieces, blocks, psi, rights, left_sizes, right_sizes)

    out = lax.all_to_all(done, "mpo", 0, 0).reshape(2, SIDE, SIDE, rows, right_dim)
    return out.transpose(2, 1, 0, 3, 4).reshape(sectors, rows, right_dim)


def solution(mesh):
    placed = (P("blk", None), P("mpo", "blk", None), P("mpo", "blk", None), P(), P())
    return jax.shard_map(
        local, mesh=mesh, in_specs=placed, out_specs=P(None, "mpo", "blk"), check_vma=False
    )
```

time: 136 us -> 146 us (1.074)
  starting transfers between devices: 56.1 us -> 87.8 us
  waiting for transfers between devices: 37.4 us -> 17.9 us
  Pallas kernels: 19.4 us -> 16.4 us
  blocking collectives: 18.8 us -> 21.4 us
    ppermute x0 -> x7, starting transfers between devices: none -> 51 us  [the longest x4 43.1 us: turned(): return lax.ppermute(block, ('blk', 'mpo'), turn)]
    all_to_all x2 -> x0, waiting for transfers between devices: 21.1 us -> none  [the longest x1 11.3 us: local(): psi = lax.all_to_all(spread, 'mpo', 0, 0)]
    all_to_all x2 -> x0, starting transfers between devices: 14.2 us -> none  [the longest x1 9.8 us: local(): spread = lax.all_to_all(mine, 'blk', 0, 0, axis_index_groups=[order])]
    ppermute x0 -> x7, waiting for transfers between devices: none -> 9.32 us  [the longest x3 6.44 us: rows_on(): return lax.ppermute(block, 'blk', pairs)]
    ppermute x4, waiting for transfers between devices: 12.5 us -> 3.77 us  [up(): lax.ppermute(block, 'mpo', [(z, (z + 1) % ranks) for z in range(ranks)])]
    ppermute x6, starting transfers between devices: 13.8 us -> 9.48 us  [far_step(): return lax.ppermute(block, 'blk', step(True, by))]
    ppermute x3, starting transfers between devices: 6.16 us -> 2.75 us  [down(): lax.ppermute(block, 'mpo', [(z, (z - 1) % ranks) for z in range(ranks)])]
    pallas_call x3 -> x2, Pallas kernels: 19.3 us -> 16.3 us  [the longest x1 13.7 us: apply(): pl.pallas_call(functools.partial(apply_kernel, pieces), out_shape=jax.Sha...]
  transfers between devices with their start and end apart: 27 -> 32, of which waited for: 9 -> 10; matrix products, arithmetic and copies ran while one was open for 0% -> 0% of each run, Pallas kernels for 10% -> 2%
where the time goes in v5:
time: 146 us
  starting transfers between devices  87.8 us (60%)
  blocking collectives  21.4 us (15%)
  waiting for transfers between devices  17.9 us (12%)
  Pallas kernels  16.4 us (11%)
  local copies, waits for them, and re-layouts  1.74 us (1%)
    ppermute x4, starting transfers between devices, turned(): return lax.ppermute(block, ('blk', 'mpo'), turn)  43.1 us
    all_to_all x1, blocking collectives, local(): lax.all_to_all(done, 'mpo', 0, 0).reshape(2, SIDE, SIDE, rows, right_dim)  21.4 us
    pallas_call x1, Pallas kernels, apply(): pl.pallas_call(functools.partial(apply_kernel, pieces), out_shape=jax.Sha...  13.7 us
    ppermute x1, starting transfers between devices, local(): own = lax.ppermute(left_env, ('blk', 'mpo'), turn)  10.2 us
    ppermute x8, starting transfers between devices, swap(): return lax.ppermute(block, 'blk', [(i, i ^ 1) for i in range(sectors)])  9.77 us
    ppermute x6, starting transfers between devices, far_step(): return lax.ppermute(block, 'blk', step(True, by))  9.48 us
    ppermute x3, starting transfers between devices, rows_on(): return lax.ppermute(block, 'blk', pairs)  7.89 us
    ppermute x3, waiting for transfers between devices, rows_on(): return lax.ppermute(block, 'blk', pairs)  6.44 us
  transfers between devices with their start and end apart: 32, of which 10 were waited for; matrix products, arithmetic and copies ran while one was open for 0% of the time, Pallas kernels for 2%

profile of v5, /device:TPU:1, one launch (start us, length us, event | category | flops | bytes accessed | tf_op | source)
XLA Modules:
  0.0 145.6 jit_solution(4459736840259327066)
XLA Ops:
  0.0 10.2 %collective-permute-start = (bf16[2,256,256]{2,1,0:T(8,128)(2,1)}, bf16[2,256,256]{2,1,0:T(8,128)(2,1)S(1)}, u32[]{:S(2)}, u32[]{:S(2)}) collective-permute-start(bf16[2,256,256]{2,1,0:T(8,128)(2,1)} %param.6), channel_id=1, source_target_pairs={{0,0},{1,8},{2,16},{3,24},{4,32},{5,40},{6,48},{7,56},{8,4},{9,12}... | collective-permute-start | bytes 786440 | tf_op jit(solution)/shard_map/ppermute | solution.py:188
  10.2 0.1 collective-permute-start.3
  10.3 2.7 %collective-permute-start.4 = (bf16[2,256,256]{2,1,0:T(8,128)(2,1)}, bf16[2,256,256]{2,1,0:T(8,128)(2,1)S(1)}, u32[]{:S(2)}, u32[]{:S(2)}) collective-permute-start(bf16[2,256,256]{2,1,0:T(8,128)(2,1)} %refs_20_.1), channel_id=1, source_target_pairs={{0,7},{1,0},{2,1},{3,2},{4,3},{5,4},{6,5},{7,6},{8,15},{9,8},{10,9... | collective-permute-start | bytes 786440 | tf_op jit(solution)/shard_map/ppermute | solution.py:181
  13.0 2.6 %shard_map.55 = (bf16[1,256,256]{2,1,0:T(8,128)(2,1)}, bf16[1,256,256]{2,1,0:T(8,128)(2,1)}, bf16[1,256,256]{2,1,0:T(8,128)(2,1)}, bf16[1,256,256]{2,1,0:T(8,128)(2,1)}) custom-call(s32[32]{0:T(128)} %left_sizes.3, s32[32]{0:T(128)} %right_sizes.3, bf16[256,8192]{1,0:T(8,128)(2,1)} %psi_ref.1), custom_call_target="tpu_custom_call" | custom-call | tf_op jit(solution)/shard_map/pallas_call | solution.py:75
  15.6 0.0 collective-permute-done.refs_0_
  15.6 2.8 %collective-permute-start.2 = (bf16[2,256,256]{2,1,0:T(8,128)(2,1)S(1)}, bf16[2,256,256]{2,1,0:T(8,128)(2,1)S(1)}, u32[]{:S(2)}, u32[]{:S(2)}) collective-permute-start(bf16[2,256,256]{2,1,0:T(8,128)(2,1)S(1)} %collective-permute-done.refs_0_), channel_id=1, source_target_pairs={{0,48},{8,200},{16,0},{24,216},{32,16},{40,232},{48,32},{56,248},{... | collective-permute-start | bytes 786440 | tf_op jit(solution)/shard_map/ppermute | solution.py:169
  18.4 0.0 collective-permute-start.1
  18.4 11.8 %collective-permute-start.5 = (bf16[1,256,256]{2,1,0:T(8,128)(2,1)}, bf16[1,256,256]{2,1,0:T(8,128)(2,1)S(1)}, u32[]{:S(2)}, u32[]{:S(2)}) collective-permute-start(bf16[1,256,256]{2,1,0:T(8,128)(2,1)} %get-tuple-element.32), channel_id=1, source_target_pairs={{0,0},{1,8},{2,16},{3,24},{4,32},{5,40},{6,48},{7,56},{8,4},{9,12}... | collective-permute-start | bytes 393224 | tf_op jit(solution)/shard_map/ppermute | solution.py:194
  30.2 0.0 collective-permute-done.3.refs_27_
  30.2 0.0 collective-permute-done.4.refs_21_
  30.2 2.2 %collective-permute-done.5 = bf16[1,256,256]{2,1,0:T(8,128)(2,1)S(1)} collective-permute-done((bf16[1,256,256]{2,1,0:T(8,128)(2,1)}, bf16[1,256,256]{2,1,0:T(8,128)(2,1)S(1)}, u32[]{:S(2)}, u32[]{:S(2)}) %collective-permute-start.5) | collective-permute-done | bytes 131104 | tf_op jit(solution)/shard_map/ppermute | solution.py:194
  32.4 0.0 collective-permute-done.2.refs_0_
  32.4 0.0 collective-permute-done.1.refs_1_
  32.4 1.3 collective-permute-start.6
  33.7 0.0 collective-permute-start.7
  33.7 11.9 %collective-permute-start.9 = (bf16[1,256,256]{2,1,0:T(8,128)(2,1)}, bf16[1,256,256]{2,1,0:T(8,128)(2,1)S(1)}, u32[]{:S(2)}, u32[]{:S(2)}) collective-permute-start(bf16[1,256,256]{2,1,0:T(8,128)(2,1)} %get-tuple-element.37), channel_id=1, source_target_pairs={{0,0},{1,8},{2,16},{3,24},{4,32},{5,40},{6,48},{7,56},{8,4},{9,12}... | collective-permute-start | bytes 393224 | tf_op jit(solution)/shard_map/ppermute | solution.py:194
  45.6 0.1 collective-permute-start.8
  45.7 0.1 shard_map.56.refs_0_
  45.8 0.0 copy-start
  45.8 2.7 %collective-permute-start.11 = (bf16[2,2,256,256]{3,2,1,0:T(8,128)(2,1)S(1)}, bf16[2,2,256,256]{3,2,1,0:T(8,128)(2,1)S(1)}, u32[]{:S(2)}, u32[]{:S(2)}) collective-permute-start(bf16[2,2,256,256]{3,2,1,0:T(8,128)(2,1)S(1)} %shard_map.56.refs_0_), channel_id=1, source_target_pairs={{0,192},{8,56},{16,208},{24,8},{32,224},{40,24},{48,240},{56,40},{... | collective-permute-start | bytes 1572872 | tf_op jit(solution)/shard_map/ppermute | solution.py:172
  48.5 0.0 collective-permute-done.9
  48.5 9.2 %collective-permute-start.13 = (bf16[1,256,256]{2,1,0:T(8,128)(2,1)}, bf16[1,256,256]{2,1,0:T(8,128)(2,1)S(1)}, u32[]{:S(2)}, u32[]{:S(2)}) collective-permute-start(bf16[1,256,256]{2,1,0:T(8,128)(2,1)} %get-tuple-element.40), channel_id=1, source_target_pairs={{0,0},{1,8},{2,16},{3,24},{4,32},{5,40},{6,48},{7,56},{8,4},{9,12}... | collective-permute-start | bytes 393224 | tf_op jit(solution)/shard_map/ppermute | solution.py:194
  57.7 10.3 %collective-permute-start.26 = (bf16[1,256,256]{2,1,0:T(8,128)(2,1)}, bf16[1,256,256]{2,1,0:T(8,128)(2,1)S(1)}, u32[]{:S(2)}, u32[]{:S(2)}) collective-permute-start(bf16[1,256,256]{2,1,0:T(8,128)(2,1)} %get-tuple-element.43), channel_id=1, source_target_pairs={{0,0},{1,8},{2,16},{3,24},{4,32},{5,40},{6,48},{7,56},{8,4},{9,12}... | collective-permute-start | bytes 393224 | tf_op jit(solution)/shard_map/ppermute | solution.py:194
  68.0 0.0 collective-permute-done.8.refs_22_
  68.0 1.5 %collective-permute-start.27 = (bf16[1,256,256]{2,1,0:T(8,128)(2,1)S(1)}, bf16[1,256,256]{2,1,0:T(8,128)(2,1)S(1)}, u32[]{:S(2)}, u32[]{:S(2)}) collective-permute-start(bf16[1,256,256]{2,1,0:T(8,128)(2,1)S(1)} %collective-permute-done.5), channel_id=1, source_target_pairs={{0,64},{8,72},{16,80},{24,88},{32,96},{40,104},{48,112},{56,120},{... | collective-permute-start | bytes 393224 | tf_op jit(solution)/shard_map/ppermute | solution.py:198
  69.6 0.0 collective-permute-done.13
  69.6 0.0 collective-permute-start.12
  69.6 0.7 collective-permute-done.26.refs_16_
  70.3 0.0 collective-permute-start.18
  70.3 0.1 shard_map.57.refs_1_
  70.4 2.8 %collective-permute-done.27.refs_17_ = bf16[1,256,256]{2,1,0:T(8,128)(2,1)S(1)} collective-permute-done((bf16[1,256,256]{2,1,0:T(8,128)(2,1)S(1)}, bf16[1,256,256]{2,1,0:T(8,128)(2,1)S(1)}, u32[]{:S(2)}, u32[]{:S(2)}) %collective-permute-start.27) | collective-permute-done | bytes 131104 | tf_op jit(solution)/shard_map/ppermute | solution.py:198
  73.2 4.0 %collective-permute-start.15 = (bf16[2,2,256,256]{3,2,1,0:T(8,128)(2,1)S(1)}, bf16[2,2,256,256]{3,2,1,0:T(8,128)(2,1)S(1)}, u32[]{:S(2)}, u32[]{:S(2)}) collective-permute-start(bf16[2,2,256,256]{3,2,1,0:T(8,128)(2,1)S(1)} %shard_map.57.refs_1_), channel_id=1, source_target_pairs={{0,192},{8,56},{16,208},{24,8},{32,224},{40,24},{48,240},{56,40},{... | collective-permute-start | bytes 1572872 | tf_op jit(solution)/shard_map/ppermute | solution.py:172
  77.1 2.7 %collective-permute-done.12.refs_25_ = bf16[2,256,256]{2,1,0:T(8,128)(2,1)S(1)} collective-permute-done((bf16[2,256,256]{2,1,0:T(8,128)(2,1)S(1)}, bf16[2,256,256]{2,1,0:T(8,128)(2,1)S(1)}, u32[]{:S(2)}, u32[]{:S(2)}) %collective-permute-start.12) | collective-permute-done | bytes 262176 | tf_op jit(solution)/shard_map/ppermute | solution.py:178
  79.8 0.7 collective-permute-start.19
  80.6 0.0 collective-permute-done.11.refs_3_
  80.6 0.0 collective-permute-start.30
  80.6 3.3 %collective-permute-start.29 = (bf16[1,256,256]{2,1,0:T(8,128)(2,1)S(1)}, bf16[1,256,256]{2,1,0:T(8,128)(2,1)S(1)}, u32[]{:S(2)}, u32[]{:S(2)}) collective-permute-start(bf16[1,256,256]{2,1,0:T(8,128)(2,1)S(1)} %collective-permute-done.9), channel_id=1, source_target_pairs={{0,192},{8,200},{16,208},{24,216},{32,224},{40,232},{48,240},{56,2... | collective-permute-start | bytes 393224 | tf_op jit(solution)/shard_map/ppermute | solution.py:198
  83.9 3.0 %collective-permute-done.29.refs_19_ = bf16[1,256,256]{2,1,0:T(8,128)(2,1)S(1)} collective-permute-done((bf16[1,256,256]{2,1,0:T(8,128)(2,1)S(1)}, bf16[1,256,256]{2,1,0:T(8,128)(2,1)S(1)}, u32[]{:S(2)}, u32[]{:S(2)}) %collective-permute-start.29) | collective-permute-done | bytes 131104 | tf_op jit(solution)/shard_map/ppermute | solution.py:198
  86.8 3.1 %collective-permute-start.28 = (bf16[1,256,256]{2,1,0:T(8,128)(2,1)S(1)}, bf16[1,256,256]{2,1,0:T(8,128)(2,1)}, u32[]{:S(2)}, u32[]{:S(2)}) collective-permute-start(bf16[1,256,256]{2,1,0:T(8,128)(2,1)S(1)} %collective-permute-done.13), channel_id=1, source_target_pairs={{0,128},{8,136},{16,144},{24,152},{32,160},{40,168},{48,176},{56,1... | collective-permute-start | bytes 393224 | tf_op jit(solution)/shard_map/ppermute | solution.py:198
  89.9 0.0 collective-permute-start.14
  90.0 2.3 %collective-permute-start.21 = (bf16[2,2,256,256]{3,2,1,0:T(8,128)(2,1)S(1)}, bf16[2,2,256,256]{3,2,1,0:T(8,128)(2,1)S(1)}, u32[]{:S(2)}, u32[]{:S(2)}) collective-permute-start(bf16[2,2,256,256]{3,2,1,0:T(8,128)(2,1)S(1)} %collective-permute-done.11.refs_3_), channel_id=1, source_target_pairs={{0,8},{8,0},{16,24},{24,16},{32,40},{40,32},{48,56},{56,48},{64,72... | collective-permute-start | bytes 1572872 | tf_op jit(solution)/shard_map/ppermute | solution.py:175
  92.3 0.7 collective-permute-done.28.refs_18_
  92.9 0.0 collective-permute-start.16
  92.9 0.0 collective-permute-done.15.refs_5_
  92.9 2.8 %collective-permute-start.17 = (bf16[2,2,256,256]{3,2,1,0:T(8,128)(2,1)S(1)}, bf16[2,2,256,256]{3,2,1,0:T(8,128)(2,1)S(1)}, u32[]{:S(2)}, u32[]{:S(2)}) collective-permute-start(bf16[2,2,256,256]{3,2,1,0:T(8,128)(2,1)S(1)} %collective-permute-done.15.refs_5_), channel_id=1, source_target_pairs={{0,192},{8,56},{16,208},{24,8},{32,224},{40,24},{48,240},{56,40},{... | collective-permute-start | bytes 1572872 | tf_op jit(solution)/shard_map/ppermute | solution.py:172
  95.7 0.4 collective-permute-start.31
  96.1 3.3 %collective-permute-done.14.refs_4_ = bf16[2,2,256,256]{3,2,1,0:T(8,128)(2,1)S(1)} collective-permute-done((bf16[2,2,256,256]{3,2,1,0:T(8,128)(2,1)S(1)}, bf16[2,2,256,256]{3,2,1,0:T(8,128)(2,1)S(1)}, u32[]{:S(2)}, u32[]{:S(2)}) %collective-permute-start.14) | collective-permute-done | bytes 524320 | tf_op jit(solution)/shard_map/ppermute | solution.py:172
  99.4 1.9 %collective-permute-start.20 = (bf16[2,2,256,256]{3,2,1,0:T(8,128)(2,1)S(1)}, bf16[2,2,256,256]{3,2,1,0:T(8,128)(2,1)S(1)}, u32[]{:S(2)}, u32[]{:S(2)}) collective-permute-start(bf16[2,2,256,256]{3,2,1,0:T(8,128)(2,1)S(1)} %collective-permute-done.10.refs_2_), channel_id=1, source_target_pairs={{0,8},{8,0},{16,24},{24,16},{32,40},{40,32},{48,56},{56,48},{64,72... | collective-permute-start | bytes 1572872 | tf_op jit(solution)/shard_map/ppermute | solution.py:175
  101.4 1.1 collective-permute-done.31.refs_24_
  102.4 3.3 %collective-permute-start.23 = (bf16[2,2,256,256]{3,2,1,0:T(8,128)(2,1)S(1)}, bf16[2,2,256,256]{3,2,1,0:T(8,128)(2,1)S(1)}, u32[]{:S(2)}, u32[]{:S(2)}) collective-permute-start(bf16[2,2,256,256]{3,2,1,0:T(8,128)(2,1)S(1)} %collective-permute-done.15.refs_5_), channel_id=1, source_target_pairs={{0,8},{8,0},{16,24},{24,16},{32,40},{40,32},{48,56},{56,48},{64,72... | collective-permute-start | bytes 1572872 | tf_op jit(solution)/shard_map/ppermute | solution.py:175
  105.7 0.1 collective-permute-start.22
  105.8 1.1 collective-permute-start.24
  107.0 0.0 collective-permute-done.17.refs_7_
  107.0 0.3 collective-permute-start.25
  107.3 0.0 collective-permute-done.20.refs_10_
  107.3 0.0 collective-permute-done.23.refs_13_
  107.3 0.7 collective-permute-done.22.refs_12_
  108.0 0.7 collective-permute-done.24.refs_14_
  108.8 0.0 copy-done.13
  108.8 0.8 copy-done.14
  109.6 0.0 collective-permute-done.25.refs_15_
  109.7 13.7 %shard_map.58 = bf16[8,4,32,256]{3,2,1,0:T(8,128)(2,1)} custom-call(s32[32]{0:T(128)} %left_sizes.3, s32[32]{0:T(128)} %right_sizes.3, bf16[2,2,256,256]{3,2,1,0:T(8,128)(2,1)} %copy-done, bf16[2,2,256,256]{3,2,1,0:T(8,128)(2,1)} %copy-done.1, bf16[2,2,256,256]{3,2,1,0:T(8,128)(2,1)} %copy-done.3, bf16[2,2,256,256]{3,2,1,0:T(8,128)(2,1)} %copy-done.2, ...), custom_call_target="tpu_custom_call" | custom-call | tf_op jit(solution)/shard_map/pallas_call | solution.py:135
  123.4 21.4 %all_to_all.5 = bf16[8,4,32,256]{3,2,1,0:T(8,128)(2,1)S(1)} all-to-all(bf16[8,4,32,256]{3,2,1,0:T(8,128)(2,1)} %shard_map.58), channel_id=1, replica_groups=mesh['blk'=32,'mpo'=8] {'mpo'}, dimensions={0} | all-to-all | bytes 1048576 | tf_op jit(solution)/shard_map/all_to_all | solution.py:230
  144.8 0.8 copy.6
  (52 shorter events, 0.1 us)
Async XLA Ops:
  0.0 15.6 %collective-permute-start = (bf16[2,256,256]{2,1,0:T(8,128)(2,1)}, bf16[2,256,256]{2,1,0:T(8,128)(2,1)S(1)}, u32[]{:S(2)}, u32[]{:S(2)}) collective-permute-start(bf16[2,256,256]{2,1,0:T(8,128)(2,1)} %param.6), channel_id=1, source_target_pairs={{0,0},{1,8},{2,16},{3,24},{4,32},{5,40},{6,48},{7,56},{8,4},{9,12}... | collective-permute-start | bytes 786440 | tf_op jit(solution)/shard_map/ppermute | solution.py:188
  10.2 20.0 %collective-permute-start.3 = (bf16[2,256,256]{2,1,0:T(8,128)(2,1)}, bf16[2,256,256]{2,1,0:T(8,128)(2,1)S(1)}, u32[]{:S(2)}, u32[]{:S(2)}) collective-permute-start(bf16[2,256,256]{2,1,0:T(8,128)(2,1)} %refs_20_.1), channel_id=1, source_target_pairs={{0,1},{1,2},{2,3},{3,4},{4,5},{5,6},{6,7},{7,0},{8,9},{9,10},{10,1... | collective-permute-start | bytes 786440 | tf_op jit(solution)/shard_map/ppermute | solution.py:178
  10.3 19.9 %collective-permute-start.4 = (bf16[2,256,256]{2,1,0:T(8,128)(2,1)}, bf16[2,256,256]{2,1,0:T(8,128)(2,1)S(1)}, u32[]{:S(2)}, u32[]{:S(2)}) collective-permute-start(bf16[2,256,256]{2,1,0:T(8,128)(2,1)} %refs_20_.1), channel_id=1, source_target_pairs={{0,7},{1,0},{2,1},{3,2},{4,3},{5,4},{6,5},{7,6},{8,15},{9,8},{10,9... | collective-permute-start | bytes 786440 | tf_op jit(solution)/shard_map/ppermute | solution.py:181
  15.6 16.8 %collective-permute-start.2 = (bf16[2,256,256]{2,1,0:T(8,128)(2,1)S(1)}, bf16[2,256,256]{2,1,0:T(8,128)(2,1)S(1)}, u32[]{:S(2)}, u32[]{:S(2)}) collective-permute-start(bf16[2,256,256]{2,1,0:T(8,128)(2,1)S(1)} %collective-permute-done.refs_0_), channel_id=1, source_target_pairs={{0,48},{8,200},{16,0},{24,216},{32,16},{40,232},{48,32},{56,248},{... | collective-permute-start | bytes 786440 | tf_op jit(solution)/shard_map/ppermute | solution.py:169
  18.4 14.0 %collective-permute-start.1 = (bf16[2,256,256]{2,1,0:T(8,128)(2,1)S(1)}, bf16[2,256,256]{2,1,0:T(8,128)(2,1)S(1)}, u32[]{:S(2)}, u32[]{:S(2)}) collective-permute-start(bf16[2,256,256]{2,1,0:T(8,128)(2,1)S(1)} %collective-permute-done.refs_0_), channel_id=1, source_target_pairs={{0,16},{8,72},{16,32},{24,88},{32,48},{40,104},{48,0},{56,120},{64... | collective-permute-start | bytes 786440 | tf_op jit(solution)/shard_map/ppermute | solution.py:169
  18.4 14.0 %collective-permute-start.5 = (bf16[1,256,256]{2,1,0:T(8,128)(2,1)}, bf16[1,256,256]{2,1,0:T(8,128)(2,1)S(1)}, u32[]{:S(2)}, u32[]{:S(2)}) collective-permute-start(bf16[1,256,256]{2,1,0:T(8,128)(2,1)} %get-tuple-element.32), channel_id=1, source_target_pairs={{0,0},{1,8},{2,16},{3,24},{4,32},{5,40},{6,48},{7,56},{8,4},{9,12}... | collective-permute-start | bytes 393224 | tf_op jit(solution)/shard_map/ppermute | solution.py:194
  30.2 79.5 %copy-start.15 = (bf16[2,256,256]{2,1,0:T(8,128)(2,1)}, bf16[2,256,256]{2,1,0:T(8,128)(2,1)S(1)}, u32[]{:S(2)}) copy-start(bf16[2,256,256]{2,1,0:T(8,128)(2,1)S(1)} %collective-permute-done.3.refs_27_) | copy-start | bytes 786436
  30.2 40.1 %copy-start.16 = (bf16[2,256,256]{2,1,0:T(8,128)(2,1)}, bf16[2,256,256]{2,1,0:T(8,128)(2,1)S(1)}, u32[]{:S(2)}) copy-start(bf16[2,256,256]{2,1,0:T(8,128)(2,1)S(1)} %collective-permute-done.4.refs_21_) | copy-start | bytes 786436
  32.4 16.1 %collective-permute-start.6 = (bf16[2,256,256]{2,1,0:T(8,128)(2,1)S(1)}, bf16[2,256,256]{2,1,0:T(8,128)(2,1)S(1)}, u32[]{:S(2)}, u32[]{:S(2)}) collective-permute-start(bf16[2,256,256]{2,1,0:T(8,128)(2,1)S(1)} %collective-permute-done.1.refs_1_), channel_id=1, source_target_pairs={{0,16},{8,72},{16,32},{24,88},{32,48},{40,104},{48,0},{56,120},{64... | collective-permute-start | bytes 786440 | tf_op jit(solution)/shard_map/ppermute | solution.py:169
  33.7 24.0 %collective-permute-start.7 = (bf16[2,256,256]{2,1,0:T(8,128)(2,1)S(1)}, bf16[2,256,256]{2,1,0:T(8,128)(2,1)S(1)}, u32[]{:S(2)}, u32[]{:S(2)}) collective-permute-start(bf16[2,256,256]{2,1,0:T(8,128)(2,1)S(1)} %collective-permute-done.3.refs_27_), channel_id=1, source_target_pairs={{0,1},{1,2},{2,3},{3,4},{4,5},{5,6},{6,7},{7,0},{8,9},{9,10},{10,1... | collective-permute-start | bytes 786440 | tf_op jit(solution)/shard_map/ppermute | solution.py:178
  33.7 14.8 %collective-permute-start.9 = (bf16[1,256,256]{2,1,0:T(8,128)(2,1)}, bf16[1,256,256]{2,1,0:T(8,128)(2,1)S(1)}, u32[]{:S(2)}, u32[]{:S(2)}) collective-permute-start(bf16[1,256,256]{2,1,0:T(8,128)(2,1)} %get-tuple-element.37), channel_id=1, source_target_pairs={{0,0},{1,8},{2,16},{3,24},{4,32},{5,40},{6,48},{7,56},{8,4},{9,12}... | collective-permute-start | bytes 393224 | tf_op jit(solution)/shard_map/ppermute | solution.py:194
  45.6 22.4 %collective-permute-start.8 = (bf16[2,256,256]{2,1,0:T(8,128)(2,1)S(1)}, bf16[2,256,256]{2,1,0:T(8,128)(2,1)S(1)}, u32[]{:S(2)}, u32[]{:S(2)}) collective-permute-start(bf16[2,256,256]{2,1,0:T(8,128)(2,1)S(1)} %collective-permute-done.4.refs_21_), channel_id=1, source_target_pairs={{0,7},{1,0},{2,1},{3,2},{4,3},{5,4},{6,5},{7,6},{8,15},{9,8},{10,9... | collective-permute-start | bytes 786440 | tf_op jit(solution)/shard_map/ppermute | solution.py:181
  45.8 63.9 %copy-start = (bf16[2,2,256,256]{3,2,1,0:T(8,128)(2,1)}, bf16[2,2,256,256]{3,2,1,0:T(8,128)(2,1)S(1)}, u32[]{:S(2)}) copy-start(bf16[2,2,256,256]{3,2,1,0:T(8,128)(2,1)S(1)} %shard_map.56.refs_0_) | copy-start | bytes 1572868
  45.8 34.8 %collective-permute-start.11 = (bf16[2,2,256,256]{3,2,1,0:T(8,128)(2,1)S(1)}, bf16[2,2,256,256]{3,2,1,0:T(8,128)(2,1)S(1)}, u32[]{:S(2)}, u32[]{:S(2)}) collective-permute-start(bf16[2,2,256,256]{3,2,1,0:T(8,128)(2,1)S(1)} %shard_map.56.refs_0_), channel_id=1, source_target_pairs={{0,192},{8,56},{16,208},{24,8},{32,224},{40,24},{48,240},{56,40},{... | collective-permute-start | bytes 1572872 | tf_op jit(solution)/shard_map/ppermute | solution.py:172
  48.5 32.0 %collective-permute-start.10 = (bf16[2,2,256,256]{3,2,1,0:T(8,128)(2,1)S(1)}, bf16[2,2,256,256]{3,2,1,0:T(8,128)(2,1)S(1)}, u32[]{:S(2)}, u32[]{:S(2)}) collective-permute-start(bf16[2,2,256,256]{3,2,1,0:T(8,128)(2,1)S(1)} %shard_map.56.refs_0_), channel_id=1, source_target_pairs={{0,64},{8,24},{16,80},{24,40},{32,96},{40,56},{48,112},{56,8},{64,... | collective-permute-start | bytes 1572872 | tf_op jit(solution)/shard_map/ppermute | solution.py:172
  48.5 21.0 %collective-permute-start.13 = (bf16[1,256,256]{2,1,0:T(8,128)(2,1)}, bf16[1,256,256]{2,1,0:T(8,128)(2,1)S(1)}, u32[]{:S(2)}, u32[]{:S(2)}) collective-permute-start(bf16[1,256,256]{2,1,0:T(8,128)(2,1)} %get-tuple-element.40), channel_id=1, source_target_pairs={{0,0},{1,8},{2,16},{3,24},{4,32},{5,40},{6,48},{7,56},{8,4},{9,12}... | collective-permute-start | bytes 393224 | tf_op jit(solution)/shard_map/ppermute | solution.py:194
  57.7 19.4 %copy-start.17 = (bf16[2,256,256]{2,1,0:T(8,128)(2,1)}, bf16[2,256,256]{2,1,0:T(8,128)(2,1)S(1)}, u32[]{:S(2)}) copy-start(bf16[2,256,256]{2,1,0:T(8,128)(2,1)S(1)} %collective-permute-done.7.refs_26_) | copy-start | bytes 786436
  57.7 12.5 %collective-permute-start.26 = (bf16[1,256,256]{2,1,0:T(8,128)(2,1)}, bf16[1,256,256]{2,1,0:T(8,128)(2,1)S(1)}, u32[]{:S(2)}, u32[]{:S(2)}) collective-permute-start(bf16[1,256,256]{2,1,0:T(8,128)(2,1)} %get-tuple-element.43), channel_id=1, source_target_pairs={{0,0},{1,8},{2,16},{3,24},{4,32},{5,40},{6,48},{7,56},{8,4},{9,12}... | collective-permute-start | bytes 393224 | tf_op jit(solution)/shard_map/ppermute | solution.py:194
  68.0 21.9 %copy-start.18 = (bf16[2,256,256]{2,1,0:T(8,128)(2,1)}, bf16[2,256,256]{2,1,0:T(8,128)(2,1)S(1)}, u32[]{:S(2)}) copy-start(bf16[2,256,256]{2,1,0:T(8,128)(2,1)S(1)} %collective-permute-done.8.refs_22_) | copy-start | bytes 786436
  68.0 5.1 %collective-permute-start.27 = (bf16[1,256,256]{2,1,0:T(8,128)(2,1)S(1)}, bf16[1,256,256]{2,1,0:T(8,128)(2,1)S(1)}, u32[]{:S(2)}, u32[]{:S(2)}) collective-permute-start(bf16[1,256,256]{2,1,0:T(8,128)(2,1)S(1)} %collective-permute-done.5), channel_id=1, source_target_pairs={{0,64},{8,72},{16,80},{24,88},{32,96},{40,104},{48,112},{56,120},{... | collective-permute-start | bytes 393224 | tf_op jit(solution)/shard_map/ppermute | solution.py:198
  69.6 10.2 %collective-permute-start.12 = (bf16[2,256,256]{2,1,0:T(8,128)(2,1)S(1)}, bf16[2,256,256]{2,1,0:T(8,128)(2,1)S(1)}, u32[]{:S(2)}, u32[]{:S(2)}) collective-permute-start(bf16[2,256,256]{2,1,0:T(8,128)(2,1)S(1)} %collective-permute-done.7.refs_26_), channel_id=1, source_target_pairs={{0,1},{1,2},{2,3},{3,4},{4,5},{5,6},{6,7},{7,0},{8,9},{9,10},{10,1... | collective-permute-start | bytes 786440 | tf_op jit(solution)/shard_map/ppermute | solution.py:178
  70.3 39.4 %copy-start.20 = (bf16[1,256,256]{2,1,0:T(8,128)(2,1)}, bf16[1,256,256]{2,1,0:T(8,128)(2,1)S(1)}, u32[]{:S(2)}) copy-start(bf16[1,256,256]{2,1,0:T(8,128)(2,1)S(1)} %collective-permute-done.26.refs_16_) | copy-start | bytes 393220
  70.3 19.7 %collective-permute-start.18 = (bf16[2,2,256,256]{3,2,1,0:T(8,128)(2,1)S(1)}, bf16[2,2,256,256]{3,2,1,0:T(8,128)(2,1)S(1)}, u32[]{:S(2)}, u32[]{:S(2)}) collective-permute-start(bf16[2,2,256,256]{3,2,1,0:T(8,128)(2,1)S(1)} %shard_map.56.refs_0_), channel_id=1, source_target_pairs={{0,8},{8,0},{16,24},{24,16},{32,40},{40,32},{48,56},{56,48},{64,72... | collective-permute-start | bytes 1572872 | tf_op jit(solution)/shard_map/ppermute | solution.py:175
  70.3 39.3 %copy-start.1 = (bf16[2,2,256,256]{3,2,1,0:T(8,128)(2,1)}, bf16[2,2,256,256]{3,2,1,0:T(8,128)(2,1)S(1)}, u32[]{:S(2)}) copy-start(bf16[2,2,256,256]{3,2,1,0:T(8,128)(2,1)S(1)} %shard_map.57.refs_1_) | copy-start | bytes 1572868
  73.2 16.8 %copy-start.21 = (bf16[1,256,256]{2,1,0:T(8,128)(2,1)}, bf16[1,256,256]{2,1,0:T(8,128)(2,1)S(1)}, u32[]{:S(2)}) copy-start(bf16[1,256,256]{2,1,0:T(8,128)(2,1)S(1)} %collective-permute-done.27.refs_17_) | copy-start | bytes 393220
  73.2 19.8 %collective-permute-start.15 = (bf16[2,2,256,256]{3,2,1,0:T(8,128)(2,1)S(1)}, bf16[2,2,256,256]{3,2,1,0:T(8,128)(2,1)S(1)}, u32[]{:S(2)}, u32[]{:S(2)}) collective-permute-start(bf16[2,2,256,256]{3,2,1,0:T(8,128)(2,1)S(1)} %shard_map.57.refs_1_), channel_id=1, source_target_pairs={{0,192},{8,56},{16,208},{24,8},{32,224},{40,24},{48,240},{56,40},{... | collective-permute-start | bytes 1572872 | tf_op jit(solution)/shard_map/ppermute | solution.py:172
  79.8 21.5 %copy-start.19 = (bf16[2,256,256]{2,1,0:T(8,128)(2,1)}, bf16[2,256,256]{2,1,0:T(8,128)(2,1)S(1)}, u32[]{:S(2)}) copy-start(bf16[2,256,256]{2,1,0:T(8,128)(2,1)S(1)} %collective-permute-done.12.refs_25_) | copy-start | bytes 786436
  79.8 15.9 %collective-permute-start.19 = (bf16[2,2,256,256]{3,2,1,0:T(8,128)(2,1)S(1)}, bf16[2,2,256,256]{3,2,1,0:T(8,128)(2,1)S(1)}, u32[]{:S(2)}, u32[]{:S(2)}) collective-permute-start(bf16[2,2,256,256]{3,2,1,0:T(8,128)(2,1)S(1)} %shard_map.57.refs_1_), channel_id=1, source_target_pairs={{0,8},{8,0},{16,24},{24,16},{32,40},{40,32},{48,56},{56,48},{64,72... | collective-permute-start | bytes 1572872 | tf_op jit(solution)/shard_map/ppermute | solution.py:175
  80.6 29.1 %copy-start.2 = (bf16[2,2,256,256]{3,2,1,0:T(8,128)(2,1)}, bf16[2,2,256,256]{3,2,1,0:T(8,128)(2,1)S(1)}, u32[]{:S(2)}) copy-start(bf16[2,2,256,256]{3,2,1,0:T(8,128)(2,1)S(1)} %collective-permute-done.11.refs_3_) | copy-start | bytes 1572868
  80.6 9.3 %collective-permute-start.30 = (bf16[2,256,256]{2,1,0:T(8,128)(2,1)S(1)}, bf16[2,256,256]{2,1,0:T(8,128)(2,1)}, u32[]{:S(2)}, u32[]{:S(2)}) collective-permute-start(bf16[2,256,256]{2,1,0:T(8,128)(2,1)S(1)} %collective-permute-done.8.refs_22_), channel_id=1, source_target_pairs={{0,7},{1,0},{2,1},{3,2},{4,3},{5,4},{6,5},{7,6},{8,15},{9,8},{10,9... | collective-permute-start | bytes 786440 | tf_op jit(solution)/shard_map/ppermute | solution.py:181
  80.6 29.1 %copy-start.3 = (bf16[2,2,256,256]{3,2,1,0:T(8,128)(2,1)}, bf16[2,2,256,256]{3,2,1,0:T(8,128)(2,1)S(1)}, u32[]{:S(2)}) copy-start(bf16[2,2,256,256]{3,2,1,0:T(8,128)(2,1)S(1)} %collective-permute-done.10.refs_2_) | copy-start | bytes 1572868
  80.6 6.3 %collective-permute-start.29 = (bf16[1,256,256]{2,1,0:T(8,128)(2,1)S(1)}, bf16[1,256,256]{2,1,0:T(8,128)(2,1)S(1)}, u32[]{:S(2)}, u32[]{:S(2)}) collective-permute-start(bf16[1,256,256]{2,1,0:T(8,128)(2,1)S(1)} %collective-permute-done.9), channel_id=1, source_target_pairs={{0,192},{8,200},{16,208},{24,216},{32,224},{40,232},{48,240},{56,2... | collective-permute-start | bytes 393224 | tf_op jit(solution)/shard_map/ppermute | solution.py:198
  86.8 3.1 %copy-start.22 = (bf16[1,256,256]{2,1,0:T(8,128)(2,1)}, bf16[1,256,256]{2,1,0:T(8,128)(2,1)S(1)}, u32[]{:S(2)}) copy-start(bf16[1,256,256]{2,1,0:T(8,128)(2,1)S(1)} %collective-permute-done.29.refs_19_) | copy-start | bytes 393220
  86.8 6.1 %collective-permute-start.28 = (bf16[1,256,256]{2,1,0:T(8,128)(2,1)S(1)}, bf16[1,256,256]{2,1,0:T(8,128)(2,1)}, u32[]{:S(2)}, u32[]{:S(2)}) collective-permute-start(bf16[1,256,256]{2,1,0:T(8,128)(2,1)S(1)} %collective-permute-done.13), channel_id=1, source_target_pairs={{0,128},{8,136},{16,144},{24,152},{32,160},{40,168},{48,176},{56,1... | collective-permute-start | bytes 393224 | tf_op jit(solution)/shard_map/ppermute | solution.py:198
  89.9 9.5 %collective-permute-start.14 = (bf16[2,2,256,256]{3,2,1,0:T(8,128)(2,1)S(1)}, bf16[2,2,256,256]{3,2,1,0:T(8,128)(2,1)S(1)}, u32[]{:S(2)}, u32[]{:S(2)}) collective-permute-start(bf16[2,2,256,256]{3,2,1,0:T(8,128)(2,1)S(1)} %shard_map.57.refs_1_), channel_id=1, source_target_pairs={{0,64},{8,24},{16,80},{24,40},{32,96},{40,56},{48,112},{56,8},{64,... | collective-permute-start | bytes 1572872 | tf_op jit(solution)/shard_map/ppermute | solution.py:172
  89.9 19.7 %copy-start.4 = (bf16[2,2,256,256]{3,2,1,0:T(8,128)(2,1)}, bf16[2,2,256,256]{3,2,1,0:T(8,128)(2,1)S(1)}, u32[]{:S(2)}) copy-start(bf16[2,2,256,256]{3,2,1,0:T(8,128)(2,1)S(1)} %collective-permute-done.18.refs_8_) | copy-start | bytes 1572868
  90.0 15.8 %collective-permute-start.21 = (bf16[2,2,256,256]{3,2,1,0:T(8,128)(2,1)S(1)}, bf16[2,2,256,256]{3,2,1,0:T(8,128)(2,1)S(1)}, u32[]{:S(2)}, u32[]{:S(2)}) collective-permute-start(bf16[2,2,256,256]{3,2,1,0:T(8,128)(2,1)S(1)} %collective-permute-done.11.refs_3_), channel_id=1, source_target_pairs={{0,8},{8,0},{16,24},{24,16},{32,40},{40,32},{48,56},{56,48},{64,72... | collective-permute-start | bytes 1572872 | tf_op jit(solution)/shard_map/ppermute | solution.py:175
  92.9 12.9 %collective-permute-start.16 = (bf16[2,2,256,256]{3,2,1,0:T(8,128)(2,1)S(1)}, bf16[2,2,256,256]{3,2,1,0:T(8,128)(2,1)S(1)}, u32[]{:S(2)}, u32[]{:S(2)}) collective-permute-start(bf16[2,2,256,256]{3,2,1,0:T(8,128)(2,1)S(1)} %collective-permute-done.10.refs_2_), channel_id=1, source_target_pairs={{0,64},{8,24},{16,80},{24,40},{32,96},{40,56},{48,112},{56,8},{64,... | collective-permute-start | bytes 1572872 | tf_op jit(solution)/shard_map/ppermute | solution.py:172
  92.9 16.8 %copy-start.5 = (bf16[2,2,256,256]{3,2,1,0:T(8,128)(2,1)}, bf16[2,2,256,256]{3,2,1,0:T(8,128)(2,1)S(1)}, u32[]{:S(2)}) copy-start(bf16[2,2,256,256]{3,2,1,0:T(8,128)(2,1)S(1)} %collective-permute-done.15.refs_5_) | copy-start | bytes 1572868
  92.9 14.0 %collective-permute-start.17 = (bf16[2,2,256,256]{3,2,1,0:T(8,128)(2,1)S(1)}, bf16[2,2,256,256]{3,2,1,0:T(8,128)(2,1)S(1)}, u32[]{:S(2)}, u32[]{:S(2)}) collective-permute-start(bf16[2,2,256,256]{3,2,1,0:T(8,128)(2,1)S(1)} %collective-permute-done.15.refs_5_), channel_id=1, source_target_pairs={{0,192},{8,56},{16,208},{24,8},{32,224},{40,24},{48,240},{56,40},{... | collective-permute-start | bytes 1572872 | tf_op jit(solution)/shard_map/ppermute | solution.py:172
  95.7 14.0 %copy-start.6 = (bf16[2,2,256,256]{3,2,1,0:T(8,128)(2,1)}, bf16[2,2,256,256]{3,2,1,0:T(8,128)(2,1)S(1)}, u32[]{:S(2)}) copy-start(bf16[2,2,256,256]{3,2,1,0:T(8,128)(2,1)S(1)} %collective-permute-done.19.refs_9_) | copy-start | bytes 1572868
  95.7 6.7 %collective-permute-start.31 = (bf16[2,256,256]{2,1,0:T(8,128)(2,1)S(1)}, bf16[2,256,256]{2,1,0:T(8,128)(2,1)}, u32[]{:S(2)}, u32[]{:S(2)}) collective-permute-start(bf16[2,256,256]{2,1,0:T(8,128)(2,1)S(1)} %collective-permute-done.12.refs_25_), channel_id=1, source_target_pairs={{0,1},{1,2},{2,3},{3,4},{4,5},{5,6},{6,7},{7,0},{8,9},{9,10},{10,1... | collective-permute-start | bytes 786440 | tf_op jit(solution)/shard_map/ppermute | solution.py:178
  99.4 7.9 %copy-start.7 = (bf16[2,2,256,256]{3,2,1,0:T(8,128)(2,1)}, bf16[2,2,256,256]{3,2,1,0:T(8,128)(2,1)S(1)}, u32[]{:S(2)}) copy-start(bf16[2,2,256,256]{3,2,1,0:T(8,128)(2,1)S(1)} %collective-permute-done.14.refs_4_) | copy-start | bytes 1572868
  99.4 7.8 %collective-permute-start.20 = (bf16[2,2,256,256]{3,2,1,0:T(8,128)(2,1)S(1)}, bf16[2,2,256,256]{3,2,1,0:T(8,128)(2,1)S(1)}, u32[]{:S(2)}, u32[]{:S(2)}) collective-permute-start(bf16[2,2,256,256]{3,2,1,0:T(8,128)(2,1)S(1)} %collective-permute-done.10.refs_2_), channel_id=1, source_target_pairs={{0,8},{8,0},{16,24},{24,16},{32,40},{40,32},{48,56},{56,48},{64,72... | collective-permute-start | bytes 1572872 | tf_op jit(solution)/shard_map/ppermute | solution.py:175
  102.4 4.9 %collective-permute-start.23 = (bf16[2,2,256,256]{3,2,1,0:T(8,128)(2,1)S(1)}, bf16[2,2,256,256]{3,2,1,0:T(8,128)(2,1)S(1)}, u32[]{:S(2)}, u32[]{:S(2)}) collective-permute-start(bf16[2,2,256,256]{3,2,1,0:T(8,128)(2,1)S(1)} %collective-permute-done.15.refs_5_), channel_id=1, source_target_pairs={{0,8},{8,0},{16,24},{24,16},{32,40},{40,32},{48,56},{56,48},{64,72... | collective-permute-start | bytes 1572872 | tf_op jit(solution)/shard_map/ppermute | solution.py:175
  105.7 2.3 %copy-start.8 = (bf16[2,2,256,256]{3,2,1,0:T(8,128)(2,1)}, bf16[2,2,256,256]{3,2,1,0:T(8,128)(2,1)S(1)}, u32[]{:S(2)}) copy-start(bf16[2,2,256,256]{3,2,1,0:T(8,128)(2,1)S(1)} %collective-permute-done.21.refs_11_) | copy-start | bytes 1572868
  105.7 2.3 %collective-permute-start.22 = (bf16[2,2,256,256]{3,2,1,0:T(8,128)(2,1)S(1)}, bf16[2,2,256,256]{3,2,1,0:T(8,128)(2,1)S(1)}, u32[]{:S(2)}, u32[]{:S(2)}) collective-permute-start(bf16[2,2,256,256]{3,2,1,0:T(8,128)(2,1)S(1)} %collective-permute-done.14.refs_4_), channel_id=1, source_target_pairs={{0,8},{8,0},{16,24},{24,16},{32,40},{40,32},{48,56},{56,48},{64,72... | collective-permute-start | bytes 1572872 | tf_op jit(solution)/shard_map/ppermute | solution.py:175
  105.8 2.9 %copy-start.9 = (bf16[2,2,256,256]{3,2,1,0:T(8,128)(2,1)}, bf16[2,2,256,256]{3,2,1,0:T(8,128)(2,1)S(1)}, u32[]{:S(2)}) copy-start(bf16[2,2,256,256]{3,2,1,0:T(8,128)(2,1)S(1)} %collective-permute-done.16.refs_6_) | copy-start | bytes 1572868
  105.8 2.9 %collective-permute-start.24 = (bf16[2,2,256,256]{3,2,1,0:T(8,128)(2,1)S(1)}, bf16[2,2,256,256]{3,2,1,0:T(8,128)(2,1)S(1)}, u32[]{:S(2)}, u32[]{:S(2)}) collective-permute-start(bf16[2,2,256,256]{3,2,1,0:T(8,128)(2,1)S(1)} %collective-permute-done.16.refs_6_), channel_id=1, source_target_pairs={{0,8},{8,0},{16,24},{24,16},{32,40},{40,32},{48,56},{56,48},{64,72... | collective-permute-start | bytes 1572872 | tf_op jit(solution)/shard_map/ppermute | solution.py:175
  107.0 1.8 %copy-start.10 = (bf16[2,2,256,256]{3,2,1,0:T(8,128)(2,1)}, bf16[2,2,256,256]{3,2,1,0:T(8,128)(2,1)S(1)}, u32[]{:S(2)}) copy-start(bf16[2,2,256,256]{3,2,1,0:T(8,128)(2,1)S(1)} %collective-permute-done.17.refs_7_) | copy-start | bytes 1572868
  107.0 2.7 %collective-permute-start.25 = (bf16[2,2,256,256]{3,2,1,0:T(8,128)(2,1)S(1)}, bf16[2,2,256,256]{3,2,1,0:T(8,128)(2,1)}, u32[]{:S(2)}, u32[]{:S(2)}) collective-permute-start(bf16[2,2,256,256]{3,2,1,0:T(8,128)(2,1)S(1)} %collective-permute-done.17.refs_7_), channel_id=1, source_target_pairs={{0,8},{8,0},{16,24},{24,16},{32,40},{40,32},{48,56},{56,48},{64,72... | collective-permute-start | bytes 1572872 | tf_op jit(solution)/shard_map/ppermute | solution.py:175
  107.3 1.5 %copy-start.11 = (bf16[2,2,256,256]{3,2,1,0:T(8,128)(2,1)}, bf16[2,2,256,256]{3,2,1,0:T(8,128)(2,1)S(1)}, u32[]{:S(2)}) copy-start(bf16[2,2,256,256]{3,2,1,0:T(8,128)(2,1)S(1)} %collective-permute-done.20.refs_10_) | copy-start | bytes 1572868
  107.3 1.5 %copy-start.12 = (bf16[2,2,256,256]{3,2,1,0:T(8,128)(2,1)}, bf16[2,2,256,256]{3,2,1,0:T(8,128)(2,1)S(1)}, u32[]{:S(2)}) copy-start(bf16[2,2,256,256]{3,2,1,0:T(8,128)(2,1)S(1)} %collective-permute-done.23.refs_13_) | copy-start | bytes 1572868
  108.0 0.8 copy-start.13
  108.8 0.8 copy-start.14

commit v6 on v0

v6 whole, which is shorter than its diff:
```python
import functools

import jax
import jax.numpy as jnp
from jax import lax
from jax.experimental import pallas as pl
from jax.experimental.pallas import tpu as pltpu
from jax.sharding import PartitionSpec as P

MIB = 1024 * 1024
SIDE = 4
OFFSETS = (0, SIDE - 1, 1, 2)
ANYWHERE = pl.BlockSpec(memory_space=pl.ANY)
SMEM = pl.BlockSpec(memory_space=pltpu.SMEM)
VMEM = pl.BlockSpec(memory_space=pltpu.VMEM)


def place(y, x, core):
    return ((y % SIDE) * SIDE + x % SIDE) * 2 + core


def stack_kernel(*refs):
    inputs, out, sems = refs[:-2], refs[-2], refs[-1]
    copies = [pltpu.make_async_copy(ref, out.at[i], sems.at[i]) for i, ref in enumerate(inputs)]
    for copy in copies:
        copy.start()
    for copy in copies:
        copy.wait()


def stack(*pieces):
    return pl.pallas_call(
        stack_kernel,
        out_shape=jax.ShapeDtypeStruct((len(pieces), *pieces[0].shape), pieces[0].dtype),
        in_specs=[ANYWHERE] * len(pieces),
        out_specs=ANYWHERE,
        scratch_shapes=[pltpu.SemaphoreType.DMA((len(pieces),))],
        compiler_params=pltpu.CompilerParams(vmem_limit_bytes=MIB),
    )(*pieces)


def split_kernel(psi_ref, out_ref, sems):
    sectors, _, right_dim = out_ref.shape
    copies = []
    for b in range(sectors):
        source = psi_ref.at[:, pl.ds(b * right_dim, right_dim)]
        copies.append(pltpu.make_async_copy(source, out_ref.at[b], sems.at[b]))
    for copy in copies:
        copy.start()
    for copy in copies:
        copy.wait()


def split(wavefunction, sectors):
    left_dim, columns = wavefunction.shape
    return pl.pallas_call(
        split_kernel,
        out_shape=jax.ShapeDtypeStruct((sectors, left_dim, columns // sectors), wavefunction.dtype),
        in_specs=[ANYWHERE],
        out_specs=ANYWHERE,
        scratch_shapes=[pltpu.SemaphoreType.DMA((sectors,))],
        compiler_params=pltpu.CompilerParams(vmem_limit_bytes=60 * MIB),
    )(wavefunction)


def fetch(refs, held, sems, first):
    copies = [pltpu.make_async_copy(r, h, sems.at[first + i]) for i, (r, h) in enumerate(zip(refs, held))]
    for copy in copies:
        copy.start()
    return copies


def apply_kernel(groups, carried, left_sizes, right_sizes, *refs):
    refs, (out_ref, held, psi_held, right_held, middle, result, sems, out_sems) = refs[:-8], refs[-8:]
    refs = refs[1:] if carried else refs
    sector, rank = lax.axis_index("blk"), lax.axis_index("mpo")
    core, x0, y0 = sector % 2, sector // 2 % SIDE, sector // (2 * SIDE)
    sectors, rows, right_dim = out_ref.shape
    pieces = [piece for group in groups for piece in group]
    blocks, psi_ref, rights = refs[: len(pieces)], refs[len(pieces)], refs[len(pieces) + 1 :]
    ranks = len(rights)
    coming = fetch(blocks[: len(groups[0])], [held.at[i] for i in range(len(groups[0]))], sems, 0)
    psi_copy = pltpu.make_async_copy(psi_ref, psi_held, sems.at[len(pieces)])
    psi_copy.start()
    right_copies = fetch(rights, [right_held.at[i] for i in range(ranks)], sems, len(pieces) + 1)
    for i in range(len(groups[0]), len(pieces)):
        coming += fetch(blocks[i : i + 1], [held.at[i]], sems, i)
    own_right = right_sizes[sector]
    left_dim = psi_held.shape[1]
    psi_row = lax.broadcasted_iota(jnp.int32, (left_dim, right_dim), 0)
    psi_col = lax.broadcasted_iota(jnp.int32, (left_dim, right_dim), 1)
    row = rank * rows + lax.broadcasted_iota(jnp.int32, (rows, right_dim), 0)
    col = lax.broadcasted_iota(jnp.int32, (rows, right_dim), 1)
    psi_copy.wait()
    at, going = 0, []
    for number, group in enumerate(groups):
        places = []
        for sibling, far, first in group:
            coming[at].wait()
            tree = 1 - core if sibling else core
            for k in range(held.shape[1]):
                near = OFFSETS[first + k]
                y = jnp.where(tree == 0, y0 + far, y0 + near) & (SIDE - 1)
                x = jnp.where(tree == 0, x0 + near, x0 + far) & (SIDE - 1)
                a = (y * SIDE + x) * 2 + tree
                inside = jnp.logical_and(psi_row < left_sizes[a], psi_col < own_right)
                psi = jnp.where(inside, psi_held[a].astype(jnp.float32), 0.0).astype(middle.dtype)
                block = held[at, k].reshape(2 * ranks * rows, left_dim)
                both = jnp.dot(block, psi, preferred_element_type=jnp.float32).astype(middle.dtype)
                middle[:, len(places)] = both.reshape(2 * ranks, rows, right_dim)
                places.append(a)
            at += 1
        if number == 0:
            for copy in right_copies:
                copy.wait()
        count = len(places)
        total = jnp.zeros((count * rows, right_dim), jnp.float32)
        for w in range(2 * ranks):
            right = right_held[(w // 2 - rank) & (ranks - 1), w % 2]
            block = middle[w, :count].reshape(count * rows, right_dim)
            total += jnp.dot(block, right, preferred_element_type=jnp.float32)
        for i, a in enumerate(places):
            inside = jnp.logical_and(row < left_sizes[a], col < own_right)
            part = jnp.where(inside, total[i * rows : (i + 1) * rows], 0.0)
            slot = number * count + i
            result[slot] = part.astype(result.dtype)
            going.append(pltpu.make_async_copy(result.at[slot], out_ref.at[a], out_sems.at[slot]))
            going[-1].start()
    for copy in going:
        copy.wait()


def apply(groups, blocks, psi, rights, left_sizes, right_sizes, carried):
    dtype, ranks = psi.dtype, len(rights)
    sectors, left_dim, right_dim = psi.shape
    rows = left_dim // ranks
    pieces, some = len(blocks), blocks[0].shape[0]
    count = some * len(groups[0])
    before = () if carried is None else (carried,)
    others = (*before, *blocks, psi, *rights)
    return pl.pallas_call(
        functools.partial(apply_kernel, groups, carried is not None),
        out_shape=jax.ShapeDtypeStruct((sectors, rows, right_dim), dtype),
        in_specs=[SMEM, SMEM] + [ANYWHERE] * len(others),
        out_specs=ANYWHERE,
        scratch_shapes=[
            pltpu.VMEM((pieces, *blocks[0].shape), dtype),
            pltpu.VMEM(psi.shape, dtype),
            pltpu.VMEM((ranks, *rights[0].shape), dtype),
            pltpu.VMEM((2 * ranks, count, rows, right_dim), dtype),
            pltpu.VMEM((count * len(groups), rows, right_dim), dtype),
            pltpu.SemaphoreType.DMA((pieces + ranks + 1,)),
            pltpu.SemaphoreType.DMA((count * len(groups),)),
        ],
        input_output_aliases={} if carried is None else {2: 0},
        compiler_params=pltpu.CompilerParams(vmem_limit_bytes=60 * MIB),
    )(left_sizes, right_sizes, *others)


def together(*values):
    return lax.optimization_barrier(values)


def local(wavefunction, left_env, right_env, left_sizes, right_sizes):
    sectors, ranks = lax.axis_size("blk"), lax.axis_size("mpo")
    own_w, left_dim, _ = left_env.shape
    rows = left_dim // ranks
    spots = [(y, x, c) for y in range(SIDE) for x in range(SIDE) for c in range(2)]

    def step(second, by):
        pairs = []
        for y, x, c in spots:
            along_x = (c == 0) != second
            to = place(y, x + by, c) if along_x else place(y + by, x, c)
            pairs.append((place(y, x, c), to))
        return pairs

    def near_step(block, by):
        return lax.ppermute(block, "blk", step(False, by))

    def far_step(block, by):
        return lax.ppermute(block, "blk", step(True, by))

    def swap(block):
        return lax.ppermute(block, "blk", [(i, i ^ 1) for i in range(sectors)])

    def up(block):
        return lax.ppermute(block, "mpo", [(z, (z + 1) % ranks) for z in range(ranks)])

    def down(block):
        return lax.ppermute(block, "mpo", [(z, (z - 1) % ranks) for z in range(ranks)])

    by_right = split(wavefunction, sectors)
    left_env, by_right = together(left_env, by_right)
    psi = lax.all_to_all(by_right, "blk", 0, 0)

    pieces = left_env.reshape(own_w, ranks, rows, left_dim).transpose(1, 0, 2, 3)
    own = lax.all_to_all(pieces, "mpo", 0, 0)
    below, above = near_step(own, 1), near_step(own, -1)
    up1, down1 = up(right_env), down(right_env)
    below, above, up1, down1 = together(below, above, up1, down1)

    two = near_step(below, 1)
    up2, down2 = up(up1), down(down1)
    two, up2, down2 = together(two, up2, down2)

    line = stack(own, below, above, two)
    line_below, line_above = far_step(line, 1), far_step(line, -1)
    line_other = swap(line)
    up3, down3 = up(up2), down(down2)
    line_below, line_above, up3, down3 = together(line_below, line_above, up3, down3)

    half = SIDE // 2
    far_below = far_step(line_below[:half], 1)
    far_above = far_step(line_above[half:], -1)
    below_other, above_other = swap(line_below), swap(line_above)
    up4 = up(up3)
    far_below_other, far_above_other = swap(far_below), swap(far_above)

    rights = (right_env, down1, down2, down3, up4, up3, up2, up1)
    groups = tuple(((False, far, 0), (True, far, 0)) for far in (0, SIDE - 1, 1))
    blocks = (line, line_other, line_below, below_other, line_above, above_other)
    begun = apply(groups, blocks, psi, rights, left_sizes, right_sizes, None)
    groups = (tuple((s, 2, first) for s in (False, True) for first in (0, half)),)
    blocks = (far_below, far_above, far_below_other, far_above_other)
    return apply(groups, blocks, psi, rights, left_sizes, right_sizes, begun)


def solution(mesh):
    placed = (P("blk", None), P("mpo", "blk", None), P("mpo", "blk", None), P(), P())
    return jax.shard_map(
        local, mesh=mesh, in_specs=placed, out_specs=P(None, "mpo", "blk"), check_vma=False
    )
```

time: 285 us -> 281 us (0.986)
  Pallas kernels: 0 us -> 148 us
  waiting for transfers between devices: 197 us -> 76.2 us
  local copies, waits for them, and re-layouts: 37.3 us -> 1.82 us
  starting transfers between devices: 8.84 us -> 35.7 us
  blocking collectives: 0 us -> 19.2 us
  matrix products: 15.1 us -> 0 us
  between operations: 13.5 us -> 0.37 us
  other arithmetic: 12.3 us -> 0 us
    pallas_call x0 -> x4, Pallas kernels: none -> 148 us  [the longest x1 128 us: split(): pl.pallas_call(split_kernel, out_shape=jax.ShapeDtypeStruct((sectors, lef...]
    reduce_scatter x1 -> x0, waiting for transfers between devices: 99.2 us -> none  [local(): lax.psum_scatter(summed_terms, 'mpo', scatter_dimension=1, tiled=True)]
    all_to_all x1, waiting for transfers between devices: 98.3 us -> 0.01 us  [local(): psi = lax.all_to_all(by_right, 'blk', 0, 0)]
    ppermute x0 -> x19, waiting for transfers between devices: none -> 76.2 us  [the longest x3 43.9 us: near_step(): return lax.ppermute(block, 'blk', step(False, by))]
    ppermute x0 -> x19, starting transfers between devices: none -> 26 us  [the longest x5 9.76 us: swap(): return lax.ppermute(block, 'blk', [(i, i ^ 1) for i in range(sectors)])]
    all_to_all x1 -> x0, local copies, waits for them, and re-layouts: 20.9 us -> none  [local(): lax.all_to_all(products, 'blk', split_axis=2, concat_axis=1, tiled=True)]
    all_to_all x0 -> x1, blocking collectives: none -> 19.2 us  [local(): own = lax.all_to_all(pieces, 'mpo', 0, 0)]
    another operation x1 -> x0, local copies, waits for them, and re-layouts: 16.4 us -> none  [local(): jnp.stack([jnp.dot(left_env[mpo_index], masked, preferred_element_type=jn...]
  transfers between devices with their start and end apart: 2 -> 20, of which waited for: 2 -> 10; matrix products, arithmetic and copies ran while one was open for 0% -> 0% of each run, Pallas kernels for 0% -> 4%
where the time goes in v6:
time: 281 us
  Pallas kernels  148 us (53%)
  waiting for transfers between devices  76.2 us (27%)
  starting transfers between devices  35.7 us (13%)
  blocking collectives  19.2 us (7%)
    pallas_call x1, Pallas kernels, split(): pl.pallas_call(split_kernel, out_shape=jax.ShapeDtypeStruct((sectors, lef...  128 us
    ppermute x3, waiting for transfers between devices, near_step(): return lax.ppermute(block, 'blk', step(False, by))  43.9 us
    pallas_call x2, Pallas kernels, apply(): pl.pallas_call(functools.partial(apply_kernel, groups, carried is not Non...  19.2 us
    all_to_all x1, blocking collectives, local(): own = lax.all_to_all(pieces, 'mpo', 0, 0)  19.2 us
    ppermute x4, waiting for transfers between devices, far_step(): return lax.ppermute(block, 'blk', step(True, by))  16.6 us
    ppermute x4, waiting for transfers between devices, up(): lax.ppermute(block, 'mpo', [(z, (z + 1) % ranks) for z in range(ranks)])  12.2 us
    ppermute x5, starting transfers between devices, swap(): return lax.ppermute(block, 'blk', [(i, i ^ 1) for i in range(sectors)])  9.76 us
    all_to_all x1, starting transfers between devices, local(): psi = lax.all_to_all(by_right, 'blk', 0, 0)  9.73 us
  transfers between devices with their start and end apart: 20, of which 10 were waited for; matrix products, arithmetic and copies ran while one was open for 0% of the time, Pallas kernels for 4%

profile of v6, /device:TPU:1, one launch (start us, length us, event | category | flops | bytes accessed | tf_op | source)
XLA Modules:
  0.0 281.2 jit_solution(12561409267991862636)
XLA Ops:
  0.0 0.0 copy-start.13
  0.0 128.4 %shard_map.55 = bf16[32,256,256]{2,1,0:T(8,128)(2,1)} custom-call(bf16[256,8192]{1,0:T(8,128)(2,1)} %psi_ref.1), custom_call_target="tpu_custom_call" | custom-call | tf_op jit(solution)/shard_map/pallas_call | solution.py:56
  128.5 0.0 copy-done.13
  128.5 19.2 %all_to_all.10.refs_0_ = bf16[8,2,32,256]{3,2,1,0:T(8,128)(2,1)S(1)} all-to-all(bf16[8,2,32,256]{3,2,1,0:T(8,128)(2,1)S(1)} %bitcast.4), channel_id=1, replica_groups=mesh['blk'=32,'mpo'=8] {'mpo'}, dimensions={0} | all-to-all | bytes 524288 | tf_op jit(solution)/shard_map/all_to_all | solution.py:198
  147.7 0.0 copy-start.5
  147.7 9.7 %all-to-all-start.1 = ((bf16[32,256,256]{2,1,0:T(8,128)(2,1)}), bf16[32,256,256]{2,1,0:T(8,128)(2,1)}, u32[]{:S(2)}, u32[]{:S(2)}) async-start(bf16[32,256,256]{2,1,0:T(8,128)(2,1)} %shard_map.55), calls=%async_computation.1 | async-start | bytes 8388608 | tf_op jit(solution)/shard_map/all_to_all | solution.py:195
  157.4 0.0 copy-done.5
  157.4 0.1 collective-permute-start.3
  157.5 1.5 collective-permute-start.2
  159.0 2.6 collective-permute-start.1
  161.6 0.0 collective-permute-start
  161.6 3.6 %collective-permute-done.3.refs_8_.refs_7_ = bf16[2,256,256]{2,1,0:T(8,128)(2,1)S(1)} collective-permute-done((bf16[2,256,256]{2,1,0:T(8,128)(2,1)S(1)}, bf16[2,256,256]{2,1,0:T(8,128)(2,1)S(1)}, u32[]{:S(2)}, u32[]{:S(2)}) %collective-permute-start.3) | collective-permute-done | bytes 262176 | tf_op jit(solution)/shard_map/ppermute | solution.py:191
  165.2 1.3 collective-permute-done.2.refs_14_.refs_13_
  166.5 41.2 %collective-permute-done.1.refs_2_ = bf16[8,2,32,256]{3,2,1,0:T(8,128)(2,1)S(1)} collective-permute-done((bf16[8,2,32,256]{3,2,1,0:T(8,128)(2,1)S(1)}, bf16[8,2,32,256]{3,2,1,0:T(8,128)(2,1)S(1)}, u32[]{:S(2)}, u32[]{:S(2)}) %collective-permute-start.1) | collective-permute-done | bytes 262176 | tf_op jit(solution)/shard_map/ppermute | solution.py:179
  207.7 0.0 collective-permute-done.refs_1_
  207.7 1.4 collective-permute-start.4
  209.1 0.3 collective-permute-start.5
  209.4 2.4 collective-permute-start.6
  211.8 2.7 collective-permute-done.4.refs_3_
  214.5 1.4 collective-permute-done.5.refs_13_.refs_12_
  215.9 0.0 collective-permute-done.6.refs_9_.refs_8_
  215.9 0.0 copy-done.6
  215.9 0.0 copy-done.7
  215.9 0.0 copy-start.9
  215.9 0.1 shard_map.56.refs_0_
  216.0 0.0 copy-start
  216.0 3.1 %collective-permute-start.9 = (bf16[4,8,2,32,256]{4,3,2,1,0:T(8,128)(2,1)S(1)}, bf16[4,8,2,32,256]{4,3,2,1,0:T(8,128)(2,1)S(1)}, u32[]{:S(2)}, u32[]{:S(2)}) collective-permute-start(bf16[4,8,2,32,256]{4,3,2,1,0:T(8,128)(2,1)S(1)} %shard_map.56.refs_0_), channel_id=1, source_target_pairs={{0,192},{8,56},{16,208},{24,8},{32,224},{40,24},{48,240},{56,40},{... | collective-permute-start | bytes 3145736 | tf_op jit(solution)/shard_map/ppermute | solution.py:182
  219.1 0.0 collective-permute-start.8
  219.1 0.0 collective-permute-start.10
  219.1 2.7 collective-permute-start.11
  221.8 4.3 %collective-permute-start.7 = (bf16[4,8,2,32,256]{4,3,2,1,0:T(8,128)(2,1)S(1)}, bf16[4,8,2,32,256]{4,3,2,1,0:T(8,128)(2,1)S(1)}, u32[]{:S(2)}, u32[]{:S(2)}) collective-permute-start(bf16[4,8,2,32,256]{4,3,2,1,0:T(8,128)(2,1)S(1)} %shard_map.56.refs_0_), channel_id=1, source_target_pairs={{0,8},{8,0},{16,24},{24,16},{32,40},{40,32},{48,56},{56,48},{64,72... | collective-permute-start | bytes 3145736 | tf_op jit(solution)/shard_map/ppermute | solution.py:185
  226.1 0.0 collective-permute-done.10.refs_12_.refs_11_
  226.1 0.0 collective-permute-done.11.refs_10_.refs_9_
  226.1 0.0 copy-start.11
  226.1 4.8 %collective-permute-done.9.refs_4_ = bf16[4,8,2,32,256]{4,3,2,1,0:T(8,128)(2,1)S(1)} collective-permute-done((bf16[4,8,2,32,256]{4,3,2,1,0:T(8,128)(2,1)S(1)}, bf16[4,8,2,32,256]{4,3,2,1,0:T(8,128)(2,1)S(1)}, u32[]{:S(2)}, u32[]{:S(2)}) %collective-permute-start.9) | collective-permute-done | bytes 1048608 | tf_op jit(solution)/shard_map/ppermute | solution.py:182
  230.9 3.4 %collective-permute-done.8.refs_2_ = bf16[4,8,2,32,256]{4,3,2,1,0:T(8,128)(2,1)S(1)} collective-permute-done((bf16[4,8,2,32,256]{4,3,2,1,0:T(8,128)(2,1)S(1)}, bf16[4,8,2,32,256]{4,3,2,1,0:T(8,128)(2,1)S(1)}, u32[]{:S(2)}, u32[]{:S(2)}) %collective-permute-start.8) | collective-permute-done | bytes 1048608 | tf_op jit(solution)/shard_map/ppermute | solution.py:182
  234.3 0.0 copy-done.9
  234.3 3.6 %collective-permute-start.12 = (bf16[4,8,2,32,256]{4,3,2,1,0:T(8,128)(2,1)S(1)}, bf16[4,8,2,32,256]{4,3,2,1,0:T(8,128)(2,1)S(1)}, u32[]{:S(2)}, u32[]{:S(2)}) collective-permute-start(bf16[4,8,2,32,256]{4,3,2,1,0:T(8,128)(2,1)S(1)} %collective-permute-done.8.refs_2_), channel_id=1, source_target_pairs={{0,8},{8,0},{16,24},{24,16},{32,40},{40,32},{48,56},{56,48},{64,72... | collective-permute-start | bytes 3145736 | tf_op jit(solution)/shard_map/ppermute | solution.py:185
  237.9 0.0 copy-done.11
  237.9 0.1 collective-permute-start.13
  238.1 2.0 collective-permute-start.16
  240.1 0.3 collective-permute-start.15
  240.3 6.2 %collective-permute-done.16.refs_2_ = bf16[2,8,2,32,256]{4,3,2,1,0:T(8,128)(2,1)} collective-permute-done((bf16[2,8,2,32,256]{4,3,2,1,0:T(8,128)(2,1)S(1)}, bf16[2,8,2,32,256]{4,3,2,1,0:T(8,128)(2,1)}, u32[]{:S(2)}, u32[]{:S(2)}) %collective-permute-start.16) | collective-permute-done | bytes 524320 | tf_op jit(solution)/shard_map/ppermute | solution.py:182
  246.6 1.3 collective-permute-start.18
  247.8 2.1 collective-permute-done.15.refs_1_
  250.0 0.5 collective-permute-start.17
  250.5 0.0 collective-permute-done.7.refs_1_
  250.5 0.0 collective-permute-start.14
  250.5 9.5 %collective-permute-done.14.refs_11_.refs_10_ = bf16[2,256,256]{2,1,0:T(8,128)(2,1)S(1)} collective-permute-done((bf16[2,256,256]{2,1,0:T(8,128)(2,1)S(1)}, bf16[2,256,256]{2,1,0:T(8,128)(2,1)S(1)}, u32[]{:S(2)}, u32[]{:S(2)}) %collective-permute-start.14) | collective-permute-done | bytes 262176 | tf_op jit(solution)/shard_map/ppermute | solution.py:188
  260.0 0.0 collective-permute-done.12.refs_3_
  260.0 0.0 copy-done.10
  260.0 0.0 copy-done.3
  260.0 0.7 copy-done.12
  260.7 1.0 copy-done.4
  261.7 0.0 collective-permute-done.13.refs_5_
  261.7 0.0 all-to-all-done.1.refs_6_.refs_5_
  261.7 0.0 copy-done.8
  261.7 0.0 copy-done
  261.7 0.0 copy-done.1
  261.7 0.0 copy-done.2
  261.7 12.0 %shard_map.57.refs_0_ = bf16[32,32,256]{2,1,0:T(8,128)(2,1)} custom-call(s32[32]{0:T(128)} %left_sizes.3, s32[32]{0:T(128)} %right_sizes.3, bf16[4,8,2,32,256]{4,3,2,1,0:T(8,128)(2,1)} %copy-done, bf16[4,8,2,32,256]{4,3,2,1,0:T(8,128)(2,1)} %copy-done.3, bf16[4,8,2,32,256]{4,3,2,1,0:T(8,128)(2,1)} %copy-done.2, bf16[4,8,2,32,256]{4,3,2,1,0:T(8,128)(2,1)} %copy-done.4, ...), custom_call_target="tpu_custom_call" | custom-call | tf_op jit(solution)/shard_map/pallas_call | solution.py:141
  273.7 0.0 collective-permute-done.18.refs_4_
  273.7 0.0 collective-permute-done.17.refs_3_
  273.7 7.3 %shard_map.58 = bf16[32,32,256]{2,1,0:T(8,128)(2,1)} custom-call(s32[32]{0:T(128)} %left_sizes.3, s32[32]{0:T(128)} %right_sizes.3, bf16[32,32,256]{2,1,0:T(8,128)(2,1)} %shard_map.57.refs_0_, bf16[2,8,2,32,256]{4,3,2,1,0:T(8,128)(2,1)} %collective-permute-done.15.refs_1_, ...), custom_call_target="tpu_custom_call", output_to_operand_aliasing={{}: (2, {})} | custom-call | tf_op jit(solution)/shard_map/pallas_call | solution.py:141
  (12 shorter events, 0.1 us)
Async XLA Ops:
  0.0 128.5 %copy-start.13 = (bf16[2,256,256]{2,1,0:T(8,128)(2,1)S(1)}, bf16[2,256,256]{2,1,0:T(8,128)(2,1)}, u32[]{:S(2)}) copy-start(bf16[2,256,256]{2,1,0:T(8,128)(2,1)} %param.6) | copy-start | bytes 786436
  147.7 9.7 %copy-start.5 = (bf16[2,256,256]{2,1,0:T(8,128)(2,1)S(1)}, bf16[2,256,256]{2,1,0:T(8,128)(2,1)}, u32[]{:S(2)}) copy-start(bf16[2,256,256]{2,1,0:T(8,128)(2,1)} %refs_6_.1) | copy-start | bytes 786436
  147.7 114.0 %all-to-all-start.1 = ((bf16[32,256,256]{2,1,0:T(8,128)(2,1)}), bf16[32,256,256]{2,1,0:T(8,128)(2,1)}, u32[]{:S(2)}, u32[]{:S(2)}) async-start(bf16[32,256,256]{2,1,0:T(8,128)(2,1)} %shard_map.55), calls=%async_computation.1 | async-start | bytes 8388608 | tf_op jit(solution)/shard_map/all_to_all | solution.py:195
  157.4 7.8 %collective-permute-start.3 = (bf16[2,256,256]{2,1,0:T(8,128)(2,1)S(1)}, bf16[2,256,256]{2,1,0:T(8,128)(2,1)S(1)}, u32[]{:S(2)}, u32[]{:S(2)}) collective-permute-start(bf16[2,256,256]{2,1,0:T(8,128)(2,1)S(1)} %copy-done.5), channel_id=1, source_target_pairs={{0,7},{1,0},{2,1},{3,2},{4,3},{5,4},{6,5},{7,6},{8,15},{9,8},{10,9... | collective-permute-start | bytes 786440 | tf_op jit(solution)/shard_map/ppermute | solution.py:191
  157.5 9.0 %collective-permute-start.2 = (bf16[2,256,256]{2,1,0:T(8,128)(2,1)S(1)}, bf16[2,256,256]{2,1,0:T(8,128)(2,1)S(1)}, u32[]{:S(2)}, u32[]{:S(2)}) collective-permute-start(bf16[2,256,256]{2,1,0:T(8,128)(2,1)S(1)} %copy-done.5), channel_id=1, source_target_pairs={{0,1},{1,2},{2,3},{3,4},{4,5},{5,6},{6,7},{7,0},{8,9},{9,10},{10,1... | collective-permute-start | bytes 786440 | tf_op jit(solution)/shard_map/ppermute | solution.py:188
  159.0 48.8 %collective-permute-start.1 = (bf16[8,2,32,256]{3,2,1,0:T(8,128)(2,1)S(1)}, bf16[8,2,32,256]{3,2,1,0:T(8,128)(2,1)S(1)}, u32[]{:S(2)}, u32[]{:S(2)}) collective-permute-start(bf16[8,2,32,256]{3,2,1,0:T(8,128)(2,1)S(1)} %all_to_all.10.refs_0_), channel_id=1, source_target_pairs={{0,48},{8,200},{16,0},{24,216},{32,16},{40,232},{48,32},{56,248},{... | collective-permute-start | bytes 786440 | tf_op jit(solution)/shard_map/ppermute | solution.py:179
  161.6 46.1 %collective-permute-start = (bf16[8,2,32,256]{3,2,1,0:T(8,128)(2,1)S(1)}, bf16[8,2,32,256]{3,2,1,0:T(8,128)(2,1)S(1)}, u32[]{:S(2)}, u32[]{:S(2)}) collective-permute-start(bf16[8,2,32,256]{3,2,1,0:T(8,128)(2,1)S(1)} %all_to_all.10.refs_0_), channel_id=1, source_target_pairs={{0,16},{8,72},{16,32},{24,88},{32,48},{40,104},{48,0},{56,120},{64... | collective-permute-start | bytes 786440 | tf_op jit(solution)/shard_map/ppermute | solution.py:179
  165.2 50.7 %copy-start.6 = (bf16[2,256,256]{2,1,0:T(8,128)(2,1)}, bf16[2,256,256]{2,1,0:T(8,128)(2,1)S(1)}, u32[]{:S(2)}) copy-start(bf16[2,256,256]{2,1,0:T(8,128)(2,1)S(1)} %collective-permute-done.3.refs_8_.refs_7_) | copy-start | bytes 786436
  166.5 49.4 %copy-start.7 = (bf16[2,256,256]{2,1,0:T(8,128)(2,1)}, bf16[2,256,256]{2,1,0:T(8,128)(2,1)S(1)}, u32[]{:S(2)}) copy-start(bf16[2,256,256]{2,1,0:T(8,128)(2,1)S(1)} %collective-permute-done.2.refs_14_.refs_13_) | copy-start | bytes 786436
  207.7 6.7 %collective-permute-start.4 = (bf16[8,2,32,256]{3,2,1,0:T(8,128)(2,1)S(1)}, bf16[8,2,32,256]{3,2,1,0:T(8,128)(2,1)S(1)}, u32[]{:S(2)}, u32[]{:S(2)}) collective-permute-start(bf16[8,2,32,256]{3,2,1,0:T(8,128)(2,1)S(1)} %collective-permute-done.refs_1_), channel_id=1, source_target_pairs={{0,16},{8,72},{16,32},{24,88},{32,48},{40,104},{48,0},{56,120},{64... | collective-permute-start | bytes 786440 | tf_op jit(solution)/shard_map/ppermute | solution.py:179
  209.1 6.7 %collective-permute-start.5 = (bf16[2,256,256]{2,1,0:T(8,128)(2,1)S(1)}, bf16[2,256,256]{2,1,0:T(8,128)(2,1)S(1)}, u32[]{:S(2)}, u32[]{:S(2)}) collective-permute-start(bf16[2,256,256]{2,1,0:T(8,128)(2,1)S(1)} %collective-permute-done.2.refs_14_.refs_13_), channel_id=1, source_target_pairs={{0,1},{1,2},{2,3},{3,4},{4,5},{5,6},{6,7},{7,0},{8,9},{9,10},{10,1... | collective-permute-start | bytes 786440 | tf_op jit(solution)/shard_map/ppermute | solution.py:188
  209.4 6.4 %collective-permute-start.6 = (bf16[2,256,256]{2,1,0:T(8,128)(2,1)S(1)}, bf16[2,256,256]{2,1,0:T(8,128)(2,1)S(1)}, u32[]{:S(2)}, u32[]{:S(2)}) collective-permute-start(bf16[2,256,256]{2,1,0:T(8,128)(2,1)S(1)} %collective-permute-done.3.refs_8_.refs_7_), channel_id=1, source_target_pairs={{0,7},{1,0},{2,1},{3,2},{4,3},{5,4},{6,5},{7,6},{8,15},{9,8},{10,9... | collective-permute-start | bytes 786440 | tf_op jit(solution)/shard_map/ppermute | solution.py:191
  215.9 45.8 %copy-start.8 = (bf16[2,256,256]{2,1,0:T(8,128)(2,1)}, bf16[2,256,256]{2,1,0:T(8,128)(2,1)S(1)}, u32[]{:S(2)}) copy-start(bf16[2,256,256]{2,1,0:T(8,128)(2,1)S(1)} %collective-permute-done.5.refs_13_.refs_12_) | copy-start | bytes 786436
  215.9 18.4 %copy-start.9 = (bf16[2,256,256]{2,1,0:T(8,128)(2,1)}, bf16[2,256,256]{2,1,0:T(8,128)(2,1)S(1)}, u32[]{:S(2)}) copy-start(bf16[2,256,256]{2,1,0:T(8,128)(2,1)S(1)} %collective-permute-done.6.refs_9_.refs_8_) | copy-start | bytes 786436
  216.0 45.7 %copy-start = (bf16[4,8,2,32,256]{4,3,2,1,0:T(8,128)(2,1)}, bf16[4,8,2,32,256]{4,3,2,1,0:T(8,128)(2,1)S(1)}, u32[]{:S(2)}) copy-start(bf16[4,8,2,32,256]{4,3,2,1,0:T(8,128)(2,1)S(1)} %shard_map.56.refs_0_) | copy-start | bytes 3145732
  216.0 14.8 %collective-permute-start.9 = (bf16[4,8,2,32,256]{4,3,2,1,0:T(8,128)(2,1)S(1)}, bf16[4,8,2,32,256]{4,3,2,1,0:T(8,128)(2,1)S(1)}, u32[]{:S(2)}, u32[]{:S(2)}) collective-permute-start(bf16[4,8,2,32,256]{4,3,2,1,0:T(8,128)(2,1)S(1)} %shard_map.56.refs_0_), channel_id=1, source_target_pairs={{0,192},{8,56},{16,208},{24,8},{32,224},{40,24},{48,240},{56,40},{... | collective-permute-start | bytes 3145736 | tf_op jit(solution)/shard_map/ppermute | solution.py:182
  219.1 15.2 %collective-permute-start.8 = (bf16[4,8,2,32,256]{4,3,2,1,0:T(8,128)(2,1)S(1)}, bf16[4,8,2,32,256]{4,3,2,1,0:T(8,128)(2,1)S(1)}, u32[]{:S(2)}, u32[]{:S(2)}) collective-permute-start(bf16[4,8,2,32,256]{4,3,2,1,0:T(8,128)(2,1)S(1)} %shard_map.56.refs_0_), channel_id=1, source_target_pairs={{0,64},{8,24},{16,80},{24,40},{32,96},{40,56},{48,112},{56,8},{64,... | collective-permute-start | bytes 3145736 | tf_op jit(solution)/shard_map/ppermute | solution.py:182
  219.1 6.9 %collective-permute-start.10 = (bf16[2,256,256]{2,1,0:T(8,128)(2,1)S(1)}, bf16[2,256,256]{2,1,0:T(8,128)(2,1)S(1)}, u32[]{:S(2)}, u32[]{:S(2)}) collective-permute-start(bf16[2,256,256]{2,1,0:T(8,128)(2,1)S(1)} %collective-permute-done.5.refs_13_.refs_12_), channel_id=1, source_target_pairs={{0,1},{1,2},{2,3},{3,4},{4,5},{5,6},{6,7},{7,0},{8,9},{9,10},{10,1... | collective-permute-start | bytes 786440 | tf_op jit(solution)/shard_map/ppermute | solution.py:188
  219.1 6.9 %collective-permute-start.11 = (bf16[2,256,256]{2,1,0:T(8,128)(2,1)S(1)}, bf16[2,256,256]{2,1,0:T(8,128)(2,1)S(1)}, u32[]{:S(2)}, u32[]{:S(2)}) collective-permute-start(bf16[2,256,256]{2,1,0:T(8,128)(2,1)S(1)} %collective-permute-done.6.refs_9_.refs_8_), channel_id=1, source_target_pairs={{0,7},{1,0},{2,1},{3,2},{4,3},{5,4},{6,5},{7,6},{8,15},{9,8},{10,9... | collective-permute-start | bytes 786440 | tf_op jit(solution)/shard_map/ppermute | solution.py:191
  221.8 28.7 %collective-permute-start.7 = (bf16[4,8,2,32,256]{4,3,2,1,0:T(8,128)(2,1)S(1)}, bf16[4,8,2,32,256]{4,3,2,1,0:T(8,128)(2,1)S(1)}, u32[]{:S(2)}, u32[]{:S(2)}) collective-permute-start(bf16[4,8,2,32,256]{4,3,2,1,0:T(8,128)(2,1)S(1)} %shard_map.56.refs_0_), channel_id=1, source_target_pairs={{0,8},{8,0},{16,24},{24,16},{32,40},{40,32},{48,56},{56,48},{64,72... | collective-permute-start | bytes 3145736 | tf_op jit(solution)/shard_map/ppermute | solution.py:185
  226.1 33.9 %copy-start.10 = (bf16[2,256,256]{2,1,0:T(8,128)(2,1)}, bf16[2,256,256]{2,1,0:T(8,128)(2,1)S(1)}, u32[]{:S(2)}) copy-start(bf16[2,256,256]{2,1,0:T(8,128)(2,1)S(1)} %collective-permute-done.10.refs_12_.refs_11_) | copy-start | bytes 786436
  226.1 11.8 %copy-start.11 = (bf16[2,256,256]{2,1,0:T(8,128)(2,1)}, bf16[2,256,256]{2,1,0:T(8,128)(2,1)S(1)}, u32[]{:S(2)}) copy-start(bf16[2,256,256]{2,1,0:T(8,128)(2,1)S(1)} %collective-permute-done.11.refs_10_.refs_9_) | copy-start | bytes 786436
  230.9 30.8 %copy-start.1 = (bf16[4,8,2,32,256]{4,3,2,1,0:T(8,128)(2,1)}, bf16[4,8,2,32,256]{4,3,2,1,0:T(8,128)(2,1)S(1)}, u32[]{:S(2)}) copy-start(bf16[4,8,2,32,256]{4,3,2,1,0:T(8,128)(2,1)S(1)} %collective-permute-done.9.refs_4_) | copy-start | bytes 3145732
  234.3 27.4 %copy-start.2 = (bf16[4,8,2,32,256]{4,3,2,1,0:T(8,128)(2,1)}, bf16[4,8,2,32,256]{4,3,2,1,0:T(8,128)(2,1)S(1)}, u32[]{:S(2)}) copy-start(bf16[4,8,2,32,256]{4,3,2,1,0:T(8,128)(2,1)S(1)} %collective-permute-done.8.refs_2_) | copy-start | bytes 3145732
  234.3 25.7 %collective-permute-start.12 = (bf16[4,8,2,32,256]{4,3,2,1,0:T(8,128)(2,1)S(1)}, bf16[4,8,2,32,256]{4,3,2,1,0:T(8,128)(2,1)S(1)}, u32[]{:S(2)}, u32[]{:S(2)}) collective-permute-start(bf16[4,8,2,32,256]{4,3,2,1,0:T(8,128)(2,1)S(1)} %collective-permute-done.8.refs_2_), channel_id=1, source_target_pairs={{0,8},{8,0},{16,24},{24,16},{32,40},{40,32},{48,56},{56,48},{64,72... | collective-permute-start | bytes 3145736 | tf_op jit(solution)/shard_map/ppermute | solution.py:185
  237.9 23.8 %collective-permute-start.13 = (bf16[4,8,2,32,256]{4,3,2,1,0:T(8,128)(2,1)S(1)}, bf16[4,8,2,32,256]{4,3,2,1,0:T(8,128)(2,1)}, u32[]{:S(2)}, u32[]{:S(2)}) collective-permute-start(bf16[4,8,2,32,256]{4,3,2,1,0:T(8,128)(2,1)S(1)} %collective-permute-done.9.refs_4_), channel_id=1, source_target_pairs={{0,8},{8,0},{16,24},{24,16},{32,40},{40,32},{48,56},{56,48},{64,72... | collective-permute-start | bytes 3145736 | tf_op jit(solution)/shard_map/ppermute | solution.py:185
  238.1 8.5 %collective-permute-start.16 = (bf16[2,8,2,32,256]{4,3,2,1,0:T(8,128)(2,1)S(1)}, bf16[2,8,2,32,256]{4,3,2,1,0:T(8,128)(2,1)}, u32[]{:S(2)}, u32[]{:S(2)}) collective-permute-start(bf16[2,8,2,32,256]{4,3,2,1,0:T(8,128)(2,1)S(1)} %slice.7), channel_id=1, source_target_pairs={{0,192},{8,56},{16,208},{24,8},{32,224},{40,24},{48,240},{56,40},{... | collective-permute-start | bytes 1572872 | tf_op jit(solution)/shard_map/ppermute | solution.py:182
  240.1 9.9 %collective-permute-start.15 = (bf16[2,8,2,32,256]{4,3,2,1,0:T(8,128)(2,1)S(1)}, bf16[2,8,2,32,256]{4,3,2,1,0:T(8,128)(2,1)}, u32[]{:S(2)}, u32[]{:S(2)}) collective-permute-start(bf16[2,8,2,32,256]{4,3,2,1,0:T(8,128)(2,1)S(1)} %slice.6), channel_id=1, source_target_pairs={{0,64},{8,24},{16,80},{24,40},{32,96},{40,56},{48,112},{56,8},{64,... | collective-permute-start | bytes 1572872 | tf_op jit(solution)/shard_map/ppermute | solution.py:182
  246.6 27.1 %collective-permute-start.18 = (bf16[2,8,2,32,256]{4,3,2,1,0:T(8,128)(2,1)}, bf16[2,8,2,32,256]{4,3,2,1,0:T(8,128)(2,1)}, u32[]{:S(2)}, u32[]{:S(2)}) collective-permute-start(bf16[2,8,2,32,256]{4,3,2,1,0:T(8,128)(2,1)} %collective-permute-done.16.refs_2_), channel_id=1, source_target_pairs={{0,8},{8,0},{16,24},{24,16},{32,40},{40,32},{48,56},{56,48},{64,72... | collective-permute-start | bytes 1572872 | tf_op jit(solution)/shard_map/ppermute | solution.py:185
  250.0 23.8 %collective-permute-start.17 = (bf16[2,8,2,32,256]{4,3,2,1,0:T(8,128)(2,1)}, bf16[2,8,2,32,256]{4,3,2,1,0:T(8,128)(2,1)}, u32[]{:S(2)}, u32[]{:S(2)}) collective-permute-start(bf16[2,8,2,32,256]{4,3,2,1,0:T(8,128)(2,1)} %collective-permute-done.15.refs_1_), channel_id=1, source_target_pairs={{0,8},{8,0},{16,24},{24,16},{32,40},{40,32},{48,56},{56,48},{64,72... | collective-permute-start | bytes 1572872 | tf_op jit(solution)/shard_map/ppermute | solution.py:185
  250.5 9.5 %copy-start.3 = (bf16[4,8,2,32,256]{4,3,2,1,0:T(8,128)(2,1)}, bf16[4,8,2,32,256]{4,3,2,1,0:T(8,128)(2,1)S(1)}, u32[]{:S(2)}) copy-start(bf16[4,8,2,32,256]{4,3,2,1,0:T(8,128)(2,1)S(1)} %collective-permute-done.7.refs_1_) | copy-start | bytes 3145732
  250.5 9.5 %collective-permute-start.14 = (bf16[2,256,256]{2,1,0:T(8,128)(2,1)S(1)}, bf16[2,256,256]{2,1,0:T(8,128)(2,1)S(1)}, u32[]{:S(2)}, u32[]{:S(2)}) collective-permute-start(bf16[2,256,256]{2,1,0:T(8,128)(2,1)S(1)} %collective-permute-done.10.refs_12_.refs_11_), channel_id=1, source_target_pairs={{0,1},{1,2},{2,3},{3,4},{4,5},{5,6},{6,7},{7,0},{8,9},{9,10},{10,1... | collective-permute-start | bytes 786440 | tf_op jit(solution)/shard_map/ppermute | solution.py:188
  260.0 0.7 copy-start.12
  260.7 1.0 copy-start.4

commit v7 on v0

v7 whole, which is shorter than its diff:
```python
import functools

import jax
import jax.numpy as jnp
from jax import lax
from jax.experimental import pallas as pl
from jax.experimental.pallas import tpu as pltpu
from jax.sharding import PartitionSpec as P

MIB = 1024 * 1024
SIDE = 4
OFFSETS = (0, SIDE - 1, 1, 2)
ANYWHERE = pl.BlockSpec(memory_space=pl.ANY)
SMEM = pl.BlockSpec(memory_space=pltpu.SMEM)
VMEM = pl.BlockSpec(memory_space=pltpu.VMEM)


def place(y, x, core):
    return ((y % SIDE) * SIDE + x % SIDE) * 2 + core


def stack_kernel(*refs):
    inputs, out, sems = refs[:-2], refs[-2], refs[-1]
    copies = [pltpu.make_async_copy(ref, out.at[i], sems.at[i]) for i, ref in enumerate(inputs)]
    for copy in copies:
        copy.start()
    for copy in copies:
        copy.wait()


def stack(*pieces):
    return pl.pallas_call(
        stack_kernel,
        out_shape=jax.ShapeDtypeStruct((len(pieces), *pieces[0].shape), pieces[0].dtype),
        in_specs=[ANYWHERE] * len(pieces),
        out_specs=ANYWHERE,
        scratch_shapes=[pltpu.SemaphoreType.DMA((len(pieces),))],
        compiler_params=pltpu.CompilerParams(vmem_limit_bytes=MIB),
    )(*pieces)


def coordinates():
    sector, rank = lax.axis_index("blk"), lax.axis_index("mpo")
    return sector, rank, sector % 2, sector // 2 % SIDE, sector // (2 * SIDE)


def right_sector(rank, core, which):
    y = ((rank // SIDE + core) & 1) + 2 * which
    return (y * SIDE + rank % SIDE) * 2 + core


def cut_kernel(left_sizes, right_sizes, psi_ref, keep_ref, give_ref, held, sems):
    sector, rank, core, _, _ = coordinates()
    _, left_dim, right_dim = keep_ref.shape
    wanted = [right_sector(rank, c, i) for c in (core, 1 - core) for i in range(2)]
    copies = []
    for i, b in enumerate(wanted):
        first = pl.multiple_of(b * right_dim, right_dim)
        copies.append(pltpu.make_async_copy(psi_ref.at[:, pl.ds(first, right_dim)], held.at[i], sems.at[i]))
    for copy in copies:
        copy.start()
    row = lax.broadcasted_iota(jnp.int32, (left_dim, right_dim), 0)
    col = lax.broadcasted_iota(jnp.int32, (left_dim, right_dim), 1)
    own_left = left_sizes[sector]
    for i, b in enumerate(wanted):
        copies[i].wait()
        inside = jnp.logical_and(row < own_left, col < right_sizes[b])
        block = jnp.where(inside, held[i].astype(jnp.float32), 0.0).astype(held.dtype)
        (keep_ref if i < 2 else give_ref)[i % 2] = block


def cut(wavefunction, left_sizes, right_sizes):
    left_dim, columns = wavefunction.shape
    block = (left_dim, columns // right_sizes.shape[0])
    shape = jax.ShapeDtypeStruct((2, *block), wavefunction.dtype)
    return pl.pallas_call(
        cut_kernel,
        out_shape=(shape, shape),
        in_specs=[SMEM, SMEM, ANYWHERE],
        out_specs=(VMEM, VMEM),
        scratch_shapes=[pltpu.VMEM((4, *block), wavefunction.dtype), pltpu.SemaphoreType.DMA((4,))],
        compiler_params=pltpu.CompilerParams(vmem_limit_bytes=60 * MIB),
    )(left_sizes, right_sizes, wavefunction)


def contract_kernel(left_ref, other_ref, psi_ref, other_psi_ref, out_ref):
    for w in range(2):
        for a, (left, psi) in enumerate(((left_ref, psi_ref), (other_ref, other_psi_ref))):
            for b in range(2):
                product = jnp.dot(left[0, w], psi[b], preferred_element_type=jnp.float32)
                out_ref[0, b, w, a] = product.astype(out_ref.dtype)


def contract(lefts, others, psi, other_psi):
    ranks, _, left_dim, _ = lefts.shape
    right_dim = psi.shape[2]
    left = pl.BlockSpec((1, *lefts.shape[1:]), lambda i: (i, 0, 0, 0))
    whole = pl.BlockSpec(psi.shape, lambda i: (0, 0, 0))
    block = (2, 2, 2, left_dim, right_dim)
    return pl.pallas_call(
        contract_kernel,
        out_shape=jax.ShapeDtypeStruct((ranks, *block), psi.dtype),
        grid=(ranks,),
        in_specs=[left, left, whole, whole],
        out_specs=pl.BlockSpec((1, *block), lambda i: (i, 0, 0, 0, 0, 0)),
        compiler_params=pltpu.CompilerParams(vmem_limit_bytes=60 * MIB),
    )(lefts, others, psi, other_psi)


def add_shards(pieces, refs, products, total, held, factors, sems, more):
    _, rank, core, x0, y0 = coordinates()
    ranks, _, _, _, left_dim, right_dim = products.shape
    shards, at = [], 0
    copies = []
    for ref, (far, first) in zip(refs, pieces):
        for k in range(ref.shape[0]):
            near = OFFSETS[first + k]
            y = jnp.where(core == 0, y0 + far, y0 + near) & (SIDE - 1)
            x = jnp.where(core == 0, x0 + near, x0 + far) & (SIDE - 1)
            which, pair = y // 2, x + SIDE * (y & 1)
            source = products.at[(pair - rank) & (ranks - 1), which]
            copies.append(pltpu.make_async_copy(source, factors.at[at], sems.at[2 * at]))
            copies.append(pltpu.make_async_copy(ref.at[k], held.at[at], sems.at[2 * at + 1]))
            shards.append(which)
            at += 1
    for copy in copies + more:
        copy.start()
    if not more:
        total[...] = jnp.zeros_like(total)
    for copy in more:
        copy.wait()
    for i, which in enumerate(shards):
        copies[2 * i].wait()
        copies[2 * i + 1].wait()
        term = None
        for w in range(2):
            product = factors[i, w].reshape(2 * left_dim, right_dim)
            part = jnp.dot(product, held[i, w], preferred_element_type=jnp.float32)
            term = part if term is None else term + part
        total[which] += term


def early_kernel(pieces, *refs):
    shards, (products, total, held, factors, sems) = refs[:-5], refs[-5:]
    add_shards(pieces, shards, products, total, held, factors, sems, [])


def late_kernel(pieces, left_sizes, right_sizes, *refs):
    shards, (products, before, out_ref, total, held, factors, sems) = refs[:-7], refs[-7:]
    more = [pltpu.make_async_copy(before, total, sems.at[sems.shape[0] - 1])]
    add_shards(pieces, shards, products, total, held, factors, sems, more)
    sector, rank, core, _, _ = coordinates()
    ranks, _, _, rows, right_dim = out_ref.shape
    left_dim = ranks * rows
    row = lax.broadcasted_iota(jnp.int32, (left_dim, right_dim), 0)
    col = lax.broadcasted_iota(jnp.int32, (left_dim, right_dim), 1)
    for b in range(2):
        own_right = right_sizes[right_sector(rank, core, b)]
        for a, spot in enumerate((core, 1 - core)):
            inside = jnp.logical_and(row < left_sizes[sector - core + spot], col < own_right)
            block = jnp.where(inside, total[b, a * left_dim : (a + 1) * left_dim], 0.0)
            block = block.astype(out_ref.dtype).reshape(ranks, 1, rows, right_dim)
            out_ref[:, b, pl.ds(spot, 1)] = block


def add(kernel, pieces, sizes, shards, products, before, shape, scratch):
    count = sum(shard.shape[0] for shard in shards)
    others = (*shards, products, *before)
    return pl.pallas_call(
        functools.partial(kernel, pieces),
        out_shape=shape,
        in_specs=[SMEM] * len(sizes) + [ANYWHERE] * len(others),
        out_specs=VMEM,
        scratch_shapes=scratch
        + [
            pltpu.VMEM((count, *shards[0].shape[1:]), products.dtype),
            pltpu.VMEM((count, *products.shape[2:]), products.dtype),
            pltpu.SemaphoreType.DMA((2 * count + 1,)),
        ],
        compiler_params=pltpu.CompilerParams(vmem_limit_bytes=60 * MIB),
    )(*sizes, *others)


def order_kernel(in_ref, out_ref, sems):
    _, _, core, _, _ = coordinates()
    copies = []
    for i in range(SIDE * SIDE):
        half, x, which = i // (2 * SIDE), i // 2 % SIDE, i % 2
        chip = (2 * which + (half + core) % 2) * SIDE + x
        copies.append(pltpu.make_async_copy(in_ref.at[i], out_ref.at[chip], sems.at[i]))
    for copy in copies:
        copy.start()
    for copy in copies:
        copy.wait()


def order(blocks):
    return pl.pallas_call(
        order_kernel,
        out_shape=jax.ShapeDtypeStruct(blocks.shape, blocks.dtype),
        in_specs=[VMEM],
        out_specs=ANYWHERE,
        scratch_shapes=[pltpu.SemaphoreType.DMA((blocks.shape[0],))],
        compiler_params=pltpu.CompilerParams(vmem_limit_bytes=8 * MIB),
    )(blocks)


def together(*values):
    return lax.optimization_barrier(values)


def local(wavefunction, left_env, right_env, left_sizes, right_sizes):
    sectors, ranks = lax.axis_size("blk"), lax.axis_size("mpo")
    left_dim, right_dim = left_env.shape[2], right_env.shape[2]
    rows = left_dim // ranks
    spots = [(y, x, c) for y in range(SIDE) for x in range(SIDE) for c in range(2)]

    def step(second, by):
        pairs = []
        for y, x, c in spots:
            along_x = (c == 0) != second
            to = place(y, x + by, c) if along_x else place(y + by, x, c)
            pairs.append((place(y, x, c), to))
        return pairs

    def near_step(block, by):
        return lax.ppermute(block, "blk", step(False, by))

    def far_step(block, by):
        return lax.ppermute(block, "blk", step(True, by))

    def swap(block):
        return lax.ppermute(block, "blk", [(i, i ^ 1) for i in range(sectors)])

    def up(block):
        return lax.ppermute(block, "mpo", [(z, (z + 1) % ranks) for z in range(ranks)])

    def down(block):
        return lax.ppermute(block, "mpo", [(z, (z - 1) % ranks) for z in range(ranks)])

    turn = [
        (
            place(y, x, c) * ranks + z,
            place(2 * (y // 2) + z // SIDE, z % SIDE, c) * ranks + x + SIDE * ((y + c) % 2),
        )
        for y, x, c in spots
        for z in range(ranks)
    ]
    own = lax.ppermute(right_env, ("blk", "mpo"), turn)
    up1, down1 = up(left_env), down(left_env)
    keep, give = cut(wavefunction, left_sizes, right_sizes)
    own, up1, down1, keep, give = together(own, up1, down1, keep, give)

    below, above = near_step(own, 1), near_step(own, -1)
    up2, down2 = up(up1), down(down1)
    got = swap(give)
    below, above, up2, down2 = together(below, above, up2, down2)
    two = near_step(below, 1)
    up3, down3 = up(up2), down(down2)
    two, up3, down3, got = together(two, up3, down3, got)
    line = stack(own, below, above, two)
    line, up3, down3 = together(line, up3, down3)
    line_below, line_above = far_step(line, 1), far_step(line, -1)
    up4 = up(up3)
    lefts = stack(left_env, down1, down2, down3, up4, up3, up2, up1)
    others = swap(lefts)
    line_below, line_above, others = together(line_below, line_above, others)
    half = SIDE // 2
    far_below = far_step(line_below[:half], 1)
    far_above = far_step(line_above[half:], -1)

    products = contract(lefts, others, keep, got)
    total = jax.ShapeDtypeStruct((2, 2 * left_dim, right_dim), jnp.float32)
    pieces = ((0, 0), (SIDE - 1, 0), (1, 0))
    shards = (line, line_below, line_above)
    begun = add(early_kernel, pieces, (), shards, products, (), total, [])
    done = add(
        late_kernel,
        ((2, 0), (2, half)),
        (left_sizes, right_sizes),
        (far_below, far_above),
        products,
        (begun,),
        jax.ShapeDtypeStruct((ranks, 2, 2, rows, right_dim), wavefunction.dtype),
        [pltpu.VMEM(total.shape, total.dtype)],
    )

    by_plane = lax.all_to_all(done, "mpo", 0, 0)
    chips = SIDE * SIDE
    by_plane = by_plane.reshape(chips, 2, rows, right_dim)
    groups = [
        [place(2 * i + (g // SIDE + c) % 2, g % SIDE, c) for g in range(ranks) for i in range(2)]
        for c in range(2)
    ]
    out = order(lax.all_to_all(by_plane, "blk", 0, 0, axis_index_groups=groups))
    return out.reshape(sectors, rows, right_dim)


def solution(mesh):
    placed = (P("blk", None), P("mpo", "blk", None), P("mpo", "blk", None), P(), P())
    return jax.shard_map(
        local, mesh=mesh, in_specs=placed, out_specs=P(None, "mpo", "blk"), check_vma=False
    )
```

time: 285 us -> 142 us (0.50)
  waiting for transfers between devices: 197 us -> 34.9 us
  blocking collectives: 0 us -> 40 us
  local copies, waits for them, and re-layouts: 37.3 us -> 3.42 us
  starting transfers between devices: 8.84 us -> 36.5 us
  Pallas kernels: 0 us -> 25.9 us
  matrix products: 15.1 us -> 0 us
  between operations: 13.5 us -> 0.28 us
  other arithmetic: 12.3 us -> 0 us
    reduce_scatter x1 -> x0, waiting for transfers between devices: 99.2 us -> none  [local(): lax.psum_scatter(summed_terms, 'mpo', scatter_dimension=1, tiled=True)]
    all_to_all x1 -> x0, waiting for transfers between devices: 98.3 us -> none  [local(): lax.all_to_all(products, 'blk', split_axis=2, concat_axis=1, tiled=True)]
    all_to_all x0 -> x2, blocking collectives: none -> 40 us  [the longest x1 20.4 us: local(): by_plane = lax.all_to_all(done, 'mpo', 0, 0)]
    ppermute x0 -> x17, starting transfers between devices: none -> 36.5 us  [the longest x1 9.77 us: local(): own = lax.ppermute(right_env, ('blk', 'mpo'), turn)]
    ppermute x0 -> x17, waiting for transfers between devices: none -> 34.9 us  [the longest x4 15.1 us: up(): lax.ppermute(block, 'mpo', [(z, (z + 1) % ranks) for z in range(ranks)])]
    pallas_call x0 -> x7, Pallas kernels: none -> 25.9 us  [the longest x2 13.1 us: add(): pl.pallas_call(functools.partial(kernel, pieces), out_shape=shape, in_spe...]
    all_to_all x1 -> x0, local copies, waits for them, and re-layouts: 20.9 us -> none  [local(): lax.all_to_all(products, 'blk', split_axis=2, concat_axis=1, tiled=True)]
    another operation x1 -> x0, local copies, waits for them, and re-layouts: 16.4 us -> none  [local(): jnp.stack([jnp.dot(left_env[mpo_index], masked, preferred_element_type=jn...]
  transfers between devices with their start and end apart: 2 -> 17, of which waited for: 2 -> 7; matrix products, arithmetic and copies ran while one was open for 0% -> 1% of each run, Pallas kernels for 0% -> 14%
where the time goes in v7:
time: 142 us; the launch traced here: 141 us
  blocking collectives  40 us (28%)
  starting transfers between devices  36.5 us (26%)
  waiting for transfers between devices  34.9 us (25%)
  Pallas kernels  25.9 us (18%)
  local copies, waits for them, and re-layouts  3.42 us (2%)
    all_to_all x1, blocking collectives, local(): by_plane = lax.all_to_all(done, 'mpo', 0, 0)  20.4 us
    all_to_all x1, blocking collectives, local(): out = order(lax.all_to_all(by_plane, 'blk', 0, 0, axis_index_groups=groups))  19.6 us
    ppermute x4, waiting for transfers between devices, up(): lax.ppermute(block, 'mpo', [(z, (z + 1) % ranks) for z in range(ranks)])  15.1 us
    pallas_call x2, Pallas kernels, add(): pl.pallas_call(functools.partial(kernel, pieces), out_shape=shape, in_spe...  13.1 us
    ppermute x4, waiting for transfers between devices, far_step(): return lax.ppermute(block, 'blk', step(True, by))  12.5 us
    ppermute x1, starting transfers between devices, local(): own = lax.ppermute(right_env, ('blk', 'mpo'), turn)  9.77 us
    pallas_call x1, Pallas kernels, contract(): pl.pallas_call(contract_kernel, out_shape=jax.ShapeDtypeStruct((ranks, *b...  8.99 us
    ppermute x3, starting transfers between devices, down(): lax.ppermute(block, 'mpo', [(z, (z - 1) % ranks) for z in range(ranks)])  6.86 us
  transfers between devices with their start and end apart: 17, of which 7 were waited for; matrix products, arithmetic and copies ran while one was open for 1% of the time, Pallas kernels for 14%

profile of v7, /device:TPU:1, one launch (start us, length us, event | category | flops | bytes accessed | tf_op | source)
XLA Modules:
  0.0 141.1 jit_solution(9352036761885863202)
XLA Ops:
  0.0 0.0 copy-start.2
  0.0 9.8 %collective-permute-start = (bf16[2,256,256]{2,1,0:T(8,128)(2,1)}, bf16[2,256,256]{2,1,0:T(8,128)(2,1)S(1)}, u32[]{:S(2)}, u32[]{:S(2)}) collective-permute-start(bf16[2,256,256]{2,1,0:T(8,128)(2,1)} %param.7), channel_id=1, source_target_pairs={{0,0},{1,16},{2,32},{3,48},{4,64},{5,80},{6,96},{7,112},{8,12},{9,... | collective-permute-start | bytes 786440 | tf_op jit(solution)/shard_map/ppermute | solution.py:249
  9.8 1.3 collective-permute-start.1
  11.1 2.4 %collective-permute-start.2 = (bf16[2,256,256]{2,1,0:T(8,128)(2,1)}, bf16[2,256,256]{2,1,0:T(8,128)(2,1)S(1)}, u32[]{:S(2)}, u32[]{:S(2)}) collective-permute-start(bf16[2,256,256]{2,1,0:T(8,128)(2,1)} %refs_0_.1), channel_id=1, source_target_pairs={{0,7},{1,0},{2,1},{3,2},{4,3},{5,4},{6,5},{7,6},{8,15},{9,8},{10,9... | collective-permute-start | bytes 786440 | tf_op jit(solution)/shard_map/ppermute | solution.py:239
  13.4 2.6 %shard_map.55 = (bf16[2,256,256]{2,1,0:T(8,128)(2,1)}, bf16[2,256,256]{2,1,0:T(8,128)(2,1)}) custom-call(s32[32]{0:T(128)} %left_sizes.3, s32[32]{0:T(128)} %right_sizes.3, bf16[256,8192]{1,0:T(8,128)(2,1)} %psi_ref.1), custom_call_target="tpu_custom_call" | custom-call | tf_op jit(solution)/shard_map/pallas_call | solution.py:76
  16.1 0.0 collective-permute-done.refs_0_
  16.1 10.0 %collective-permute-done.1.refs_7_ = bf16[2,256,256]{2,1,0:T(8,128)(2,1)S(1)} collective-permute-done((bf16[2,256,256]{2,1,0:T(8,128)(2,1)}, bf16[2,256,256]{2,1,0:T(8,128)(2,1)S(1)}, u32[]{:S(2)}, u32[]{:S(2)}) %collective-permute-start.1) | collective-permute-done | bytes 262176 | tf_op jit(solution)/shard_map/ppermute | solution.py:236
  26.1 0.0 collective-permute-done.2.refs_1_
  26.1 1.7 %collective-permute-start.3 = (bf16[2,256,256]{2,1,0:T(8,128)(2,1)S(1)}, bf16[2,256,256]{2,1,0:T(8,128)(2,1)S(1)}, u32[]{:S(2)}, u32[]{:S(2)}) collective-permute-start(bf16[2,256,256]{2,1,0:T(8,128)(2,1)S(1)} %collective-permute-done.refs_0_), channel_id=1, source_target_pairs={{0,16},{8,72},{16,32},{24,88},{32,48},{40,104},{48,0},{56,120},{64... | collective-permute-start | bytes 786440 | tf_op jit(solution)/shard_map/ppermute | solution.py:227
  27.7 1.4 %collective-permute-start.4 = (bf16[2,256,256]{2,1,0:T(8,128)(2,1)S(1)}, bf16[2,256,256]{2,1,0:T(8,128)(2,1)S(1)}, u32[]{:S(2)}, u32[]{:S(2)}) collective-permute-start(bf16[2,256,256]{2,1,0:T(8,128)(2,1)S(1)} %collective-permute-done.refs_0_), channel_id=1, source_target_pairs={{0,48},{8,200},{16,0},{24,216},{32,16},{40,232},{48,32},{56,248},{... | collective-permute-start | bytes 786440 | tf_op jit(solution)/shard_map/ppermute | solution.py:227
  29.2 0.0 collective-permute-start.5
  29.2 2.7 %collective-permute-start.6 = (bf16[2,256,256]{2,1,0:T(8,128)(2,1)S(1)}, bf16[2,256,256]{2,1,0:T(8,128)(2,1)S(1)}, u32[]{:S(2)}, u32[]{:S(2)}) collective-permute-start(bf16[2,256,256]{2,1,0:T(8,128)(2,1)S(1)} %collective-permute-done.2.refs_1_), channel_id=1, source_target_pairs={{0,7},{1,0},{2,1},{3,2},{4,3},{5,4},{6,5},{7,6},{8,15},{9,8},{10,9... | collective-permute-start | bytes 786440 | tf_op jit(solution)/shard_map/ppermute | solution.py:239
  31.9 3.2 %collective-permute-start.10 = (bf16[2,256,256]{2,1,0:T(8,128)(2,1)}, bf16[2,256,256]{2,1,0:T(8,128)(2,1)S(1)}, u32[]{:S(2)}, u32[]{:S(2)}) collective-permute-start(bf16[2,256,256]{2,1,0:T(8,128)(2,1)} %get-tuple-element.35), channel_id=1, source_target_pairs={{0,8},{8,0},{16,24},{24,16},{32,40},{40,32},{48,56},{56,48},{64,72... | collective-permute-start | bytes 786440 | tf_op jit(solution)/shard_map/ppermute | solution.py:233
  35.0 0.0 collective-permute-done.3.refs_1_
  35.0 0.0 collective-permute-done.4.refs_2_
  35.1 0.7 collective-permute-done.5.refs_6_
  35.8 0.0 collective-permute-done.6.refs_2_
  35.8 0.0 collective-permute-start.7
  35.8 1.0 collective-permute-start.8
  36.8 1.8 %collective-permute-start.9 = (bf16[2,256,256]{2,1,0:T(8,128)(2,1)S(1)}, bf16[2,256,256]{2,1,0:T(8,128)(2,1)S(1)}, u32[]{:S(2)}, u32[]{:S(2)}) collective-permute-start(bf16[2,256,256]{2,1,0:T(8,128)(2,1)S(1)} %collective-permute-done.6.refs_2_), channel_id=1, source_target_pairs={{0,7},{1,0},{2,1},{3,2},{4,3},{5,4},{6,5},{7,6},{8,15},{9,8},{10,9... | collective-permute-start | bytes 786440 | tf_op jit(solution)/shard_map/ppermute | solution.py:239
  38.6 0.0 collective-permute-done.10.other_psi_ref
  38.6 0.0 copy-start.6
  38.6 3.6 %collective-permute-done.7.refs_3_ = bf16[2,256,256]{2,1,0:T(8,128)(2,1)S(1)} collective-permute-done((bf16[2,256,256]{2,1,0:T(8,128)(2,1)S(1)}, bf16[2,256,256]{2,1,0:T(8,128)(2,1)S(1)}, u32[]{:S(2)}, u32[]{:S(2)}) %collective-permute-start.7) | collective-permute-done | bytes 262176 | tf_op jit(solution)/shard_map/ppermute | solution.py:227
  42.2 0.2 collective-permute-done.8.refs_5_
  42.4 3.8 %collective-permute-done.9.refs_3_ = bf16[2,256,256]{2,1,0:T(8,128)(2,1)S(1)} collective-permute-done((bf16[2,256,256]{2,1,0:T(8,128)(2,1)S(1)}, bf16[2,256,256]{2,1,0:T(8,128)(2,1)S(1)}, u32[]{:S(2)}, u32[]{:S(2)}) %collective-permute-start.9) | collective-permute-done | bytes 262176 | tf_op jit(solution)/shard_map/ppermute | solution.py:239
  46.2 0.1 shard_map.56.refs_0_
  46.3 0.0 copy-start.1
  46.3 3.4 %collective-permute-start.13 = (bf16[2,256,256]{2,1,0:T(8,128)(2,1)S(1)}, bf16[2,256,256]{2,1,0:T(8,128)(2,1)S(1)}, u32[]{:S(2)}, u32[]{:S(2)}) collective-permute-start(bf16[2,256,256]{2,1,0:T(8,128)(2,1)S(1)} %collective-permute-done.8.refs_5_), channel_id=1, source_target_pairs={{0,1},{1,2},{2,3},{3,4},{4,5},{5,6},{6,7},{7,0},{8,9},{9,10},{10,1... | collective-permute-start | bytes 786440 | tf_op jit(solution)/shard_map/ppermute | solution.py:236
  49.7 0.0 copy-done.6
  49.7 4.2 %collective-permute-done.13.refs_4_ = bf16[2,256,256]{2,1,0:T(8,128)(2,1)S(1)} collective-permute-done((bf16[2,256,256]{2,1,0:T(8,128)(2,1)S(1)}, bf16[2,256,256]{2,1,0:T(8,128)(2,1)S(1)}, u32[]{:S(2)}, u32[]{:S(2)}) %collective-permute-start.13) | collective-permute-done | bytes 262176 | tf_op jit(solution)/shard_map/ppermute | solution.py:236
  53.9 0.0 copy-done.2
  53.9 0.2 shard_map.57.left_ref
  54.1 0.0 copy-start
  54.2 2.5 %collective-permute-start.14 = (bf16[8,2,256,256]{3,2,1,0:T(8,128)(2,1)S(1)}, bf16[8,2,256,256]{3,2,1,0:T(8,128)(2,1)}, u32[]{:S(2)}, u32[]{:S(2)}) collective-permute-start(bf16[8,2,256,256]{3,2,1,0:T(8,128)(2,1)S(1)} %shard_map.57.left_ref), channel_id=1, source_target_pairs={{0,8},{8,0},{16,24},{24,16},{32,40},{40,32},{48,56},{56,48},{64,72... | collective-permute-start | bytes 6291464 | tf_op jit(solution)/shard_map/ppermute | solution.py:233
  56.6 0.0 collective-permute-start.11
  56.6 2.7 %collective-permute-start.12 = (bf16[4,2,256,256]{3,2,1,0:T(8,128)(2,1)S(1)}, bf16[4,2,256,256]{3,2,1,0:T(8,128)(2,1)S(1)}, u32[]{:S(2)}, u32[]{:S(2)}) collective-permute-start(bf16[4,2,256,256]{3,2,1,0:T(8,128)(2,1)S(1)} %shard_map.56.refs_0_), channel_id=1, source_target_pairs={{0,192},{8,56},{16,208},{24,8},{32,224},{40,24},{48,240},{56,40},{... | collective-permute-start | bytes 3145736 | tf_op jit(solution)/shard_map/ppermute | solution.py:230
  59.3 12.5 %collective-permute-done.11.refs_1_ = bf16[4,2,256,256]{3,2,1,0:T(8,128)(2,1)S(1)} collective-permute-done((bf16[4,2,256,256]{3,2,1,0:T(8,128)(2,1)S(1)}, bf16[4,2,256,256]{3,2,1,0:T(8,128)(2,1)S(1)}, u32[]{:S(2)}, u32[]{:S(2)}) %collective-permute-start.11) | collective-permute-done | bytes 1048608 | tf_op jit(solution)/shard_map/ppermute | solution.py:230
  71.8 0.0 copy-start.3
  71.8 0.0 collective-permute-done.12.refs_2_
  71.8 0.0 copy-start.4
  71.8 0.0 collective-permute-done.14.other_ref
  71.8 1.0 copy-done.3
  72.8 0.8 slice.6
  73.6 0.0 collective-permute-start.15
  73.6 0.0 copy-done.4
  73.6 0.8 slice.7
  74.4 2.7 %collective-permute-start.16 = (bf16[2,2,256,256]{3,2,1,0:T(8,128)(2,1)}, bf16[2,2,256,256]{3,2,1,0:T(8,128)(2,1)}, u32[]{:S(2)}, u32[]{:S(2)}) collective-permute-start(bf16[2,2,256,256]{3,2,1,0:T(8,128)(2,1)} %slice.7), channel_id=1, source_target_pairs={{0,192},{8,56},{16,208},{24,8},{32,224},{40,24},{48,240},{56,40},{... | collective-permute-start | bytes 1572872 | tf_op jit(solution)/shard_map/ppermute | solution.py:230
  77.1 0.0 copy-done
  77.1 9.0 %shard_map.58.refs_3_.refs_2_ = bf16[8,2,2,2,256,256]{5,4,3,2,1,0:T(8,128)(2,1)} custom-call(bf16[8,2,256,256]{3,2,1,0:T(8,128)(2,1)} %copy-done, bf16[8,2,256,256]{3,2,1,0:T(8,128)(2,1)} %collective-permute-done.14.other_ref, bf16[2,256,256]{2,1,0:T(8,128)(2,1)} %get-tuple-element.45.psi_ref, bf16[2,256,256]{2,1,0:T(8,128)(2,1)} %copy-done.6), custom_call_target="tpu_custom_call" | custom-call | tf_op jit(solution)/shard_map/pallas_call | solution.py:100
  86.1 0.0 copy-done.1
  86.1 7.5 %shard_map.59.refs_3_ = f32[2,512,256]{2,1,0:T(8,128)} custom-call(bf16[4,2,256,256]{3,2,1,0:T(8,128)(2,1)} %copy-done.1, bf16[4,2,256,256]{3,2,1,0:T(8,128)(2,1)} %copy-done.3, bf16[4,2,256,256]{3,2,1,0:T(8,128)(2,1)} %copy-done.4, bf16[8,2,2,2,256,256]{5,4,3,2,1,0:T(8,128)(2,1)} %shard_map.58.refs_3_.refs_2_), custom_call_target="tpu_custom_call" | custom-call | tf_op jit(solution)/shard_map/pallas_call | solution.py:169
  93.6 0.0 collective-permute-done.15.refs_0_
  93.6 0.0 copy-start.5
  93.6 0.0 collective-permute-done.16.refs_1_
  93.6 0.8 copy-done.5
  94.4 5.6 %shard_map.60 = bf16[8,2,2,32,256]{4,3,2,1,0:T(8,128)(2,1)} custom-call(s32[32]{0:T(128)} %left_sizes.3, s32[32]{0:T(128)} %right_sizes.3, bf16[2,2,256,256]{3,2,1,0:T(8,128)(2,1)} %copy-done.5, bf16[2,2,256,256]{3,2,1,0:T(8,128)(2,1)} %collective-permute-done.16.refs_1_, bf16[8,2,2,2,256,256]{5,4,3,2,1,0:T(8,128)(2,1)} %shard_map.58.refs_3_.refs_2_, ...), custom_call_target="tpu_custom_call" | custom-call | tf_op jit(solution)/shard_map/pallas_call | solution.py:169
  100.0 20.4 %all_to_all.10 = bf16[8,2,2,32,256]{4,3,2,1,0:T(8,128)(2,1)S(1)} all-to-all(bf16[8,2,2,32,256]{4,3,2,1,0:T(8,128)(2,1)} %shard_map.60), channel_id=1, replica_groups=mesh['blk'=32,'mpo'=8] {'mpo'}, dimensions={0} | all-to-all | bytes 1048576 | tf_op jit(solution)/shard_map/all_to_all | solution.py:288
  120.4 19.6 %all_to_all.11.in_ref = bf16[16,2,32,256]{3,2,1,0:T(8,128)(2,1)S(1)} all-to-all(bf16[16,2,32,256]{3,2,1,0:T(8,128)(2,1)S(1)} %bitcast.2), channel_id=1, replica_groups={{0,128,16,144,32,160,48,176,64,192,80,208,96,224,112,240},{72,200,88,21..., dimensions={0} | all-to-all | bytes 1048576 | tf_op jit(solution)/shard_map/all_to_all | solution.py:295
  140.0 0.9 shard_map.61
Async XLA Ops:
  0.0 53.9 %copy-start.2 = (bf16[2,256,256]{2,1,0:T(8,128)(2,1)S(1)}, bf16[2,256,256]{2,1,0:T(8,128)(2,1)}, u32[]{:S(2)}) copy-start(bf16[2,256,256]{2,1,0:T(8,128)(2,1)} %refs_0_.1) | copy-start | bytes 786436
  0.0 16.1 %collective-permute-start = (bf16[2,256,256]{2,1,0:T(8,128)(2,1)}, bf16[2,256,256]{2,1,0:T(8,128)(2,1)S(1)}, u32[]{:S(2)}, u32[]{:S(2)}) collective-permute-start(bf16[2,256,256]{2,1,0:T(8,128)(2,1)} %param.7), channel_id=1, source_target_pairs={{0,0},{1,16},{2,32},{3,48},{4,64},{5,80},{6,96},{7,112},{8,12},{9,... | collective-permute-start | bytes 786440 | tf_op jit(solution)/shard_map/ppermute | solution.py:249
  9.8 16.3 %collective-permute-start.1 = (bf16[2,256,256]{2,1,0:T(8,128)(2,1)}, bf16[2,256,256]{2,1,0:T(8,128)(2,1)S(1)}, u32[]{:S(2)}, u32[]{:S(2)}) collective-permute-start(bf16[2,256,256]{2,1,0:T(8,128)(2,1)} %refs_0_.1), channel_id=1, source_target_pairs={{0,1},{1,2},{2,3},{3,4},{4,5},{5,6},{6,7},{7,0},{8,9},{9,10},{10,1... | collective-permute-start | bytes 786440 | tf_op jit(solution)/shard_map/ppermute | solution.py:236
  11.1 15.0 %collective-permute-start.2 = (bf16[2,256,256]{2,1,0:T(8,128)(2,1)}, bf16[2,256,256]{2,1,0:T(8,128)(2,1)S(1)}, u32[]{:S(2)}, u32[]{:S(2)}) collective-permute-start(bf16[2,256,256]{2,1,0:T(8,128)(2,1)} %refs_0_.1), channel_id=1, source_target_pairs={{0,7},{1,0},{2,1},{3,2},{4,3},{5,4},{6,5},{7,6},{8,15},{9,8},{10,9... | collective-permute-start | bytes 786440 | tf_op jit(solution)/shard_map/ppermute | solution.py:239
  26.1 9.0 %collective-permute-start.3 = (bf16[2,256,256]{2,1,0:T(8,128)(2,1)S(1)}, bf16[2,256,256]{2,1,0:T(8,128)(2,1)S(1)}, u32[]{:S(2)}, u32[]{:S(2)}) collective-permute-start(bf16[2,256,256]{2,1,0:T(8,128)(2,1)S(1)} %collective-permute-done.refs_0_), channel_id=1, source_target_pairs={{0,16},{8,72},{16,32},{24,88},{32,48},{40,104},{48,0},{56,120},{64... | collective-permute-start | bytes 786440 | tf_op jit(solution)/shard_map/ppermute | solution.py:227
  27.7 7.3 %collective-permute-start.4 = (bf16[2,256,256]{2,1,0:T(8,128)(2,1)S(1)}, bf16[2,256,256]{2,1,0:T(8,128)(2,1)S(1)}, u32[]{:S(2)}, u32[]{:S(2)}) collective-permute-start(bf16[2,256,256]{2,1,0:T(8,128)(2,1)S(1)} %collective-permute-done.refs_0_), channel_id=1, source_target_pairs={{0,48},{8,200},{16,0},{24,216},{32,16},{40,232},{48,32},{56,248},{... | collective-permute-start | bytes 786440 | tf_op jit(solution)/shard_map/ppermute | solution.py:227
  29.2 6.6 %collective-permute-start.5 = (bf16[2,256,256]{2,1,0:T(8,128)(2,1)S(1)}, bf16[2,256,256]{2,1,0:T(8,128)(2,1)S(1)}, u32[]{:S(2)}, u32[]{:S(2)}) collective-permute-start(bf16[2,256,256]{2,1,0:T(8,128)(2,1)S(1)} %collective-permute-done.1.refs_7_), channel_id=1, source_target_pairs={{0,1},{1,2},{2,3},{3,4},{4,5},{5,6},{6,7},{7,0},{8,9},{9,10},{10,1... | collective-permute-start | bytes 786440 | tf_op jit(solution)/shard_map/ppermute | solution.py:236
  29.2 6.6 %collective-permute-start.6 = (bf16[2,256,256]{2,1,0:T(8,128)(2,1)S(1)}, bf16[2,256,256]{2,1,0:T(8,128)(2,1)S(1)}, u32[]{:S(2)}, u32[]{:S(2)}) collective-permute-start(bf16[2,256,256]{2,1,0:T(8,128)(2,1)S(1)} %collective-permute-done.2.refs_1_), channel_id=1, source_target_pairs={{0,7},{1,0},{2,1},{3,2},{4,3},{5,4},{6,5},{7,6},{8,15},{9,8},{10,9... | collective-permute-start | bytes 786440 | tf_op jit(solution)/shard_map/ppermute | solution.py:239
  31.9 6.8 %collective-permute-start.10 = (bf16[2,256,256]{2,1,0:T(8,128)(2,1)}, bf16[2,256,256]{2,1,0:T(8,128)(2,1)S(1)}, u32[]{:S(2)}, u32[]{:S(2)}) collective-permute-start(bf16[2,256,256]{2,1,0:T(8,128)(2,1)} %get-tuple-element.35), channel_id=1, source_target_pairs={{0,8},{8,0},{16,24},{24,16},{32,40},{40,32},{48,56},{56,48},{64,72... | collective-permute-start | bytes 786440 | tf_op jit(solution)/shard_map/ppermute | solution.py:233
  35.8 6.4 %collective-permute-start.7 = (bf16[2,256,256]{2,1,0:T(8,128)(2,1)S(1)}, bf16[2,256,256]{2,1,0:T(8,128)(2,1)S(1)}, u32[]{:S(2)}, u32[]{:S(2)}) collective-permute-start(bf16[2,256,256]{2,1,0:T(8,128)(2,1)S(1)} %collective-permute-done.3.refs_1_), channel_id=1, source_target_pairs={{0,16},{8,72},{16,32},{24,88},{32,48},{40,104},{48,0},{56,120},{64... | collective-permute-start | bytes 786440 | tf_op jit(solution)/shard_map/ppermute | solution.py:227
  35.8 6.6 %collective-permute-start.8 = (bf16[2,256,256]{2,1,0:T(8,128)(2,1)S(1)}, bf16[2,256,256]{2,1,0:T(8,128)(2,1)S(1)}, u32[]{:S(2)}, u32[]{:S(2)}) collective-permute-start(bf16[2,256,256]{2,1,0:T(8,128)(2,1)S(1)} %collective-permute-done.5.refs_6_), channel_id=1, source_target_pairs={{0,1},{1,2},{2,3},{3,4},{4,5},{5,6},{6,7},{7,0},{8,9},{9,10},{10,1... | collective-permute-start | bytes 786440 | tf_op jit(solution)/shard_map/ppermute | solution.py:236
  36.8 9.4 %collective-permute-start.9 = (bf16[2,256,256]{2,1,0:T(8,128)(2,1)S(1)}, bf16[2,256,256]{2,1,0:T(8,128)(2,1)S(1)}, u32[]{:S(2)}, u32[]{:S(2)}) collective-permute-start(bf16[2,256,256]{2,1,0:T(8,128)(2,1)S(1)} %collective-permute-done.6.refs_2_), channel_id=1, source_target_pairs={{0,7},{1,0},{2,1},{3,2},{4,3},{5,4},{6,5},{7,6},{8,15},{9,8},{10,9... | collective-permute-start | bytes 786440 | tf_op jit(solution)/shard_map/ppermute | solution.py:239
  38.6 11.1 %copy-start.6 = (bf16[2,256,256]{2,1,0:T(8,128)(2,1)}, bf16[2,256,256]{2,1,0:T(8,128)(2,1)S(1)}, u32[]{:S(2)}) copy-start(bf16[2,256,256]{2,1,0:T(8,128)(2,1)S(1)} %collective-permute-done.10.other_psi_ref) | copy-start | bytes 786436
  46.3 39.8 %copy-start.1 = (bf16[4,2,256,256]{3,2,1,0:T(8,128)(2,1)}, bf16[4,2,256,256]{3,2,1,0:T(8,128)(2,1)S(1)}, u32[]{:S(2)}) copy-start(bf16[4,2,256,256]{3,2,1,0:T(8,128)(2,1)S(1)} %shard_map.56.refs_0_) | copy-start | bytes 3145732
  46.3 7.6 %collective-permute-start.13 = (bf16[2,256,256]{2,1,0:T(8,128)(2,1)S(1)}, bf16[2,256,256]{2,1,0:T(8,128)(2,1)S(1)}, u32[]{:S(2)}, u32[]{:S(2)}) collective-permute-start(bf16[2,256,256]{2,1,0:T(8,128)(2,1)S(1)} %collective-permute-done.8.refs_5_), channel_id=1, source_target_pairs={{0,1},{1,2},{2,3},{3,4},{4,5},{5,6},{6,7},{7,0},{8,9},{9,10},{10,1... | collective-permute-start | bytes 786440 | tf_op jit(solution)/shard_map/ppermute | solution.py:236
  54.1 23.0 %copy-start = (bf16[8,2,256,256]{3,2,1,0:T(8,128)(2,1)}, bf16[8,2,256,256]{3,2,1,0:T(8,128)(2,1)S(1)}, u32[]{:S(2)}) copy-start(bf16[8,2,256,256]{3,2,1,0:T(8,128)(2,1)S(1)} %shard_map.57.left_ref) | copy-start | bytes 6291460
  54.2 17.7 %collective-permute-start.14 = (bf16[8,2,256,256]{3,2,1,0:T(8,128)(2,1)S(1)}, bf16[8,2,256,256]{3,2,1,0:T(8,128)(2,1)}, u32[]{:S(2)}, u32[]{:S(2)}) collective-permute-start(bf16[8,2,256,256]{3,2,1,0:T(8,128)(2,1)S(1)} %shard_map.57.left_ref), channel_id=1, source_target_pairs={{0,8},{8,0},{16,24},{24,16},{32,40},{40,32},{48,56},{56,48},{64,72... | collective-permute-start | bytes 6291464 | tf_op jit(solution)/shard_map/ppermute | solution.py:233
  56.6 15.2 %collective-permute-start.11 = (bf16[4,2,256,256]{3,2,1,0:T(8,128)(2,1)S(1)}, bf16[4,2,256,256]{3,2,1,0:T(8,128)(2,1)S(1)}, u32[]{:S(2)}, u32[]{:S(2)}) collective-permute-start(bf16[4,2,256,256]{3,2,1,0:T(8,128)(2,1)S(1)} %shard_map.56.refs_0_), channel_id=1, source_target_pairs={{0,64},{8,24},{16,80},{24,40},{32,96},{40,56},{48,112},{56,8},{64,... | collective-permute-start | bytes 3145736 | tf_op jit(solution)/shard_map/ppermute | solution.py:230
  56.6 15.2 %collective-permute-start.12 = (bf16[4,2,256,256]{3,2,1,0:T(8,128)(2,1)S(1)}, bf16[4,2,256,256]{3,2,1,0:T(8,128)(2,1)S(1)}, u32[]{:S(2)}, u32[]{:S(2)}) collective-permute-start(bf16[4,2,256,256]{3,2,1,0:T(8,128)(2,1)S(1)} %shard_map.56.refs_0_), channel_id=1, source_target_pairs={{0,192},{8,56},{16,208},{24,8},{32,224},{40,24},{48,240},{56,40},{... | collective-permute-start | bytes 3145736 | tf_op jit(solution)/shard_map/ppermute | solution.py:230
  71.8 1.0 copy-start.3
  71.8 1.8 %copy-start.4 = (bf16[4,2,256,256]{3,2,1,0:T(8,128)(2,1)}, bf16[4,2,256,256]{3,2,1,0:T(8,128)(2,1)S(1)}, u32[]{:S(2)}) copy-start(bf16[4,2,256,256]{3,2,1,0:T(8,128)(2,1)S(1)} %collective-permute-done.12.refs_2_) | copy-start | bytes 3145732
  73.6 20.0 %collective-permute-start.15 = (bf16[2,2,256,256]{3,2,1,0:T(8,128)(2,1)}, bf16[2,2,256,256]{3,2,1,0:T(8,128)(2,1)S(1)}, u32[]{:S(2)}, u32[]{:S(2)}) collective-permute-start(bf16[2,2,256,256]{3,2,1,0:T(8,128)(2,1)} %slice.6), channel_id=1, source_target_pairs={{0,64},{8,24},{16,80},{24,40},{32,96},{40,56},{48,112},{56,8},{64,... | collective-permute-start | bytes 1572872 | tf_op jit(solution)/shard_map/ppermute | solution.py:230
  74.4 19.2 %collective-permute-start.16 = (bf16[2,2,256,256]{3,2,1,0:T(8,128)(2,1)}, bf16[2,2,256,256]{3,2,1,0:T(8,128)(2,1)}, u32[]{:S(2)}, u32[]{:S(2)}) collective-permute-start(bf16[2,2,256,256]{3,2,1,0:T(8,128)(2,1)} %slice.7), channel_id=1, source_target_pairs={{0,192},{8,56},{16,208},{24,8},{32,224},{40,24},{48,240},{56,40},{... | collective-permute-start | bytes 1572872 | tf_op jit(solution)/shard_map/ppermute | solution.py:230
  93.6 0.8 copy-start.5

commit v8 on v7

--- a/solution.py
+++ b/solution.py
@@ -84,36 +84,44 @@
 
 
 def contract_kernel(left_ref, other_ref, psi_ref, other_psi_ref, out_ref):
-    for w in range(2):
-        for a, (left, psi) in enumerate(((left_ref, psi_ref), (other_ref, other_psi_ref))):
-            for b in range(2):
-                product = jnp.dot(left[0, w], psi[b], preferred_element_type=jnp.float32)
-                out_ref[0, b, w, a] = product.astype(out_ref.dtype)
+    _, pair, left_dim, inner = left_ref.shape
+    right_dim = psi_ref.shape[2]
+    for a, (left, psi) in enumerate(((left_ref, psi_ref), (other_ref, other_psi_ref))):
+        block = left[0].reshape(pair * left_dim, inner)
+        for b in range(2):
+            product = jnp.dot(block, psi[b], preferred_element_type=jnp.float32).astype(out_ref.dtype)
+            for w in range(pair):
+                columns = slice(w * right_dim, (w + 1) * right_dim)
+                out_ref[0, b, a * left_dim : (a + 1) * left_dim, columns] = product[
+                    w * left_dim : (w + 1) * left_dim
+                ]
 
 
 def contract(lefts, others, psi, other_psi):
-    ranks, _, left_dim, _ = lefts.shape
+    ranks, pair, left_dim, _ = lefts.shape
     right_dim = psi.shape[2]
     left = pl.BlockSpec((1, *lefts.shape[1:]), lambda i: (i, 0, 0, 0))
     whole = pl.BlockSpec(psi.shape, lambda i: (0, 0, 0))
-    block = (2, 2, 2, left_dim, right_dim)
+    block = (2, 2 * left_dim, pair * right_dim)
     return pl.pallas_call(
         contract_kernel,
         out_shape=jax.ShapeDtypeStruct((ranks, *block), psi.dtype),
         grid=(ranks,),
         in_specs=[left, left, whole, whole],
-        out_specs=pl.BlockSpec((1, *block), lambda i: (i, 0, 0, 0, 0, 0)),
+        out_specs=pl.BlockSpec((1, *block), lambda i: (i, 0, 0, 0)),
         compiler_params=pltpu.CompilerParams(vmem_limit_bytes=60 * MIB),
     )(lefts, others, psi, other_psi)
 
 
-def add_shards(pieces, refs, products, total, held, factors, sems, more):
-    _, rank, core, x0, y0 = coordinates()
-    ranks, _, _, _, left_dim, right_dim = products.shape
-    shards, at = [], 0
-    copies = []
-    for ref, (far, first) in zip(refs, pieces):
+def add_kernel(pieces, left_sizes, right_sizes, *refs):
+    shards, (products, out_ref, total, held, factors, sems) = refs[:-6], refs[-6:]
+    sector, rank, core, x0, y0 = coordinates()
+    ranks, _, _, rows, right_dim = out_ref.shape
+    left_dim = ranks * rows
+    sectors_of, copies = [], []
+    for ref, (far, first) in zip(shards, pieces):
         for k in range(ref.shape[0]):
+            at = len(sectors_of)
             near = OFFSETS[first + k]
             y = jnp.where(core == 0, y0 + far, y0 + near) & (SIDE - 1)
             x = jnp.where(core == 0, x0 + near, x0 + far) & (SIDE - 1)
@@ -121,37 +129,15 @@
             source = products.at[(pair - rank) & (ranks - 1), which]
             copies.append(pltpu.make_async_copy(source, factors.at[at], sems.at[2 * at]))
             copies.append(pltpu.make_async_copy(ref.at[k], held.at[at], sems.at[2 * at + 1]))
-            shards.append(which)
-            at += 1
-    for copy in copies + more:
-        copy.start()
-    if not more:
-        total[...] = jnp.zeros_like(total)
-    for copy in more:
-        copy.wait()
-    for i, which in enumerate(shards):
+            sectors_of.append(which)
+    for copy in copies:
+        copy.start()
+    total[...] = jnp.zeros_like(total)
+    for i, which in enumerate(sectors_of):
         copies[2 * i].wait()
         copies[2 * i + 1].wait()
-        term = None
-        for w in range(2):
-            product = factors[i, w].reshape(2 * left_dim, right_dim)
-            part = jnp.dot(product, held[i, w], preferred_element_type=jnp.float32)
-            term = part if term is None else term + part
-        total[which] += term
-
-
-def early_kernel(pieces, *refs):
-    shards, (products, total, held, factors, sems) = refs[:-5], refs[-5:]
-    add_shards(pieces, shards, products, total, held, factors, sems, [])
-
-
-def late_kernel(pieces, left_sizes, right_sizes, *refs):
-    shards, (products, before, out_ref, total, held, factors, sems) = refs[:-7], refs[-7:]
-    more = [pltpu.make_async_copy(before, total, sems.at[sems.shape[0] - 1])]
-    add_shards(pieces, shards, products, total, held, factors, sems, more)
-    sector, rank, core, _, _ = coordinates()
-    ranks, _, _, rows, right_dim = out_ref.shape
-    left_dim = ranks * rows
+        shard = held[i].reshape(factors.shape[2], right_dim)
+        total[which] += jnp.dot(factors[i], shard, preferred_element_type=jnp.float32)
     row = lax.broadcasted_iota(jnp.int32, (left_dim, right_dim), 0)
     col = lax.broadcasted_iota(jnp.int32, (left_dim, right_dim), 1)
     for b in range(2):
@@ -163,22 +149,24 @@
             out_ref[:, b, pl.ds(spot, 1)] = block
 
 
-def add(kernel, pieces, sizes, shards, products, before, shape, scratch):
+def add(pieces, shards, products, left_sizes, right_sizes):
     count = sum(shard.shape[0] for shard in shards)
-    others = (*shards, products, *before)
-    return pl.pallas_call(
-        functools.partial(kernel, pieces),
-        out_shape=shape,
-        in_specs=[SMEM] * len(sizes) + [ANYWHERE] * len(others),
+    dtype, ranks = products.dtype, products.shape[0]
+    _, pair, right_inner, right_dim = shards[0].shape
+    left_dim = products.shape[2] // 2
+    return pl.pallas_call(
+        functools.partial(add_kernel, pieces),
+        out_shape=jax.ShapeDtypeStruct((ranks, 2, 2, left_dim // ranks, right_dim), dtype),
+        in_specs=[SMEM, SMEM] + [ANYWHERE] * (len(shards) + 1),
         out_specs=VMEM,
-        scratch_shapes=scratch
-        + [
-            pltpu.VMEM((count, *shards[0].shape[1:]), products.dtype),
-            pltpu.VMEM((count, *products.shape[2:]), products.dtype),
-            pltpu.SemaphoreType.DMA((2 * count + 1,)),
+        scratch_shapes=[
+            pltpu.VMEM((2, 2 * left_dim, right_dim), jnp.float32),
+            pltpu.VMEM((count, pair, right_inner, right_dim), dtype),
+            pltpu.VMEM((count, *products.shape[2:]), dtype),
+            pltpu.SemaphoreType.DMA((2 * count,)),
         ],
         compiler_params=pltpu.CompilerParams(vmem_limit_bytes=60 * MIB),
-    )(*sizes, *others)
+    )(left_sizes, right_sizes, *shards, products)
 
 
 def order_kernel(in_ref, out_ref, sems):
@@ -211,8 +199,7 @@
 
 def local(wavefunction, left_env, right_env, left_sizes, right_sizes):
     sectors, ranks = lax.axis_size("blk"), lax.axis_size("mpo")
-    left_dim, right_dim = left_env.shape[2], right_env.shape[2]
-    rows = left_dim // ranks
+    rows, right_dim = left_env.shape[1] // ranks, right_env.shape[2]
     spots = [(y, x, c) for y in range(SIDE) for x in range(SIDE) for c in range(2)]
 
     def step(second, by):
@@ -249,41 +236,31 @@
     own = lax.ppermute(right_env, ("blk", "mpo"), turn)
     up1, down1 = up(left_env), down(left_env)
     keep, give = cut(wavefunction, left_sizes, right_sizes)
-    own, up1, down1, keep, give = together(own, up1, down1, keep, give)
+    own, keep, give = together(own, keep, give)
 
     below, above = near_step(own, 1), near_step(own, -1)
+    got = swap(give)
+    below, above, up1, down1 = together(below, above, up1, down1)
+    two = near_step(below, 1)
+    line_a = stack(own, below)
+    a_below, a_above = far_step(line_a, 1), far_step(line_a, -1)
     up2, down2 = up(up1), down(down1)
-    got = swap(give)
-    below, above, up2, down2 = together(below, above, up2, down2)
-    two = near_step(below, 1)
+    two, up2, down2, got = together(two, up2, down2, got)
+    line_b = stack(above, two)
+    line_b, a_below, a_above, up2, down2 = together(line_b, a_below, a_above, up2, down2)
+    b_below, b_above = far_step(line_b, 1), far_step(line_b, -1)
     up3, down3 = up(up2), down(down2)
-    two, up3, down3, got = together(two, up3, down3, got)
-    line = stack(own, below, above, two)
-    line, up3, down3 = together(line, up3, down3)
-    line_below, line_above = far_step(line, 1), far_step(line, -1)
+    a_two = far_step(a_below, 1)
     up4 = up(up3)
+    b_below, b_above, up4 = together(b_below, b_above, up4)
+    b_two = far_step(b_above, -1)
     lefts = stack(left_env, down1, down2, down3, up4, up3, up2, up1)
     others = swap(lefts)
-    line_below, line_above, others = together(line_below, line_above, others)
-    half = SIDE // 2
-    far_below = far_step(line_below[:half], 1)
-    far_above = far_step(line_above[half:], -1)
 
     products = contract(lefts, others, keep, got)
-    total = jax.ShapeDtypeStruct((2, 2 * left_dim, right_dim), jnp.float32)
-    pieces = ((0, 0), (SIDE - 1, 0), (1, 0))
-    shards = (line, line_below, line_above)
-    begun = add(early_kernel, pieces, (), shards, products, (), total, [])
-    done = add(
-        late_kernel,
-        ((2, 0), (2, half)),
-        (left_sizes, right_sizes),
-        (far_below, far_above),
-        products,
-        (begun,),
-        jax.ShapeDtypeStruct((ranks, 2, 2, rows, right_dim), wavefunction.dtype),
-        [pltpu.VMEM(total.shape, total.dtype)],
-    )
+    pieces = ((0, 0), (SIDE - 1, 0), (1, 0), (0, 2), (2, 0), (SIDE - 1, 2), (1, 2), (2, 2))
+    shards = (line_a, a_below, a_above, line_b, a_two, b_below, b_above, b_two)
+    done = add(pieces, shards, products, left_sizes, right_sizes)
 
     by_plane = lax.all_to_all(done, "mpo", 0, 0)
     chips = SIDE * SIDE

time: 142 us -> 131 us (0.923); the launches traced: 141 us -> 128 us
  waiting for transfers between devices: 34.9 us -> 24.3 us
  starting transfers between devices: 36.5 us -> 43.5 us
  blocking collectives: 40 us -> 36.7 us
  Pallas kernels: 25.9 us -> 22.7 us
  local copies, waits for them, and re-layouts: 3.42 us -> 0.86 us
    ppermute x4 -> x6, starting transfers between devices: 5.35 us -> 13.7 us  [far_step(): return lax.ppermute(block, 'blk', step(True, by))]
    ppermute x4 -> x6, waiting for transfers between devices: 12.5 us -> 4.41 us  [far_step(): return lax.ppermute(block, 'blk', step(True, by))]
    all_to_all x1, blocking collectives: 19.6 us -> 14.5 us  [local(): out = order(lax.all_to_all(by_plane, 'blk', 0, 0, axis_index_groups=groups))]
    ppermute x4, starting transfers between devices: 5.75 us -> 1.3 us  [up(): lax.ppermute(block, 'mpo', [(z, (z + 1) % ranks) for z in range(ranks)])]
    ppermute x3, waiting for transfers between devices: 3.79 us -> 0.01 us  [down(): lax.ppermute(block, 'mpo', [(z, (z - 1) % ranks) for z in range(ranks)])]
    pallas_call x2 -> x1, Pallas kernels: 13.1 us -> 9.81 us  [add(): pl.pallas_call(functools.partial(add_kernel, pieces), out_shape=jax.Shape...]
    ppermute x4, waiting for transfers between devices: 15.1 us -> 17 us  [up(): lax.ppermute(block, 'mpo', [(z, (z + 1) % ranks) for z in range(ranks)])]
    all_to_all x1, blocking collectives: 20.4 us -> 22.2 us  [local(): by_plane = lax.all_to_all(done, 'mpo', 0, 0)]
  transfers between devices with their start and end apart: 17 -> 19, of which waited for: 7 -> 7; matrix products, arithmetic and copies ran while one was open for 1% -> 0% of each run, Pallas kernels for 14% -> 9%
where the time goes in v8:
time: 131 us; the launch traced here: 128 us
  starting transfers between devices  43.5 us (33%)
  blocking collectives  36.7 us (28%)
  waiting for transfers between devices  24.3 us (19%)
  Pallas kernels  22.7 us (17%)
    all_to_all x1, blocking collectives, local(): by_plane = lax.all_to_all(done, 'mpo', 0, 0)  22.2 us
    ppermute x4, waiting for transfers between devices, up(): lax.ppermute(block, 'mpo', [(z, (z + 1) % ranks) for z in range(ranks)])  17 us
    all_to_all x1, blocking collectives, local(): out = order(lax.all_to_all(by_plane, 'blk', 0, 0, axis_index_groups=groups))  14.5 us
    ppermute x6, starting transfers between devices, far_step(): return lax.ppermute(block, 'blk', step(True, by))  13.7 us
    pallas_call x1, Pallas kernels, add(): pl.pallas_call(functools.partial(add_kernel, pieces), out_shape=jax.Shape...  9.81 us
    ppermute x1, starting transfers between devices, local(): own = lax.ppermute(right_env, ('blk', 'mpo'), turn)  9.77 us
    pallas_call x1, Pallas kernels, contract(): pl.pallas_call(contract_kernel, out_shape=jax.ShapeDtypeStruct((ranks, *b...  9.02 us
    ppermute x3, starting transfers between devices, down(): lax.ppermute(block, 'mpo', [(z, (z - 1) % ranks) for z in range(ranks)])  7.72 us
  transfers between devices with their start and end apart: 19, of which 7 were waited for; matrix products, arithmetic and copies ran while one was open for 0% of the time, Pallas kernels for 9%

profile of v8, /device:TPU:1, one launch (start us, length us, event | category | flops | bytes accessed | tf_op | source)
XLA Modules:
  0.0 128.5 jit_solution(1029698659303711192)
XLA Ops:
  0.0 0.0 copy-start.3
  0.0 9.8 %collective-permute-start = (bf16[2,256,256]{2,1,0:T(8,128)(2,1)}, bf16[2,256,256]{2,1,0:T(8,128)(2,1)S(1)}, u32[]{:S(2)}, u32[]{:S(2)}) collective-permute-start(bf16[2,256,256]{2,1,0:T(8,128)(2,1)} %param.7), channel_id=1, source_target_pairs={{0,0},{1,16},{2,32},{3,48},{4,64},{5,80},{6,96},{7,112},{8,12},{9,... | collective-permute-start | bytes 786440 | tf_op jit(solution)/shard_map/ppermute | solution.py:236
  9.8 1.3 %collective-permute-start.3 = (bf16[2,256,256]{2,1,0:T(8,128)(2,1)}, bf16[2,256,256]{2,1,0:T(8,128)(2,1)S(1)}, u32[]{:S(2)}, u32[]{:S(2)}) collective-permute-start(bf16[2,256,256]{2,1,0:T(8,128)(2,1)} %refs_0_.1), channel_id=1, source_target_pairs={{0,1},{1,2},{2,3},{3,4},{4,5},{5,6},{6,7},{7,0},{8,9},{9,10},{10,1... | collective-permute-start | bytes 786440 | tf_op jit(solution)/shard_map/ppermute | solution.py:223
  11.1 2.4 %collective-permute-start.4 = (bf16[2,256,256]{2,1,0:T(8,128)(2,1)}, bf16[2,256,256]{2,1,0:T(8,128)(2,1)S(1)}, u32[]{:S(2)}, u32[]{:S(2)}) collective-permute-start(bf16[2,256,256]{2,1,0:T(8,128)(2,1)} %refs_0_.1), channel_id=1, source_target_pairs={{0,7},{1,0},{2,1},{3,2},{4,3},{5,4},{6,5},{7,6},{8,15},{9,8},{10,9... | collective-permute-start | bytes 786440 | tf_op jit(solution)/shard_map/ppermute | solution.py:226
  13.4 2.6 %shard_map.55 = (bf16[2,256,256]{2,1,0:T(8,128)(2,1)}, bf16[2,256,256]{2,1,0:T(8,128)(2,1)}) custom-call(s32[32]{0:T(128)} %left_sizes.3, s32[32]{0:T(128)} %right_sizes.3, bf16[256,8192]{1,0:T(8,128)(2,1)} %psi_ref.1), custom_call_target="tpu_custom_call" | custom-call | tf_op jit(solution)/shard_map/pallas_call | solution.py:76
  16.1 0.0 collective-permute-done.refs_0_
  16.1 0.1 collective-permute-start.1
  16.2 2.7 %collective-permute-start.2 = (bf16[2,256,256]{2,1,0:T(8,128)(2,1)S(1)}, bf16[2,256,256]{2,1,0:T(8,128)(2,1)S(1)}, u32[]{:S(2)}, u32[]{:S(2)}) collective-permute-start(bf16[2,256,256]{2,1,0:T(8,128)(2,1)S(1)} %collective-permute-done.refs_0_), channel_id=1, source_target_pairs={{0,48},{8,200},{16,0},{24,216},{32,16},{40,232},{48,32},{56,248},{... | collective-permute-start | bytes 786440 | tf_op jit(solution)/shard_map/ppermute | solution.py:214
  18.9 0.0 collective-permute-start.8
  18.9 7.2 %collective-permute-done.3.refs_7_ = bf16[2,256,256]{2,1,0:T(8,128)(2,1)S(1)} collective-permute-done((bf16[2,256,256]{2,1,0:T(8,128)(2,1)}, bf16[2,256,256]{2,1,0:T(8,128)(2,1)S(1)}, u32[]{:S(2)}, u32[]{:S(2)}) %collective-permute-start.3) | collective-permute-done | bytes 262176 | tf_op jit(solution)/shard_map/ppermute | solution.py:223
  26.1 0.0 collective-permute-done.4.refs_1_
  26.1 0.0 collective-permute-done.1.refs_1_
  26.1 0.0 collective-permute-done.2.refs_0_
  26.1 0.1 shard_map.56.refs_0_
  26.1 0.0 copy-start.1
  26.1 6.2 %collective-permute-start.10 = (bf16[2,2,256,256]{3,2,1,0:T(8,128)(2,1)S(1)}, bf16[2,2,256,256]{3,2,1,0:T(8,128)(2,1)S(1)}, u32[]{:S(2)}, u32[]{:S(2)}) collective-permute-start(bf16[2,2,256,256]{3,2,1,0:T(8,128)(2,1)S(1)} %shard_map.56.refs_0_), channel_id=1, source_target_pairs={{0,192},{8,56},{16,208},{24,8},{32,224},{40,24},{48,240},{56,40},{... | collective-permute-start | bytes 1572872 | tf_op jit(solution)/shard_map/ppermute | solution.py:217
  32.4 0.0 collective-permute-start.9
  32.4 1.1 collective-permute-start.5
  33.5 0.0 collective-permute-start.6
  33.5 0.0 collective-permute-done.8.other_psi_ref
  33.5 2.7 %collective-permute-start.7 = (bf16[2,256,256]{2,1,0:T(8,128)(2,1)S(1)}, bf16[2,256,256]{2,1,0:T(8,128)(2,1)S(1)}, u32[]{:S(2)}, u32[]{:S(2)}) collective-permute-start(bf16[2,256,256]{2,1,0:T(8,128)(2,1)S(1)} %collective-permute-done.4.refs_1_), channel_id=1, source_target_pairs={{0,7},{1,0},{2,1},{3,2},{4,3},{5,4},{6,5},{7,6},{8,15},{9,8},{10,9... | collective-permute-start | bytes 786440 | tf_op jit(solution)/shard_map/ppermute | solution.py:226
  36.2 2.9 %collective-permute-done.5.refs_1_ = bf16[2,256,256]{2,1,0:T(8,128)(2,1)S(1)} collective-permute-done((bf16[2,256,256]{2,1,0:T(8,128)(2,1)S(1)}, bf16[2,256,256]{2,1,0:T(8,128)(2,1)S(1)}, u32[]{:S(2)}, u32[]{:S(2)}) %collective-permute-start.5) | collective-permute-done | bytes 262176 | tf_op jit(solution)/shard_map/ppermute | solution.py:214
  39.1 1.3 collective-permute-done.6.refs_6_
  40.4 0.0 collective-permute-done.7.refs_2_
  40.4 0.1 shard_map.57.refs_3_
  40.4 0.0 copy-start.2
  40.4 0.0 collective-permute-done.10.refs_2_
  40.5 0.0 copy-start.4
  40.5 4.0 %collective-permute-done.9.refs_1_ = bf16[2,2,256,256]{3,2,1,0:T(8,128)(2,1)} collective-permute-done((bf16[2,2,256,256]{3,2,1,0:T(8,128)(2,1)S(1)}, bf16[2,2,256,256]{3,2,1,0:T(8,128)(2,1)}, u32[]{:S(2)}, u32[]{:S(2)}) %collective-permute-start.9) | collective-permute-done | bytes 524320 | tf_op jit(solution)/shard_map/ppermute | solution.py:217
  44.4 0.0 collective-permute-start.14
  44.4 0.0 collective-permute-start.12
  44.4 2.7 %collective-permute-start.13 = (bf16[2,2,256,256]{3,2,1,0:T(8,128)(2,1)S(1)}, bf16[2,2,256,256]{3,2,1,0:T(8,128)(2,1)}, u32[]{:S(2)}, u32[]{:S(2)}) collective-permute-start(bf16[2,2,256,256]{3,2,1,0:T(8,128)(2,1)S(1)} %shard_map.57.refs_3_), channel_id=1, source_target_pairs={{0,192},{8,56},{16,208},{24,8},{32,224},{40,24},{48,240},{56,40},{... | collective-permute-start | bytes 1572872 | tf_op jit(solution)/shard_map/ppermute | solution.py:217
  47.1 3.8 %collective-permute-done.14.refs_5_ = bf16[2,256,256]{2,1,0:T(8,128)(2,1)S(1)} collective-permute-done((bf16[2,256,256]{2,1,0:T(8,128)(2,1)S(1)}, bf16[2,256,256]{2,1,0:T(8,128)(2,1)S(1)}, u32[]{:S(2)}, u32[]{:S(2)}) %collective-permute-start.14) | collective-permute-done | bytes 262176 | tf_op jit(solution)/shard_map/ppermute | solution.py:223
  50.9 0.0 collective-permute-start.15
  50.9 2.7 %collective-permute-start.17 = (bf16[2,256,256]{2,1,0:T(8,128)(2,1)S(1)}, bf16[2,256,256]{2,1,0:T(8,128)(2,1)S(1)}, u32[]{:S(2)}, u32[]{:S(2)}) collective-permute-start(bf16[2,256,256]{2,1,0:T(8,128)(2,1)S(1)} %collective-permute-done.7.refs_2_), channel_id=1, source_target_pairs={{0,7},{1,0},{2,1},{3,2},{4,3},{5,4},{6,5},{7,6},{8,15},{9,8},{10,9... | collective-permute-start | bytes 786440 | tf_op jit(solution)/shard_map/ppermute | solution.py:226
  53.5 0.4 collective-permute-done.12.refs_5_
  54.0 0.0 copy-start.5
  54.0 0.0 collective-permute-done.13.refs_6_
  54.0 4.8 %collective-permute-done.15.refs_4_ = bf16[2,256,256]{2,1,0:T(8,128)(2,1)S(1)} collective-permute-done((bf16[2,256,256]{2,1,0:T(8,128)(2,1)S(1)}, bf16[2,256,256]{2,1,0:T(8,128)(2,1)S(1)}, u32[]{:S(2)}, u32[]{:S(2)}) %collective-permute-start.15) | collective-permute-done | bytes 262176 | tf_op jit(solution)/shard_map/ppermute | solution.py:223
  58.7 0.0 collective-permute-done.17.refs_3_
  58.7 0.0 copy-done.3
  58.8 0.2 shard_map.58.left_ref
  59.0 0.0 copy-done.4
  59.0 0.0 copy-start
  59.0 7.1 %collective-permute-start.18 = (bf16[8,2,256,256]{3,2,1,0:T(8,128)(2,1)S(1)}, bf16[8,2,256,256]{3,2,1,0:T(8,128)(2,1)}, u32[]{:S(2)}, u32[]{:S(2)}) collective-permute-start(bf16[8,2,256,256]{3,2,1,0:T(8,128)(2,1)S(1)} %shard_map.58.left_ref), channel_id=1, source_target_pairs={{0,8},{8,0},{16,24},{24,16},{32,40},{40,32},{48,56},{56,48},{64,72... | collective-permute-start | bytes 6291464 | tf_op jit(solution)/shard_map/ppermute | solution.py:220
  66.1 0.0 copy-done.5
  66.1 2.6 %collective-permute-start.11 = (bf16[2,2,256,256]{3,2,1,0:T(8,128)(2,1)}, bf16[2,2,256,256]{3,2,1,0:T(8,128)(2,1)S(1)}, u32[]{:S(2)}, u32[]{:S(2)}) collective-permute-start(bf16[2,2,256,256]{3,2,1,0:T(8,128)(2,1)} %collective-permute-done.9.refs_1_), channel_id=1, source_target_pairs={{0,64},{8,24},{16,80},{24,40},{32,96},{40,56},{48,112},{56,8},{64,... | collective-permute-start | bytes 1572872 | tf_op jit(solution)/shard_map/ppermute | solution.py:217
  68.7 2.2 %collective-permute-start.16 = (bf16[2,2,256,256]{3,2,1,0:T(8,128)(2,1)}, bf16[2,2,256,256]{3,2,1,0:T(8,128)(2,1)}, u32[]{:S(2)}, u32[]{:S(2)}) collective-permute-start(bf16[2,2,256,256]{3,2,1,0:T(8,128)(2,1)} %collective-permute-done.13.refs_6_), channel_id=1, source_target_pairs={{0,192},{8,56},{16,208},{24,8},{32,224},{40,24},{48,240},{56,40},{... | collective-permute-start | bytes 1572872 | tf_op jit(solution)/shard_map/ppermute | solution.py:217
  71.0 0.0 collective-permute-done.18.other_ref
  71.0 0.0 copy-done
  71.0 9.0 %shard_map.59.refs_8_ = bf16[8,2,512,512]{3,2,1,0:T(8,128)(2,1)} custom-call(bf16[8,2,256,256]{3,2,1,0:T(8,128)(2,1)} %copy-done, bf16[8,2,256,256]{3,2,1,0:T(8,128)(2,1)} %collective-permute-done.18.other_ref, bf16[2,256,256]{2,1,0:T(8,128)(2,1)} %get-tuple-element.45.psi_ref, bf16[2,256,256]{2,1,0:T(8,128)(2,1)} %collective-permute-done.8.other_psi_ref), custom_call_target="tpu_custom_call" | custom-call | tf_op jit(solution)/shard_map/pallas_call | solution.py:106
  80.0 0.0 copy-done.1
  80.0 0.0 copy-done.2
  80.0 0.0 collective-permute-done.11.refs_4_
  80.0 0.0 copy-start.6
  80.0 0.0 collective-permute-done.16.refs_7_
  80.0 0.8 copy-done.6
  80.9 9.8 %shard_map.60 = bf16[8,2,2,32,256]{4,3,2,1,0:T(8,128)(2,1)} custom-call(s32[32]{0:T(128)} %left_sizes.3, s32[32]{0:T(128)} %right_sizes.3, bf16[2,2,256,256]{3,2,1,0:T(8,128)(2,1)} %copy-done.1, bf16[2,2,256,256]{3,2,1,0:T(8,128)(2,1)} %collective-permute-done.9.refs_1_, bf16[2,2,256,256]{3,2,1,0:T(8,128)(2,1)} %copy-done.4, ...), custom_call_target="tpu_custom_call" | custom-call | tf_op jit(solution)/shard_map/pallas_call | solution.py:157
  90.7 22.2 %all_to_all.10 = bf16[8,2,2,32,256]{4,3,2,1,0:T(8,128)(2,1)S(1)} all-to-all(bf16[8,2,2,32,256]{4,3,2,1,0:T(8,128)(2,1)} %shard_map.60), channel_id=1, replica_groups=mesh['blk'=32,'mpo'=8] {'mpo'}, dimensions={0} | all-to-all | bytes 1048576 | tf_op jit(solution)/shard_map/all_to_all | solution.py:265
  112.9 14.5 %all_to_all.11.in_ref = bf16[16,2,32,256]{3,2,1,0:T(8,128)(2,1)S(1)} all-to-all(bf16[16,2,32,256]{3,2,1,0:T(8,128)(2,1)S(1)} %bitcast.2), channel_id=1, replica_groups={{0,128,16,144,32,160,48,176,64,192,80,208,96,224,112,240},{72,200,88,21..., dimensions={0} | all-to-all | bytes 1048576 | tf_op jit(solution)/shard_map/all_to_all | solution.py:272
  127.4 0.9 shard_map.61
Async XLA Ops:
  0.0 58.7 %copy-start.3 = (bf16[2,256,256]{2,1,0:T(8,128)(2,1)S(1)}, bf16[2,256,256]{2,1,0:T(8,128)(2,1)}, u32[]{:S(2)}) copy-start(bf16[2,256,256]{2,1,0:T(8,128)(2,1)} %refs_0_.1) | copy-start | bytes 786436
  0.0 16.1 %collective-permute-start = (bf16[2,256,256]{2,1,0:T(8,128)(2,1)}, bf16[2,256,256]{2,1,0:T(8,128)(2,1)S(1)}, u32[]{:S(2)}, u32[]{:S(2)}) collective-permute-start(bf16[2,256,256]{2,1,0:T(8,128)(2,1)} %param.7), channel_id=1, source_target_pairs={{0,0},{1,16},{2,32},{3,48},{4,64},{5,80},{6,96},{7,112},{8,12},{9,... | collective-permute-start | bytes 786440 | tf_op jit(solution)/shard_map/ppermute | solution.py:236
  9.8 16.3 %collective-permute-start.3 = (bf16[2,256,256]{2,1,0:T(8,128)(2,1)}, bf16[2,256,256]{2,1,0:T(8,128)(2,1)S(1)}, u32[]{:S(2)}, u32[]{:S(2)}) collective-permute-start(bf16[2,256,256]{2,1,0:T(8,128)(2,1)} %refs_0_.1), channel_id=1, source_target_pairs={{0,1},{1,2},{2,3},{3,4},{4,5},{5,6},{6,7},{7,0},{8,9},{9,10},{10,1... | collective-permute-start | bytes 786440 | tf_op jit(solution)/shard_map/ppermute | solution.py:223
  11.1 15.0 %collective-permute-start.4 = (bf16[2,256,256]{2,1,0:T(8,128)(2,1)}, bf16[2,256,256]{2,1,0:T(8,128)(2,1)S(1)}, u32[]{:S(2)}, u32[]{:S(2)}) collective-permute-start(bf16[2,256,256]{2,1,0:T(8,128)(2,1)} %refs_0_.1), channel_id=1, source_target_pairs={{0,7},{1,0},{2,1},{3,2},{4,3},{5,4},{6,5},{7,6},{8,15},{9,8},{10,9... | collective-permute-start | bytes 786440 | tf_op jit(solution)/shard_map/ppermute | solution.py:226
  16.1 10.0 %collective-permute-start.1 = (bf16[2,256,256]{2,1,0:T(8,128)(2,1)S(1)}, bf16[2,256,256]{2,1,0:T(8,128)(2,1)S(1)}, u32[]{:S(2)}, u32[]{:S(2)}) collective-permute-start(bf16[2,256,256]{2,1,0:T(8,128)(2,1)S(1)} %collective-permute-done.refs_0_), channel_id=1, source_target_pairs={{0,16},{8,72},{16,32},{24,88},{32,48},{40,104},{48,0},{56,120},{64... | collective-permute-start | bytes 786440 | tf_op jit(solution)/shard_map/ppermute | solution.py:214
  16.2 9.9 %collective-permute-start.2 = (bf16[2,256,256]{2,1,0:T(8,128)(2,1)S(1)}, bf16[2,256,256]{2,1,0:T(8,128)(2,1)S(1)}, u32[]{:S(2)}, u32[]{:S(2)}) collective-permute-start(bf16[2,256,256]{2,1,0:T(8,128)(2,1)S(1)} %collective-permute-done.refs_0_), channel_id=1, source_target_pairs={{0,48},{8,200},{16,0},{24,216},{32,16},{40,232},{48,32},{56,248},{... | collective-permute-start | bytes 786440 | tf_op jit(solution)/shard_map/ppermute | solution.py:214
  18.9 14.7 %collective-permute-start.8 = (bf16[2,256,256]{2,1,0:T(8,128)(2,1)}, bf16[2,256,256]{2,1,0:T(8,128)(2,1)}, u32[]{:S(2)}, u32[]{:S(2)}) collective-permute-start(bf16[2,256,256]{2,1,0:T(8,128)(2,1)} %get-tuple-element.33), channel_id=1, source_target_pairs={{0,8},{8,0},{16,24},{24,16},{32,40},{40,32},{48,56},{56,48},{64,72... | collective-permute-start | bytes 786440 | tf_op jit(solution)/shard_map/ppermute | solution.py:220
  26.1 53.9 %copy-start.1 = (bf16[2,2,256,256]{3,2,1,0:T(8,128)(2,1)}, bf16[2,2,256,256]{3,2,1,0:T(8,128)(2,1)S(1)}, u32[]{:S(2)}) copy-start(bf16[2,2,256,256]{3,2,1,0:T(8,128)(2,1)S(1)} %shard_map.56.refs_0_) | copy-start | bytes 1572868
  26.1 14.3 %collective-permute-start.10 = (bf16[2,2,256,256]{3,2,1,0:T(8,128)(2,1)S(1)}, bf16[2,2,256,256]{3,2,1,0:T(8,128)(2,1)S(1)}, u32[]{:S(2)}, u32[]{:S(2)}) collective-permute-start(bf16[2,2,256,256]{3,2,1,0:T(8,128)(2,1)S(1)} %shard_map.56.refs_0_), channel_id=1, source_target_pairs={{0,192},{8,56},{16,208},{24,8},{32,224},{40,24},{48,240},{56,40},{... | collective-permute-start | bytes 1572872 | tf_op jit(solution)/shard_map/ppermute | solution.py:217
  32.4 12.0 %collective-permute-start.9 = (bf16[2,2,256,256]{3,2,1,0:T(8,128)(2,1)S(1)}, bf16[2,2,256,256]{3,2,1,0:T(8,128)(2,1)}, u32[]{:S(2)}, u32[]{:S(2)}) collective-permute-start(bf16[2,2,256,256]{3,2,1,0:T(8,128)(2,1)S(1)} %shard_map.56.refs_0_), channel_id=1, source_target_pairs={{0,64},{8,24},{16,80},{24,40},{32,96},{40,56},{48,112},{56,8},{64,... | collective-permute-start | bytes 1572872 | tf_op jit(solution)/shard_map/ppermute | solution.py:217
  32.4 6.7 %collective-permute-start.5 = (bf16[2,256,256]{2,1,0:T(8,128)(2,1)S(1)}, bf16[2,256,256]{2,1,0:T(8,128)(2,1)S(1)}, u32[]{:S(2)}, u32[]{:S(2)}) collective-permute-start(bf16[2,256,256]{2,1,0:T(8,128)(2,1)S(1)} %collective-permute-done.1.refs_1_), channel_id=1, source_target_pairs={{0,16},{8,72},{16,32},{24,88},{32,48},{40,104},{48,0},{56,120},{64... | collective-permute-start | bytes 786440 | tf_op jit(solution)/shard_map/ppermute | solution.py:214
  33.5 6.8 %collective-permute-start.6 = (bf16[2,256,256]{2,1,0:T(8,128)(2,1)S(1)}, bf16[2,256,256]{2,1,0:T(8,128)(2,1)S(1)}, u32[]{:S(2)}, u32[]{:S(2)}) collective-permute-start(bf16[2,256,256]{2,1,0:T(8,128)(2,1)S(1)} %collective-permute-done.3.refs_7_), channel_id=1, source_target_pairs={{0,1},{1,2},{2,3},{3,4},{4,5},{5,6},{6,7},{7,0},{8,9},{9,10},{10,1... | collective-permute-start | bytes 786440 | tf_op jit(solution)/shard_map/ppermute | solution.py:223
  33.5 6.8 %collective-permute-start.7 = (bf16[2,256,256]{2,1,0:T(8,128)(2,1)S(1)}, bf16[2,256,256]{2,1,0:T(8,128)(2,1)S(1)}, u32[]{:S(2)}, u32[]{:S(2)}) collective-permute-start(bf16[2,256,256]{2,1,0:T(8,128)(2,1)S(1)} %collective-permute-done.4.refs_1_), channel_id=1, source_target_pairs={{0,7},{1,0},{2,1},{3,2},{4,3},{5,4},{6,5},{7,6},{8,15},{9,8},{10,9... | collective-permute-start | bytes 786440 | tf_op jit(solution)/shard_map/ppermute | solution.py:226
  40.4 39.6 %copy-start.2 = (bf16[2,2,256,256]{3,2,1,0:T(8,128)(2,1)}, bf16[2,2,256,256]{3,2,1,0:T(8,128)(2,1)S(1)}, u32[]{:S(2)}) copy-start(bf16[2,2,256,256]{3,2,1,0:T(8,128)(2,1)S(1)} %shard_map.57.refs_3_) | copy-start | bytes 1572868
  40.5 18.5 %copy-start.4 = (bf16[2,2,256,256]{3,2,1,0:T(8,128)(2,1)}, bf16[2,2,256,256]{3,2,1,0:T(8,128)(2,1)S(1)}, u32[]{:S(2)}) copy-start(bf16[2,2,256,256]{3,2,1,0:T(8,128)(2,1)S(1)} %collective-permute-done.10.refs_2_) | copy-start | bytes 1572868
  44.4 6.4 %collective-permute-start.14 = (bf16[2,256,256]{2,1,0:T(8,128)(2,1)S(1)}, bf16[2,256,256]{2,1,0:T(8,128)(2,1)S(1)}, u32[]{:S(2)}, u32[]{:S(2)}) collective-permute-start(bf16[2,256,256]{2,1,0:T(8,128)(2,1)S(1)} %collective-permute-done.6.refs_6_), channel_id=1, source_target_pairs={{0,1},{1,2},{2,3},{3,4},{4,5},{5,6},{6,7},{7,0},{8,9},{9,10},{10,1... | collective-permute-start | bytes 786440 | tf_op jit(solution)/shard_map/ppermute | solution.py:223
  44.4 9.5 %collective-permute-start.12 = (bf16[2,2,256,256]{3,2,1,0:T(8,128)(2,1)S(1)}, bf16[2,2,256,256]{3,2,1,0:T(8,128)(2,1)S(1)}, u32[]{:S(2)}, u32[]{:S(2)}) collective-permute-start(bf16[2,2,256,256]{3,2,1,0:T(8,128)(2,1)S(1)} %shard_map.57.refs_3_), channel_id=1, source_target_pairs={{0,64},{8,24},{16,80},{24,40},{32,96},{40,56},{48,112},{56,8},{64,... | collective-permute-start | bytes 1572872 | tf_op jit(solution)/shard_map/ppermute | solution.py:217
  44.4 9.5 %collective-permute-start.13 = (bf16[2,2,256,256]{3,2,1,0:T(8,128)(2,1)S(1)}, bf16[2,2,256,256]{3,2,1,0:T(8,128)(2,1)}, u32[]{:S(2)}, u32[]{:S(2)}) collective-permute-start(bf16[2,2,256,256]{3,2,1,0:T(8,128)(2,1)S(1)} %shard_map.57.refs_3_), channel_id=1, source_target_pairs={{0,192},{8,56},{16,208},{24,8},{32,224},{40,24},{48,240},{56,40},{... | collective-permute-start | bytes 1572872 | tf_op jit(solution)/shard_map/ppermute | solution.py:217
  50.9 7.9 %collective-permute-start.15 = (bf16[2,256,256]{2,1,0:T(8,128)(2,1)S(1)}, bf16[2,256,256]{2,1,0:T(8,128)(2,1)S(1)}, u32[]{:S(2)}, u32[]{:S(2)}) collective-permute-start(bf16[2,256,256]{2,1,0:T(8,128)(2,1)S(1)} %collective-permute-done.14.refs_5_), channel_id=1, source_target_pairs={{0,1},{1,2},{2,3},{3,4},{4,5},{5,6},{6,7},{7,0},{8,9},{9,10},{10,1... | collective-permute-start | bytes 786440 | tf_op jit(solution)/shard_map/ppermute | solution.py:223
  50.9 7.9 %collective-permute-start.17 = (bf16[2,256,256]{2,1,0:T(8,128)(2,1)S(1)}, bf16[2,256,256]{2,1,0:T(8,128)(2,1)S(1)}, u32[]{:S(2)}, u32[]{:S(2)}) collective-permute-start(bf16[2,256,256]{2,1,0:T(8,128)(2,1)S(1)} %collective-permute-done.7.refs_2_), channel_id=1, source_target_pairs={{0,7},{1,0},{2,1},{3,2},{4,3},{5,4},{6,5},{7,6},{8,15},{9,8},{10,9... | collective-permute-start | bytes 786440 | tf_op jit(solution)/shard_map/ppermute | solution.py:226
  54.0 12.2 %copy-start.5 = (bf16[2,2,256,256]{3,2,1,0:T(8,128)(2,1)}, bf16[2,2,256,256]{3,2,1,0:T(8,128)(2,1)S(1)}, u32[]{:S(2)}) copy-start(bf16[2,2,256,256]{3,2,1,0:T(8,128)(2,1)S(1)} %collective-permute-done.12.refs_5_) | copy-start | bytes 1572868
  59.0 12.0 %copy-start = (bf16[8,2,256,256]{3,2,1,0:T(8,128)(2,1)}, bf16[8,2,256,256]{3,2,1,0:T(8,128)(2,1)S(1)}, u32[]{:S(2)}) copy-start(bf16[8,2,256,256]{3,2,1,0:T(8,128)(2,1)S(1)} %shard_map.58.left_ref) | copy-start | bytes 6291460
  59.0 12.0 %collective-permute-start.18 = (bf16[8,2,256,256]{3,2,1,0:T(8,128)(2,1)S(1)}, bf16[8,2,256,256]{3,2,1,0:T(8,128)(2,1)}, u32[]{:S(2)}, u32[]{:S(2)}) collective-permute-start(bf16[8,2,256,256]{3,2,1,0:T(8,128)(2,1)S(1)} %shard_map.58.left_ref), channel_id=1, source_target_pairs={{0,8},{8,0},{16,24},{24,16},{32,40},{40,32},{48,56},{56,48},{64,72... | collective-permute-start | bytes 6291464 | tf_op jit(solution)/shard_map/ppermute | solution.py:220
  66.1 13.9 %collective-permute-start.11 = (bf16[2,2,256,256]{3,2,1,0:T(8,128)(2,1)}, bf16[2,2,256,256]{3,2,1,0:T(8,128)(2,1)S(1)}, u32[]{:S(2)}, u32[]{:S(2)}) collective-permute-start(bf16[2,2,256,256]{3,2,1,0:T(8,128)(2,1)} %collective-permute-done.9.refs_1_), channel_id=1, source_target_pairs={{0,64},{8,24},{16,80},{24,40},{32,96},{40,56},{48,112},{56,8},{64,... | collective-permute-start | bytes 1572872 | tf_op jit(solution)/shard_map/ppermute | solution.py:217
  68.7 11.3 %collective-permute-start.16 = (bf16[2,2,256,256]{3,2,1,0:T(8,128)(2,1)}, bf16[2,2,256,256]{3,2,1,0:T(8,128)(2,1)}, u32[]{:S(2)}, u32[]{:S(2)}) collective-permute-start(bf16[2,2,256,256]{3,2,1,0:T(8,128)(2,1)} %collective-permute-done.13.refs_6_), channel_id=1, source_target_pairs={{0,192},{8,56},{16,208},{24,8},{32,224},{40,24},{48,240},{56,40},{... | collective-permute-start | bytes 1572872 | tf_op jit(solution)/shard_map/ppermute | solution.py:217
  80.0 0.9 copy-start.6

commit v9 on v8

--- a/solution.py
+++ b/solution.py
@@ -83,61 +83,37 @@
     )(left_sizes, right_sizes, wavefunction)
 
 
-def contract_kernel(left_ref, other_ref, psi_ref, other_psi_ref, out_ref):
-    _, pair, left_dim, inner = left_ref.shape
-    right_dim = psi_ref.shape[2]
-    for a, (left, psi) in enumerate(((left_ref, psi_ref), (other_ref, other_psi_ref))):
-        block = left[0].reshape(pair * left_dim, inner)
-        for b in range(2):
-            product = jnp.dot(block, psi[b], preferred_element_type=jnp.float32).astype(out_ref.dtype)
-            for w in range(pair):
-                columns = slice(w * right_dim, (w + 1) * right_dim)
-                out_ref[0, b, a * left_dim : (a + 1) * left_dim, columns] = product[
-                    w * left_dim : (w + 1) * left_dim
-                ]
-
-
-def contract(lefts, others, psi, other_psi):
-    ranks, pair, left_dim, _ = lefts.shape
-    right_dim = psi.shape[2]
-    left = pl.BlockSpec((1, *lefts.shape[1:]), lambda i: (i, 0, 0, 0))
-    whole = pl.BlockSpec(psi.shape, lambda i: (0, 0, 0))
-    block = (2, 2 * left_dim, pair * right_dim)
-    return pl.pallas_call(
-        contract_kernel,
-        out_shape=jax.ShapeDtypeStruct((ranks, *block), psi.dtype),
-        grid=(ranks,),
-        in_specs=[left, left, whole, whole],
-        out_specs=pl.BlockSpec((1, *block), lambda i: (i, 0, 0, 0)),
-        compiler_params=pltpu.CompilerParams(vmem_limit_bytes=60 * MIB),
-    )(lefts, others, psi, other_psi)
-
-
-def add_kernel(pieces, left_sizes, right_sizes, *refs):
-    shards, (products, out_ref, total, held, factors, sems) = refs[:-6], refs[-6:]
+def apply_kernel(pieces, left_sizes, right_sizes, *refs):
+    ins, (out_ref, total, held, left_held, psi_held, middle, sems) = refs[:-7], refs[-7:]
+    shards, lefts, psis = ins[: len(pieces)], ins[len(pieces) : -2], ins[-2:]
     sector, rank, core, x0, y0 = coordinates()
     ranks, _, _, rows, right_dim = out_ref.shape
     left_dim = ranks * rows
-    sectors_of, copies = [], []
-    for ref, (far, first) in zip(shards, pieces):
-        for k in range(ref.shape[0]):
-            at = len(sectors_of)
-            near = OFFSETS[first + k]
+    first = [pltpu.make_async_copy(psis[a], psi_held.at[a], sems.at[a]) for a in range(2)]
+    first += [pltpu.make_async_copy(lefts[a], left_held.at[a], sems.at[2 + a]) for a in range(2)]
+    coming = [pltpu.make_async_copy(r, held.at[i], sems.at[4 + i]) for i, r in enumerate(shards)]
+    for copy in first + coming:
+        copy.start()
+    total[...] = jnp.zeros_like(total)
+    for copy in first:
+        copy.wait()
+    for i, (far, start) in enumerate(pieces):
+        coming[i].wait()
+        for k in range(held.shape[1]):
+            near = OFFSETS[start + k]
             y = jnp.where(core == 0, y0 + far, y0 + near) & (SIDE - 1)
             x = jnp.where(core == 0, x0 + near, x0 + far) & (SIDE - 1)
-            which, pair = y // 2, x + SIDE * (y & 1)
-            source = products.at[(pair - rank) & (ranks - 1), which]
-            copies.append(pltpu.make_async_copy(source, factors.at[at], sems.at[2 * at]))
-            copies.append(pltpu.make_async_copy(ref.at[k], held.at[at], sems.at[2 * at + 1]))
-            sectors_of.append(which)
-    for copy in copies:
-        copy.start()
-    total[...] = jnp.zeros_like(total)
-    for i, which in enumerate(sectors_of):
-        copies[2 * i].wait()
-        copies[2 * i + 1].wait()
-        shard = held[i].reshape(factors.shape[2], right_dim)
-        total[which] += jnp.dot(factors[i], shard, preferred_element_type=jnp.float32)
+            which, pair = y // 2, (x + SIDE * (y & 1) - rank) & (ranks - 1)
+            for a in range(2):
+                block = left_held[a, pair].reshape(2 * left_dim, left_dim)
+                product = jnp.dot(block, psi_held[a, which], preferred_element_type=jnp.float32)
+                product = product.astype(middle.dtype)
+                for w in range(2):
+                    middle[k % 2, a * left_dim : (a + 1) * left_dim, w * right_dim : (w + 1) * right_dim] = (
+                        product[w * left_dim : (w + 1) * left_dim]
+                    )
+            shard = held[i, k].reshape(2 * right_dim, right_dim)
+            total[which] += jnp.dot(middle[k % 2], shard, preferred_element_type=jnp.float32)
     row = lax.broadcasted_iota(jnp.int32, (left_dim, right_dim), 0)
     col = lax.broadcasted_iota(jnp.int32, (left_dim, right_dim), 1)
     for b in range(2):
@@ -149,24 +125,26 @@
             out_ref[:, b, pl.ds(spot, 1)] = block
 
 
-def add(pieces, shards, products, left_sizes, right_sizes):
-    count = sum(shard.shape[0] for shard in shards)
-    dtype, ranks = products.dtype, products.shape[0]
-    _, pair, right_inner, right_dim = shards[0].shape
-    left_dim = products.shape[2] // 2
-    return pl.pallas_call(
-        functools.partial(add_kernel, pieces),
+def apply(pieces, shards, lefts, psis, left_sizes, right_sizes):
+    dtype = psis[0].dtype
+    ranks, pair, left_dim, _ = lefts[0].shape
+    right_dim = psis[0].shape[2]
+    others = (*shards, *lefts, *psis)
+    return pl.pallas_call(
+        functools.partial(apply_kernel, pieces),
         out_shape=jax.ShapeDtypeStruct((ranks, 2, 2, left_dim // ranks, right_dim), dtype),
-        in_specs=[SMEM, SMEM] + [ANYWHERE] * (len(shards) + 1),
+        in_specs=[SMEM, SMEM] + [ANYWHERE] * len(others),
         out_specs=VMEM,
         scratch_shapes=[
             pltpu.VMEM((2, 2 * left_dim, right_dim), jnp.float32),
-            pltpu.VMEM((count, pair, right_inner, right_dim), dtype),
-            pltpu.VMEM((count, *products.shape[2:]), dtype),
-            pltpu.SemaphoreType.DMA((2 * count,)),
+            pltpu.VMEM((len(shards), *shards[0].shape), dtype),
+            pltpu.VMEM((2, *lefts[0].shape), dtype),
+            pltpu.VMEM((2, *psis[0].shape), dtype),
+            pltpu.VMEM((2, 2 * left_dim, pair * right_dim), dtype),
+            pltpu.SemaphoreType.DMA((len(shards) + 4,)),
         ],
         compiler_params=pltpu.CompilerParams(vmem_limit_bytes=60 * MIB),
-    )(left_sizes, right_sizes, *shards, products)
+    )(left_sizes, right_sizes, *others)
 
 
 def order_kernel(in_ref, out_ref, sems):
@@ -238,29 +216,27 @@
     keep, give = cut(wavefunction, left_sizes, right_sizes)
     own, keep, give = together(own, keep, give)
 
-    below, above = near_step(own, 1), near_step(own, -1)
+    below, above, two = near_step(own, 1), near_step(own, -1), near_step(own, 2)
     got = swap(give)
     below, above, up1, down1 = together(below, above, up1, down1)
-    two = near_step(below, 1)
     line_a = stack(own, below)
     a_below, a_above = far_step(line_a, 1), far_step(line_a, -1)
     up2, down2 = up(up1), down(down1)
-    two, up2, down2, got = together(two, up2, down2, got)
+    two, got, line_a = together(two, got, line_a)
     line_b = stack(above, two)
-    line_b, a_below, a_above, up2, down2 = together(line_b, a_below, a_above, up2, down2)
     b_below, b_above = far_step(line_b, 1), far_step(line_b, -1)
+    a_below, a_above, up2, down2 = together(a_below, a_above, up2, down2)
+    a_two = far_step(a_below, 1)
     up3, down3 = up(up2), down(down2)
-    a_two = far_step(a_below, 1)
+    b_below, b_above, a_two, up3, down3 = together(b_below, b_above, a_two, up3, down3)
+    b_two = far_step(b_above, -1)
     up4 = up(up3)
-    b_below, b_above, up4 = together(b_below, b_above, up4)
-    b_two = far_step(b_above, -1)
     lefts = stack(left_env, down1, down2, down3, up4, up3, up2, up1)
     others = swap(lefts)
 
-    products = contract(lefts, others, keep, got)
-    pieces = ((0, 0), (SIDE - 1, 0), (1, 0), (0, 2), (2, 0), (SIDE - 1, 2), (1, 2), (2, 2))
-    shards = (line_a, a_below, a_above, line_b, a_two, b_below, b_above, b_two)
-    done = add(pieces, shards, products, left_sizes, right_sizes)
+    pieces = ((0, 0), (SIDE - 1, 0), (1, 0), (0, 2), (SIDE - 1, 2), (1, 2), (2, 0), (2, 2))
+    shards = (line_a, a_below, a_above, line_b, b_below, b_above, a_two, b_two)
+    done = apply(pieces, shards, (lefts, others), (keep, got), left_sizes, right_sizes)
 
     by_plane = lax.all_to_all(done, "mpo", 0, 0)
     chips = SIDE * SIDE

time: 131 us -> 131 us (level)
  waiting for transfers between devices: 24.3 us -> 40.1 us
  Pallas kernels: 22.7 us -> 15.3 us
  starting transfers between devices: 43.5 us -> 39.1 us
  blocking collectives: 36.7 us -> 33.7 us
    ppermute x6, waiting for transfers between devices: 4.41 us -> 19.9 us  [far_step(): return lax.ppermute(block, 'blk', step(True, by))]
    pallas_call x2 -> x1, Pallas kernels: 18.8 us -> 11.4 us  [apply(): pl.pallas_call(functools.partial(apply_kernel, pieces), out_shape=jax.Sha...]
    all_to_all x1, blocking collectives: 22.2 us -> 19.3 us  [local(): by_plane = lax.all_to_all(done, 'mpo', 0, 0)]
    ppermute x2, starting transfers between devices: 7.13 us -> 4.23 us  [swap(): return lax.ppermute(block, 'blk', [(i, i ^ 1) for i in range(sectors)])]
    ppermute x3, waiting for transfers between devices: 2.89 us -> 5.34 us  [near_step(): return lax.ppermute(block, 'blk', step(False, by))]
    ppermute x3, starting transfers between devices: 3.88 us -> 1.55 us  [near_step(): return lax.ppermute(block, 'blk', step(False, by))]
    ppermute x4, waiting for transfers between devices: 17 us -> 14.9 us  [up(): lax.ppermute(block, 'mpo', [(z, (z + 1) % ranks) for z in range(ranks)])]
  transfers between devices with their start and end apart: 19 -> 19, of which waited for: 7 -> 7; matrix products, arithmetic and copies ran while one was open for 0% -> 0% of each run, Pallas kernels for 9% -> 2%
where the time goes in v9:
time: 131 us; the launch traced here: 129 us
  waiting for transfers between devices  40.1 us (31%)
  starting transfers between devices  39.1 us (30%)
  blocking collectives  33.7 us (26%)
  Pallas kernels  15.3 us (12%)
    ppermute x6, waiting for transfers between devices, far_step(): return lax.ppermute(block, 'blk', step(True, by))  19.9 us
    all_to_all x1, blocking collectives, local(): by_plane = lax.all_to_all(done, 'mpo', 0, 0)  19.3 us
    ppermute x4, waiting for transfers between devices, up(): lax.ppermute(block, 'mpo', [(z, (z + 1) % ranks) for z in range(ranks)])  14.9 us
    ppermute x6, starting transfers between devices, far_step(): return lax.ppermute(block, 'blk', step(True, by))  14.6 us
    all_to_all x1, blocking collectives, local(): out = order(lax.all_to_all(by_plane, 'blk', 0, 0, axis_index_groups=groups))  14.4 us
    pallas_call x1, Pallas kernels, apply(): pl.pallas_call(functools.partial(apply_kernel, pieces), out_shape=jax.Sha...  11.4 us
    ppermute x1, starting transfers between devices, local(): own = lax.ppermute(right_env, ('blk', 'mpo'), turn)  9.63 us
    ppermute x3, starting transfers between devices, down(): lax.ppermute(block, 'mpo', [(z, (z - 1) % ranks) for z in range(ranks)])  7.7 us
  transfers between devices with their start and end apart: 19, of which 7 were waited for; matrix products, arithmetic and copies ran while one was open for 0% of the time, Pallas kernels for 2%

profile of v9, /device:TPU:1, one launch (start us, length us, event | category | flops | bytes accessed | tf_op | source)
XLA Modules:
  0.0 129.4 jit_solution(12041892619443813885)
XLA Ops:
  0.0 9.6 %collective-permute-start = (bf16[2,256,256]{2,1,0:T(8,128)(2,1)}, bf16[2,256,256]{2,1,0:T(8,128)(2,1)S(1)}, u32[]{:S(2)}, u32[]{:S(2)}) collective-permute-start(bf16[2,256,256]{2,1,0:T(8,128)(2,1)} %param.7), channel_id=1, source_target_pairs={{0,0},{1,16},{2,32},{3,48},{4,64},{5,80},{6,96},{7,112},{8,12},{9,... | collective-permute-start | bytes 786440 | tf_op jit(solution)/shard_map/ppermute | solution.py:214
  9.6 1.3 collective-permute-start.5
  10.9 2.4 %collective-permute-start.6 = (bf16[2,256,256]{2,1,0:T(8,128)(2,1)}, bf16[2,256,256]{2,1,0:T(8,128)(2,1)S(1)}, u32[]{:S(2)}, u32[]{:S(2)}) collective-permute-start(bf16[2,256,256]{2,1,0:T(8,128)(2,1)} %refs_0_.1), channel_id=1, source_target_pairs={{0,7},{1,0},{2,1},{3,2},{4,3},{5,4},{6,5},{7,6},{8,15},{9,8},{10,9... | collective-permute-start | bytes 786440 | tf_op jit(solution)/shard_map/ppermute | solution.py:204
  13.3 2.6 %shard_map.55 = (bf16[2,256,256]{2,1,0:T(8,128)(2,1)}, bf16[2,256,256]{2,1,0:T(8,128)(2,1)}) custom-call(s32[32]{0:T(128)} %left_sizes.3, s32[32]{0:T(128)} %right_sizes.3, bf16[256,8192]{1,0:T(8,128)(2,1)} %psi_ref.1), custom_call_target="tpu_custom_call" | custom-call | tf_op jit(solution)/shard_map/pallas_call | solution.py:76
  15.9 0.0 copy-start.3
  15.9 0.0 collective-permute-done.refs_0_
  16.0 0.8 collective-permute-start.4
  16.8 0.7 collective-permute-start.3
  17.5 0.0 collective-permute-start.2
  17.5 8.4 %collective-permute-done.5.refs_7_ = bf16[2,256,256]{2,1,0:T(8,128)(2,1)S(1)} collective-permute-done((bf16[2,256,256]{2,1,0:T(8,128)(2,1)}, bf16[2,256,256]{2,1,0:T(8,128)(2,1)S(1)}, u32[]{:S(2)}, u32[]{:S(2)}) %collective-permute-start.5) | collective-permute-done | bytes 262176 | tf_op jit(solution)/shard_map/ppermute | solution.py:201
  25.9 0.0 collective-permute-done.6.refs_1_
  25.9 0.0 collective-permute-done.4.refs_0_
  25.9 0.0 collective-permute-done.3.refs_1_
  25.9 0.1 shard_map.56.refs_0_
  26.0 0.0 copy-start.1
  26.0 8.9 %collective-permute-start.8 = (bf16[2,2,256,256]{3,2,1,0:T(8,128)(2,1)S(1)}, bf16[2,2,256,256]{3,2,1,0:T(8,128)(2,1)S(1)}, u32[]{:S(2)}, u32[]{:S(2)}) collective-permute-start(bf16[2,2,256,256]{3,2,1,0:T(8,128)(2,1)S(1)} %shard_map.56.refs_0_), channel_id=1, source_target_pairs={{0,192},{8,56},{16,208},{24,8},{32,224},{40,24},{48,240},{56,40},{... | collective-permute-start | bytes 1572872 | tf_op jit(solution)/shard_map/ppermute | solution.py:195
  34.9 0.0 collective-permute-start.7
  34.9 0.0 collective-permute-start.1
  34.9 0.0 collective-permute-start.9
  34.9 0.0 collective-permute-done.2.refs_11_
  34.9 2.7 %collective-permute-start.10 = (bf16[2,256,256]{2,1,0:T(8,128)(2,1)S(1)}, bf16[2,256,256]{2,1,0:T(8,128)(2,1)S(1)}, u32[]{:S(2)}, u32[]{:S(2)}) collective-permute-start(bf16[2,256,256]{2,1,0:T(8,128)(2,1)S(1)} %collective-permute-done.6.refs_1_), channel_id=1, source_target_pairs={{0,7},{1,0},{2,1},{3,2},{4,3},{5,4},{6,5},{7,6},{8,15},{9,8},{10,9... | collective-permute-start | bytes 786440 | tf_op jit(solution)/shard_map/ppermute | solution.py:204
  37.6 5.3 %collective-permute-done.1.refs_1_ = bf16[2,256,256]{2,1,0:T(8,128)(2,1)S(1)} collective-permute-done((bf16[2,256,256]{2,1,0:T(8,128)(2,1)S(1)}, bf16[2,256,256]{2,1,0:T(8,128)(2,1)S(1)}, u32[]{:S(2)}, u32[]{:S(2)}) %collective-permute-start.1) | collective-permute-done | bytes 262176 | tf_op jit(solution)/shard_map/ppermute | solution.py:192
  42.9 0.1 shard_map.57.refs_3_
  43.0 0.0 copy-start.2
  43.0 4.3 %collective-permute-start.12 = (bf16[2,2,256,256]{3,2,1,0:T(8,128)(2,1)S(1)}, bf16[2,2,256,256]{3,2,1,0:T(8,128)(2,1)S(1)}, u32[]{:S(2)}, u32[]{:S(2)}) collective-permute-start(bf16[2,2,256,256]{3,2,1,0:T(8,128)(2,1)S(1)} %shard_map.57.refs_3_), channel_id=1, source_target_pairs={{0,192},{8,56},{16,208},{24,8},{32,224},{40,24},{48,240},{56,40},{... | collective-permute-start | bytes 1572872 | tf_op jit(solution)/shard_map/ppermute | solution.py:195
  47.3 0.0 collective-permute-done.9.refs_6_
  47.3 0.0 collective-permute-start.11
  47.3 0.0 collective-permute-done.10.refs_2_
  47.3 0.0 collective-permute-done.8.refs_2_
  47.3 0.0 copy-start.4
  47.3 0.0 collective-permute-done.7.refs_1_
  47.3 0.0 copy-start.5
  47.3 0.1 collective-permute-start.13
  47.4 0.1 collective-permute-start.14
  47.5 2.7 %collective-permute-start.15 = (bf16[2,256,256]{2,1,0:T(8,128)(2,1)S(1)}, bf16[2,256,256]{2,1,0:T(8,128)(2,1)S(1)}, u32[]{:S(2)}, u32[]{:S(2)}) collective-permute-start(bf16[2,256,256]{2,1,0:T(8,128)(2,1)S(1)} %collective-permute-done.10.refs_2_), channel_id=1, source_target_pairs={{0,7},{1,0},{2,1},{3,2},{4,3},{5,4},{6,5},{7,6},{8,15},{9,8},{10,9... | collective-permute-start | bytes 786440 | tf_op jit(solution)/shard_map/ppermute | solution.py:204
  50.2 3.2 %collective-permute-done.12.refs_5_ = bf16[2,2,256,256]{3,2,1,0:T(8,128)(2,1)S(1)} collective-permute-done((bf16[2,2,256,256]{3,2,1,0:T(8,128)(2,1)S(1)}, bf16[2,2,256,256]{3,2,1,0:T(8,128)(2,1)S(1)}, u32[]{:S(2)}, u32[]{:S(2)}) %collective-permute-start.12) | collective-permute-done | bytes 524320 | tf_op jit(solution)/shard_map/ppermute | solution.py:195
  53.4 0.0 copy-start.6
  53.4 3.4 %collective-permute-done.11.refs_4_ = bf16[2,2,256,256]{3,2,1,0:T(8,128)(2,1)S(1)} collective-permute-done((bf16[2,2,256,256]{3,2,1,0:T(8,128)(2,1)S(1)}, bf16[2,2,256,256]{3,2,1,0:T(8,128)(2,1)S(1)}, u32[]{:S(2)}, u32[]{:S(2)}) %collective-permute-start.11) | collective-permute-done | bytes 524320 | tf_op jit(solution)/shard_map/ppermute | solution.py:195
  56.8 0.0 copy-start.7
  56.8 0.0 collective-permute-done.14.refs_5_
  56.8 0.0 collective-permute-done.15.refs_3_
  56.8 5.6 %collective-permute-done.13.refs_6_ = bf16[2,2,256,256]{3,2,1,0:T(8,128)(2,1)S(1)} collective-permute-done((bf16[2,2,256,256]{3,2,1,0:T(8,128)(2,1)S(1)}, bf16[2,2,256,256]{3,2,1,0:T(8,128)(2,1)S(1)}, u32[]{:S(2)}, u32[]{:S(2)}) %collective-permute-start.13) | collective-permute-done | bytes 524320 | tf_op jit(solution)/shard_map/ppermute | solution.py:195
  62.5 0.0 collective-permute-start.17
  62.5 6.4 %collective-permute-done.17.refs_4_ = bf16[2,256,256]{2,1,0:T(8,128)(2,1)S(1)} collective-permute-done((bf16[2,256,256]{2,1,0:T(8,128)(2,1)S(1)}, bf16[2,256,256]{2,1,0:T(8,128)(2,1)S(1)}, u32[]{:S(2)}, u32[]{:S(2)}) %collective-permute-start.17) | collective-permute-done | bytes 262176 | tf_op jit(solution)/shard_map/ppermute | solution.py:201
  68.9 0.0 copy-done.3
  68.9 0.2 shard_map.58.refs_8_
  69.1 0.0 copy-done.1
  69.1 0.0 copy-done.2
  69.1 0.0 copy-done.4
  69.2 0.0 copy-done.5
  69.2 0.0 copy-done.7
  69.2 0.0 copy-done.8
  69.2 0.0 copy-start
  69.2 4.2 %collective-permute-start.18 = (bf16[8,2,256,256]{3,2,1,0:T(8,128)(2,1)S(1)}, bf16[8,2,256,256]{3,2,1,0:T(8,128)(2,1)}, u32[]{:S(2)}, u32[]{:S(2)}) collective-permute-start(bf16[8,2,256,256]{3,2,1,0:T(8,128)(2,1)S(1)} %shard_map.58.refs_8_), channel_id=1, source_target_pairs={{0,8},{8,0},{16,24},{24,16},{32,40},{40,32},{48,56},{56,48},{64,72... | collective-permute-start | bytes 6291464 | tf_op jit(solution)/shard_map/ppermute | solution.py:198
  73.4 0.0 copy-done.6
  73.4 1.3 %collective-permute-start.16 = (bf16[2,2,256,256]{3,2,1,0:T(8,128)(2,1)S(1)}, bf16[2,2,256,256]{3,2,1,0:T(8,128)(2,1)S(1)}, u32[]{:S(2)}, u32[]{:S(2)}) collective-permute-start(bf16[2,2,256,256]{3,2,1,0:T(8,128)(2,1)S(1)} %collective-permute-done.12.refs_5_), channel_id=1, source_target_pairs={{0,192},{8,56},{16,208},{24,8},{32,224},{40,24},{48,240},{56,40},{... | collective-permute-start | bytes 1572872 | tf_op jit(solution)/shard_map/ppermute | solution.py:195
  74.8 7.7 %collective-permute-done.16.refs_7_ = bf16[2,2,256,256]{3,2,1,0:T(8,128)(2,1)S(1)} collective-permute-done((bf16[2,2,256,256]{3,2,1,0:T(8,128)(2,1)S(1)}, bf16[2,2,256,256]{3,2,1,0:T(8,128)(2,1)S(1)}, u32[]{:S(2)}, u32[]{:S(2)}) %collective-permute-start.16) | collective-permute-done | bytes 524320 | tf_op jit(solution)/shard_map/ppermute | solution.py:195
  82.4 0.0 collective-permute-done.18.refs_9_
  82.4 0.0 copy-done
  82.4 0.8 copy-done.9
  83.2 11.4 %shard_map.59 = bf16[8,2,2,32,256]{4,3,2,1,0:T(8,128)(2,1)} custom-call(s32[32]{0:T(128)} %left_sizes.3, s32[32]{0:T(128)} %right_sizes.3, bf16[2,2,256,256]{3,2,1,0:T(8,128)(2,1)} %copy-done.1, bf16[2,2,256,256]{3,2,1,0:T(8,128)(2,1)} %copy-done.5, bf16[2,2,256,256]{3,2,1,0:T(8,128)(2,1)} %copy-done.4, bf16[2,2,256,256]{3,2,1,0:T(8,128)(2,1)} %copy-done.2, ...), custom_call_target="tpu_custom_call" | custom-call | tf_op jit(solution)/shard_map/pallas_call | solution.py:133
  94.6 19.3 %all_to_all.10 = bf16[8,2,2,32,256]{4,3,2,1,0:T(8,128)(2,1)S(1)} all-to-all(bf16[8,2,2,32,256]{4,3,2,1,0:T(8,128)(2,1)} %shard_map.59), channel_id=1, replica_groups=mesh['blk'=32,'mpo'=8] {'mpo'}, dimensions={0} | all-to-all | bytes 1048576 | tf_op jit(solution)/shard_map/all_to_all | solution.py:241
  113.9 14.4 %all_to_all.11.in_ref = bf16[16,2,32,256]{3,2,1,0:T(8,128)(2,1)S(1)} all-to-all(bf16[16,2,32,256]{3,2,1,0:T(8,128)(2,1)S(1)} %bitcast.2), channel_id=1, replica_groups={{0,128,16,144,32,160,48,176,64,192,80,208,96,224,112,240},{72,200,88,21..., dimensions={0} | all-to-all | bytes 1048576 | tf_op jit(solution)/shard_map/all_to_all | solution.py:248
  128.3 0.9 shard_map.60
  (2 shorter events, 0.0 us)
Async XLA Ops:
  0.0 15.9 %collective-permute-start = (bf16[2,256,256]{2,1,0:T(8,128)(2,1)}, bf16[2,256,256]{2,1,0:T(8,128)(2,1)S(1)}, u32[]{:S(2)}, u32[]{:S(2)}) collective-permute-start(bf16[2,256,256]{2,1,0:T(8,128)(2,1)} %param.7), channel_id=1, source_target_pairs={{0,0},{1,16},{2,32},{3,48},{4,64},{5,80},{6,96},{7,112},{8,12},{9,... | collective-permute-start | bytes 786440 | tf_op jit(solution)/shard_map/ppermute | solution.py:214
  9.6 16.3 %collective-permute-start.5 = (bf16[2,256,256]{2,1,0:T(8,128)(2,1)}, bf16[2,256,256]{2,1,0:T(8,128)(2,1)S(1)}, u32[]{:S(2)}, u32[]{:S(2)}) collective-permute-start(bf16[2,256,256]{2,1,0:T(8,128)(2,1)} %refs_0_.1), channel_id=1, source_target_pairs={{0,1},{1,2},{2,3},{3,4},{4,5},{5,6},{6,7},{7,0},{8,9},{9,10},{10,1... | collective-permute-start | bytes 786440 | tf_op jit(solution)/shard_map/ppermute | solution.py:201
  10.9 15.0 %collective-permute-start.6 = (bf16[2,256,256]{2,1,0:T(8,128)(2,1)}, bf16[2,256,256]{2,1,0:T(8,128)(2,1)S(1)}, u32[]{:S(2)}, u32[]{:S(2)}) collective-permute-start(bf16[2,256,256]{2,1,0:T(8,128)(2,1)} %refs_0_.1), channel_id=1, source_target_pairs={{0,7},{1,0},{2,1},{3,2},{4,3},{5,4},{6,5},{7,6},{8,15},{9,8},{10,9... | collective-permute-start | bytes 786440 | tf_op jit(solution)/shard_map/ppermute | solution.py:204
  15.9 53.0 %copy-start.3 = (bf16[2,256,256]{2,1,0:T(8,128)(2,1)S(1)}, bf16[2,256,256]{2,1,0:T(8,128)(2,1)}, u32[]{:S(2)}) copy-start(bf16[2,256,256]{2,1,0:T(8,128)(2,1)} %refs_0_.1) | copy-start | bytes 786436
  16.0 10.0 %collective-permute-start.4 = (bf16[2,256,256]{2,1,0:T(8,128)(2,1)S(1)}, bf16[2,256,256]{2,1,0:T(8,128)(2,1)S(1)}, u32[]{:S(2)}, u32[]{:S(2)}) collective-permute-start(bf16[2,256,256]{2,1,0:T(8,128)(2,1)S(1)} %collective-permute-done.refs_0_), channel_id=1, source_target_pairs={{0,48},{8,200},{16,0},{24,216},{32,16},{40,232},{48,32},{56,248},{... | collective-permute-start | bytes 786440 | tf_op jit(solution)/shard_map/ppermute | solution.py:192
  16.8 9.2 %collective-permute-start.3 = (bf16[2,256,256]{2,1,0:T(8,128)(2,1)S(1)}, bf16[2,256,256]{2,1,0:T(8,128)(2,1)S(1)}, u32[]{:S(2)}, u32[]{:S(2)}) collective-permute-start(bf16[2,256,256]{2,1,0:T(8,128)(2,1)S(1)} %collective-permute-done.refs_0_), channel_id=1, source_target_pairs={{0,16},{8,72},{16,32},{24,88},{32,48},{40,104},{48,0},{56,120},{64... | collective-permute-start | bytes 786440 | tf_op jit(solution)/shard_map/ppermute | solution.py:192
  17.5 17.4 %collective-permute-start.2 = (bf16[2,256,256]{2,1,0:T(8,128)(2,1)}, bf16[2,256,256]{2,1,0:T(8,128)(2,1)}, u32[]{:S(2)}, u32[]{:S(2)}) collective-permute-start(bf16[2,256,256]{2,1,0:T(8,128)(2,1)} %get-tuple-element.29), channel_id=1, source_target_pairs={{0,8},{8,0},{16,24},{24,16},{32,40},{40,32},{48,56},{56,48},{64,72... | collective-permute-start | bytes 786440 | tf_op jit(solution)/shard_map/ppermute | solution.py:198
  26.0 43.1 %copy-start.1 = (bf16[2,2,256,256]{3,2,1,0:T(8,128)(2,1)}, bf16[2,2,256,256]{3,2,1,0:T(8,128)(2,1)S(1)}, u32[]{:S(2)}) copy-start(bf16[2,2,256,256]{3,2,1,0:T(8,128)(2,1)S(1)} %shard_map.56.refs_0_) | copy-start | bytes 1572868
  26.0 21.3 %collective-permute-start.8 = (bf16[2,2,256,256]{3,2,1,0:T(8,128)(2,1)S(1)}, bf16[2,2,256,256]{3,2,1,0:T(8,128)(2,1)S(1)}, u32[]{:S(2)}, u32[]{:S(2)}) collective-permute-start(bf16[2,2,256,256]{3,2,1,0:T(8,128)(2,1)S(1)} %shard_map.56.refs_0_), channel_id=1, source_target_pairs={{0,192},{8,56},{16,208},{24,8},{32,224},{40,24},{48,240},{56,40},{... | collective-permute-start | bytes 1572872 | tf_op jit(solution)/shard_map/ppermute | solution.py:195
  34.9 12.4 %collective-permute-start.7 = (bf16[2,2,256,256]{3,2,1,0:T(8,128)(2,1)S(1)}, bf16[2,2,256,256]{3,2,1,0:T(8,128)(2,1)S(1)}, u32[]{:S(2)}, u32[]{:S(2)}) collective-permute-start(bf16[2,2,256,256]{3,2,1,0:T(8,128)(2,1)S(1)} %shard_map.56.refs_0_), channel_id=1, source_target_pairs={{0,64},{8,24},{16,80},{24,40},{32,96},{40,56},{48,112},{56,8},{64,... | collective-permute-start | bytes 1572872 | tf_op jit(solution)/shard_map/ppermute | solution.py:195
  34.9 8.0 %collective-permute-start.1 = (bf16[2,256,256]{2,1,0:T(8,128)(2,1)S(1)}, bf16[2,256,256]{2,1,0:T(8,128)(2,1)S(1)}, u32[]{:S(2)}, u32[]{:S(2)}) collective-permute-start(bf16[2,256,256]{2,1,0:T(8,128)(2,1)S(1)} %collective-permute-done.refs_0_), channel_id=1, source_target_pairs={{0,32},{8,136},{16,48},{24,152},{32,0},{40,168},{48,16},{56,184},{... | collective-permute-start | bytes 786440 | tf_op jit(solution)/shard_map/ppermute | solution.py:192
  34.9 12.4 %collective-permute-start.9 = (bf16[2,256,256]{2,1,0:T(8,128)(2,1)S(1)}, bf16[2,256,256]{2,1,0:T(8,128)(2,1)S(1)}, u32[]{:S(2)}, u32[]{:S(2)}) collective-permute-start(bf16[2,256,256]{2,1,0:T(8,128)(2,1)S(1)} %collective-permute-done.5.refs_7_), channel_id=1, source_target_pairs={{0,1},{1,2},{2,3},{3,4},{4,5},{5,6},{6,7},{7,0},{8,9},{9,10},{10,1... | collective-permute-start | bytes 786440 | tf_op jit(solution)/shard_map/ppermute | solution.py:201
  34.9 12.4 %collective-permute-start.10 = (bf16[2,256,256]{2,1,0:T(8,128)(2,1)S(1)}, bf16[2,256,256]{2,1,0:T(8,128)(2,1)S(1)}, u32[]{:S(2)}, u32[]{:S(2)}) collective-permute-start(bf16[2,256,256]{2,1,0:T(8,128)(2,1)S(1)} %collective-permute-done.6.refs_1_), channel_id=1, source_target_pairs={{0,7},{1,0},{2,1},{3,2},{4,3},{5,4},{6,5},{7,6},{8,15},{9,8},{10,9... | collective-permute-start | bytes 786440 | tf_op jit(solution)/shard_map/ppermute | solution.py:204
  43.0 26.1 %copy-start.2 = (bf16[2,2,256,256]{3,2,1,0:T(8,128)(2,1)}, bf16[2,2,256,256]{3,2,1,0:T(8,128)(2,1)S(1)}, u32[]{:S(2)}) copy-start(bf16[2,2,256,256]{3,2,1,0:T(8,128)(2,1)S(1)} %shard_map.57.refs_3_) | copy-start | bytes 1572868
  43.0 10.4 %collective-permute-start.12 = (bf16[2,2,256,256]{3,2,1,0:T(8,128)(2,1)S(1)}, bf16[2,2,256,256]{3,2,1,0:T(8,128)(2,1)S(1)}, u32[]{:S(2)}, u32[]{:S(2)}) collective-permute-start(bf16[2,2,256,256]{3,2,1,0:T(8,128)(2,1)S(1)} %shard_map.57.refs_3_), channel_id=1, source_target_pairs={{0,192},{8,56},{16,208},{24,8},{32,224},{40,24},{48,240},{56,40},{... | collective-permute-start | bytes 1572872 | tf_op jit(solution)/shard_map/ppermute | solution.py:195
  47.3 9.5 %collective-permute-start.11 = (bf16[2,2,256,256]{3,2,1,0:T(8,128)(2,1)S(1)}, bf16[2,2,256,256]{3,2,1,0:T(8,128)(2,1)S(1)}, u32[]{:S(2)}, u32[]{:S(2)}) collective-permute-start(bf16[2,2,256,256]{3,2,1,0:T(8,128)(2,1)S(1)} %shard_map.57.refs_3_), channel_id=1, source_target_pairs={{0,64},{8,24},{16,80},{24,40},{32,96},{40,56},{48,112},{56,8},{64,... | collective-permute-start | bytes 1572872 | tf_op jit(solution)/shard_map/ppermute | solution.py:195
  47.3 21.8 %copy-start.4 = (bf16[2,2,256,256]{3,2,1,0:T(8,128)(2,1)}, bf16[2,2,256,256]{3,2,1,0:T(8,128)(2,1)S(1)}, u32[]{:S(2)}) copy-start(bf16[2,2,256,256]{3,2,1,0:T(8,128)(2,1)S(1)} %collective-permute-done.8.refs_2_) | copy-start | bytes 1572868
  47.3 21.8 %copy-start.5 = (bf16[2,2,256,256]{3,2,1,0:T(8,128)(2,1)}, bf16[2,2,256,256]{3,2,1,0:T(8,128)(2,1)S(1)}, u32[]{:S(2)}) copy-start(bf16[2,2,256,256]{3,2,1,0:T(8,128)(2,1)S(1)} %collective-permute-done.7.refs_1_) | copy-start | bytes 1572868
  47.3 15.1 %collective-permute-start.13 = (bf16[2,2,256,256]{3,2,1,0:T(8,128)(2,1)S(1)}, bf16[2,2,256,256]{3,2,1,0:T(8,128)(2,1)S(1)}, u32[]{:S(2)}, u32[]{:S(2)}) collective-permute-start(bf16[2,2,256,256]{3,2,1,0:T(8,128)(2,1)S(1)} %collective-permute-done.7.refs_1_), channel_id=1, source_target_pairs={{0,64},{8,24},{16,80},{24,40},{32,96},{40,56},{48,112},{56,8},{64,... | collective-permute-start | bytes 1572872 | tf_op jit(solution)/shard_map/ppermute | solution.py:195
  47.4 9.4 %collective-permute-start.14 = (bf16[2,256,256]{2,1,0:T(8,128)(2,1)S(1)}, bf16[2,256,256]{2,1,0:T(8,128)(2,1)S(1)}, u32[]{:S(2)}, u32[]{:S(2)}) collective-permute-start(bf16[2,256,256]{2,1,0:T(8,128)(2,1)S(1)} %collective-permute-done.9.refs_6_), channel_id=1, source_target_pairs={{0,1},{1,2},{2,3},{3,4},{4,5},{5,6},{6,7},{7,0},{8,9},{9,10},{10,1... | collective-permute-start | bytes 786440 | tf_op jit(solution)/shard_map/ppermute | solution.py:201
  47.5 9.3 %collective-permute-start.15 = (bf16[2,256,256]{2,1,0:T(8,128)(2,1)S(1)}, bf16[2,256,256]{2,1,0:T(8,128)(2,1)S(1)}, u32[]{:S(2)}, u32[]{:S(2)}) collective-permute-start(bf16[2,256,256]{2,1,0:T(8,128)(2,1)S(1)} %collective-permute-done.10.refs_2_), channel_id=1, source_target_pairs={{0,7},{1,0},{2,1},{3,2},{4,3},{5,4},{6,5},{7,6},{8,15},{9,8},{10,9... | collective-permute-start | bytes 786440 | tf_op jit(solution)/shard_map/ppermute | solution.py:204
  53.4 20.0 %copy-start.6 = (bf16[2,2,256,256]{3,2,1,0:T(8,128)(2,1)}, bf16[2,2,256,256]{3,2,1,0:T(8,128)(2,1)S(1)}, u32[]{:S(2)}) copy-start(bf16[2,2,256,256]{3,2,1,0:T(8,128)(2,1)S(1)} %collective-permute-done.12.refs_5_) | copy-start | bytes 1572868
  56.8 12.3 %copy-start.7 = (bf16[2,2,256,256]{3,2,1,0:T(8,128)(2,1)}, bf16[2,2,256,256]{3,2,1,0:T(8,128)(2,1)S(1)}, u32[]{:S(2)}) copy-start(bf16[2,2,256,256]{3,2,1,0:T(8,128)(2,1)S(1)} %collective-permute-done.11.refs_4_) | copy-start | bytes 1572868
  62.5 6.7 %copy-start.8 = (bf16[2,2,256,256]{3,2,1,0:T(8,128)(2,1)}, bf16[2,2,256,256]{3,2,1,0:T(8,128)(2,1)S(1)}, u32[]{:S(2)}) copy-start(bf16[2,2,256,256]{3,2,1,0:T(8,128)(2,1)S(1)} %collective-permute-done.13.refs_6_) | copy-start | bytes 1572868
  62.5 6.4 %collective-permute-start.17 = (bf16[2,256,256]{2,1,0:T(8,128)(2,1)S(1)}, bf16[2,256,256]{2,1,0:T(8,128)(2,1)S(1)}, u32[]{:S(2)}, u32[]{:S(2)}) collective-permute-start(bf16[2,256,256]{2,1,0:T(8,128)(2,1)S(1)} %collective-permute-done.14.refs_5_), channel_id=1, source_target_pairs={{0,1},{1,2},{2,3},{3,4},{4,5},{5,6},{6,7},{7,0},{8,9},{9,10},{10,1... | collective-permute-start | bytes 786440 | tf_op jit(solution)/shard_map/ppermute | solution.py:201
  69.2 13.3 %copy-start = (bf16[8,2,256,256]{3,2,1,0:T(8,128)(2,1)}, bf16[8,2,256,256]{3,2,1,0:T(8,128)(2,1)S(1)}, u32[]{:S(2)}) copy-start(bf16[8,2,256,256]{3,2,1,0:T(8,128)(2,1)S(1)} %shard_map.58.refs_8_) | copy-start | bytes 6291460
  69.2 13.2 %collective-permute-start.18 = (bf16[8,2,256,256]{3,2,1,0:T(8,128)(2,1)S(1)}, bf16[8,2,256,256]{3,2,1,0:T(8,128)(2,1)}, u32[]{:S(2)}, u32[]{:S(2)}) collective-permute-start(bf16[8,2,256,256]{3,2,1,0:T(8,128)(2,1)S(1)} %shard_map.58.refs_8_), channel_id=1, source_target_pairs={{0,8},{8,0},{16,24},{24,16},{32,40},{40,32},{48,56},{56,48},{64,72... | collective-permute-start | bytes 6291464 | tf_op jit(solution)/shard_map/ppermute | solution.py:198
  73.4 9.0 %collective-permute-start.16 = (bf16[2,2,256,256]{3,2,1,0:T(8,128)(2,1)S(1)}, bf16[2,2,256,256]{3,2,1,0:T(8,128)(2,1)S(1)}, u32[]{:S(2)}, u32[]{:S(2)}) collective-permute-start(bf16[2,2,256,256]{3,2,1,0:T(8,128)(2,1)S(1)} %collective-permute-done.12.refs_5_), channel_id=1, source_target_pairs={{0,192},{8,56},{16,208},{24,8},{32,224},{40,24},{48,240},{56,40},{... | collective-permute-start | bytes 1572872 | tf_op jit(solution)/shard_map/ppermute | solution.py:195
  82.4 0.8 copy-start.9

commit v10 on v9

--- a/solution.py
+++ b/solution.py
@@ -85,12 +85,21 @@
 
 def apply_kernel(pieces, left_sizes, right_sizes, *refs):
     ins, (out_ref, total, held, left_held, psi_held, middle, sems) = refs[:-7], refs[-7:]
-    shards, lefts, psis = ins[: len(pieces)], ins[len(pieces) : -2], ins[-2:]
+    shards, (own, other, psi) = ins[: len(pieces)], ins[len(pieces) :]
     sector, rank, core, x0, y0 = coordinates()
     ranks, _, _, rows, right_dim = out_ref.shape
     left_dim = ranks * rows
-    first = [pltpu.make_async_copy(psis[a], psi_held.at[a], sems.at[a]) for a in range(2)]
-    first += [pltpu.make_async_copy(lefts[a], left_held.at[a], sems.at[2 + a]) for a in range(2)]
+    first = [
+        pltpu.make_async_copy(source, place_in, sems.at[i])
+        for i, (source, place_in) in enumerate(
+            (
+                (psi, psi_held.at[0]),
+                (other.at[ranks], psi_held.at[1]),
+                (own.at[pl.ds(0, ranks)], left_held.at[0]),
+                (other.at[pl.ds(0, ranks)], left_held.at[1]),
+            )
+        )
+    ]
     coming = [pltpu.make_async_copy(r, held.at[i], sems.at[4 + i]) for i, r in enumerate(shards)]
     for copy in first + coming:
         copy.start()
@@ -125,11 +134,11 @@
             out_ref[:, b, pl.ds(spot, 1)] = block
 
 
-def apply(pieces, shards, lefts, psis, left_sizes, right_sizes):
-    dtype = psis[0].dtype
-    ranks, pair, left_dim, _ = lefts[0].shape
-    right_dim = psis[0].shape[2]
-    others = (*shards, *lefts, *psis)
+def apply(pieces, shards, own, other, psi, left_sizes, right_sizes):
+    dtype = psi.dtype
+    slots, pair, left_dim, _ = own.shape
+    ranks, right_dim = slots - 1, psi.shape[2]
+    others = (*shards, own, other, psi)
     return pl.pallas_call(
         functools.partial(apply_kernel, pieces),
         out_shape=jax.ShapeDtypeStruct((ranks, 2, 2, left_dim // ranks, right_dim), dtype),
@@ -138,8 +147,8 @@
         scratch_shapes=[
             pltpu.VMEM((2, 2 * left_dim, right_dim), jnp.float32),
             pltpu.VMEM((len(shards), *shards[0].shape), dtype),
-            pltpu.VMEM((2, *lefts[0].shape), dtype),
-            pltpu.VMEM((2, *psis[0].shape), dtype),
+            pltpu.VMEM((2, ranks, *own.shape[1:]), dtype),
+            pltpu.VMEM((2, *psi.shape), dtype),
             pltpu.VMEM((2, 2 * left_dim, pair * right_dim), dtype),
             pltpu.SemaphoreType.DMA((len(shards) + 4,)),
         ],
@@ -217,26 +226,24 @@
     own, keep, give = together(own, keep, give)
 
     below, above, two = near_step(own, 1), near_step(own, -1), near_step(own, 2)
-    got = swap(give)
-    below, above, up1, down1 = together(below, above, up1, down1)
-    line_a = stack(own, below)
+    below, above, two, up1, down1 = together(below, above, two, up1, down1)
+    line_a, line_b = stack(own, below), stack(above, two)
     a_below, a_above = far_step(line_a, 1), far_step(line_a, -1)
+    b_below, b_above = far_step(line_b, 1), far_step(line_b, -1)
     up2, down2 = up(up1), down(down1)
-    two, got, line_a = together(two, got, line_a)
-    line_b = stack(above, two)
-    b_below, b_above = far_step(line_b, 1), far_step(line_b, -1)
-    a_below, a_above, up2, down2 = together(a_below, a_above, up2, down2)
-    a_two = far_step(a_below, 1)
     up3, down3 = up(up2), down(down2)
-    b_below, b_above, a_two, up3, down3 = together(b_below, b_above, a_two, up3, down3)
-    b_two = far_step(b_above, -1)
+    a_below, a_above, b_below, b_above, up3, down3 = together(
+        a_below, a_above, b_below, b_above, up3, down3
+    )
+    a_two, b_two = far_step(a_below, 1), far_step(b_above, -1)
     up4 = up(up3)
-    lefts = stack(left_env, down1, down2, down3, up4, up3, up2, up1)
+    lefts = stack(left_env, down1, down2, down3, up4, up3, up2, up1, give)
+    lefts, a_two, b_two = together(lefts, a_two, b_two)
     others = swap(lefts)
 
     pieces = ((0, 0), (SIDE - 1, 0), (1, 0), (0, 2), (SIDE - 1, 2), (1, 2), (2, 0), (2, 2))
     shards = (line_a, a_below, a_above, line_b, b_below, b_above, a_two, b_two)
-    done = apply(pieces, shards, (lefts, others), (keep, got), left_sizes, right_sizes)
+    done = apply(pieces, shards, lefts, others, keep, left_sizes, right_sizes)
 
     by_plane = lax.all_to_all(done, "mpo", 0, 0)
     chips = SIDE * SIDE

time: 131 us -> 130 us (level)
  waiting for transfers between devices: 40.1 us -> 27.1 us
  starting transfers between devices: 39.1 us -> 50 us
  local copies, waits for them, and re-layouts: 0.83 us -> 2.79 us
    ppermute x6, waiting for transfers between devices: 19.9 us -> 2.34 us  [far_step(): return lax.ppermute(block, 'blk', step(True, by))]
    ppermute x2 -> x1, starting transfers between devices: 4.23 us -> 10.2 us  [swap(): return lax.ppermute(block, 'blk', [(i, i ^ 1) for i in range(sectors)])]
    ppermute x3, waiting for transfers between devices: 5.34 us -> 0.01 us  [near_step(): return lax.ppermute(block, 'blk', step(False, by))]
    ppermute x4, starting transfers between devices: 1.38 us -> 6.42 us  [up(): lax.ppermute(block, 'mpo', [(z, (z + 1) % ranks) for z in range(ranks)])]
    ppermute x6, starting transfers between devices: 14.6 us -> 9.57 us  [far_step(): return lax.ppermute(block, 'blk', step(True, by))]
    ppermute x2 -> x1, waiting for transfers between devices: 0.01 us -> 4.29 us  [swap(): return lax.ppermute(block, 'blk', [(i, i ^ 1) for i in range(sectors)])]
    ppermute x3, waiting for transfers between devices: 0.01 us -> 3.85 us  [down(): lax.ppermute(block, 'mpo', [(z, (z - 1) % ranks) for z in range(ranks)])]
    ppermute x3, starting transfers between devices: 1.55 us -> 4.17 us  [near_step(): return lax.ppermute(block, 'blk', step(False, by))]
  transfers between devices with their start and end apart: 19 -> 18, of which waited for: 7 -> 7; matrix products, arithmetic and copies ran while one was open for 0% -> 0% of each run, Pallas kernels for 2% -> 2%
where the time goes in v10:
time: 130 us; the launch traced here: 129 us
  starting transfers between devices  50 us (38%)
  blocking collectives  33 us (25%)
  waiting for transfers between devices  27.1 us (21%)
  Pallas kernels  15.3 us (12%)
  local copies, waits for them, and re-layouts  2.79 us (2%)
    all_to_all x1, blocking collectives, local(): by_plane = lax.all_to_all(done, 'mpo', 0, 0)  20.1 us
    ppermute x4, waiting for transfers between devices, up(): lax.ppermute(block, 'mpo', [(z, (z + 1) % ranks) for z in range(ranks)])  16.6 us
    all_to_all x1, blocking collectives, local(): out = order(lax.all_to_all(by_plane, 'blk', 0, 0, axis_index_groups=groups))  12.9 us
    pallas_call x1, Pallas kernels, apply(): pl.pallas_call(functools.partial(apply_kernel, pieces), out_shape=jax.Sha...  11.4 us
    ppermute x1, starting transfers between devices, swap(): return lax.ppermute(block, 'blk', [(i, i ^ 1) for i in range(sectors)])  10.2 us
    ppermute x3, starting transfers between devices, down(): lax.ppermute(block, 'mpo', [(z, (z - 1) % ranks) for z in range(ranks)])  9.93 us
    ppermute x1, starting transfers between devices, local(): own = lax.ppermute(right_env, ('blk', 'mpo'), turn)  9.77 us
    ppermute x6, starting transfers between devices, far_step(): return lax.ppermute(block, 'blk', step(True, by))  9.57 us
  transfers between devices with their start and end apart: 18, of which 7 were waited for; matrix products, arithmetic and copies ran while one was open for 0% of the time, Pallas kernels for 2%

profile of v10, /device:TPU:1, one launch (start us, length us, event | category | flops | bytes accessed | tf_op | source)
XLA Modules:
  0.0 128.6 jit_solution(6573132300837194942)
XLA Ops:
  0.0 0.0 copy-start.3
  0.0 9.8 %collective-permute-start = (bf16[2,256,256]{2,1,0:T(8,128)(2,1)}, bf16[2,256,256]{2,1,0:T(8,128)(2,1)S(1)}, u32[]{:S(2)}, u32[]{:S(2)}) collective-permute-start(bf16[2,256,256]{2,1,0:T(8,128)(2,1)} %param.7), channel_id=1, source_target_pairs={{0,0},{1,16},{2,32},{3,48},{4,64},{5,80},{6,96},{7,112},{8,12},{9,... | collective-permute-start | bytes 786440 | tf_op jit(solution)/shard_map/ppermute | solution.py:223
  9.8 1.3 %collective-permute-start.4 = (bf16[2,256,256]{2,1,0:T(8,128)(2,1)}, bf16[2,256,256]{2,1,0:T(8,128)(2,1)S(1)}, u32[]{:S(2)}, u32[]{:S(2)}) collective-permute-start(bf16[2,256,256]{2,1,0:T(8,128)(2,1)} %refs_0_.1), channel_id=1, source_target_pairs={{0,1},{1,2},{2,3},{3,4},{4,5},{5,6},{6,7},{7,0},{8,9},{9,10},{10,1... | collective-permute-start | bytes 786440 | tf_op jit(solution)/shard_map/ppermute | solution.py:210
  11.1 2.4 %collective-permute-start.5 = (bf16[2,256,256]{2,1,0:T(8,128)(2,1)}, bf16[2,256,256]{2,1,0:T(8,128)(2,1)S(1)}, u32[]{:S(2)}, u32[]{:S(2)}) collective-permute-start(bf16[2,256,256]{2,1,0:T(8,128)(2,1)} %refs_0_.1), channel_id=1, source_target_pairs={{0,7},{1,0},{2,1},{3,2},{4,3},{5,4},{6,5},{7,6},{8,15},{9,8},{10,9... | collective-permute-start | bytes 786440 | tf_op jit(solution)/shard_map/ppermute | solution.py:213
  13.4 2.6 %shard_map.55 = (bf16[2,256,256]{2,1,0:T(8,128)(2,1)}, bf16[2,256,256]{2,1,0:T(8,128)(2,1)}) custom-call(s32[32]{0:T(128)} %left_sizes.3, s32[32]{0:T(128)} %right_sizes.3, bf16[256,8192]{1,0:T(8,128)(2,1)} %psi_ref.1), custom_call_target="tpu_custom_call" | custom-call | tf_op jit(solution)/shard_map/pallas_call | solution.py:76
  16.1 0.0 collective-permute-done.refs_0_
  16.1 2.7 %collective-permute-start.3 = (bf16[2,256,256]{2,1,0:T(8,128)(2,1)S(1)}, bf16[2,256,256]{2,1,0:T(8,128)(2,1)S(1)}, u32[]{:S(2)}, u32[]{:S(2)}) collective-permute-start(bf16[2,256,256]{2,1,0:T(8,128)(2,1)S(1)} %collective-permute-done.refs_0_), channel_id=1, source_target_pairs={{0,32},{8,136},{16,48},{24,152},{32,0},{40,168},{48,16},{56,184},{... | collective-permute-start | bytes 786440 | tf_op jit(solution)/shard_map/ppermute | solution.py:201
  18.8 0.0 collective-permute-start.2
  18.8 1.5 %collective-permute-start.1 = (bf16[2,256,256]{2,1,0:T(8,128)(2,1)S(1)}, bf16[2,256,256]{2,1,0:T(8,128)(2,1)S(1)}, u32[]{:S(2)}, u32[]{:S(2)}) collective-permute-start(bf16[2,256,256]{2,1,0:T(8,128)(2,1)S(1)} %collective-permute-done.refs_0_), channel_id=1, source_target_pairs={{0,16},{8,72},{16,32},{24,88},{32,48},{40,104},{48,0},{56,120},{64... | collective-permute-start | bytes 786440 | tf_op jit(solution)/shard_map/ppermute | solution.py:201
  20.2 5.8 %collective-permute-done.4.refs_7_ = bf16[2,256,256]{2,1,0:T(8,128)(2,1)S(1)} collective-permute-done((bf16[2,256,256]{2,1,0:T(8,128)(2,1)}, bf16[2,256,256]{2,1,0:T(8,128)(2,1)S(1)}, u32[]{:S(2)}, u32[]{:S(2)}) %collective-permute-start.4) | collective-permute-done | bytes 262176 | tf_op jit(solution)/shard_map/ppermute | solution.py:210
  26.1 0.0 collective-permute-done.5.refs_1_
  26.1 0.0 collective-permute-done.3.refs_1_
  26.1 0.0 collective-permute-done.2.refs_0_
  26.1 0.0 collective-permute-done.1.refs_1_
  26.1 4.0 %collective-permute-start.10 = (bf16[2,256,256]{2,1,0:T(8,128)(2,1)S(1)}, bf16[2,256,256]{2,1,0:T(8,128)(2,1)S(1)}, u32[]{:S(2)}, u32[]{:S(2)}) collective-permute-start(bf16[2,256,256]{2,1,0:T(8,128)(2,1)S(1)} %collective-permute-done.4.refs_7_), channel_id=1, source_target_pairs={{0,1},{1,2},{2,3},{3,4},{4,5},{5,6},{6,7},{7,0},{8,9},{9,10},{10,1... | collective-permute-start | bytes 786440 | tf_op jit(solution)/shard_map/ppermute | solution.py:210
  30.1 5.9 %collective-permute-start.12 = (bf16[2,256,256]{2,1,0:T(8,128)(2,1)S(1)}, bf16[2,256,256]{2,1,0:T(8,128)(2,1)S(1)}, u32[]{:S(2)}, u32[]{:S(2)}) collective-permute-start(bf16[2,256,256]{2,1,0:T(8,128)(2,1)S(1)} %collective-permute-done.5.refs_1_), channel_id=1, source_target_pairs={{0,7},{1,0},{2,1},{3,2},{4,3},{5,4},{6,5},{7,6},{8,15},{9,8},{10,9... | collective-permute-start | bytes 786440 | tf_op jit(solution)/shard_map/ppermute | solution.py:213
  36.0 0.1 shard_map.57.refs_3_
  36.1 0.0 copy-start.1
  36.1 2.6 %collective-permute-start.9 = (bf16[2,2,256,256]{3,2,1,0:T(8,128)(2,1)S(1)}, bf16[2,2,256,256]{3,2,1,0:T(8,128)(2,1)S(1)}, u32[]{:S(2)}, u32[]{:S(2)}) collective-permute-start(bf16[2,2,256,256]{3,2,1,0:T(8,128)(2,1)S(1)} %shard_map.57.refs_3_), channel_id=1, source_target_pairs={{0,192},{8,56},{16,208},{24,8},{32,224},{40,24},{48,240},{56,40},{... | collective-permute-start | bytes 1572872 | tf_op jit(solution)/shard_map/ppermute | solution.py:204
  38.7 1.1 collective-permute-done.10.refs_6_
  39.7 0.0 collective-permute-start.11
  39.7 1.5 %collective-permute-start.8 = (bf16[2,2,256,256]{3,2,1,0:T(8,128)(2,1)S(1)}, bf16[2,2,256,256]{3,2,1,0:T(8,128)(2,1)S(1)}, u32[]{:S(2)}, u32[]{:S(2)}) collective-permute-start(bf16[2,2,256,256]{3,2,1,0:T(8,128)(2,1)S(1)} %shard_map.57.refs_3_), channel_id=1, source_target_pairs={{0,64},{8,24},{16,80},{24,40},{32,96},{40,56},{48,112},{56,8},{64,... | collective-permute-start | bytes 1572872 | tf_op jit(solution)/shard_map/ppermute | solution.py:204
  41.3 0.1 shard_map.56.refs_0_
  41.3 0.0 copy-start.2
  41.4 2.8 %collective-permute-start.7 = (bf16[2,2,256,256]{3,2,1,0:T(8,128)(2,1)S(1)}, bf16[2,2,256,256]{3,2,1,0:T(8,128)(2,1)S(1)}, u32[]{:S(2)}, u32[]{:S(2)}) collective-permute-start(bf16[2,2,256,256]{3,2,1,0:T(8,128)(2,1)S(1)} %shard_map.56.refs_0_), channel_id=1, source_target_pairs={{0,192},{8,56},{16,208},{24,8},{32,224},{40,24},{48,240},{56,40},{... | collective-permute-start | bytes 1572872 | tf_op jit(solution)/shard_map/ppermute | solution.py:204
  44.1 0.0 collective-permute-done.12.refs_2_
  44.1 0.0 collective-permute-start.6
  44.1 4.4 %collective-permute-done.11.refs_5_ = bf16[2,256,256]{2,1,0:T(8,128)(2,1)S(1)} collective-permute-done((bf16[2,256,256]{2,1,0:T(8,128)(2,1)S(1)}, bf16[2,256,256]{2,1,0:T(8,128)(2,1)S(1)}, u32[]{:S(2)}, u32[]{:S(2)}) %collective-permute-start.11) | collective-permute-done | bytes 262176 | tf_op jit(solution)/shard_map/ppermute | solution.py:210
  48.6 1.7 %collective-permute-start.13 = (bf16[2,256,256]{2,1,0:T(8,128)(2,1)S(1)}, bf16[2,256,256]{2,1,0:T(8,128)(2,1)S(1)}, u32[]{:S(2)}, u32[]{:S(2)}) collective-permute-start(bf16[2,256,256]{2,1,0:T(8,128)(2,1)S(1)} %collective-permute-done.12.refs_2_), channel_id=1, source_target_pairs={{0,7},{1,0},{2,1},{3,2},{4,3},{5,4},{6,5},{7,6},{8,15},{9,8},{10,9... | collective-permute-start | bytes 786440 | tf_op jit(solution)/shard_map/ppermute | solution.py:213
  50.2 3.8 %collective-permute-done.13.refs_3_ = bf16[2,256,256]{2,1,0:T(8,128)(2,1)S(1)} collective-permute-done((bf16[2,256,256]{2,1,0:T(8,128)(2,1)S(1)}, bf16[2,256,256]{2,1,0:T(8,128)(2,1)S(1)}, u32[]{:S(2)}, u32[]{:S(2)}) %collective-permute-start.13) | collective-permute-done | bytes 262176 | tf_op jit(solution)/shard_map/ppermute | solution.py:213
  54.1 0.0 collective-permute-done.9.refs_5_
  54.1 0.0 collective-permute-done.8.refs_4_
  54.1 0.0 copy-start.8
  54.1 0.0 collective-permute-done.7.refs_2_
  54.1 0.0 copy-start.9
  54.1 2.3 %collective-permute-done.6.refs_1_ = bf16[2,2,256,256]{3,2,1,0:T(8,128)(2,1)S(1)} collective-permute-done((bf16[2,2,256,256]{3,2,1,0:T(8,128)(2,1)S(1)}, bf16[2,2,256,256]{3,2,1,0:T(8,128)(2,1)S(1)}, u32[]{:S(2)}, u32[]{:S(2)}) %collective-permute-start.6) | collective-permute-done | bytes 524320 | tf_op jit(solution)/shard_map/ppermute | solution.py:204
  56.4 0.0 collective-permute-start.15
  56.4 2.7 %collective-permute-start.16 = (bf16[2,2,256,256]{3,2,1,0:T(8,128)(2,1)S(1)}, bf16[2,2,256,256]{3,2,1,0:T(8,128)(2,1)S(1)}, u32[]{:S(2)}, u32[]{:S(2)}) collective-permute-start(bf16[2,2,256,256]{3,2,1,0:T(8,128)(2,1)S(1)} %collective-permute-done.9.refs_5_), channel_id=1, source_target_pairs={{0,192},{8,56},{16,208},{24,8},{32,224},{40,24},{48,240},{56,40},{... | collective-permute-start | bytes 1572872 | tf_op jit(solution)/shard_map/ppermute | solution.py:204
  59.1 1.1 collective-permute-start.14
  60.2 0.0 copy-done.4
  60.2 0.0 copy-done.8
  60.3 0.0 copy-done.9
  60.3 5.3 %collective-permute-done.14.refs_4_ = bf16[2,256,256]{2,1,0:T(8,128)(2,1)S(1)} collective-permute-done((bf16[2,256,256]{2,1,0:T(8,128)(2,1)S(1)}, bf16[2,256,256]{2,1,0:T(8,128)(2,1)S(1)}, u32[]{:S(2)}, u32[]{:S(2)}) %collective-permute-start.14) | collective-permute-done | bytes 262176 | tf_op jit(solution)/shard_map/ppermute | solution.py:210
  65.6 0.0 copy-done.3
  65.6 0.9 copy-done.5
  66.5 0.9 copy-done.6
  67.5 0.3 shard_map.58.refs_8_
  67.7 0.0 copy-done.1
  67.7 0.0 copy-done.2
  67.7 0.0 copy-done.7
  67.8 0.0 copy-done.10
  67.8 0.0 copy-start
  67.8 0.0 collective-permute-done.15.refs_6_
  67.8 0.0 copy-start.11
  67.8 0.0 collective-permute-done.16.refs_7_
  67.8 0.8 copy-done.11
  68.7 10.2 %collective-permute-start.17 = (bf16[9,2,256,256]{3,2,1,0:T(8,128)(2,1)S(1)}, bf16[9,2,256,256]{3,2,1,0:T(8,128)(2,1)}, u32[]{:S(2)}, u32[]{:S(2)}) collective-permute-start(bf16[9,2,256,256]{3,2,1,0:T(8,128)(2,1)S(1)} %shard_map.58.refs_8_), channel_id=1, source_target_pairs={{0,8},{8,0},{16,24},{24,16},{32,40},{40,32},{48,56},{56,48},{64,72... | collective-permute-start | bytes 7077896 | tf_op jit(solution)/shard_map/ppermute | solution.py:207
  78.8 0.0 copy-done.12
  78.8 4.3 %collective-permute-done.17.refs_9_ = bf16[9,2,256,256]{3,2,1,0:T(8,128)(2,1)} collective-permute-done((bf16[9,2,256,256]{3,2,1,0:T(8,128)(2,1)S(1)}, bf16[9,2,256,256]{3,2,1,0:T(8,128)(2,1)}, u32[]{:S(2)}, u32[]{:S(2)}) %collective-permute-start.17) | collective-permute-done | bytes 2359328 | tf_op jit(solution)/shard_map/ppermute | solution.py:207
  83.1 0.0 copy-done
  83.1 11.4 %shard_map.59 = bf16[8,2,2,32,256]{4,3,2,1,0:T(8,128)(2,1)} custom-call(s32[32]{0:T(128)} %left_sizes.3, s32[32]{0:T(128)} %right_sizes.3, bf16[2,2,256,256]{3,2,1,0:T(8,128)(2,1)} %copy-done.2, bf16[2,2,256,256]{3,2,1,0:T(8,128)(2,1)} %copy-done.10, bf16[2,2,256,256]{3,2,1,0:T(8,128)(2,1)} %copy-done.9, bf16[2,2,256,256]{3,2,1,0:T(8,128)(2,1)} %copy-done.1, ...), custom_call_target="tpu_custom_call" | custom-call | tf_op jit(solution)/shard_map/pallas_call | solution.py:142
  94.5 20.1 %all_to_all.10 = bf16[8,2,2,32,256]{4,3,2,1,0:T(8,128)(2,1)S(1)} all-to-all(bf16[8,2,2,32,256]{4,3,2,1,0:T(8,128)(2,1)} %shard_map.59), channel_id=1, replica_groups=mesh['blk'=32,'mpo'=8] {'mpo'}, dimensions={0} | all-to-all | bytes 1048576 | tf_op jit(solution)/shard_map/all_to_all | solution.py:248
  114.6 12.9 %all_to_all.11.in_ref = bf16[16,2,32,256]{3,2,1,0:T(8,128)(2,1)S(1)} all-to-all(bf16[16,2,32,256]{3,2,1,0:T(8,128)(2,1)S(1)} %bitcast.2), channel_id=1, replica_groups={{0,128,16,144,32,160,48,176,64,192,80,208,96,224,112,240},{72,200,88,21..., dimensions={0} | all-to-all | bytes 1048576 | tf_op jit(solution)/shard_map/all_to_all | solution.py:255
  127.6 0.9 shard_map.60
  (6 shorter events, 0.0 us)
Async XLA Ops:
  0.0 65.6 %copy-start.3 = (bf16[2,256,256]{2,1,0:T(8,128)(2,1)S(1)}, bf16[2,256,256]{2,1,0:T(8,128)(2,1)}, u32[]{:S(2)}) copy-start(bf16[2,256,256]{2,1,0:T(8,128)(2,1)} %refs_0_.1) | copy-start | bytes 786436
  0.0 16.1 %collective-permute-start = (bf16[2,256,256]{2,1,0:T(8,128)(2,1)}, bf16[2,256,256]{2,1,0:T(8,128)(2,1)S(1)}, u32[]{:S(2)}, u32[]{:S(2)}) collective-permute-start(bf16[2,256,256]{2,1,0:T(8,128)(2,1)} %param.7), channel_id=1, source_target_pairs={{0,0},{1,16},{2,32},{3,48},{4,64},{5,80},{6,96},{7,112},{8,12},{9,... | collective-permute-start | bytes 786440 | tf_op jit(solution)/shard_map/ppermute | solution.py:223
  9.8 16.3 %collective-permute-start.4 = (bf16[2,256,256]{2,1,0:T(8,128)(2,1)}, bf16[2,256,256]{2,1,0:T(8,128)(2,1)S(1)}, u32[]{:S(2)}, u32[]{:S(2)}) collective-permute-start(bf16[2,256,256]{2,1,0:T(8,128)(2,1)} %refs_0_.1), channel_id=1, source_target_pairs={{0,1},{1,2},{2,3},{3,4},{4,5},{5,6},{6,7},{7,0},{8,9},{9,10},{10,1... | collective-permute-start | bytes 786440 | tf_op jit(solution)/shard_map/ppermute | solution.py:210
  11.1 15.0 %collective-permute-start.5 = (bf16[2,256,256]{2,1,0:T(8,128)(2,1)}, bf16[2,256,256]{2,1,0:T(8,128)(2,1)S(1)}, u32[]{:S(2)}, u32[]{:S(2)}) collective-permute-start(bf16[2,256,256]{2,1,0:T(8,128)(2,1)} %refs_0_.1), channel_id=1, source_target_pairs={{0,7},{1,0},{2,1},{3,2},{4,3},{5,4},{6,5},{7,6},{8,15},{9,8},{10,9... | collective-permute-start | bytes 786440 | tf_op jit(solution)/shard_map/ppermute | solution.py:213
  16.1 10.0 %collective-permute-start.3 = (bf16[2,256,256]{2,1,0:T(8,128)(2,1)S(1)}, bf16[2,256,256]{2,1,0:T(8,128)(2,1)S(1)}, u32[]{:S(2)}, u32[]{:S(2)}) collective-permute-start(bf16[2,256,256]{2,1,0:T(8,128)(2,1)S(1)} %collective-permute-done.refs_0_), channel_id=1, source_target_pairs={{0,32},{8,136},{16,48},{24,152},{32,0},{40,168},{48,16},{56,184},{... | collective-permute-start | bytes 786440 | tf_op jit(solution)/shard_map/ppermute | solution.py:201
  18.8 7.3 %collective-permute-start.2 = (bf16[2,256,256]{2,1,0:T(8,128)(2,1)S(1)}, bf16[2,256,256]{2,1,0:T(8,128)(2,1)S(1)}, u32[]{:S(2)}, u32[]{:S(2)}) collective-permute-start(bf16[2,256,256]{2,1,0:T(8,128)(2,1)S(1)} %collective-permute-done.refs_0_), channel_id=1, source_target_pairs={{0,48},{8,200},{16,0},{24,216},{32,16},{40,232},{48,32},{56,248},{... | collective-permute-start | bytes 786440 | tf_op jit(solution)/shard_map/ppermute | solution.py:201
  18.8 7.3 %collective-permute-start.1 = (bf16[2,256,256]{2,1,0:T(8,128)(2,1)S(1)}, bf16[2,256,256]{2,1,0:T(8,128)(2,1)S(1)}, u32[]{:S(2)}, u32[]{:S(2)}) collective-permute-start(bf16[2,256,256]{2,1,0:T(8,128)(2,1)S(1)} %collective-permute-done.refs_0_), channel_id=1, source_target_pairs={{0,16},{8,72},{16,32},{24,88},{32,48},{40,104},{48,0},{56,120},{64... | collective-permute-start | bytes 786440 | tf_op jit(solution)/shard_map/ppermute | solution.py:201
  26.1 34.2 %copy-start.4 = (bf16[2,256,256]{2,1,0:T(8,128)(2,1)}, bf16[2,256,256]{2,1,0:T(8,128)(2,1)S(1)}, u32[]{:S(2)}) copy-start(bf16[2,256,256]{2,1,0:T(8,128)(2,1)S(1)} %collective-permute-done.5.refs_1_) | copy-start | bytes 786436
  26.1 13.7 %collective-permute-start.10 = (bf16[2,256,256]{2,1,0:T(8,128)(2,1)S(1)}, bf16[2,256,256]{2,1,0:T(8,128)(2,1)S(1)}, u32[]{:S(2)}, u32[]{:S(2)}) collective-permute-start(bf16[2,256,256]{2,1,0:T(8,128)(2,1)S(1)} %collective-permute-done.4.refs_7_), channel_id=1, source_target_pairs={{0,1},{1,2},{2,3},{3,4},{4,5},{5,6},{6,7},{7,0},{8,9},{9,10},{10,1... | collective-permute-start | bytes 786440 | tf_op jit(solution)/shard_map/ppermute | solution.py:210
  30.1 14.0 %collective-permute-start.12 = (bf16[2,256,256]{2,1,0:T(8,128)(2,1)S(1)}, bf16[2,256,256]{2,1,0:T(8,128)(2,1)S(1)}, u32[]{:S(2)}, u32[]{:S(2)}) collective-permute-start(bf16[2,256,256]{2,1,0:T(8,128)(2,1)S(1)} %collective-permute-done.5.refs_1_), channel_id=1, source_target_pairs={{0,7},{1,0},{2,1},{3,2},{4,3},{5,4},{6,5},{7,6},{8,15},{9,8},{10,9... | collective-permute-start | bytes 786440 | tf_op jit(solution)/shard_map/ppermute | solution.py:213
  36.1 31.7 %copy-start.1 = (bf16[2,2,256,256]{3,2,1,0:T(8,128)(2,1)}, bf16[2,2,256,256]{3,2,1,0:T(8,128)(2,1)S(1)}, u32[]{:S(2)}) copy-start(bf16[2,2,256,256]{3,2,1,0:T(8,128)(2,1)S(1)} %shard_map.57.refs_3_) | copy-start | bytes 1572868
  36.1 18.0 %collective-permute-start.9 = (bf16[2,2,256,256]{3,2,1,0:T(8,128)(2,1)S(1)}, bf16[2,2,256,256]{3,2,1,0:T(8,128)(2,1)S(1)}, u32[]{:S(2)}, u32[]{:S(2)}) collective-permute-start(bf16[2,2,256,256]{3,2,1,0:T(8,128)(2,1)S(1)} %shard_map.57.refs_3_), channel_id=1, source_target_pairs={{0,192},{8,56},{16,208},{24,8},{32,224},{40,24},{48,240},{56,40},{... | collective-permute-start | bytes 1572872 | tf_op jit(solution)/shard_map/ppermute | solution.py:204
  39.7 8.8 %collective-permute-start.11 = (bf16[2,256,256]{2,1,0:T(8,128)(2,1)S(1)}, bf16[2,256,256]{2,1,0:T(8,128)(2,1)S(1)}, u32[]{:S(2)}, u32[]{:S(2)}) collective-permute-start(bf16[2,256,256]{2,1,0:T(8,128)(2,1)S(1)} %collective-permute-done.10.refs_6_), channel_id=1, source_target_pairs={{0,1},{1,2},{2,3},{3,4},{4,5},{5,6},{6,7},{7,0},{8,9},{9,10},{10,1... | collective-permute-start | bytes 786440 | tf_op jit(solution)/shard_map/ppermute | solution.py:210
  39.7 14.3 %collective-permute-start.8 = (bf16[2,2,256,256]{3,2,1,0:T(8,128)(2,1)S(1)}, bf16[2,2,256,256]{3,2,1,0:T(8,128)(2,1)S(1)}, u32[]{:S(2)}, u32[]{:S(2)}) collective-permute-start(bf16[2,2,256,256]{3,2,1,0:T(8,128)(2,1)S(1)} %shard_map.57.refs_3_), channel_id=1, source_target_pairs={{0,64},{8,24},{16,80},{24,40},{32,96},{40,56},{48,112},{56,8},{64,... | collective-permute-start | bytes 1572872 | tf_op jit(solution)/shard_map/ppermute | solution.py:204
  41.3 26.4 %copy-start.2 = (bf16[2,2,256,256]{3,2,1,0:T(8,128)(2,1)}, bf16[2,2,256,256]{3,2,1,0:T(8,128)(2,1)S(1)}, u32[]{:S(2)}) copy-start(bf16[2,2,256,256]{3,2,1,0:T(8,128)(2,1)S(1)} %shard_map.56.refs_0_) | copy-start | bytes 1572868
  41.4 12.7 %collective-permute-start.7 = (bf16[2,2,256,256]{3,2,1,0:T(8,128)(2,1)S(1)}, bf16[2,2,256,256]{3,2,1,0:T(8,128)(2,1)S(1)}, u32[]{:S(2)}, u32[]{:S(2)}) collective-permute-start(bf16[2,2,256,256]{3,2,1,0:T(8,128)(2,1)S(1)} %shard_map.56.refs_0_), channel_id=1, source_target_pairs={{0,192},{8,56},{16,208},{24,8},{32,224},{40,24},{48,240},{56,40},{... | collective-permute-start | bytes 1572872 | tf_op jit(solution)/shard_map/ppermute | solution.py:204
  44.1 12.3 %collective-permute-start.6 = (bf16[2,2,256,256]{3,2,1,0:T(8,128)(2,1)S(1)}, bf16[2,2,256,256]{3,2,1,0:T(8,128)(2,1)S(1)}, u32[]{:S(2)}, u32[]{:S(2)}) collective-permute-start(bf16[2,2,256,256]{3,2,1,0:T(8,128)(2,1)S(1)} %shard_map.56.refs_0_), channel_id=1, source_target_pairs={{0,64},{8,24},{16,80},{24,40},{32,96},{40,56},{48,112},{56,8},{64,... | collective-permute-start | bytes 1572872 | tf_op jit(solution)/shard_map/ppermute | solution.py:204
  48.6 5.5 %collective-permute-start.13 = (bf16[2,256,256]{2,1,0:T(8,128)(2,1)S(1)}, bf16[2,256,256]{2,1,0:T(8,128)(2,1)S(1)}, u32[]{:S(2)}, u32[]{:S(2)}) collective-permute-start(bf16[2,256,256]{2,1,0:T(8,128)(2,1)S(1)} %collective-permute-done.12.refs_2_), channel_id=1, source_target_pairs={{0,7},{1,0},{2,1},{3,2},{4,3},{5,4},{6,5},{7,6},{8,15},{9,8},{10,9... | collective-permute-start | bytes 786440 | tf_op jit(solution)/shard_map/ppermute | solution.py:213
  54.1 13.7 %copy-start.7 = (bf16[2,2,256,256]{3,2,1,0:T(8,128)(2,1)}, bf16[2,2,256,256]{3,2,1,0:T(8,128)(2,1)S(1)}, u32[]{:S(2)}) copy-start(bf16[2,2,256,256]{3,2,1,0:T(8,128)(2,1)S(1)} %collective-permute-done.9.refs_5_) | copy-start | bytes 1572868
  54.1 6.2 %copy-start.8 = (bf16[2,2,256,256]{3,2,1,0:T(8,128)(2,1)}, bf16[2,2,256,256]{3,2,1,0:T(8,128)(2,1)S(1)}, u32[]{:S(2)}) copy-start(bf16[2,2,256,256]{3,2,1,0:T(8,128)(2,1)S(1)} %collective-permute-done.8.refs_4_) | copy-start | bytes 1572868
  54.1 6.1 %copy-start.9 = (bf16[2,2,256,256]{3,2,1,0:T(8,128)(2,1)}, bf16[2,2,256,256]{3,2,1,0:T(8,128)(2,1)S(1)}, u32[]{:S(2)}) copy-start(bf16[2,2,256,256]{3,2,1,0:T(8,128)(2,1)S(1)} %collective-permute-done.7.refs_2_) | copy-start | bytes 1572868
  56.4 11.3 %copy-start.10 = (bf16[2,2,256,256]{3,2,1,0:T(8,128)(2,1)}, bf16[2,2,256,256]{3,2,1,0:T(8,128)(2,1)S(1)}, u32[]{:S(2)}) copy-start(bf16[2,2,256,256]{3,2,1,0:T(8,128)(2,1)S(1)} %collective-permute-done.6.refs_1_) | copy-start | bytes 1572868
  56.4 11.3 %collective-permute-start.15 = (bf16[2,2,256,256]{3,2,1,0:T(8,128)(2,1)S(1)}, bf16[2,2,256,256]{3,2,1,0:T(8,128)(2,1)S(1)}, u32[]{:S(2)}, u32[]{:S(2)}) collective-permute-start(bf16[2,2,256,256]{3,2,1,0:T(8,128)(2,1)S(1)} %collective-permute-done.6.refs_1_), channel_id=1, source_target_pairs={{0,64},{8,24},{16,80},{24,40},{32,96},{40,56},{48,112},{56,8},{64,... | collective-permute-start | bytes 1572872 | tf_op jit(solution)/shard_map/ppermute | solution.py:204
  56.4 11.3 %collective-permute-start.16 = (bf16[2,2,256,256]{3,2,1,0:T(8,128)(2,1)S(1)}, bf16[2,2,256,256]{3,2,1,0:T(8,128)(2,1)S(1)}, u32[]{:S(2)}, u32[]{:S(2)}) collective-permute-start(bf16[2,2,256,256]{3,2,1,0:T(8,128)(2,1)S(1)} %collective-permute-done.9.refs_5_), channel_id=1, source_target_pairs={{0,192},{8,56},{16,208},{24,8},{32,224},{40,24},{48,240},{56,40},{... | collective-permute-start | bytes 1572872 | tf_op jit(solution)/shard_map/ppermute | solution.py:204
  59.1 6.4 %collective-permute-start.14 = (bf16[2,256,256]{2,1,0:T(8,128)(2,1)S(1)}, bf16[2,256,256]{2,1,0:T(8,128)(2,1)S(1)}, u32[]{:S(2)}, u32[]{:S(2)}) collective-permute-start(bf16[2,256,256]{2,1,0:T(8,128)(2,1)S(1)} %collective-permute-done.11.refs_5_), channel_id=1, source_target_pairs={{0,1},{1,2},{2,3},{3,4},{4,5},{5,6},{6,7},{7,0},{8,9},{9,10},{10,1... | collective-permute-start | bytes 786440 | tf_op jit(solution)/shard_map/ppermute | solution.py:210
  65.6 1.0 copy-start.5
  66.5 0.9 copy-start.6
  67.8 15.4 %copy-start = (bf16[9,2,256,256]{3,2,1,0:T(8,128)(2,1)}, bf16[9,2,256,256]{3,2,1,0:T(8,128)(2,1)S(1)}, u32[]{:S(2)}) copy-start(bf16[9,2,256,256]{3,2,1,0:T(8,128)(2,1)S(1)} %shard_map.58.refs_8_) | copy-start | bytes 7077892
  67.8 0.9 copy-start.11
  68.7 10.2 %copy-start.12 = (bf16[2,2,256,256]{3,2,1,0:T(8,128)(2,1)}, bf16[2,2,256,256]{3,2,1,0:T(8,128)(2,1)S(1)}, u32[]{:S(2)}) copy-start(bf16[2,2,256,256]{3,2,1,0:T(8,128)(2,1)S(1)} %collective-permute-done.16.refs_7_) | copy-start | bytes 1572868
  68.7 14.5 %collective-permute-start.17 = (bf16[9,2,256,256]{3,2,1,0:T(8,128)(2,1)S(1)}, bf16[9,2,256,256]{3,2,1,0:T(8,128)(2,1)}, u32[]{:S(2)}, u32[]{:S(2)}) collective-permute-start(bf16[9,2,256,256]{3,2,1,0:T(8,128)(2,1)S(1)} %shard_map.58.refs_8_), channel_id=1, source_target_pairs={{0,8},{8,0},{16,24},{24,16},{32,40},{40,32},{48,56},{56,48},{64,72... | collective-permute-start | bytes 7077896 | tf_op jit(solution)/shard_map/ppermute | solution.py:207

commit v11 on v10

--- a/solution.py
+++ b/solution.py
@@ -85,7 +85,7 @@
 
 def apply_kernel(pieces, left_sizes, right_sizes, *refs):
     ins, (out_ref, total, held, left_held, psi_held, middle, sems) = refs[:-7], refs[-7:]
-    shards, (own, other, psi) = ins[: len(pieces)], ins[len(pieces) :]
+    shards, (own, other, psi, other_psi) = ins[: len(pieces)], ins[len(pieces) :]
     sector, rank, core, x0, y0 = coordinates()
     ranks, _, _, rows, right_dim = out_ref.shape
     left_dim = ranks * rows
@@ -94,9 +94,9 @@
         for i, (source, place_in) in enumerate(
             (
                 (psi, psi_held.at[0]),
-                (other.at[ranks], psi_held.at[1]),
-                (own.at[pl.ds(0, ranks)], left_held.at[0]),
-                (other.at[pl.ds(0, ranks)], left_held.at[1]),
+                (other_psi, psi_held.at[1]),
+                (own, left_held.at[0]),
+                (other, left_held.at[1]),
             )
         )
     ]
@@ -112,7 +112,7 @@
             near = OFFSETS[start + k]
             y = jnp.where(core == 0, y0 + far, y0 + near) & (SIDE - 1)
             x = jnp.where(core == 0, x0 + near, x0 + far) & (SIDE - 1)
-            which, pair = y // 2, (x + SIDE * (y & 1) - rank) & (ranks - 1)
+            which, pair = y // 2, x + SIDE * (y & 1)
             for a in range(2):
                 block = left_held[a, pair].reshape(2 * left_dim, left_dim)
                 product = jnp.dot(block, psi_held[a, which], preferred_element_type=jnp.float32)
@@ -134,11 +134,11 @@
             out_ref[:, b, pl.ds(spot, 1)] = block
 
 
-def apply(pieces, shards, own, other, psi, left_sizes, right_sizes):
+def apply(pieces, shards, own, other, psi, other_psi, left_sizes, right_sizes):
     dtype = psi.dtype
-    slots, pair, left_dim, _ = own.shape
-    ranks, right_dim = slots - 1, psi.shape[2]
-    others = (*shards, own, other, psi)
+    ranks, pair, left_dim, _ = own.shape
+    right_dim = psi.shape[2]
+    others = (*shards, own, other, psi, other_psi)
     return pl.pallas_call(
         functools.partial(apply_kernel, pieces),
         out_shape=jax.ShapeDtypeStruct((ranks, 2, 2, left_dim // ranks, right_dim), dtype),
@@ -206,12 +206,6 @@
     def swap(block):
         return lax.ppermute(block, "blk", [(i, i ^ 1) for i in range(sectors)])
 
-    def up(block):
-        return lax.ppermute(block, "mpo", [(z, (z + 1) % ranks) for z in range(ranks)])
-
-    def down(block):
-        return lax.ppermute(block, "mpo", [(z, (z - 1) % ranks) for z in range(ranks)])
-
     turn = [
         (
             place(y, x, c) * ranks + z,
@@ -221,29 +215,24 @@
         for z in range(ranks)
     ]
     own = lax.ppermute(right_env, ("blk", "mpo"), turn)
-    up1, down1 = up(left_env), down(left_env)
+    lefts = lax.all_gather(left_env, "mpo")
     keep, give = cut(wavefunction, left_sizes, right_sizes)
     own, keep, give = together(own, keep, give)
 
     below, above, two = near_step(own, 1), near_step(own, -1), near_step(own, 2)
-    below, above, two, up1, down1 = together(below, above, two, up1, down1)
+    below, above, two = together(below, above, two)
     line_a, line_b = stack(own, below), stack(above, two)
     a_below, a_above = far_step(line_a, 1), far_step(line_a, -1)
     b_below, b_above = far_step(line_b, 1), far_step(line_b, -1)
-    up2, down2 = up(up1), down(down1)
-    up3, down3 = up(up2), down(down2)
-    a_below, a_above, b_below, b_above, up3, down3 = together(
-        a_below, a_above, b_below, b_above, up3, down3
-    )
+    got = swap(give)
+    a_below, a_above, b_below, b_above, got = together(a_below, a_above, b_below, b_above, got)
     a_two, b_two = far_step(a_below, 1), far_step(b_above, -1)
-    up4 = up(up3)
-    lefts = stack(left_env, down1, down2, down3, up4, up3, up2, up1, give)
     lefts, a_two, b_two = together(lefts, a_two, b_two)
     others = swap(lefts)
 
     pieces = ((0, 0), (SIDE - 1, 0), (1, 0), (0, 2), (SIDE - 1, 2), (1, 2), (2, 0), (2, 2))
     shards = (line_a, a_below, a_above, line_b, b_below, b_above, a_two, b_two)
-    done = apply(pieces, shards, lefts, others, keep, left_sizes, right_sizes)
+    done = apply(pieces, shards, lefts, others, keep, got, left_sizes, right_sizes)
 
     by_plane = lax.all_to_all(done, "mpo", 0, 0)
     chips = SIDE * SIDE

time: 130 us -> 141 us (1.085)
  between operations: 0.37 us -> 13.5 us
  waiting for transfers between devices: 27.1 us -> 22.2 us
  blocking collectives: 33 us -> 37.6 us
    ppermute x7 -> x0, waiting for transfers between devices: 20.5 us -> none  [the longest x4 16.6 us: up(): lax.ppermute(block, 'mpo', [(z, (z + 1) % ranks) for z in range(ranks)])]
    ppermute x7 -> x0, starting transfers between devices: 16.4 us -> none  [the longest x3 9.93 us: down(): lax.ppermute(block, 'mpo', [(z, (z - 1) % ranks) for z in range(ranks)])]
    ppermute x1 -> x2, starting transfers between devices: 10.2 us -> 19.8 us  [swap(): return lax.ppermute(block, 'blk', [(i, i ^ 1) for i in range(sectors)])]
    ppermute x3, waiting for transfers between devices: 0.01 us -> 6.83 us  [near_step(): return lax.ppermute(block, 'blk', step(False, by))]
    ppermute x6, waiting for transfers between devices: 2.34 us -> 8.53 us  [far_step(): return lax.ppermute(block, 'blk', step(True, by))]
    ppermute x6, starting transfers between devices: 9.57 us -> 15 us  [far_step(): return lax.ppermute(block, 'blk', step(True, by))]
    all_to_all x1, blocking collectives: 20.1 us -> 25.4 us  [local(): by_plane = lax.all_to_all(done, 'mpo', 0, 0)]
    ppermute x1 -> x2, waiting for transfers between devices: 4.29 us -> 5.16 us  [swap(): return lax.ppermute(block, 'blk', [(i, i ^ 1) for i in range(sectors)])]
  transfers between devices with their start and end apart: 18 -> 13, of which waited for: 7 -> 8; matrix products, arithmetic and copies ran while one was open for 0% -> 0% of each run, Pallas kernels for 2% -> 2%
where the time goes in v11:
time: 141 us; the launch traced here: 139 us
  starting transfers between devices  48.9 us (35%)
  blocking collectives  37.6 us (27%)
  waiting for transfers between devices  22.2 us (16%)
  Pallas kernels  15.1 us (11%)
  between operations  13.5 us (10%)
  local copies, waits for them, and re-layouts  2.13 us (2%)
    all_to_all x1, blocking collectives, local(): by_plane = lax.all_to_all(done, 'mpo', 0, 0)  25.4 us
    ppermute x2, starting transfers between devices, swap(): return lax.ppermute(block, 'blk', [(i, i ^ 1) for i in range(sectors)])  19.8 us
    ppermute x6, starting transfers between devices, far_step(): return lax.ppermute(block, 'blk', step(True, by))  15 us
    all_to_all x1, blocking collectives, local(): out = order(lax.all_to_all(by_plane, 'blk', 0, 0, axis_index_groups=groups))  12.2 us
    pallas_call x1, Pallas kernels, apply(): pl.pallas_call(functools.partial(apply_kernel, pieces), out_shape=jax.Sha...  11.4 us
    ppermute x1, starting transfers between devices, local(): own = lax.ppermute(right_env, ('blk', 'mpo'), turn)  9.65 us
    ppermute x6, waiting for transfers between devices, far_step(): return lax.ppermute(block, 'blk', step(True, by))  8.53 us
    ppermute x3, waiting for transfers between devices, near_step(): return lax.ppermute(block, 'blk', step(False, by))  6.83 us
  transfers between devices with their start and end apart: 13, of which 8 were waited for; matrix products, arithmetic and copies ran while one was open for 0% of the time, Pallas kernels for 2%

profile of v11, /device:TPU:1, one launch (start us, length us, event | category | flops | bytes accessed | tf_op | source)
XLA Modules:
  0.0 139.4 jit_solution(8330607493176248873)
XLA Ops:
  6.5 0.0 all-gather.3.cloned.1.call-start
  6.5 0.7 all-gather.3.cloned.1.call-update
  7.3 9.6 %collective-permute-start = (bf16[2,256,256]{2,1,0:T(8,128)(2,1)}, bf16[2,256,256]{2,1,0:T(8,128)(2,1)S(1)}, u32[]{:S(2)}, u32[]{:S(2)}) collective-permute-start(bf16[2,256,256]{2,1,0:T(8,128)(2,1)} %param.7), channel_id=1, source_target_pairs={{0,0},{1,16},{2,32},{3,48},{4,64},{5,80},{6,96},{7,112},{8,12},{9,... | collective-permute-start | bytes 786440 | tf_op jit(solution)/shard_map/ppermute | solution.py:217
  16.9 2.6 %shard_map.55 = (bf16[2,256,256]{2,1,0:T(8,128)(2,1)}, bf16[2,256,256]{2,1,0:T(8,128)(2,1)}) custom-call(s32[32]{0:T(128)} %left_sizes.3, s32[32]{0:T(128)} %right_sizes.3, bf16[256,8192]{1,0:T(8,128)(2,1)} %psi_ref.1), custom_call_target="tpu_custom_call" | custom-call | tf_op jit(solution)/shard_map/pallas_call | solution.py:76
  19.6 0.0 copy-start.9
  19.6 1.0 collective-permute-done.refs_0_
  20.6 2.9 %collective-permute-start.3 = (bf16[2,256,256]{2,1,0:T(8,128)(2,1)S(1)}, bf16[2,256,256]{2,1,0:T(8,128)(2,1)S(1)}, u32[]{:S(2)}, u32[]{:S(2)}) collective-permute-start(bf16[2,256,256]{2,1,0:T(8,128)(2,1)S(1)} %collective-permute-done.refs_0_), channel_id=1, source_target_pairs={{0,32},{8,136},{16,48},{24,152},{32,0},{40,168},{48,16},{56,184},{... | collective-permute-start | bytes 786440 | tf_op jit(solution)/shard_map/ppermute | solution.py:201
  23.5 1.5 %collective-permute-start.2 = (bf16[2,256,256]{2,1,0:T(8,128)(2,1)S(1)}, bf16[2,256,256]{2,1,0:T(8,128)(2,1)S(1)}, u32[]{:S(2)}, u32[]{:S(2)}) collective-permute-start(bf16[2,256,256]{2,1,0:T(8,128)(2,1)S(1)} %collective-permute-done.refs_0_), channel_id=1, source_target_pairs={{0,48},{8,200},{16,0},{24,216},{32,16},{40,232},{48,32},{56,248},{... | collective-permute-start | bytes 786440 | tf_op jit(solution)/shard_map/ppermute | solution.py:201
  25.0 0.0 collective-permute-start.1
  25.0 2.5 %collective-permute-done.3.refs_1_ = bf16[2,256,256]{2,1,0:T(8,128)(2,1)S(1)} collective-permute-done((bf16[2,256,256]{2,1,0:T(8,128)(2,1)S(1)}, bf16[2,256,256]{2,1,0:T(8,128)(2,1)S(1)}, u32[]{:S(2)}, u32[]{:S(2)}) %collective-permute-start.3) | collective-permute-done | bytes 262176 | tf_op jit(solution)/shard_map/ppermute | solution.py:201
  27.5 4.2 %collective-permute-done.2.refs_0_ = bf16[2,256,256]{2,1,0:T(8,128)(2,1)S(1)} collective-permute-done((bf16[2,256,256]{2,1,0:T(8,128)(2,1)S(1)}, bf16[2,256,256]{2,1,0:T(8,128)(2,1)S(1)}, u32[]{:S(2)}, u32[]{:S(2)}) %collective-permute-start.2) | collective-permute-done | bytes 262176 | tf_op jit(solution)/shard_map/ppermute | solution.py:201
  31.6 0.2 collective-permute-done.1.refs_1_
  31.8 0.1 shard_map.57.refs_3_
  31.9 0.0 copy-start
  31.9 9.6 %collective-permute-start.7 = (bf16[2,2,256,256]{3,2,1,0:T(8,128)(2,1)S(1)}, bf16[2,2,256,256]{3,2,1,0:T(8,128)(2,1)S(1)}, u32[]{:S(2)}, u32[]{:S(2)}) collective-permute-start(bf16[2,2,256,256]{3,2,1,0:T(8,128)(2,1)S(1)} %shard_map.57.refs_3_), channel_id=1, source_target_pairs={{0,192},{8,56},{16,208},{24,8},{32,224},{40,24},{48,240},{56,40},{... | collective-permute-start | bytes 1572872 | tf_op jit(solution)/shard_map/ppermute | solution.py:204
  41.5 0.0 collective-permute-start.6
  41.5 0.1 shard_map.56.refs_0_
  41.6 0.0 copy-start.1
  41.6 2.8 %collective-permute-start.5 = (bf16[2,2,256,256]{3,2,1,0:T(8,128)(2,1)S(1)}, bf16[2,2,256,256]{3,2,1,0:T(8,128)(2,1)S(1)}, u32[]{:S(2)}, u32[]{:S(2)}) collective-permute-start(bf16[2,2,256,256]{3,2,1,0:T(8,128)(2,1)S(1)} %shard_map.56.refs_0_), channel_id=1, source_target_pairs={{0,192},{8,56},{16,208},{24,8},{32,224},{40,24},{48,240},{56,40},{... | collective-permute-start | bytes 1572872 | tf_op jit(solution)/shard_map/ppermute | solution.py:204
  44.3 0.0 collective-permute-start.4
  44.3 0.0 copy-done.9
  44.3 9.2 %collective-permute-start.8 = (bf16[2,256,256]{2,1,0:T(8,128)(2,1)S(1)}, bf16[2,256,256]{2,1,0:T(8,128)(2,1)S(1)}, u32[]{:S(2)}, u32[]{:S(2)}) collective-permute-start(bf16[2,256,256]{2,1,0:T(8,128)(2,1)S(1)} %copy-done.9), channel_id=1, source_target_pairs={{0,8},{8,0},{16,24},{24,16},{32,40},{40,32},{48,56},{56,48},{64,72... | collective-permute-start | bytes 786440 | tf_op jit(solution)/shard_map/ppermute | solution.py:207
  53.5 1.2 collective-permute-done.8.refs_11_
  54.7 0.0 copy-start.8
  54.7 0.0 collective-permute-done.7.refs_5_
  54.7 0.0 copy-start.3
  54.7 0.0 collective-permute-done.6.refs_4_
  54.7 0.0 copy-start.4
  54.7 0.0 collective-permute-done.5.refs_2_
  54.7 0.0 copy-start.5
  54.7 2.0 %collective-permute-done.4.refs_1_ = bf16[2,2,256,256]{3,2,1,0:T(8,128)(2,1)S(1)} collective-permute-done((bf16[2,2,256,256]{3,2,1,0:T(8,128)(2,1)S(1)}, bf16[2,2,256,256]{3,2,1,0:T(8,128)(2,1)S(1)}, u32[]{:S(2)}, u32[]{:S(2)}) %collective-permute-start.4) | collective-permute-done | bytes 524320 | tf_op jit(solution)/shard_map/ppermute | solution.py:204
  56.7 0.0 copy-start.6
  56.7 0.0 collective-permute-start.9
  56.7 0.0 copy-done.3
  56.7 2.7 %collective-permute-start.10 = (bf16[2,2,256,256]{3,2,1,0:T(8,128)(2,1)S(1)}, bf16[2,2,256,256]{3,2,1,0:T(8,128)(2,1)}, u32[]{:S(2)}, u32[]{:S(2)}) collective-permute-start(bf16[2,2,256,256]{3,2,1,0:T(8,128)(2,1)S(1)} %collective-permute-done.7.refs_5_), channel_id=1, source_target_pairs={{0,192},{8,56},{16,208},{24,8},{32,224},{40,24},{48,240},{56,40},{... | collective-permute-start | bytes 1572872 | tf_op jit(solution)/shard_map/ppermute | solution.py:204
  59.3 0.0 copy-done.4
  59.3 6.6 %collective-permute-done.9.refs_6_ = bf16[2,2,256,256]{3,2,1,0:T(8,128)(2,1)S(1)} collective-permute-done((bf16[2,2,256,256]{3,2,1,0:T(8,128)(2,1)S(1)}, bf16[2,2,256,256]{3,2,1,0:T(8,128)(2,1)S(1)}, u32[]{:S(2)}, u32[]{:S(2)}) %collective-permute-start.9) | collective-permute-done | bytes 524320 | tf_op jit(solution)/shard_map/ppermute | solution.py:204
  65.9 0.0 copy-done.5
  65.9 0.0 copy-done.6
  65.9 0.0 copy-start.7
  65.9 0.8 copy-done.7
  66.7 0.0 collective-permute-done.10.refs_7_
  66.7 0.0 all-gather.3.cloned.1.call-done
  66.7 10.6 %collective-permute-start.11 = (bf16[8,2,256,256]{3,2,1,0:T(8,128)(2,1)}, bf16[8,2,256,256]{3,2,1,0:T(8,128)(2,1)S(1)}, u32[]{:S(2)}, u32[]{:S(2)}) collective-permute-start(bf16[8,2,256,256]{3,2,1,0:T(8,128)(2,1)} %bitcast.3), channel_id=1, source_target_pairs={{0,8},{8,0},{16,24},{24,16},{32,40},{40,32},{48,56},{56,48},{64,72... | collective-permute-start | bytes 6291464 | tf_op jit(solution)/shard_map/ppermute | solution.py:207
  77.3 4.0 %collective-permute-done.11.refs_9_ = bf16[8,2,256,256]{3,2,1,0:T(8,128)(2,1)S(1)} collective-permute-done((bf16[8,2,256,256]{3,2,1,0:T(8,128)(2,1)}, bf16[8,2,256,256]{3,2,1,0:T(8,128)(2,1)S(1)}, u32[]{:S(2)}, u32[]{:S(2)}) %collective-permute-start.11) | collective-permute-done | bytes 2097184 | tf_op jit(solution)/shard_map/ppermute | solution.py:207
  81.3 0.0 copy-done
  81.3 0.0 copy-done.1
  81.3 0.0 copy-done.8
  81.3 0.0 copy-start.2
  81.3 1.3 copy-done.2
  82.6 11.4 %shard_map.58 = bf16[8,2,2,32,256]{4,3,2,1,0:T(8,128)(2,1)} custom-call(s32[32]{0:T(128)} %left_sizes.3, s32[32]{0:T(128)} %right_sizes.3, bf16[2,2,256,256]{3,2,1,0:T(8,128)(2,1)} %copy-done.1, bf16[2,2,256,256]{3,2,1,0:T(8,128)(2,1)} %copy-done.6, bf16[2,2,256,256]{3,2,1,0:T(8,128)(2,1)} %copy-done.5, bf16[2,2,256,256]{3,2,1,0:T(8,128)(2,1)} %copy-done, ...), custom_call_target="tpu_custom_call" | custom-call | tf_op jit(solution)/shard_map/pallas_call | solution.py:142
  94.0 25.4 %all_to_all.10 = bf16[8,2,2,32,256]{4,3,2,1,0:T(8,128)(2,1)S(1)} all-to-all(bf16[8,2,2,32,256]{4,3,2,1,0:T(8,128)(2,1)} %shard_map.58), channel_id=1, replica_groups=mesh['blk'=32,'mpo'=8] {'mpo'}, dimensions={0} | all-to-all | bytes 1048576 | tf_op jit(solution)/shard_map/all_to_all | solution.py:237
  119.4 12.2 %all_to_all.11.in_ref = bf16[16,2,32,256]{3,2,1,0:T(8,128)(2,1)S(1)} all-to-all(bf16[16,2,32,256]{3,2,1,0:T(8,128)(2,1)S(1)} %bitcast.5), channel_id=1, replica_groups={{0,128,16,144,32,160,48,176,64,192,80,208,96,224,112,240},{72,200,88,21..., dimensions={0} | all-to-all | bytes 1048576 | tf_op jit(solution)/shard_map/all_to_all | solution.py:244
  131.6 0.9 shard_map.59
Async XLA Ops:
  6.5 60.2 %all-gather.3.cloned.1.call-start = ((), (), s32[]{:S(2)}) async-start(), calls=%async_computation.2 | async-start | bytes 2359296 | tf_op jit(solution)/shard_map/all_gather | solution.py:218
  7.3 13.3 %collective-permute-start = (bf16[2,256,256]{2,1,0:T(8,128)(2,1)}, bf16[2,256,256]{2,1,0:T(8,128)(2,1)S(1)}, u32[]{:S(2)}, u32[]{:S(2)}) collective-permute-start(bf16[2,256,256]{2,1,0:T(8,128)(2,1)} %param.7), channel_id=1, source_target_pairs={{0,0},{1,16},{2,32},{3,48},{4,64},{5,80},{6,96},{7,112},{8,12},{9,... | collective-permute-start | bytes 786440 | tf_op jit(solution)/shard_map/ppermute | solution.py:217
  19.6 24.8 %copy-start.9 = (bf16[2,256,256]{2,1,0:T(8,128)(2,1)S(1)}, bf16[2,256,256]{2,1,0:T(8,128)(2,1)}, u32[]{:S(2)}) copy-start(bf16[2,256,256]{2,1,0:T(8,128)(2,1)} %get-tuple-element.27) | copy-start | bytes 786436
  20.6 6.9 %collective-permute-start.3 = (bf16[2,256,256]{2,1,0:T(8,128)(2,1)S(1)}, bf16[2,256,256]{2,1,0:T(8,128)(2,1)S(1)}, u32[]{:S(2)}, u32[]{:S(2)}) collective-permute-start(bf16[2,256,256]{2,1,0:T(8,128)(2,1)S(1)} %collective-permute-done.refs_0_), channel_id=1, source_target_pairs={{0,32},{8,136},{16,48},{24,152},{32,0},{40,168},{48,16},{56,184},{... | collective-permute-start | bytes 786440 | tf_op jit(solution)/shard_map/ppermute | solution.py:201
  23.5 8.1 %collective-permute-start.2 = (bf16[2,256,256]{2,1,0:T(8,128)(2,1)S(1)}, bf16[2,256,256]{2,1,0:T(8,128)(2,1)S(1)}, u32[]{:S(2)}, u32[]{:S(2)}) collective-permute-start(bf16[2,256,256]{2,1,0:T(8,128)(2,1)S(1)} %collective-permute-done.refs_0_), channel_id=1, source_target_pairs={{0,48},{8,200},{16,0},{24,216},{32,16},{40,232},{48,32},{56,248},{... | collective-permute-start | bytes 786440 | tf_op jit(solution)/shard_map/ppermute | solution.py:201
  25.0 6.8 %collective-permute-start.1 = (bf16[2,256,256]{2,1,0:T(8,128)(2,1)S(1)}, bf16[2,256,256]{2,1,0:T(8,128)(2,1)S(1)}, u32[]{:S(2)}, u32[]{:S(2)}) collective-permute-start(bf16[2,256,256]{2,1,0:T(8,128)(2,1)S(1)} %collective-permute-done.refs_0_), channel_id=1, source_target_pairs={{0,16},{8,72},{16,32},{24,88},{32,48},{40,104},{48,0},{56,120},{64... | collective-permute-start | bytes 786440 | tf_op jit(solution)/shard_map/ppermute | solution.py:201
  31.9 49.4 %copy-start = (bf16[2,2,256,256]{3,2,1,0:T(8,128)(2,1)}, bf16[2,2,256,256]{3,2,1,0:T(8,128)(2,1)S(1)}, u32[]{:S(2)}) copy-start(bf16[2,2,256,256]{3,2,1,0:T(8,128)(2,1)S(1)} %shard_map.57.refs_3_) | copy-start | bytes 1572868
  31.9 22.8 %collective-permute-start.7 = (bf16[2,2,256,256]{3,2,1,0:T(8,128)(2,1)S(1)}, bf16[2,2,256,256]{3,2,1,0:T(8,128)(2,1)S(1)}, u32[]{:S(2)}, u32[]{:S(2)}) collective-permute-start(bf16[2,2,256,256]{3,2,1,0:T(8,128)(2,1)S(1)} %shard_map.57.refs_3_), channel_id=1, source_target_pairs={{0,192},{8,56},{16,208},{24,8},{32,224},{40,24},{48,240},{56,40},{... | collective-permute-start | bytes 1572872 | tf_op jit(solution)/shard_map/ppermute | solution.py:204
  41.5 13.2 %collective-permute-start.6 = (bf16[2,2,256,256]{3,2,1,0:T(8,128)(2,1)S(1)}, bf16[2,2,256,256]{3,2,1,0:T(8,128)(2,1)S(1)}, u32[]{:S(2)}, u32[]{:S(2)}) collective-permute-start(bf16[2,2,256,256]{3,2,1,0:T(8,128)(2,1)S(1)} %shard_map.57.refs_3_), channel_id=1, source_target_pairs={{0,64},{8,24},{16,80},{24,40},{32,96},{40,56},{48,112},{56,8},{64,... | collective-permute-start | bytes 1572872 | tf_op jit(solution)/shard_map/ppermute | solution.py:204
  41.6 39.7 %copy-start.1 = (bf16[2,2,256,256]{3,2,1,0:T(8,128)(2,1)}, bf16[2,2,256,256]{3,2,1,0:T(8,128)(2,1)S(1)}, u32[]{:S(2)}) copy-start(bf16[2,2,256,256]{3,2,1,0:T(8,128)(2,1)S(1)} %shard_map.56.refs_0_) | copy-start | bytes 1572868
  41.6 13.1 %collective-permute-start.5 = (bf16[2,2,256,256]{3,2,1,0:T(8,128)(2,1)S(1)}, bf16[2,2,256,256]{3,2,1,0:T(8,128)(2,1)S(1)}, u32[]{:S(2)}, u32[]{:S(2)}) collective-permute-start(bf16[2,2,256,256]{3,2,1,0:T(8,128)(2,1)S(1)} %shard_map.56.refs_0_), channel_id=1, source_target_pairs={{0,192},{8,56},{16,208},{24,8},{32,224},{40,24},{48,240},{56,40},{... | collective-permute-start | bytes 1572872 | tf_op jit(solution)/shard_map/ppermute | solution.py:204
  44.3 12.3 %collective-permute-start.4 = (bf16[2,2,256,256]{3,2,1,0:T(8,128)(2,1)S(1)}, bf16[2,2,256,256]{3,2,1,0:T(8,128)(2,1)S(1)}, u32[]{:S(2)}, u32[]{:S(2)}) collective-permute-start(bf16[2,2,256,256]{3,2,1,0:T(8,128)(2,1)S(1)} %shard_map.56.refs_0_), channel_id=1, source_target_pairs={{0,64},{8,24},{16,80},{24,40},{32,96},{40,56},{48,112},{56,8},{64,... | collective-permute-start | bytes 1572872 | tf_op jit(solution)/shard_map/ppermute | solution.py:204
  44.3 10.3 %collective-permute-start.8 = (bf16[2,256,256]{2,1,0:T(8,128)(2,1)S(1)}, bf16[2,256,256]{2,1,0:T(8,128)(2,1)S(1)}, u32[]{:S(2)}, u32[]{:S(2)}) collective-permute-start(bf16[2,256,256]{2,1,0:T(8,128)(2,1)S(1)} %copy-done.9), channel_id=1, source_target_pairs={{0,8},{8,0},{16,24},{24,16},{32,40},{40,32},{48,56},{56,48},{64,72... | collective-permute-start | bytes 786440 | tf_op jit(solution)/shard_map/ppermute | solution.py:207
  54.7 26.7 %copy-start.8 = (bf16[2,256,256]{2,1,0:T(8,128)(2,1)}, bf16[2,256,256]{2,1,0:T(8,128)(2,1)S(1)}, u32[]{:S(2)}) copy-start(bf16[2,256,256]{2,1,0:T(8,128)(2,1)S(1)} %collective-permute-done.8.refs_11_) | copy-start | bytes 786436
  54.7 2.0 %copy-start.3 = (bf16[2,2,256,256]{3,2,1,0:T(8,128)(2,1)}, bf16[2,2,256,256]{3,2,1,0:T(8,128)(2,1)S(1)}, u32[]{:S(2)}) copy-start(bf16[2,2,256,256]{3,2,1,0:T(8,128)(2,1)S(1)} %collective-permute-done.7.refs_5_) | copy-start | bytes 1572868
  54.7 4.7 %copy-start.4 = (bf16[2,2,256,256]{3,2,1,0:T(8,128)(2,1)}, bf16[2,2,256,256]{3,2,1,0:T(8,128)(2,1)S(1)}, u32[]{:S(2)}) copy-start(bf16[2,2,256,256]{3,2,1,0:T(8,128)(2,1)S(1)} %collective-permute-done.6.refs_4_) | copy-start | bytes 1572868
  54.7 11.2 %copy-start.5 = (bf16[2,2,256,256]{3,2,1,0:T(8,128)(2,1)}, bf16[2,2,256,256]{3,2,1,0:T(8,128)(2,1)S(1)}, u32[]{:S(2)}) copy-start(bf16[2,2,256,256]{3,2,1,0:T(8,128)(2,1)S(1)} %collective-permute-done.5.refs_2_) | copy-start | bytes 1572868
  56.7 9.2 %copy-start.6 = (bf16[2,2,256,256]{3,2,1,0:T(8,128)(2,1)}, bf16[2,2,256,256]{3,2,1,0:T(8,128)(2,1)S(1)}, u32[]{:S(2)}) copy-start(bf16[2,2,256,256]{3,2,1,0:T(8,128)(2,1)S(1)} %collective-permute-done.4.refs_1_) | copy-start | bytes 1572868
  56.7 9.2 %collective-permute-start.9 = (bf16[2,2,256,256]{3,2,1,0:T(8,128)(2,1)S(1)}, bf16[2,2,256,256]{3,2,1,0:T(8,128)(2,1)S(1)}, u32[]{:S(2)}, u32[]{:S(2)}) collective-permute-start(bf16[2,2,256,256]{3,2,1,0:T(8,128)(2,1)S(1)} %collective-permute-done.4.refs_1_), channel_id=1, source_target_pairs={{0,64},{8,24},{16,80},{24,40},{32,96},{40,56},{48,112},{56,8},{64,... | collective-permute-start | bytes 1572872 | tf_op jit(solution)/shard_map/ppermute | solution.py:204
  56.7 10.0 %collective-permute-start.10 = (bf16[2,2,256,256]{3,2,1,0:T(8,128)(2,1)S(1)}, bf16[2,2,256,256]{3,2,1,0:T(8,128)(2,1)}, u32[]{:S(2)}, u32[]{:S(2)}) collective-permute-start(bf16[2,2,256,256]{3,2,1,0:T(8,128)(2,1)S(1)} %collective-permute-done.7.refs_5_), channel_id=1, source_target_pairs={{0,192},{8,56},{16,208},{24,8},{32,224},{40,24},{48,240},{56,40},{... | collective-permute-start | bytes 1572872 | tf_op jit(solution)/shard_map/ppermute | solution.py:204
  65.9 0.8 copy-start.7
  66.7 14.6 %collective-permute-start.11 = (bf16[8,2,256,256]{3,2,1,0:T(8,128)(2,1)}, bf16[8,2,256,256]{3,2,1,0:T(8,128)(2,1)S(1)}, u32[]{:S(2)}, u32[]{:S(2)}) collective-permute-start(bf16[8,2,256,256]{3,2,1,0:T(8,128)(2,1)} %bitcast.3), channel_id=1, source_target_pairs={{0,8},{8,0},{16,24},{24,16},{32,40},{40,32},{48,56},{56,48},{64,72... | collective-permute-start | bytes 6291464 | tf_op jit(solution)/shard_map/ppermute | solution.py:207
  81.3 1.3 copy-start.2
Sparse Core Ops, SparseCore 0:
  9.1 43.7 all-gather.2

commit v12 on v10

--- a/solution.py
+++ b/solution.py
@@ -28,14 +28,14 @@
         copy.wait()
 
 
-def stack(*pieces):
+def stack(*pieces, limit=1):
     return pl.pallas_call(
         stack_kernel,
         out_shape=jax.ShapeDtypeStruct((len(pieces), *pieces[0].shape), pieces[0].dtype),
         in_specs=[ANYWHERE] * len(pieces),
         out_specs=ANYWHERE,
         scratch_shapes=[pltpu.SemaphoreType.DMA((len(pieces),))],
-        compiler_params=pltpu.CompilerParams(vmem_limit_bytes=MIB),
+        compiler_params=pltpu.CompilerParams(vmem_limit_bytes=limit * MIB),
     )(*pieces)
 
 
@@ -104,8 +104,18 @@
     for copy in first + coming:
         copy.start()
     total[...] = jnp.zeros_like(total)
-    for copy in first:
-        copy.wait()
+    some = ranks // 2
+    for a in range(2):
+        first[a].wait()
+        first[2 + a].wait()
+        for b in range(2):
+            for part in range(0, ranks, some):
+                block = left_held[a, part : part + some].reshape(some * 2 * left_dim, left_dim)
+                product = jnp.dot(block, psi_held[a, b], preferred_element_type=jnp.float32)
+                product = product.astype(middle.dtype).reshape(some, 2, left_dim, right_dim)
+                for w in range(2):
+                    columns = slice(w * right_dim, (w + 1) * right_dim)
+                    middle[b, part : part + some, a * left_dim : (a + 1) * left_dim, columns] = product[:, w]
     for i, (far, start) in enumerate(pieces):
         coming[i].wait()
         for k in range(held.shape[1]):
@@ -113,16 +123,8 @@
             y = jnp.where(core == 0, y0 + far, y0 + near) & (SIDE - 1)
             x = jnp.where(core == 0, x0 + near, x0 + far) & (SIDE - 1)
             which, pair = y // 2, (x + SIDE * (y & 1) - rank) & (ranks - 1)
-            for a in range(2):
-                block = left_held[a, pair].reshape(2 * left_dim, left_dim)
-                product = jnp.dot(block, psi_held[a, which], preferred_element_type=jnp.float32)
-                product = product.astype(middle.dtype)
-                for w in range(2):
-                    middle[k % 2, a * left_dim : (a + 1) * left_dim, w * right_dim : (w + 1) * right_dim] = (
-                        product[w * left_dim : (w + 1) * left_dim]
-                    )
             shard = held[i, k].reshape(2 * right_dim, right_dim)
-            total[which] += jnp.dot(middle[k % 2], shard, preferred_element_type=jnp.float32)
+            total[which] += jnp.dot(middle[which, pair], shard, preferred_element_type=jnp.float32)
     row = lax.broadcasted_iota(jnp.int32, (left_dim, right_dim), 0)
     col = lax.broadcasted_iota(jnp.int32, (left_dim, right_dim), 1)
     for b in range(2):
@@ -149,7 +151,7 @@
             pltpu.VMEM((len(shards), *shards[0].shape), dtype),
             pltpu.VMEM((2, ranks, *own.shape[1:]), dtype),
             pltpu.VMEM((2, *psi.shape), dtype),
-            pltpu.VMEM((2, 2 * left_dim, pair * right_dim), dtype),
+            pltpu.VMEM((2, ranks, 2 * left_dim, pair * right_dim), dtype),
             pltpu.SemaphoreType.DMA((len(shards) + 4,)),
         ],
         compiler_params=pltpu.CompilerParams(vmem_limit_bytes=60 * MIB),
@@ -223,22 +225,19 @@
     own = lax.ppermute(right_env, ("blk", "mpo"), turn)
     up1, down1 = up(left_env), down(left_env)
     keep, give = cut(wavefunction, left_sizes, right_sizes)
-    own, keep, give = together(own, keep, give)
+    up2, down2 = up(up1), down(down1)
+    own, keep, give, up2, down2 = together(own, keep, give, up2, down2)
 
     below, above, two = near_step(own, 1), near_step(own, -1), near_step(own, 2)
-    below, above, two, up1, down1 = together(below, above, two, up1, down1)
+    up3, down3 = up(up2), down(down2)
+    below, above, two, up3, down3 = together(below, above, two, up3, down3)
     line_a, line_b = stack(own, below), stack(above, two)
     a_below, a_above = far_step(line_a, 1), far_step(line_a, -1)
     b_below, b_above = far_step(line_b, 1), far_step(line_b, -1)
-    up2, down2 = up(up1), down(down1)
-    up3, down3 = up(up2), down(down2)
-    a_below, a_above, b_below, b_above, up3, down3 = together(
-        a_below, a_above, b_below, b_above, up3, down3
-    )
+    up4 = up(up3)
+    a_below, a_above, b_below, b_above, up4 = together(a_below, a_above, b_below, b_above, up4)
     a_two, b_two = far_step(a_below, 1), far_step(b_above, -1)
-    up4 = up(up3)
-    lefts = stack(left_env, down1, down2, down3, up4, up3, up2, up1, give)
-    lefts, a_two, b_two = together(lefts, a_two, b_two)
+    lefts = stack(left_env, down1, down2, down3, up4, up3, up2, up1, give, limit=60)
     others = swap(lefts)
 
     pieces = ((0, 0), (SIDE - 1, 0), (1, 0), (0, 2), (SIDE - 1, 2), (1, 2), (2, 0), (2, 2))

time: 130 us -> 199 us (1.53)
  Pallas kernels: 15.3 us -> 86.3 us
  starting transfers between devices: 50 us -> 33.3 us
  waiting for transfers between devices: 27.1 us -> 37.6 us
  blocking collectives: 33 us -> 36.7 us
    pallas_call x3, Pallas kernels: 0.37 us -> 72.8 us  [stack(): pl.pallas_call(stack_kernel, out_shape=jax.ShapeDtypeStruct((len(pieces),...]
    ppermute x6, waiting for transfers between devices: 2.34 us -> 11.8 us  [far_step(): return lax.ppermute(block, 'blk', step(True, by))]
    ppermute x3, waiting for transfers between devices: 0.01 us -> 6.28 us  [near_step(): return lax.ppermute(block, 'blk', step(False, by))]
    ppermute x1, starting transfers between devices: 10.2 us -> 5 us  [swap(): return lax.ppermute(block, 'blk', [(i, i ^ 1) for i in range(sectors)])]
    ppermute x1, waiting for transfers between devices: 4.29 us -> 0.01 us  [swap(): return lax.ppermute(block, 'blk', [(i, i ^ 1) for i in range(sectors)])]
    ppermute x1, starting transfers between devices: 9.77 us -> 5.9 us  [local(): own = lax.ppermute(right_env, ('blk', 'mpo'), turn)]
    ppermute x3, waiting for transfers between devices: 3.85 us -> 0.01 us  [down(): lax.ppermute(block, 'mpo', [(z, (z - 1) % ranks) for z in range(ranks)])]
    ppermute x6, starting transfers between devices: 9.57 us -> 5.76 us  [far_step(): return lax.ppermute(block, 'blk', step(True, by))]
  transfers between devices with their start and end apart: 18 -> 18, of which waited for: 7 -> 9; matrix products, arithmetic and copies ran while one was open for 0% -> 0% of each run, Pallas kernels for 2% -> 1%
where the time goes in v12:
time: 199 us; the launch traced here: 198 us
  Pallas kernels  86.3 us (43%)
  waiting for transfers between devices  37.6 us (19%)
  blocking collectives  36.7 us (18%)
  starting transfers between devices  33.3 us (17%)
  local copies, waits for them, and re-layouts  3.35 us (2%)
    pallas_call x3, Pallas kernels, stack(): pl.pallas_call(stack_kernel, out_shape=jax.ShapeDtypeStruct((len(pieces),...  72.8 us
    all_to_all x1, blocking collectives, local(): by_plane = lax.all_to_all(done, 'mpo', 0, 0)  23.2 us
    ppermute x4, waiting for transfers between devices, up(): lax.ppermute(block, 'mpo', [(z, (z + 1) % ranks) for z in range(ranks)])  19.5 us
    all_to_all x1, blocking collectives, local(): out = order(lax.all_to_all(by_plane, 'blk', 0, 0, axis_index_groups=groups))  13.6 us
    ppermute x6, waiting for transfers between devices, far_step(): return lax.ppermute(block, 'blk', step(True, by))  11.8 us
    pallas_call x1, Pallas kernels, apply(): pl.pallas_call(functools.partial(apply_kernel, pieces), out_shape=jax.Sha...  9.95 us
    ppermute x3, starting transfers between devices, down(): lax.ppermute(block, 'mpo', [(z, (z - 1) % ranks) for z in range(ranks)])  8.99 us
    ppermute x3, waiting for transfers between devices, near_step(): return lax.ppermute(block, 'blk', step(False, by))  6.28 us
  transfers between devices with their start and end apart: 18, of which 9 were waited for; matrix products, arithmetic and copies ran while one was open for 0% of the time, Pallas kernels for 1%

profile of v12, /device:TPU:1, one launch (start us, length us, event | category | flops | bytes accessed | tf_op | source)
XLA Modules:
  0.0 197.7 jit_solution(16190729845847406888)
XLA Ops:
  0.0 2.5 %collective-permute-start.1 = (bf16[2,256,256]{2,1,0:T(8,128)(2,1)}, bf16[2,256,256]{2,1,0:T(8,128)(2,1)S(1)}, u32[]{:S(2)}, u32[]{:S(2)}) collective-permute-start(bf16[2,256,256]{2,1,0:T(8,128)(2,1)} %refs_0_.1), channel_id=1, source_target_pairs={{0,1},{1,2},{2,3},{3,4},{4,5},{5,6},{6,7},{7,0},{8,9},{9,10},{10,1... | collective-permute-start | bytes 786440 | tf_op jit(solution)/shard_map/ppermute | solution.py:212
  2.5 3.9 %collective-permute-start.3 = (bf16[2,256,256]{2,1,0:T(8,128)(2,1)}, bf16[2,256,256]{2,1,0:T(8,128)(2,1)S(1)}, u32[]{:S(2)}, u32[]{:S(2)}) collective-permute-start(bf16[2,256,256]{2,1,0:T(8,128)(2,1)} %refs_0_.1), channel_id=1, source_target_pairs={{0,7},{1,0},{2,1},{3,2},{4,3},{5,4},{6,5},{7,6},{8,15},{9,8},{10,9... | collective-permute-start | bytes 786440 | tf_op jit(solution)/shard_map/ppermute | solution.py:215
  6.4 5.9 %collective-permute-start = (bf16[2,256,256]{2,1,0:T(8,128)(2,1)}, bf16[2,256,256]{2,1,0:T(8,128)(2,1)S(1)}, u32[]{:S(2)}, u32[]{:S(2)}) collective-permute-start(bf16[2,256,256]{2,1,0:T(8,128)(2,1)} %param.7), channel_id=1, source_target_pairs={{0,0},{1,16},{2,32},{3,48},{4,64},{5,80},{6,96},{7,112},{8,12},{9,... | collective-permute-start | bytes 786440 | tf_op jit(solution)/shard_map/ppermute | solution.py:225
  12.3 0.3 collective-permute-done.1.refs_7_
  12.6 1.0 collective-permute-start.2
  13.6 0.0 collective-permute-done.3.refs_1_
  13.6 0.0 copy-start.9
  13.6 2.4 %collective-permute-start.4 = (bf16[2,256,256]{2,1,0:T(8,128)(2,1)S(1)}, bf16[2,256,256]{2,1,0:T(8,128)(2,1)S(1)}, u32[]{:S(2)}, u32[]{:S(2)}) collective-permute-start(bf16[2,256,256]{2,1,0:T(8,128)(2,1)S(1)} %collective-permute-done.3.refs_1_), channel_id=1, source_target_pairs={{0,7},{1,0},{2,1},{3,2},{4,3},{5,4},{6,5},{7,6},{8,15},{9,8},{10,9... | collective-permute-start | bytes 786440 | tf_op jit(solution)/shard_map/ppermute | solution.py:215
  16.0 2.7 %shard_map.55 = (bf16[2,256,256]{2,1,0:T(8,128)(2,1)}, bf16[2,256,256]{2,1,0:T(8,128)(2,1)}) custom-call(s32[32]{0:T(128)} %left_sizes.3, s32[32]{0:T(128)} %right_sizes.3, bf16[256,8192]{1,0:T(8,128)(2,1)} %psi_ref.1), custom_call_target="tpu_custom_call" | custom-call | tf_op jit(solution)/shard_map/pallas_call | solution.py:76
  18.7 0.0 collective-permute-done.refs_0_
  18.7 12.5 %collective-permute-done.2.refs_6_ = bf16[2,256,256]{2,1,0:T(8,128)(2,1)S(1)} collective-permute-done((bf16[2,256,256]{2,1,0:T(8,128)(2,1)S(1)}, bf16[2,256,256]{2,1,0:T(8,128)(2,1)S(1)}, u32[]{:S(2)}, u32[]{:S(2)}) %collective-permute-start.2) | collective-permute-done | bytes 262176 | tf_op jit(solution)/shard_map/ppermute | solution.py:212
  31.2 0.0 collective-permute-done.4.refs_2_
  31.2 0.1 collective-permute-start.8
  31.3 2.7 %collective-permute-start.9 = (bf16[2,256,256]{2,1,0:T(8,128)(2,1)S(1)}, bf16[2,256,256]{2,1,0:T(8,128)(2,1)S(1)}, u32[]{:S(2)}, u32[]{:S(2)}) collective-permute-start(bf16[2,256,256]{2,1,0:T(8,128)(2,1)S(1)} %collective-permute-done.4.refs_2_), channel_id=1, source_target_pairs={{0,7},{1,0},{2,1},{3,2},{4,3},{5,4},{6,5},{7,6},{8,15},{9,8},{10,9... | collective-permute-start | bytes 786440 | tf_op jit(solution)/shard_map/ppermute | solution.py:215
  34.0 2.6 %collective-permute-start.7 = (bf16[2,256,256]{2,1,0:T(8,128)(2,1)S(1)}, bf16[2,256,256]{2,1,0:T(8,128)(2,1)S(1)}, u32[]{:S(2)}, u32[]{:S(2)}) collective-permute-start(bf16[2,256,256]{2,1,0:T(8,128)(2,1)S(1)} %collective-permute-done.refs_0_), channel_id=1, source_target_pairs={{0,32},{8,136},{16,48},{24,152},{32,0},{40,168},{48,16},{56,184},{... | collective-permute-start | bytes 786440 | tf_op jit(solution)/shard_map/ppermute | solution.py:203
  36.6 1.0 collective-permute-start.6
  37.6 0.4 collective-permute-start.5
  38.0 0.0 collective-permute-done.8.refs_5_
  38.0 0.0 collective-permute-done.9.refs_3_
  38.1 0.0 copy-start.13
  38.1 2.6 %collective-permute-done.7.refs_1_ = bf16[2,256,256]{2,1,0:T(8,128)(2,1)S(1)} collective-permute-done((bf16[2,256,256]{2,1,0:T(8,128)(2,1)S(1)}, bf16[2,256,256]{2,1,0:T(8,128)(2,1)S(1)}, u32[]{:S(2)}, u32[]{:S(2)}) %collective-permute-start.7) | collective-permute-done | bytes 262176 | tf_op jit(solution)/shard_map/ppermute | solution.py:203
  40.7 3.5 %collective-permute-done.6.refs_0_ = bf16[2,256,256]{2,1,0:T(8,128)(2,1)S(1)} collective-permute-done((bf16[2,256,256]{2,1,0:T(8,128)(2,1)S(1)}, bf16[2,256,256]{2,1,0:T(8,128)(2,1)S(1)}, u32[]{:S(2)}, u32[]{:S(2)}) %collective-permute-start.6) | collective-permute-done | bytes 262176 | tf_op jit(solution)/shard_map/ppermute | solution.py:203
  44.1 0.2 collective-permute-done.5.refs_1_
  44.4 0.1 shard_map.57.refs_3_
  44.4 0.0 copy-done.8
  44.4 0.0 copy-done.9
  44.4 0.0 copy-start
  44.4 0.2 collective-permute-start.13
  44.6 1.3 collective-permute-start.12
  46.0 0.1 shard_map.56.refs_0_
  46.1 0.0 copy-start.1
  46.1 1.4 collective-permute-start.11
  47.5 0.1 collective-permute-start.10
  47.6 0.0 collective-permute-start.14
  47.6 6.7 %collective-permute-done.14.refs_4_ = bf16[2,256,256]{2,1,0:T(8,128)(2,1)S(1)} collective-permute-done((bf16[2,256,256]{2,1,0:T(8,128)(2,1)S(1)}, bf16[2,256,256]{2,1,0:T(8,128)(2,1)S(1)}, u32[]{:S(2)}, u32[]{:S(2)}) %collective-permute-start.14) | collective-permute-done | bytes 262176 | tf_op jit(solution)/shard_map/ppermute | solution.py:212
  54.3 0.0 collective-permute-done.13.refs_5_
  54.3 0.0 collective-permute-done.12.refs_4_
  54.4 0.0 copy-start.4
  54.4 4.1 %collective-permute-done.11.refs_2_ = bf16[2,2,256,256]{3,2,1,0:T(8,128)(2,1)S(1)} collective-permute-done((bf16[2,2,256,256]{3,2,1,0:T(8,128)(2,1)S(1)}, bf16[2,2,256,256]{3,2,1,0:T(8,128)(2,1)S(1)}, u32[]{:S(2)}, u32[]{:S(2)}) %collective-permute-start.11) | collective-permute-done | bytes 524320 | tf_op jit(solution)/shard_map/ppermute | solution.py:206
  58.5 0.0 copy-done.3
  58.5 0.0 copy-done.4
  58.5 0.8 copy-done.5
  59.3 0.6 collective-permute-done.10.refs_1_
  59.9 0.0 copy-done.10
  59.9 0.0 copy-done.11
  59.9 0.0 copy-done.12
  59.9 0.0 copy-done.13
  59.9 0.0 copy-done.14
  59.9 72.7 %shard_map.58.refs_8_ = bf16[9,2,256,256]{3,2,1,0:T(8,128)(2,1)} custom-call(bf16[2,256,256]{2,1,0:T(8,128)(2,1)} %refs_0_.1, bf16[2,256,256]{2,1,0:T(8,128)(2,1)} %copy-done.9, bf16[2,256,256]{2,1,0:T(8,128)(2,1)} %copy-done.11, bf16[2,256,256]{2,1,0:T(8,128)(2,1)} %copy-done.13, bf16[2,256,256]{2,1,0:T(8,128)(2,1)} %copy-done.14, ...), custom_call_target="tpu_custom_call" | custom-call | tf_op jit(solution)/shard_map/pallas_call | solution.py:32
  132.6 0.0 copy-done
  132.6 0.0 copy-done.1
  132.6 5.0 %collective-permute-start.17 = (bf16[9,2,256,256]{3,2,1,0:T(8,128)(2,1)}, bf16[9,2,256,256]{3,2,1,0:T(8,128)(2,1)S(1)}, u32[]{:S(2)}, u32[]{:S(2)}) collective-permute-start(bf16[9,2,256,256]{3,2,1,0:T(8,128)(2,1)} %shard_map.58.refs_8_), channel_id=1, source_target_pairs={{0,8},{8,0},{16,24},{24,16},{32,40},{40,32},{48,56},{56,48},{64,72... | collective-permute-start | bytes 7077896 | tf_op jit(solution)/shard_map/ppermute | solution.py:209
  137.6 0.7 collective-permute-start.15
  138.3 1.9 collective-permute-start.16
  140.3 7.1 %collective-permute-done.15.refs_6_ = bf16[2,2,256,256]{3,2,1,0:T(8,128)(2,1)S(1)} collective-permute-done((bf16[2,2,256,256]{3,2,1,0:T(8,128)(2,1)}, bf16[2,2,256,256]{3,2,1,0:T(8,128)(2,1)S(1)}, u32[]{:S(2)}, u32[]{:S(2)}) %collective-permute-start.15) | collective-permute-done | bytes 524320 | tf_op jit(solution)/shard_map/ppermute | solution.py:206
  147.4 0.0 collective-permute-done.16.refs_7_
  147.4 0.0 collective-permute-done.17.refs_9_
  147.4 0.8 copy-done.6
  148.2 0.3 copy-done.7
  148.4 1.4 copy-done.2
  149.9 9.9 %shard_map.59 = bf16[8,2,2,32,256]{4,3,2,1,0:T(8,128)(2,1)} custom-call(s32[32]{0:T(128)} %left_sizes.3, s32[32]{0:T(128)} %right_sizes.3, bf16[2,2,256,256]{3,2,1,0:T(8,128)(2,1)} %copy-done.1, bf16[2,2,256,256]{3,2,1,0:T(8,128)(2,1)} %collective-permute-done.10.refs_1_, bf16[2,2,256,256]{3,2,1,0:T(8,128)(2,1)} %copy-done.5, ...), custom_call_target="tpu_custom_call" | custom-call | tf_op jit(solution)/shard_map/pallas_call | solution.py:144
  159.8 23.2 %all_to_all.10 = bf16[8,2,2,32,256]{4,3,2,1,0:T(8,128)(2,1)S(1)} all-to-all(bf16[8,2,2,32,256]{4,3,2,1,0:T(8,128)(2,1)} %shard_map.59), channel_id=1, replica_groups=mesh['blk'=32,'mpo'=8] {'mpo'}, dimensions={0} | all-to-all | bytes 1048576 | tf_op jit(solution)/shard_map/all_to_all | solution.py:247
  183.0 13.6 %all_to_all.11.in_ref = bf16[16,2,32,256]{3,2,1,0:T(8,128)(2,1)S(1)} all-to-all(bf16[16,2,32,256]{3,2,1,0:T(8,128)(2,1)S(1)} %bitcast.2), channel_id=1, replica_groups={{0,128,16,144,32,160,48,176,64,192,80,208,96,224,112,240},{72,200,88,21..., dimensions={0} | all-to-all | bytes 1048576 | tf_op jit(solution)/shard_map/all_to_all | solution.py:254
  196.6 0.9 shard_map.60
  (10 shorter events, 0.0 us)
Async XLA Ops:
  0.0 12.6 %collective-permute-start.1 = (bf16[2,256,256]{2,1,0:T(8,128)(2,1)}, bf16[2,256,256]{2,1,0:T(8,128)(2,1)S(1)}, u32[]{:S(2)}, u32[]{:S(2)}) collective-permute-start(bf16[2,256,256]{2,1,0:T(8,128)(2,1)} %refs_0_.1), channel_id=1, source_target_pairs={{0,1},{1,2},{2,3},{3,4},{4,5},{5,6},{6,7},{7,0},{8,9},{9,10},{10,1... | collective-permute-start | bytes 786440 | tf_op jit(solution)/shard_map/ppermute | solution.py:212
  2.5 11.2 %collective-permute-start.3 = (bf16[2,256,256]{2,1,0:T(8,128)(2,1)}, bf16[2,256,256]{2,1,0:T(8,128)(2,1)S(1)}, u32[]{:S(2)}, u32[]{:S(2)}) collective-permute-start(bf16[2,256,256]{2,1,0:T(8,128)(2,1)} %refs_0_.1), channel_id=1, source_target_pairs={{0,7},{1,0},{2,1},{3,2},{4,3},{5,4},{6,5},{7,6},{8,15},{9,8},{10,9... | collective-permute-start | bytes 786440 | tf_op jit(solution)/shard_map/ppermute | solution.py:215
  6.4 12.3 %collective-permute-start = (bf16[2,256,256]{2,1,0:T(8,128)(2,1)}, bf16[2,256,256]{2,1,0:T(8,128)(2,1)S(1)}, u32[]{:S(2)}, u32[]{:S(2)}) collective-permute-start(bf16[2,256,256]{2,1,0:T(8,128)(2,1)} %param.7), channel_id=1, source_target_pairs={{0,0},{1,16},{2,32},{3,48},{4,64},{5,80},{6,96},{7,112},{8,12},{9,... | collective-permute-start | bytes 786440 | tf_op jit(solution)/shard_map/ppermute | solution.py:225
  12.6 31.8 %copy-start.8 = (bf16[2,256,256]{2,1,0:T(8,128)(2,1)}, bf16[2,256,256]{2,1,0:T(8,128)(2,1)S(1)}, u32[]{:S(2)}) copy-start(bf16[2,256,256]{2,1,0:T(8,128)(2,1)S(1)} %collective-permute-done.1.refs_7_) | copy-start | bytes 786436
  12.6 18.5 %collective-permute-start.2 = (bf16[2,256,256]{2,1,0:T(8,128)(2,1)S(1)}, bf16[2,256,256]{2,1,0:T(8,128)(2,1)S(1)}, u32[]{:S(2)}, u32[]{:S(2)}) collective-permute-start(bf16[2,256,256]{2,1,0:T(8,128)(2,1)S(1)} %collective-permute-done.1.refs_7_), channel_id=1, source_target_pairs={{0,1},{1,2},{2,3},{3,4},{4,5},{5,6},{6,7},{7,0},{8,9},{9,10},{10,1... | collective-permute-start | bytes 786440 | tf_op jit(solution)/shard_map/ppermute | solution.py:212
  13.6 30.8 %copy-start.9 = (bf16[2,256,256]{2,1,0:T(8,128)(2,1)}, bf16[2,256,256]{2,1,0:T(8,128)(2,1)S(1)}, u32[]{:S(2)}) copy-start(bf16[2,256,256]{2,1,0:T(8,128)(2,1)S(1)} %collective-permute-done.3.refs_1_) | copy-start | bytes 786436
  13.6 17.6 %collective-permute-start.4 = (bf16[2,256,256]{2,1,0:T(8,128)(2,1)S(1)}, bf16[2,256,256]{2,1,0:T(8,128)(2,1)S(1)}, u32[]{:S(2)}, u32[]{:S(2)}) collective-permute-start(bf16[2,256,256]{2,1,0:T(8,128)(2,1)S(1)} %collective-permute-done.3.refs_1_), channel_id=1, source_target_pairs={{0,7},{1,0},{2,1},{3,2},{4,3},{5,4},{6,5},{7,6},{8,15},{9,8},{10,9... | collective-permute-start | bytes 786440 | tf_op jit(solution)/shard_map/ppermute | solution.py:215
  31.2 28.7 %copy-start.10 = (bf16[2,256,256]{2,1,0:T(8,128)(2,1)}, bf16[2,256,256]{2,1,0:T(8,128)(2,1)S(1)}, u32[]{:S(2)}) copy-start(bf16[2,256,256]{2,1,0:T(8,128)(2,1)S(1)} %collective-permute-done.2.refs_6_) | copy-start | bytes 786436
  31.2 28.7 %copy-start.11 = (bf16[2,256,256]{2,1,0:T(8,128)(2,1)}, bf16[2,256,256]{2,1,0:T(8,128)(2,1)S(1)}, u32[]{:S(2)}) copy-start(bf16[2,256,256]{2,1,0:T(8,128)(2,1)S(1)} %collective-permute-done.4.refs_2_) | copy-start | bytes 786436
  31.2 6.8 %collective-permute-start.8 = (bf16[2,256,256]{2,1,0:T(8,128)(2,1)S(1)}, bf16[2,256,256]{2,1,0:T(8,128)(2,1)S(1)}, u32[]{:S(2)}, u32[]{:S(2)}) collective-permute-start(bf16[2,256,256]{2,1,0:T(8,128)(2,1)S(1)} %collective-permute-done.2.refs_6_), channel_id=1, source_target_pairs={{0,1},{1,2},{2,3},{3,4},{4,5},{5,6},{6,7},{7,0},{8,9},{9,10},{10,1... | collective-permute-start | bytes 786440 | tf_op jit(solution)/shard_map/ppermute | solution.py:212
  31.3 6.8 %collective-permute-start.9 = (bf16[2,256,256]{2,1,0:T(8,128)(2,1)S(1)}, bf16[2,256,256]{2,1,0:T(8,128)(2,1)S(1)}, u32[]{:S(2)}, u32[]{:S(2)}) collective-permute-start(bf16[2,256,256]{2,1,0:T(8,128)(2,1)S(1)} %collective-permute-done.4.refs_2_), channel_id=1, source_target_pairs={{0,7},{1,0},{2,1},{3,2},{4,3},{5,4},{6,5},{7,6},{8,15},{9,8},{10,9... | collective-permute-start | bytes 786440 | tf_op jit(solution)/shard_map/ppermute | solution.py:215
  34.0 6.7 %collective-permute-start.7 = (bf16[2,256,256]{2,1,0:T(8,128)(2,1)S(1)}, bf16[2,256,256]{2,1,0:T(8,128)(2,1)S(1)}, u32[]{:S(2)}, u32[]{:S(2)}) collective-permute-start(bf16[2,256,256]{2,1,0:T(8,128)(2,1)S(1)} %collective-permute-done.refs_0_), channel_id=1, source_target_pairs={{0,32},{8,136},{16,48},{24,152},{32,0},{40,168},{48,16},{56,184},{... | collective-permute-start | bytes 786440 | tf_op jit(solution)/shard_map/ppermute | solution.py:203
  36.6 7.6 %collective-permute-start.6 = (bf16[2,256,256]{2,1,0:T(8,128)(2,1)S(1)}, bf16[2,256,256]{2,1,0:T(8,128)(2,1)S(1)}, u32[]{:S(2)}, u32[]{:S(2)}) collective-permute-start(bf16[2,256,256]{2,1,0:T(8,128)(2,1)S(1)} %collective-permute-done.refs_0_), channel_id=1, source_target_pairs={{0,48},{8,200},{16,0},{24,216},{32,16},{40,232},{48,32},{56,248},{... | collective-permute-start | bytes 786440 | tf_op jit(solution)/shard_map/ppermute | solution.py:203
  37.6 6.7 %collective-permute-start.5 = (bf16[2,256,256]{2,1,0:T(8,128)(2,1)S(1)}, bf16[2,256,256]{2,1,0:T(8,128)(2,1)S(1)}, u32[]{:S(2)}, u32[]{:S(2)}) collective-permute-start(bf16[2,256,256]{2,1,0:T(8,128)(2,1)S(1)} %collective-permute-done.refs_0_), channel_id=1, source_target_pairs={{0,16},{8,72},{16,32},{24,88},{32,48},{40,104},{48,0},{56,120},{64... | collective-permute-start | bytes 786440 | tf_op jit(solution)/shard_map/ppermute | solution.py:203
  38.0 21.9 %copy-start.12 = (bf16[2,256,256]{2,1,0:T(8,128)(2,1)}, bf16[2,256,256]{2,1,0:T(8,128)(2,1)S(1)}, u32[]{:S(2)}) copy-start(bf16[2,256,256]{2,1,0:T(8,128)(2,1)S(1)} %collective-permute-done.8.refs_5_) | copy-start | bytes 786436
  38.1 21.9 %copy-start.13 = (bf16[2,256,256]{2,1,0:T(8,128)(2,1)}, bf16[2,256,256]{2,1,0:T(8,128)(2,1)S(1)}, u32[]{:S(2)}) copy-start(bf16[2,256,256]{2,1,0:T(8,128)(2,1)S(1)} %collective-permute-done.9.refs_3_) | copy-start | bytes 786436
  44.4 88.2 %copy-start = (bf16[2,2,256,256]{3,2,1,0:T(8,128)(2,1)}, bf16[2,2,256,256]{3,2,1,0:T(8,128)(2,1)S(1)}, u32[]{:S(2)}) copy-start(bf16[2,2,256,256]{3,2,1,0:T(8,128)(2,1)S(1)} %shard_map.57.refs_3_) | copy-start | bytes 1572868
  44.4 9.9 %collective-permute-start.13 = (bf16[2,2,256,256]{3,2,1,0:T(8,128)(2,1)S(1)}, bf16[2,2,256,256]{3,2,1,0:T(8,128)(2,1)S(1)}, u32[]{:S(2)}, u32[]{:S(2)}) collective-permute-start(bf16[2,2,256,256]{3,2,1,0:T(8,128)(2,1)S(1)} %shard_map.57.refs_3_), channel_id=1, source_target_pairs={{0,192},{8,56},{16,208},{24,8},{32,224},{40,24},{48,240},{56,40},{... | collective-permute-start | bytes 1572872 | tf_op jit(solution)/shard_map/ppermute | solution.py:206
  44.6 9.7 %collective-permute-start.12 = (bf16[2,2,256,256]{3,2,1,0:T(8,128)(2,1)S(1)}, bf16[2,2,256,256]{3,2,1,0:T(8,128)(2,1)S(1)}, u32[]{:S(2)}, u32[]{:S(2)}) collective-permute-start(bf16[2,2,256,256]{3,2,1,0:T(8,128)(2,1)S(1)} %shard_map.57.refs_3_), channel_id=1, source_target_pairs={{0,64},{8,24},{16,80},{24,40},{32,96},{40,56},{48,112},{56,8},{64,... | collective-permute-start | bytes 1572872 | tf_op jit(solution)/shard_map/ppermute | solution.py:206
  46.1 86.6 %copy-start.1 = (bf16[2,2,256,256]{3,2,1,0:T(8,128)(2,1)}, bf16[2,2,256,256]{3,2,1,0:T(8,128)(2,1)S(1)}, u32[]{:S(2)}) copy-start(bf16[2,2,256,256]{3,2,1,0:T(8,128)(2,1)S(1)} %shard_map.56.refs_0_) | copy-start | bytes 1572868
  46.1 12.4 %collective-permute-start.11 = (bf16[2,2,256,256]{3,2,1,0:T(8,128)(2,1)S(1)}, bf16[2,2,256,256]{3,2,1,0:T(8,128)(2,1)S(1)}, u32[]{:S(2)}, u32[]{:S(2)}) collective-permute-start(bf16[2,2,256,256]{3,2,1,0:T(8,128)(2,1)S(1)} %shard_map.56.refs_0_), channel_id=1, source_target_pairs={{0,192},{8,56},{16,208},{24,8},{32,224},{40,24},{48,240},{56,40},{... | collective-permute-start | bytes 1572872 | tf_op jit(solution)/shard_map/ppermute | solution.py:206
  47.5 12.4 %collective-permute-start.10 = (bf16[2,2,256,256]{3,2,1,0:T(8,128)(2,1)S(1)}, bf16[2,2,256,256]{3,2,1,0:T(8,128)(2,1)}, u32[]{:S(2)}, u32[]{:S(2)}) collective-permute-start(bf16[2,2,256,256]{3,2,1,0:T(8,128)(2,1)S(1)} %shard_map.56.refs_0_), channel_id=1, source_target_pairs={{0,64},{8,24},{16,80},{24,40},{32,96},{40,56},{48,112},{56,8},{64,... | collective-permute-start | bytes 1572872 | tf_op jit(solution)/shard_map/ppermute | solution.py:206
  47.6 6.7 %collective-permute-start.14 = (bf16[2,256,256]{2,1,0:T(8,128)(2,1)S(1)}, bf16[2,256,256]{2,1,0:T(8,128)(2,1)S(1)}, u32[]{:S(2)}, u32[]{:S(2)}) collective-permute-start(bf16[2,256,256]{2,1,0:T(8,128)(2,1)S(1)} %collective-permute-done.8.refs_5_), channel_id=1, source_target_pairs={{0,1},{1,2},{2,3},{3,4},{4,5},{5,6},{6,7},{7,0},{8,9},{9,10},{10,1... | collective-permute-start | bytes 786440 | tf_op jit(solution)/shard_map/ppermute | solution.py:212
  54.3 5.6 %copy-start.14 = (bf16[2,256,256]{2,1,0:T(8,128)(2,1)}, bf16[2,256,256]{2,1,0:T(8,128)(2,1)S(1)}, u32[]{:S(2)}) copy-start(bf16[2,256,256]{2,1,0:T(8,128)(2,1)S(1)} %collective-permute-done.14.refs_4_) | copy-start | bytes 786436
  54.3 4.1 %copy-start.3 = (bf16[2,2,256,256]{3,2,1,0:T(8,128)(2,1)}, bf16[2,2,256,256]{3,2,1,0:T(8,128)(2,1)S(1)}, u32[]{:S(2)}) copy-start(bf16[2,2,256,256]{3,2,1,0:T(8,128)(2,1)S(1)} %collective-permute-done.13.refs_5_) | copy-start | bytes 1572868
  54.4 4.1 %copy-start.4 = (bf16[2,2,256,256]{3,2,1,0:T(8,128)(2,1)}, bf16[2,2,256,256]{3,2,1,0:T(8,128)(2,1)S(1)}, u32[]{:S(2)}) copy-start(bf16[2,2,256,256]{3,2,1,0:T(8,128)(2,1)S(1)} %collective-permute-done.12.refs_4_) | copy-start | bytes 1572868
  58.5 0.8 copy-start.5
  132.6 14.8 %collective-permute-start.17 = (bf16[9,2,256,256]{3,2,1,0:T(8,128)(2,1)}, bf16[9,2,256,256]{3,2,1,0:T(8,128)(2,1)S(1)}, u32[]{:S(2)}, u32[]{:S(2)}) collective-permute-start(bf16[9,2,256,256]{3,2,1,0:T(8,128)(2,1)} %shard_map.58.refs_8_), channel_id=1, source_target_pairs={{0,8},{8,0},{16,24},{24,16},{32,40},{40,32},{48,56},{56,48},{64,72... | collective-permute-start | bytes 7077896 | tf_op jit(solution)/shard_map/ppermute | solution.py:209
  137.6 9.7 %collective-permute-start.15 = (bf16[2,2,256,256]{3,2,1,0:T(8,128)(2,1)}, bf16[2,2,256,256]{3,2,1,0:T(8,128)(2,1)S(1)}, u32[]{:S(2)}, u32[]{:S(2)}) collective-permute-start(bf16[2,2,256,256]{3,2,1,0:T(8,128)(2,1)} %collective-permute-done.10.refs_1_), channel_id=1, source_target_pairs={{0,64},{8,24},{16,80},{24,40},{32,96},{40,56},{48,112},{56,8},{64,... | collective-permute-start | bytes 1572872 | tf_op jit(solution)/shard_map/ppermute | solution.py:206
  138.3 9.0 %collective-permute-start.16 = (bf16[2,2,256,256]{3,2,1,0:T(8,128)(2,1)}, bf16[2,2,256,256]{3,2,1,0:T(8,128)(2,1)S(1)}, u32[]{:S(2)}, u32[]{:S(2)}) collective-permute-start(bf16[2,2,256,256]{3,2,1,0:T(8,128)(2,1)} %copy-done.3), channel_id=1, source_target_pairs={{0,192},{8,56},{16,208},{24,8},{32,224},{40,24},{48,240},{56,40},{... | collective-permute-start | bytes 1572872 | tf_op jit(solution)/shard_map/ppermute | solution.py:206
  147.4 0.8 copy-start.6
  147.4 1.1 copy-start.7
  148.4 1.4 copy-start.2

commit v13 on v11

--- a/solution.py
+++ b/solution.py
@@ -104,8 +104,18 @@
     for copy in first + coming:
         copy.start()
     total[...] = jnp.zeros_like(total)
-    for copy in first:
-        copy.wait()
+    some = ranks // 2
+    for a in range(2):
+        first[a].wait()
+        first[2 + a].wait()
+        for b in range(2):
+            for part in range(0, ranks, some):
+                block = left_held[a, part : part + some].reshape(some * 2 * left_dim, left_dim)
+                product = jnp.dot(block, psi_held[a, b], preferred_element_type=jnp.float32)
+                product = product.astype(middle.dtype).reshape(some, 2, left_dim, right_dim)
+                for w in range(2):
+                    columns = slice(w * right_dim, (w + 1) * right_dim)
+                    middle[b, part : part + some, a * left_dim : (a + 1) * left_dim, columns] = product[:, w]
     for i, (far, start) in enumerate(pieces):
         coming[i].wait()
         for k in range(held.shape[1]):
@@ -113,16 +123,8 @@
             y = jnp.where(core == 0, y0 + far, y0 + near) & (SIDE - 1)
             x = jnp.where(core == 0, x0 + near, x0 + far) & (SIDE - 1)
             which, pair = y // 2, x + SIDE * (y & 1)
-            for a in range(2):
-                block = left_held[a, pair].reshape(2 * left_dim, left_dim)
-                product = jnp.dot(block, psi_held[a, which], preferred_element_type=jnp.float32)
-                product = product.astype(middle.dtype)
-                for w in range(2):
-                    middle[k % 2, a * left_dim : (a + 1) * left_dim, w * right_dim : (w + 1) * right_dim] = (
-                        product[w * left_dim : (w + 1) * left_dim]
-                    )
             shard = held[i, k].reshape(2 * right_dim, right_dim)
-            total[which] += jnp.dot(middle[k % 2], shard, preferred_element_type=jnp.float32)
+            total[which] += jnp.dot(middle[which, pair], shard, preferred_element_type=jnp.float32)
     row = lax.broadcasted_iota(jnp.int32, (left_dim, right_dim), 0)
     col = lax.broadcasted_iota(jnp.int32, (left_dim, right_dim), 1)
     for b in range(2):
@@ -149,7 +151,7 @@
             pltpu.VMEM((len(shards), *shards[0].shape), dtype),
             pltpu.VMEM((2, ranks, *own.shape[1:]), dtype),
             pltpu.VMEM((2, *psi.shape), dtype),
-            pltpu.VMEM((2, 2 * left_dim, pair * right_dim), dtype),
+            pltpu.VMEM((2, ranks, 2 * left_dim, pair * right_dim), dtype),
             pltpu.SemaphoreType.DMA((len(shards) + 4,)),
         ],
         compiler_params=pltpu.CompilerParams(vmem_limit_bytes=60 * MIB),
@@ -217,17 +219,16 @@
     own = lax.ppermute(right_env, ("blk", "mpo"), turn)
     lefts = lax.all_gather(left_env, "mpo")
     keep, give = cut(wavefunction, left_sizes, right_sizes)
-    own, keep, give = together(own, keep, give)
+    got = swap(give)
+    own, keep, got = together(own, keep, got)
 
     below, above, two = near_step(own, 1), near_step(own, -1), near_step(own, 2)
     below, above, two = together(below, above, two)
     line_a, line_b = stack(own, below), stack(above, two)
     a_below, a_above = far_step(line_a, 1), far_step(line_a, -1)
     b_below, b_above = far_step(line_b, 1), far_step(line_b, -1)
-    got = swap(give)
-    a_below, a_above, b_below, b_above, got = together(a_below, a_above, b_below, b_above, got)
+    a_below, a_above, b_below, b_above, lefts = together(a_below, a_above, b_below, b_above, lefts)
     a_two, b_two = far_step(a_below, 1), far_step(b_above, -1)
-    lefts, a_two, b_two = together(lefts, a_two, b_two)
     others = swap(lefts)
 
     pieces = ((0, 0), (SIDE - 1, 0), (1, 0), (0, 2), (SIDE - 1, 2), (1, 2), (2, 0), (2, 2))

time: 141 us -> 136 us (0.965)
  starting transfers between devices: 48.9 us -> 38.1 us
  waiting for transfers between devices: 22.2 us -> 27.7 us
  Pallas kernels: 15.1 us -> 13.6 us
    ppermute x2, starting transfers between devices: 19.8 us -> 9.64 us  [swap(): return lax.ppermute(block, 'blk', [(i, i ^ 1) for i in range(sectors)])]
    ppermute x6, waiting for transfers between devices: 8.53 us -> 18.6 us  [far_step(): return lax.ppermute(block, 'blk', step(True, by))]
    ppermute x2, waiting for transfers between devices: 5.16 us -> 0.81 us  [swap(): return lax.ppermute(block, 'blk', [(i, i ^ 1) for i in range(sectors)])]
    all_to_all x1, blocking collectives: 12.2 us -> 14.1 us  [local(): out = order(lax.all_to_all(by_plane, 'blk', 0, 0, axis_index_groups=groups))]
    pallas_call x1, Pallas kernels: 11.4 us -> 9.95 us  [apply(): pl.pallas_call(functools.partial(apply_kernel, pieces), out_shape=jax.Sha...]
    unnamed x20 -> x16, local copies, waits for them, and re-layouts: 2.13 us -> 2.85 us
  transfers between devices with their start and end apart: 13 -> 13, of which waited for: 8 -> 9; matrix products, arithmetic and copies ran while one was open for 0% -> 0% of each run, Pallas kernels for 2% -> 2%
where the time goes in v13:
time: 136 us; the launch traced here: 134 us
  blocking collectives  38.5 us (28%)
  starting transfers between devices  38.1 us (28%)
  waiting for transfers between devices  27.7 us (20%)
  Pallas kernels  13.6 us (10%)
  between operations  13.5 us (10%)
  local copies, waits for them, and re-layouts  2.85 us (2%)
    all_to_all x1, blocking collectives, local(): by_plane = lax.all_to_all(done, 'mpo', 0, 0)  24.5 us
    ppermute x6, waiting for transfers between devices, far_step(): return lax.ppermute(block, 'blk', step(True, by))  18.6 us
    ppermute x6, starting transfers between devices, far_step(): return lax.ppermute(block, 'blk', step(True, by))  14.4 us
    all_to_all x1, blocking collectives, local(): out = order(lax.all_to_all(by_plane, 'blk', 0, 0, axis_index_groups=groups))  14.1 us
    pallas_call x1, Pallas kernels, apply(): pl.pallas_call(functools.partial(apply_kernel, pieces), out_shape=jax.Sha...  9.95 us
    ppermute x1, starting transfers between devices, local(): own = lax.ppermute(right_env, ('blk', 'mpo'), turn)  9.65 us
    ppermute x2, starting transfers between devices, swap(): return lax.ppermute(block, 'blk', [(i, i ^ 1) for i in range(sectors)])  9.64 us
    ppermute x3, waiting for transfers between devices, near_step(): return lax.ppermute(block, 'blk', step(False, by))  6.7 us
  transfers between devices with their start and end apart: 13, of which 9 were waited for; matrix products, arithmetic and copies ran while one was open for 0% of the time, Pallas kernels for 2%

profile of v13, /device:TPU:1, one launch (start us, length us, event | category | flops | bytes accessed | tf_op | source)
XLA Modules:
  0.0 134.3 jit_solution(14377655563912669765)
XLA Ops:
  6.5 0.0 all-gather.3.cloned.1.call-start
  6.5 0.7 all-gather.3.cloned.1.call-update
  7.3 9.6 %collective-permute-start = (bf16[2,256,256]{2,1,0:T(8,128)(2,1)}, bf16[2,256,256]{2,1,0:T(8,128)(2,1)S(1)}, u32[]{:S(2)}, u32[]{:S(2)}) collective-permute-start(bf16[2,256,256]{2,1,0:T(8,128)(2,1)} %param.7), channel_id=1, source_target_pairs={{0,0},{1,16},{2,32},{3,48},{4,64},{5,80},{6,96},{7,112},{8,12},{9,... | collective-permute-start | bytes 786440 | tf_op jit(solution)/shard_map/ppermute | solution.py:219
  16.9 2.6 %shard_map.55 = (bf16[2,256,256]{2,1,0:T(8,128)(2,1)}, bf16[2,256,256]{2,1,0:T(8,128)(2,1)}) custom-call(s32[32]{0:T(128)} %left_sizes.3, s32[32]{0:T(128)} %right_sizes.3, bf16[256,8192]{1,0:T(8,128)(2,1)} %psi_ref.1), custom_call_target="tpu_custom_call" | custom-call | tf_op jit(solution)/shard_map/pallas_call | solution.py:76
  19.5 0.1 collective-permute-start.1
  19.6 0.9 collective-permute-done.refs_0_
  20.6 0.8 collective-permute-done.1.refs_11_
  21.4 0.0 copy-start.7
  21.4 2.9 %collective-permute-start.4 = (bf16[2,256,256]{2,1,0:T(8,128)(2,1)S(1)}, bf16[2,256,256]{2,1,0:T(8,128)(2,1)S(1)}, u32[]{:S(2)}, u32[]{:S(2)}) collective-permute-start(bf16[2,256,256]{2,1,0:T(8,128)(2,1)S(1)} %collective-permute-done.refs_0_), channel_id=1, source_target_pairs={{0,32},{8,136},{16,48},{24,152},{32,0},{40,168},{48,16},{56,184},{... | collective-permute-start | bytes 786440 | tf_op jit(solution)/shard_map/ppermute | solution.py:203
  24.3 1.2 collective-permute-start.3
  25.5 0.2 collective-permute-start.2
  25.8 2.3 %collective-permute-done.4.refs_1_ = bf16[2,256,256]{2,1,0:T(8,128)(2,1)S(1)} collective-permute-done((bf16[2,256,256]{2,1,0:T(8,128)(2,1)S(1)}, bf16[2,256,256]{2,1,0:T(8,128)(2,1)S(1)}, u32[]{:S(2)}, u32[]{:S(2)}) %collective-permute-start.4) | collective-permute-done | bytes 262176 | tf_op jit(solution)/shard_map/ppermute | solution.py:203
  28.1 4.4 %collective-permute-done.3.refs_0_ = bf16[2,256,256]{2,1,0:T(8,128)(2,1)S(1)} collective-permute-done((bf16[2,256,256]{2,1,0:T(8,128)(2,1)S(1)}, bf16[2,256,256]{2,1,0:T(8,128)(2,1)S(1)}, u32[]{:S(2)}, u32[]{:S(2)}) %collective-permute-start.3) | collective-permute-done | bytes 262176 | tf_op jit(solution)/shard_map/ppermute | solution.py:203
  32.5 0.0 collective-permute-done.2.refs_1_
  32.5 0.1 shard_map.57.refs_3_
  32.5 0.0 copy-start
  32.5 9.0 %collective-permute-start.8 = (bf16[2,2,256,256]{3,2,1,0:T(8,128)(2,1)S(1)}, bf16[2,2,256,256]{3,2,1,0:T(8,128)(2,1)S(1)}, u32[]{:S(2)}, u32[]{:S(2)}) collective-permute-start(bf16[2,2,256,256]{3,2,1,0:T(8,128)(2,1)S(1)} %shard_map.57.refs_3_), channel_id=1, source_target_pairs={{0,192},{8,56},{16,208},{24,8},{32,224},{40,24},{48,240},{56,40},{... | collective-permute-start | bytes 1572872 | tf_op jit(solution)/shard_map/ppermute | solution.py:206
  41.5 0.0 collective-permute-start.7
  41.5 0.1 shard_map.56.refs_0_
  41.6 0.0 copy-start.1
  41.6 2.8 %collective-permute-start.6 = (bf16[2,2,256,256]{3,2,1,0:T(8,128)(2,1)S(1)}, bf16[2,2,256,256]{3,2,1,0:T(8,128)(2,1)S(1)}, u32[]{:S(2)}, u32[]{:S(2)}) collective-permute-start(bf16[2,2,256,256]{3,2,1,0:T(8,128)(2,1)S(1)} %shard_map.56.refs_0_), channel_id=1, source_target_pairs={{0,192},{8,56},{16,208},{24,8},{32,224},{40,24},{48,240},{56,40},{... | collective-permute-start | bytes 1572872 | tf_op jit(solution)/shard_map/ppermute | solution.py:206
  44.3 0.0 collective-permute-start.5
  44.3 3.3 %collective-permute-done.8.refs_5_ = bf16[2,2,256,256]{3,2,1,0:T(8,128)(2,1)S(1)} collective-permute-done((bf16[2,2,256,256]{3,2,1,0:T(8,128)(2,1)S(1)}, bf16[2,2,256,256]{3,2,1,0:T(8,128)(2,1)S(1)}, u32[]{:S(2)}, u32[]{:S(2)}) %collective-permute-start.8) | collective-permute-done | bytes 524320 | tf_op jit(solution)/shard_map/ppermute | solution.py:206
  47.6 0.0 copy-start.3
  47.6 3.5 %collective-permute-done.7.refs_4_ = bf16[2,2,256,256]{3,2,1,0:T(8,128)(2,1)S(1)} collective-permute-done((bf16[2,2,256,256]{3,2,1,0:T(8,128)(2,1)S(1)}, bf16[2,2,256,256]{3,2,1,0:T(8,128)(2,1)S(1)}, u32[]{:S(2)}, u32[]{:S(2)}) %collective-permute-start.7) | collective-permute-done | bytes 524320 | tf_op jit(solution)/shard_map/ppermute | solution.py:206
  51.1 0.0 copy-start.4
  51.1 2.1 %collective-permute-done.6.refs_2_ = bf16[2,2,256,256]{3,2,1,0:T(8,128)(2,1)S(1)} collective-permute-done((bf16[2,2,256,256]{3,2,1,0:T(8,128)(2,1)S(1)}, bf16[2,2,256,256]{3,2,1,0:T(8,128)(2,1)S(1)}, u32[]{:S(2)}, u32[]{:S(2)}) %collective-permute-start.6) | collective-permute-done | bytes 524320 | tf_op jit(solution)/shard_map/ppermute | solution.py:206
  53.2 0.0 copy-done.3
  53.2 0.0 copy-done.4
  53.2 0.0 copy-start.5
  53.2 0.8 copy-done.5
  54.0 2.6 %collective-permute-done.5.refs_1_ = bf16[2,2,256,256]{3,2,1,0:T(8,128)(2,1)} collective-permute-done((bf16[2,2,256,256]{3,2,1,0:T(8,128)(2,1)S(1)}, bf16[2,2,256,256]{3,2,1,0:T(8,128)(2,1)}, u32[]{:S(2)}, u32[]{:S(2)}) %collective-permute-start.5) | collective-permute-done | bytes 524320 | tf_op jit(solution)/shard_map/ppermute | solution.py:206
  56.7 0.0 all-gather.3.cloned.1.call-done
  56.7 9.5 %collective-permute-start.11 = (bf16[8,2,256,256]{3,2,1,0:T(8,128)(2,1)}, bf16[8,2,256,256]{3,2,1,0:T(8,128)(2,1)S(1)}, u32[]{:S(2)}, u32[]{:S(2)}) collective-permute-start(bf16[8,2,256,256]{3,2,1,0:T(8,128)(2,1)} %bitcast.3), channel_id=1, source_target_pairs={{0,8},{8,0},{16,24},{24,16},{32,40},{40,32},{48,56},{56,48},{64,72... | collective-permute-start | bytes 6291464 | tf_op jit(solution)/shard_map/ppermute | solution.py:209
  66.2 0.0 collective-permute-start.9
  66.2 2.7 %collective-permute-start.10 = (bf16[2,2,256,256]{3,2,1,0:T(8,128)(2,1)}, bf16[2,2,256,256]{3,2,1,0:T(8,128)(2,1)}, u32[]{:S(2)}, u32[]{:S(2)}) collective-permute-start(bf16[2,2,256,256]{3,2,1,0:T(8,128)(2,1)} %copy-done.3), channel_id=1, source_target_pairs={{0,192},{8,56},{16,208},{24,8},{32,224},{40,24},{48,240},{56,40},{... | collective-permute-start | bytes 1572872 | tf_op jit(solution)/shard_map/ppermute | solution.py:206
  68.9 7.1 %collective-permute-done.9.refs_6_ = bf16[2,2,256,256]{3,2,1,0:T(8,128)(2,1)S(1)} collective-permute-done((bf16[2,2,256,256]{3,2,1,0:T(8,128)(2,1)}, bf16[2,2,256,256]{3,2,1,0:T(8,128)(2,1)S(1)}, u32[]{:S(2)}, u32[]{:S(2)}) %collective-permute-start.9) | collective-permute-done | bytes 524320 | tf_op jit(solution)/shard_map/ppermute | solution.py:206
  76.0 0.0 copy-start.6
  76.0 0.0 collective-permute-done.10.refs_7_
  76.0 0.0 collective-permute-done.11.refs_9_
  76.0 0.0 copy-done.7
  76.0 0.0 copy-done
  76.0 0.0 copy-done.1
  76.0 0.7 copy-done.6
  76.7 0.0 copy-start.2
  76.7 1.3 copy-done.2
  78.0 9.9 %shard_map.58 = bf16[8,2,2,32,256]{4,3,2,1,0:T(8,128)(2,1)} custom-call(s32[32]{0:T(128)} %left_sizes.3, s32[32]{0:T(128)} %right_sizes.3, bf16[2,2,256,256]{3,2,1,0:T(8,128)(2,1)} %copy-done.1, bf16[2,2,256,256]{3,2,1,0:T(8,128)(2,1)} %collective-permute-done.5.refs_1_, bf16[2,2,256,256]{3,2,1,0:T(8,128)(2,1)} %copy-done.5, ...), custom_call_target="tpu_custom_call" | custom-call | tf_op jit(solution)/shard_map/pallas_call | solution.py:144
  88.0 24.5 %all_to_all.10 = bf16[8,2,2,32,256]{4,3,2,1,0:T(8,128)(2,1)S(1)} all-to-all(bf16[8,2,2,32,256]{4,3,2,1,0:T(8,128)(2,1)} %shard_map.58), channel_id=1, replica_groups=mesh['blk'=32,'mpo'=8] {'mpo'}, dimensions={0} | all-to-all | bytes 1048576 | tf_op jit(solution)/shard_map/all_to_all | solution.py:238
  112.5 14.1 %all_to_all.11.in_ref = bf16[16,2,32,256]{3,2,1,0:T(8,128)(2,1)S(1)} all-to-all(bf16[16,2,32,256]{3,2,1,0:T(8,128)(2,1)S(1)} %bitcast.5), channel_id=1, replica_groups={{0,128,16,144,32,160,48,176,64,192,80,208,96,224,112,240},{72,200,88,21..., dimensions={0} | all-to-all | bytes 1048576 | tf_op jit(solution)/shard_map/all_to_all | solution.py:245
  126.5 0.9 shard_map.59
Async XLA Ops:
  6.5 50.1 %all-gather.3.cloned.1.call-start = ((), (), s32[]{:S(2)}) async-start(), calls=%async_computation.2 | async-start | bytes 2359296 | tf_op jit(solution)/shard_map/all_gather | solution.py:220
  7.3 13.3 %collective-permute-start = (bf16[2,256,256]{2,1,0:T(8,128)(2,1)}, bf16[2,256,256]{2,1,0:T(8,128)(2,1)S(1)}, u32[]{:S(2)}, u32[]{:S(2)}) collective-permute-start(bf16[2,256,256]{2,1,0:T(8,128)(2,1)} %param.7), channel_id=1, source_target_pairs={{0,0},{1,16},{2,32},{3,48},{4,64},{5,80},{6,96},{7,112},{8,12},{9,... | collective-permute-start | bytes 786440 | tf_op jit(solution)/shard_map/ppermute | solution.py:219
  19.5 1.8 %collective-permute-start.1 = (bf16[2,256,256]{2,1,0:T(8,128)(2,1)}, bf16[2,256,256]{2,1,0:T(8,128)(2,1)S(1)}, u32[]{:S(2)}, u32[]{:S(2)}) collective-permute-start(bf16[2,256,256]{2,1,0:T(8,128)(2,1)} %get-tuple-element.19), channel_id=1, source_target_pairs={{0,8},{8,0},{16,24},{24,16},{32,40},{40,32},{48,56},{56,48},{64,72... | collective-permute-start | bytes 786440 | tf_op jit(solution)/shard_map/ppermute | solution.py:209
  21.4 54.6 %copy-start.7 = (bf16[2,256,256]{2,1,0:T(8,128)(2,1)}, bf16[2,256,256]{2,1,0:T(8,128)(2,1)S(1)}, u32[]{:S(2)}) copy-start(bf16[2,256,256]{2,1,0:T(8,128)(2,1)S(1)} %collective-permute-done.1.refs_11_) | copy-start | bytes 786436
  21.4 6.7 %collective-permute-start.4 = (bf16[2,256,256]{2,1,0:T(8,128)(2,1)S(1)}, bf16[2,256,256]{2,1,0:T(8,128)(2,1)S(1)}, u32[]{:S(2)}, u32[]{:S(2)}) collective-permute-start(bf16[2,256,256]{2,1,0:T(8,128)(2,1)S(1)} %collective-permute-done.refs_0_), channel_id=1, source_target_pairs={{0,32},{8,136},{16,48},{24,152},{32,0},{40,168},{48,16},{56,184},{... | collective-permute-start | bytes 786440 | tf_op jit(solution)/shard_map/ppermute | solution.py:203
  24.3 8.2 %collective-permute-start.3 = (bf16[2,256,256]{2,1,0:T(8,128)(2,1)S(1)}, bf16[2,256,256]{2,1,0:T(8,128)(2,1)S(1)}, u32[]{:S(2)}, u32[]{:S(2)}) collective-permute-start(bf16[2,256,256]{2,1,0:T(8,128)(2,1)S(1)} %collective-permute-done.refs_0_), channel_id=1, source_target_pairs={{0,48},{8,200},{16,0},{24,216},{32,16},{40,232},{48,32},{56,248},{... | collective-permute-start | bytes 786440 | tf_op jit(solution)/shard_map/ppermute | solution.py:203
  25.5 6.9 %collective-permute-start.2 = (bf16[2,256,256]{2,1,0:T(8,128)(2,1)S(1)}, bf16[2,256,256]{2,1,0:T(8,128)(2,1)S(1)}, u32[]{:S(2)}, u32[]{:S(2)}) collective-permute-start(bf16[2,256,256]{2,1,0:T(8,128)(2,1)S(1)} %collective-permute-done.refs_0_), channel_id=1, source_target_pairs={{0,16},{8,72},{16,32},{24,88},{32,48},{40,104},{48,0},{56,120},{64... | collective-permute-start | bytes 786440 | tf_op jit(solution)/shard_map/ppermute | solution.py:203
  32.5 43.4 %copy-start = (bf16[2,2,256,256]{3,2,1,0:T(8,128)(2,1)}, bf16[2,2,256,256]{3,2,1,0:T(8,128)(2,1)S(1)}, u32[]{:S(2)}) copy-start(bf16[2,2,256,256]{3,2,1,0:T(8,128)(2,1)S(1)} %shard_map.57.refs_3_) | copy-start | bytes 1572868
  32.5 15.1 %collective-permute-start.8 = (bf16[2,2,256,256]{3,2,1,0:T(8,128)(2,1)S(1)}, bf16[2,2,256,256]{3,2,1,0:T(8,128)(2,1)S(1)}, u32[]{:S(2)}, u32[]{:S(2)}) collective-permute-start(bf16[2,2,256,256]{3,2,1,0:T(8,128)(2,1)S(1)} %shard_map.57.refs_3_), channel_id=1, source_target_pairs={{0,192},{8,56},{16,208},{24,8},{32,224},{40,24},{48,240},{56,40},{... | collective-permute-start | bytes 1572872 | tf_op jit(solution)/shard_map/ppermute | solution.py:206
  41.5 9.6 %collective-permute-start.7 = (bf16[2,2,256,256]{3,2,1,0:T(8,128)(2,1)S(1)}, bf16[2,2,256,256]{3,2,1,0:T(8,128)(2,1)S(1)}, u32[]{:S(2)}, u32[]{:S(2)}) collective-permute-start(bf16[2,2,256,256]{3,2,1,0:T(8,128)(2,1)S(1)} %shard_map.57.refs_3_), channel_id=1, source_target_pairs={{0,64},{8,24},{16,80},{24,40},{32,96},{40,56},{48,112},{56,8},{64,... | collective-permute-start | bytes 1572872 | tf_op jit(solution)/shard_map/ppermute | solution.py:206
  41.6 34.4 %copy-start.1 = (bf16[2,2,256,256]{3,2,1,0:T(8,128)(2,1)}, bf16[2,2,256,256]{3,2,1,0:T(8,128)(2,1)S(1)}, u32[]{:S(2)}) copy-start(bf16[2,2,256,256]{3,2,1,0:T(8,128)(2,1)S(1)} %shard_map.56.refs_0_) | copy-start | bytes 1572868
  41.6 11.7 %collective-permute-start.6 = (bf16[2,2,256,256]{3,2,1,0:T(8,128)(2,1)S(1)}, bf16[2,2,256,256]{3,2,1,0:T(8,128)(2,1)S(1)}, u32[]{:S(2)}, u32[]{:S(2)}) collective-permute-start(bf16[2,2,256,256]{3,2,1,0:T(8,128)(2,1)S(1)} %shard_map.56.refs_0_), channel_id=1, source_target_pairs={{0,192},{8,56},{16,208},{24,8},{32,224},{40,24},{48,240},{56,40},{... | collective-permute-start | bytes 1572872 | tf_op jit(solution)/shard_map/ppermute | solution.py:206
  44.3 12.3 %collective-permute-start.5 = (bf16[2,2,256,256]{3,2,1,0:T(8,128)(2,1)S(1)}, bf16[2,2,256,256]{3,2,1,0:T(8,128)(2,1)}, u32[]{:S(2)}, u32[]{:S(2)}) collective-permute-start(bf16[2,2,256,256]{3,2,1,0:T(8,128)(2,1)S(1)} %shard_map.56.refs_0_), channel_id=1, source_target_pairs={{0,64},{8,24},{16,80},{24,40},{32,96},{40,56},{48,112},{56,8},{64,... | collective-permute-start | bytes 1572872 | tf_op jit(solution)/shard_map/ppermute | solution.py:206
  47.6 5.6 %copy-start.3 = (bf16[2,2,256,256]{3,2,1,0:T(8,128)(2,1)}, bf16[2,2,256,256]{3,2,1,0:T(8,128)(2,1)S(1)}, u32[]{:S(2)}) copy-start(bf16[2,2,256,256]{3,2,1,0:T(8,128)(2,1)S(1)} %collective-permute-done.8.refs_5_) | copy-start | bytes 1572868
  51.1 2.1 %copy-start.4 = (bf16[2,2,256,256]{3,2,1,0:T(8,128)(2,1)}, bf16[2,2,256,256]{3,2,1,0:T(8,128)(2,1)S(1)}, u32[]{:S(2)}) copy-start(bf16[2,2,256,256]{3,2,1,0:T(8,128)(2,1)S(1)} %collective-permute-done.7.refs_4_) | copy-start | bytes 1572868
  53.2 0.8 copy-start.5
  56.7 19.3 %collective-permute-start.11 = (bf16[8,2,256,256]{3,2,1,0:T(8,128)(2,1)}, bf16[8,2,256,256]{3,2,1,0:T(8,128)(2,1)S(1)}, u32[]{:S(2)}, u32[]{:S(2)}) collective-permute-start(bf16[8,2,256,256]{3,2,1,0:T(8,128)(2,1)} %bitcast.3), channel_id=1, source_target_pairs={{0,8},{8,0},{16,24},{24,16},{32,40},{40,32},{48,56},{56,48},{64,72... | collective-permute-start | bytes 6291464 | tf_op jit(solution)/shard_map/ppermute | solution.py:209
  66.2 9.7 %collective-permute-start.9 = (bf16[2,2,256,256]{3,2,1,0:T(8,128)(2,1)}, bf16[2,2,256,256]{3,2,1,0:T(8,128)(2,1)S(1)}, u32[]{:S(2)}, u32[]{:S(2)}) collective-permute-start(bf16[2,2,256,256]{3,2,1,0:T(8,128)(2,1)} %collective-permute-done.5.refs_1_), channel_id=1, source_target_pairs={{0,64},{8,24},{16,80},{24,40},{32,96},{40,56},{48,112},{56,8},{64,... | collective-permute-start | bytes 1572872 | tf_op jit(solution)/shard_map/ppermute | solution.py:206
  66.2 9.7 %collective-permute-start.10 = (bf16[2,2,256,256]{3,2,1,0:T(8,128)(2,1)}, bf16[2,2,256,256]{3,2,1,0:T(8,128)(2,1)}, u32[]{:S(2)}, u32[]{:S(2)}) collective-permute-start(bf16[2,2,256,256]{3,2,1,0:T(8,128)(2,1)} %copy-done.3), channel_id=1, source_target_pairs={{0,192},{8,56},{16,208},{24,8},{32,224},{40,24},{48,240},{56,40},{... | collective-permute-start | bytes 1572872 | tf_op jit(solution)/shard_map/ppermute | solution.py:206
  76.0 0.8 copy-start.6
  76.7 1.3 copy-start.2
Sparse Core Ops, SparseCore 0:
  9.1 43.7 all-gather.2

commit v14 on v10

--- a/solution.py
+++ b/solution.py
@@ -83,77 +83,86 @@
     )(left_sizes, right_sizes, wavefunction)
 
 
-def apply_kernel(pieces, left_sizes, right_sizes, *refs):
-    ins, (out_ref, total, held, left_held, psi_held, middle, sems) = refs[:-7], refs[-7:]
-    shards, (own, other, psi) = ins[: len(pieces)], ins[len(pieces) :]
-    sector, rank, core, x0, y0 = coordinates()
-    ranks, _, _, rows, right_dim = out_ref.shape
-    left_dim = ranks * rows
+def half_kernel(pieces, *refs):
+    ins, (out_ref, held, left_held, psi_held, middle, sems) = refs[:-6], refs[-6:]
+    shards, (lefts, psi) = ins[: len(pieces)], ins[len(pieces) :]
+    _, rank, core, x0, y0 = coordinates()
+    ranks, pair, left_dim, inner = left_held.shape
+    right_dim = psi_held.shape[2]
     first = [
-        pltpu.make_async_copy(source, place_in, sems.at[i])
-        for i, (source, place_in) in enumerate(
-            (
-                (psi, psi_held.at[0]),
-                (other.at[ranks], psi_held.at[1]),
-                (own.at[pl.ds(0, ranks)], left_held.at[0]),
-                (other.at[pl.ds(0, ranks)], left_held.at[1]),
-            )
-        )
+        pltpu.make_async_copy(psi, psi_held, sems.at[0]),
+        pltpu.make_async_copy(lefts.at[pl.ds(0, ranks)], left_held, sems.at[1]),
     ]
-    coming = [pltpu.make_async_copy(r, held.at[i], sems.at[4 + i]) for i, r in enumerate(shards)]
+    coming = [pltpu.make_async_copy(r, held.at[i], sems.at[2 + i]) for i, r in enumerate(shards)]
     for copy in first + coming:
         copy.start()
-    total[...] = jnp.zeros_like(total)
+    out_ref[...] = jnp.zeros_like(out_ref)
     for copy in first:
         copy.wait()
+    some = ranks // 2
+    for b in range(2):
+        for part in range(0, ranks, some):
+            block = left_held[part : part + some].reshape(some * pair * left_dim, inner)
+            product = jnp.dot(block, psi_held[b], preferred_element_type=jnp.float32)
+            product = product.astype(middle.dtype).reshape(some, pair, left_dim, right_dim)
+            for w in range(pair):
+                columns = slice(w * right_dim, (w + 1) * right_dim)
+                middle[b, part : part + some, :, columns] = product[:, w]
     for i, (far, start) in enumerate(pieces):
         coming[i].wait()
         for k in range(held.shape[1]):
             near = OFFSETS[start + k]
             y = jnp.where(core == 0, y0 + far, y0 + near) & (SIDE - 1)
             x = jnp.where(core == 0, x0 + near, x0 + far) & (SIDE - 1)
-            which, pair = y // 2, (x + SIDE * (y & 1) - rank) & (ranks - 1)
-            for a in range(2):
-                block = left_held[a, pair].reshape(2 * left_dim, left_dim)
-                product = jnp.dot(block, psi_held[a, which], preferred_element_type=jnp.float32)
-                product = product.astype(middle.dtype)
-                for w in range(2):
-                    middle[k % 2, a * left_dim : (a + 1) * left_dim, w * right_dim : (w + 1) * right_dim] = (
-                        product[w * left_dim : (w + 1) * left_dim]
-                    )
-            shard = held[i, k].reshape(2 * right_dim, right_dim)
-            total[which] += jnp.dot(middle[k % 2], shard, preferred_element_type=jnp.float32)
+            which, at = y // 2, (x + SIDE * (y & 1) - rank) & (ranks - 1)
+            shard = held[i, k].reshape(pair * right_dim, right_dim)
+            out_ref[which] += jnp.dot(middle[which, at], shard, preferred_element_type=jnp.float32)
+
+
+def half(pieces, shards, lefts, psi):
+    dtype = psi.dtype
+    slots, pair, left_dim, inner = lefts.shape
+    ranks, right_dim = slots - 1, psi.shape[2]
+    return pl.pallas_call(
+        functools.partial(half_kernel, pieces),
+        out_shape=jax.ShapeDtypeStruct((2, left_dim, right_dim), jnp.float32),
+        in_specs=[ANYWHERE] * (len(shards) + 2),
+        out_specs=VMEM,
+        scratch_shapes=[
+            pltpu.VMEM((len(shards), *shards[0].shape), dtype),
+            pltpu.VMEM((ranks, pair, left_dim, inner), dtype),
+            pltpu.VMEM(psi.shape, dtype),
+            pltpu.VMEM((2, ranks, left_dim, pair * right_dim), dtype),
+            pltpu.SemaphoreType.DMA((len(shards) + 2,)),
+        ],
+        compiler_params=pltpu.CompilerParams(vmem_limit_bytes=24 * MIB),
+    )(*shards, lefts, psi)
+
+
+def join_kernel(left_sizes, right_sizes, own_ref, other_ref, out_ref):
+    sector, rank, core, _, _ = coordinates()
+    ranks, _, _, rows, right_dim = out_ref.shape
+    left_dim = ranks * rows
     row = lax.broadcasted_iota(jnp.int32, (left_dim, right_dim), 0)
     col = lax.broadcasted_iota(jnp.int32, (left_dim, right_dim), 1)
     for b in range(2):
         own_right = right_sizes[right_sector(rank, core, b)]
-        for a, spot in enumerate((core, 1 - core)):
+        for total, spot in ((own_ref, core), (other_ref, 1 - core)):
             inside = jnp.logical_and(row < left_sizes[sector - core + spot], col < own_right)
-            block = jnp.where(inside, total[b, a * left_dim : (a + 1) * left_dim], 0.0)
+            block = jnp.where(inside, total[b], 0.0)
             block = block.astype(out_ref.dtype).reshape(ranks, 1, rows, right_dim)
             out_ref[:, b, pl.ds(spot, 1)] = block
 
 
-def apply(pieces, shards, own, other, psi, left_sizes, right_sizes):
-    dtype = psi.dtype
-    slots, pair, left_dim, _ = own.shape
-    ranks, right_dim = slots - 1, psi.shape[2]
-    others = (*shards, own, other, psi)
-    return pl.pallas_call(
-        functools.partial(apply_kernel, pieces),
+def join(own, other, left_sizes, right_sizes, ranks, dtype):
+    _, left_dim, right_dim = own.shape
+    return pl.pallas_call(
+        join_kernel,
         out_shape=jax.ShapeDtypeStruct((ranks, 2, 2, left_dim // ranks, right_dim), dtype),
-        in_specs=[SMEM, SMEM] + [ANYWHERE] * len(others),
+        in_specs=[SMEM, SMEM, VMEM, VMEM],
         out_specs=VMEM,
-        scratch_shapes=[
-            pltpu.VMEM((2, 2 * left_dim, right_dim), jnp.float32),
-            pltpu.VMEM((len(shards), *shards[0].shape), dtype),
-            pltpu.VMEM((2, ranks, *own.shape[1:]), dtype),
-            pltpu.VMEM((2, *psi.shape), dtype),
-            pltpu.VMEM((2, 2 * left_dim, pair * right_dim), dtype),
-            pltpu.SemaphoreType.DMA((len(shards) + 4,)),
-        ],
-        compiler_params=pltpu.CompilerParams(vmem_limit_bytes=60 * MIB),
-    )(left_sizes, right_sizes, *others)
+        compiler_params=pltpu.CompilerParams(vmem_limit_bytes=8 * MIB),
+    )(left_sizes, right_sizes, own, other)
 
 
 def order_kernel(in_ref, out_ref, sems):
@@ -243,7 +252,9 @@
 
     pieces = ((0, 0), (SIDE - 1, 0), (1, 0), (0, 2), (SIDE - 1, 2), (1, 2), (2, 0), (2, 2))
     shards = (line_a, a_below, a_above, line_b, b_below, b_above, a_two, b_two)
-    done = apply(pieces, shards, lefts, others, keep, left_sizes, right_sizes)
+    mine = half(pieces, shards, lefts, keep)
+    theirs = half(pieces, shards, others, others[ranks])
+    done = join(mine, theirs, left_sizes, right_sizes, ranks, wavefunction.dtype)
 
     by_plane = lax.all_to_all(done, "mpo", 0, 0)
     chips = SIDE * SIDE

time: 130 us -> 124 us (0.954)
  waiting for transfers between devices: 27.1 us -> 22.9 us
  blocking collectives: 33 us -> 35.1 us
  Pallas kernels: 15.3 us -> 13.4 us
  local copies, waits for them, and re-layouts: 2.79 us -> 0.99 us
    ppermute x1, waiting for transfers between devices: 4.29 us -> 0.01 us  [swap(): return lax.ppermute(block, 'blk', [(i, i ^ 1) for i in range(sectors)])]
    pallas_call x1 -> x3, Pallas kernels: 11.4 us -> 9.54 us  [the longest x2 8.87 us: half(): pl.pallas_call(functools.partial(half_kernel, pieces), out_shape=jax.Shap...]
    unnamed x26 -> x10, local copies, waits for them, and re-layouts: 2.79 us -> 0.97 us
  transfers between devices with their start and end apart: 18 -> 18, of which waited for: 7 -> 6; matrix products, arithmetic and copies ran while one was open for 0% -> 0% of each run, Pallas kernels for 2% -> 6%
where the time goes in v14:
time: 124 us; the launch traced here: 123 us
  starting transfers between devices  50.1 us (40%)
  blocking collectives  35.1 us (28%)
  waiting for transfers between devices  22.9 us (18%)
  Pallas kernels  13.4 us (11%)
    all_to_all x1, blocking collectives, local(): by_plane = lax.all_to_all(done, 'mpo', 0, 0)  21.2 us
    ppermute x4, waiting for transfers between devices, up(): lax.ppermute(block, 'mpo', [(z, (z + 1) % ranks) for z in range(ranks)])  16.6 us
    all_to_all x1, blocking collectives, local(): out = order(lax.all_to_all(by_plane, 'blk', 0, 0, axis_index_groups=groups))  13.9 us
    ppermute x1, starting transfers between devices, swap(): return lax.ppermute(block, 'blk', [(i, i ^ 1) for i in range(sectors)])  10.3 us
    ppermute x3, starting transfers between devices, down(): lax.ppermute(block, 'mpo', [(z, (z - 1) % ranks) for z in range(ranks)])  9.93 us
    ppermute x1, starting transfers between devices, local(): own = lax.ppermute(right_env, ('blk', 'mpo'), turn)  9.77 us
    ppermute x6, starting transfers between devices, far_step(): return lax.ppermute(block, 'blk', step(True, by))  9.57 us
    pallas_call x2, Pallas kernels, half(): pl.pallas_call(functools.partial(half_kernel, pieces), out_shape=jax.Shap...  8.87 us
  transfers between devices with their start and end apart: 18, of which 6 were waited for; matrix products, arithmetic and copies ran while one was open for 0% of the time, Pallas kernels for 6%

profile of v14, /device:TPU:1, one launch (start us, length us, event | category | flops | bytes accessed | tf_op | source)
XLA Modules:
  0.0 122.9 jit_solution(12738605737774424512)
XLA Ops:
  0.0 0.0 copy-start
  0.0 9.8 %collective-permute-start = (bf16[2,256,256]{2,1,0:T(8,128)(2,1)}, bf16[2,256,256]{2,1,0:T(8,128)(2,1)S(1)}, u32[]{:S(2)}, u32[]{:S(2)}) collective-permute-start(bf16[2,256,256]{2,1,0:T(8,128)(2,1)} %param.7), channel_id=1, source_target_pairs={{0,0},{1,16},{2,32},{3,48},{4,64},{5,80},{6,96},{7,112},{8,12},{9,... | collective-permute-start | bytes 786440 | tf_op jit(solution)/shard_map/ppermute | solution.py:232
  9.8 1.3 %collective-permute-start.4 = (bf16[2,256,256]{2,1,0:T(8,128)(2,1)}, bf16[2,256,256]{2,1,0:T(8,128)(2,1)S(1)}, u32[]{:S(2)}, u32[]{:S(2)}) collective-permute-start(bf16[2,256,256]{2,1,0:T(8,128)(2,1)} %refs_0_.1), channel_id=1, source_target_pairs={{0,1},{1,2},{2,3},{3,4},{4,5},{5,6},{6,7},{7,0},{8,9},{9,10},{10,1... | collective-permute-start | bytes 786440 | tf_op jit(solution)/shard_map/ppermute | solution.py:219
  11.1 2.4 %collective-permute-start.5 = (bf16[2,256,256]{2,1,0:T(8,128)(2,1)}, bf16[2,256,256]{2,1,0:T(8,128)(2,1)S(1)}, u32[]{:S(2)}, u32[]{:S(2)}) collective-permute-start(bf16[2,256,256]{2,1,0:T(8,128)(2,1)} %refs_0_.1), channel_id=1, source_target_pairs={{0,7},{1,0},{2,1},{3,2},{4,3},{5,4},{6,5},{7,6},{8,15},{9,8},{10,9... | collective-permute-start | bytes 786440 | tf_op jit(solution)/shard_map/ppermute | solution.py:222
  13.4 2.6 %shard_map.55 = (bf16[2,256,256]{2,1,0:T(8,128)(2,1)}, bf16[2,256,256]{2,1,0:T(8,128)(2,1)}) custom-call(s32[32]{0:T(128)} %left_sizes.3, s32[32]{0:T(128)} %right_sizes.3, bf16[256,8192]{1,0:T(8,128)(2,1)} %psi_ref.1), custom_call_target="tpu_custom_call" | custom-call | tf_op jit(solution)/shard_map/pallas_call | solution.py:76
  16.1 0.0 collective-permute-done.refs_0_
  16.1 2.7 %collective-permute-start.3 = (bf16[2,256,256]{2,1,0:T(8,128)(2,1)S(1)}, bf16[2,256,256]{2,1,0:T(8,128)(2,1)S(1)}, u32[]{:S(2)}, u32[]{:S(2)}) collective-permute-start(bf16[2,256,256]{2,1,0:T(8,128)(2,1)S(1)} %collective-permute-done.refs_0_), channel_id=1, source_target_pairs={{0,32},{8,136},{16,48},{24,152},{32,0},{40,168},{48,16},{56,184},{... | collective-permute-start | bytes 786440 | tf_op jit(solution)/shard_map/ppermute | solution.py:210
  18.8 0.0 collective-permute-start.2
  18.8 1.5 %collective-permute-start.1 = (bf16[2,256,256]{2,1,0:T(8,128)(2,1)S(1)}, bf16[2,256,256]{2,1,0:T(8,128)(2,1)S(1)}, u32[]{:S(2)}, u32[]{:S(2)}) collective-permute-start(bf16[2,256,256]{2,1,0:T(8,128)(2,1)S(1)} %collective-permute-done.refs_0_), channel_id=1, source_target_pairs={{0,16},{8,72},{16,32},{24,88},{32,48},{40,104},{48,0},{56,120},{64... | collective-permute-start | bytes 786440 | tf_op jit(solution)/shard_map/ppermute | solution.py:210
  20.2 5.8 %collective-permute-done.4.refs_7_ = bf16[2,256,256]{2,1,0:T(8,128)(2,1)S(1)} collective-permute-done((bf16[2,256,256]{2,1,0:T(8,128)(2,1)}, bf16[2,256,256]{2,1,0:T(8,128)(2,1)S(1)}, u32[]{:S(2)}, u32[]{:S(2)}) %collective-permute-start.4) | collective-permute-done | bytes 262176 | tf_op jit(solution)/shard_map/ppermute | solution.py:219
  26.1 0.0 collective-permute-done.5.refs_1_
  26.1 0.0 collective-permute-done.3.refs_1_
  26.1 0.0 collective-permute-done.2.refs_0_
  26.1 0.0 collective-permute-done.1.refs_1_
  26.1 4.0 %collective-permute-start.10 = (bf16[2,256,256]{2,1,0:T(8,128)(2,1)S(1)}, bf16[2,256,256]{2,1,0:T(8,128)(2,1)S(1)}, u32[]{:S(2)}, u32[]{:S(2)}) collective-permute-start(bf16[2,256,256]{2,1,0:T(8,128)(2,1)S(1)} %collective-permute-done.4.refs_7_), channel_id=1, source_target_pairs={{0,1},{1,2},{2,3},{3,4},{4,5},{5,6},{6,7},{7,0},{8,9},{9,10},{10,1... | collective-permute-start | bytes 786440 | tf_op jit(solution)/shard_map/ppermute | solution.py:219
  30.1 5.9 %collective-permute-start.12 = (bf16[2,256,256]{2,1,0:T(8,128)(2,1)S(1)}, bf16[2,256,256]{2,1,0:T(8,128)(2,1)S(1)}, u32[]{:S(2)}, u32[]{:S(2)}) collective-permute-start(bf16[2,256,256]{2,1,0:T(8,128)(2,1)S(1)} %collective-permute-done.5.refs_1_), channel_id=1, source_target_pairs={{0,7},{1,0},{2,1},{3,2},{4,3},{5,4},{6,5},{7,6},{8,15},{9,8},{10,9... | collective-permute-start | bytes 786440 | tf_op jit(solution)/shard_map/ppermute | solution.py:222
  36.0 0.1 shard_map.57.refs_3_
  36.1 2.6 %collective-permute-start.9 = (bf16[2,2,256,256]{3,2,1,0:T(8,128)(2,1)S(1)}, bf16[2,2,256,256]{3,2,1,0:T(8,128)(2,1)S(1)}, u32[]{:S(2)}, u32[]{:S(2)}) collective-permute-start(bf16[2,2,256,256]{3,2,1,0:T(8,128)(2,1)S(1)} %shard_map.57.refs_3_), channel_id=1, source_target_pairs={{0,192},{8,56},{16,208},{24,8},{32,224},{40,24},{48,240},{56,40},{... | collective-permute-start | bytes 1572872 | tf_op jit(solution)/shard_map/ppermute | solution.py:213
  38.7 1.1 collective-permute-done.10.refs_6_
  39.7 0.0 collective-permute-start.11
  39.7 1.5 %collective-permute-start.8 = (bf16[2,2,256,256]{3,2,1,0:T(8,128)(2,1)S(1)}, bf16[2,2,256,256]{3,2,1,0:T(8,128)(2,1)S(1)}, u32[]{:S(2)}, u32[]{:S(2)}) collective-permute-start(bf16[2,2,256,256]{3,2,1,0:T(8,128)(2,1)S(1)} %shard_map.57.refs_3_), channel_id=1, source_target_pairs={{0,64},{8,24},{16,80},{24,40},{32,96},{40,56},{48,112},{56,8},{64,... | collective-permute-start | bytes 1572872 | tf_op jit(solution)/shard_map/ppermute | solution.py:213
  41.3 0.1 shard_map.56.refs_0_
  41.3 0.0 copy-start.1
  41.4 2.8 %collective-permute-start.7 = (bf16[2,2,256,256]{3,2,1,0:T(8,128)(2,1)S(1)}, bf16[2,2,256,256]{3,2,1,0:T(8,128)(2,1)S(1)}, u32[]{:S(2)}, u32[]{:S(2)}) collective-permute-start(bf16[2,2,256,256]{3,2,1,0:T(8,128)(2,1)S(1)} %shard_map.56.refs_0_), channel_id=1, source_target_pairs={{0,192},{8,56},{16,208},{24,8},{32,224},{40,24},{48,240},{56,40},{... | collective-permute-start | bytes 1572872 | tf_op jit(solution)/shard_map/ppermute | solution.py:213
  44.1 0.0 collective-permute-done.12.refs_2_
  44.1 0.0 collective-permute-start.6
  44.1 4.4 %collective-permute-done.11.refs_5_ = bf16[2,256,256]{2,1,0:T(8,128)(2,1)S(1)} collective-permute-done((bf16[2,256,256]{2,1,0:T(8,128)(2,1)S(1)}, bf16[2,256,256]{2,1,0:T(8,128)(2,1)S(1)}, u32[]{:S(2)}, u32[]{:S(2)}) %collective-permute-start.11) | collective-permute-done | bytes 262176 | tf_op jit(solution)/shard_map/ppermute | solution.py:219
  48.6 1.7 %collective-permute-start.13 = (bf16[2,256,256]{2,1,0:T(8,128)(2,1)S(1)}, bf16[2,256,256]{2,1,0:T(8,128)(2,1)S(1)}, u32[]{:S(2)}, u32[]{:S(2)}) collective-permute-start(bf16[2,256,256]{2,1,0:T(8,128)(2,1)S(1)} %collective-permute-done.12.refs_2_), channel_id=1, source_target_pairs={{0,7},{1,0},{2,1},{3,2},{4,3},{5,4},{6,5},{7,6},{8,15},{9,8},{10,9... | collective-permute-start | bytes 786440 | tf_op jit(solution)/shard_map/ppermute | solution.py:222
  50.2 3.8 %collective-permute-done.13.refs_3_ = bf16[2,256,256]{2,1,0:T(8,128)(2,1)S(1)} collective-permute-done((bf16[2,256,256]{2,1,0:T(8,128)(2,1)S(1)}, bf16[2,256,256]{2,1,0:T(8,128)(2,1)S(1)}, u32[]{:S(2)}, u32[]{:S(2)}) %collective-permute-start.13) | collective-permute-done | bytes 262176 | tf_op jit(solution)/shard_map/ppermute | solution.py:222
  54.1 0.0 collective-permute-done.9.refs_5_
  54.1 0.0 collective-permute-done.8.refs_4_
  54.1 0.0 collective-permute-done.7.refs_2_
  54.1 2.4 %collective-permute-done.6.refs_1_ = bf16[2,2,256,256]{3,2,1,0:T(8,128)(2,1)S(1)} collective-permute-done((bf16[2,2,256,256]{3,2,1,0:T(8,128)(2,1)S(1)}, bf16[2,2,256,256]{3,2,1,0:T(8,128)(2,1)S(1)}, u32[]{:S(2)}, u32[]{:S(2)}) %collective-permute-start.6) | collective-permute-done | bytes 524320 | tf_op jit(solution)/shard_map/ppermute | solution.py:213
  56.4 0.0 collective-permute-start.15
  56.4 2.7 %collective-permute-start.16 = (bf16[2,2,256,256]{3,2,1,0:T(8,128)(2,1)S(1)}, bf16[2,2,256,256]{3,2,1,0:T(8,128)(2,1)S(1)}, u32[]{:S(2)}, u32[]{:S(2)}) collective-permute-start(bf16[2,2,256,256]{3,2,1,0:T(8,128)(2,1)S(1)} %collective-permute-done.9.refs_5_), channel_id=1, source_target_pairs={{0,192},{8,56},{16,208},{24,8},{32,224},{40,24},{48,240},{56,40},{... | collective-permute-start | bytes 1572872 | tf_op jit(solution)/shard_map/ppermute | solution.py:213
  59.1 1.1 collective-permute-start.14
  60.2 5.3 %collective-permute-done.14.refs_4_ = bf16[2,256,256]{2,1,0:T(8,128)(2,1)S(1)} collective-permute-done((bf16[2,256,256]{2,1,0:T(8,128)(2,1)S(1)}, bf16[2,256,256]{2,1,0:T(8,128)(2,1)S(1)}, u32[]{:S(2)}, u32[]{:S(2)}) %collective-permute-start.14) | collective-permute-done | bytes 262176 | tf_op jit(solution)/shard_map/ppermute | solution.py:219
  65.6 0.0 copy-done
  65.6 0.0 copy-start.2
  65.6 0.9 copy-done.2
  66.5 0.3 shard_map.58.refs_8_
  66.8 0.0 collective-permute-done.15.refs_6_
  66.8 0.0 collective-permute-done.16.refs_7_
  66.8 10.3 %collective-permute-start.17 = (bf16[9,2,256,256]{3,2,1,0:T(8,128)(2,1)S(1)}, bf16[9,2,256,256]{3,2,1,0:T(8,128)(2,1)S(1)}, u32[]{:S(2)}, u32[]{:S(2)}) collective-permute-start(bf16[9,2,256,256]{3,2,1,0:T(8,128)(2,1)S(1)} %shard_map.58.refs_8_), channel_id=1, source_target_pairs={{0,8},{8,0},{16,24},{24,16},{32,40},{40,32},{48,56},{56,48},{64,72... | collective-permute-start | bytes 7077896 | tf_op jit(solution)/shard_map/ppermute | solution.py:216
  77.1 0.0 copy-done.1
  77.1 4.4 %shard_map.59.own_ref = f32[2,256,256]{2,1,0:T(8,128)S(1)} custom-call(bf16[2,2,256,256]{3,2,1,0:T(8,128)(2,1)S(1)} %shard_map.56.refs_0_, bf16[2,2,256,256]{3,2,1,0:T(8,128)(2,1)S(1)} %collective-permute-done.6.refs_1_, bf16[2,2,256,256]{3,2,1,0:T(8,128)(2,1)S(1)} %collective-permute-done.7.refs_2_, bf16[2,2,256,256]{3,2,1,0:T(8,128)(2,1)S(1)} %shard_map.57.refs_3_, ...), custom_call_target="tpu_custom_call" | custom-call | tf_op jit(solution)/shard_map/pallas_call | solution.py:126
  81.5 0.0 collective-permute-done.17.refs_8_
  81.5 0.0 copy-start.3
  81.5 0.0 copy-start.4
  81.6 4.4 %shard_map.60.other_ref = f32[2,256,256]{2,1,0:T(8,128)S(1)} custom-call(bf16[2,2,256,256]{3,2,1,0:T(8,128)(2,1)S(1)} %shard_map.56.refs_0_, bf16[2,2,256,256]{3,2,1,0:T(8,128)(2,1)S(1)} %collective-permute-done.6.refs_1_, bf16[2,2,256,256]{3,2,1,0:T(8,128)(2,1)S(1)} %collective-permute-done.7.refs_2_, bf16[2,2,256,256]{3,2,1,0:T(8,128)(2,1)S(1)} %shard_map.57.refs_3_, ...), custom_call_target="tpu_custom_call" | custom-call | tf_op jit(solution)/shard_map/pallas_call | solution.py:126
  86.0 0.0 copy-done.3
  86.0 0.0 copy-done.4
  86.0 0.7 shard_map.61
  86.7 21.2 %all_to_all.10 = bf16[8,2,2,32,256]{4,3,2,1,0:T(8,128)(2,1)S(1)} all-to-all(bf16[8,2,2,32,256]{4,3,2,1,0:T(8,128)(2,1)S(1)} %shard_map.61), channel_id=1, replica_groups=mesh['blk'=32,'mpo'=8] {'mpo'}, dimensions={0} | all-to-all | bytes 1048576 | tf_op jit(solution)/shard_map/all_to_all | solution.py:259
  107.9 13.9 %all_to_all.11.in_ref = bf16[16,2,32,256]{3,2,1,0:T(8,128)(2,1)S(1)} all-to-all(bf16[16,2,32,256]{3,2,1,0:T(8,128)(2,1)S(1)} %bitcast.4), channel_id=1, replica_groups={{0,128,16,144,32,160,48,176,64,192,80,208,96,224,112,240},{72,200,88,21..., dimensions={0} | all-to-all | bytes 1048576 | tf_op jit(solution)/shard_map/all_to_all | solution.py:266
  121.8 0.9 shard_map.62
  (1 shorter events, 0.0 us)
Async XLA Ops:
  0.0 65.6 %copy-start = (bf16[2,256,256]{2,1,0:T(8,128)(2,1)S(1)}, bf16[2,256,256]{2,1,0:T(8,128)(2,1)}, u32[]{:S(2)}) copy-start(bf16[2,256,256]{2,1,0:T(8,128)(2,1)} %refs_0_.1) | copy-start | bytes 786436
  0.0 16.1 %collective-permute-start = (bf16[2,256,256]{2,1,0:T(8,128)(2,1)}, bf16[2,256,256]{2,1,0:T(8,128)(2,1)S(1)}, u32[]{:S(2)}, u32[]{:S(2)}) collective-permute-start(bf16[2,256,256]{2,1,0:T(8,128)(2,1)} %param.7), channel_id=1, source_target_pairs={{0,0},{1,16},{2,32},{3,48},{4,64},{5,80},{6,96},{7,112},{8,12},{9,... | collective-permute-start | bytes 786440 | tf_op jit(solution)/shard_map/ppermute | solution.py:232
  9.8 16.3 %collective-permute-start.4 = (bf16[2,256,256]{2,1,0:T(8,128)(2,1)}, bf16[2,256,256]{2,1,0:T(8,128)(2,1)S(1)}, u32[]{:S(2)}, u32[]{:S(2)}) collective-permute-start(bf16[2,256,256]{2,1,0:T(8,128)(2,1)} %refs_0_.1), channel_id=1, source_target_pairs={{0,1},{1,2},{2,3},{3,4},{4,5},{5,6},{6,7},{7,0},{8,9},{9,10},{10,1... | collective-permute-start | bytes 786440 | tf_op jit(solution)/shard_map/ppermute | solution.py:219
  11.1 15.0 %collective-permute-start.5 = (bf16[2,256,256]{2,1,0:T(8,128)(2,1)}, bf16[2,256,256]{2,1,0:T(8,128)(2,1)S(1)}, u32[]{:S(2)}, u32[]{:S(2)}) collective-permute-start(bf16[2,256,256]{2,1,0:T(8,128)(2,1)} %refs_0_.1), channel_id=1, source_target_pairs={{0,7},{1,0},{2,1},{3,2},{4,3},{5,4},{6,5},{7,6},{8,15},{9,8},{10,9... | collective-permute-start | bytes 786440 | tf_op jit(solution)/shard_map/ppermute | solution.py:222
  16.1 10.0 %collective-permute-start.3 = (bf16[2,256,256]{2,1,0:T(8,128)(2,1)S(1)}, bf16[2,256,256]{2,1,0:T(8,128)(2,1)S(1)}, u32[]{:S(2)}, u32[]{:S(2)}) collective-permute-start(bf16[2,256,256]{2,1,0:T(8,128)(2,1)S(1)} %collective-permute-done.refs_0_), channel_id=1, source_target_pairs={{0,32},{8,136},{16,48},{24,152},{32,0},{40,168},{48,16},{56,184},{... | collective-permute-start | bytes 786440 | tf_op jit(solution)/shard_map/ppermute | solution.py:210
  18.8 7.3 %collective-permute-start.2 = (bf16[2,256,256]{2,1,0:T(8,128)(2,1)S(1)}, bf16[2,256,256]{2,1,0:T(8,128)(2,1)S(1)}, u32[]{:S(2)}, u32[]{:S(2)}) collective-permute-start(bf16[2,256,256]{2,1,0:T(8,128)(2,1)S(1)} %collective-permute-done.refs_0_), channel_id=1, source_target_pairs={{0,48},{8,200},{16,0},{24,216},{32,16},{40,232},{48,32},{56,248},{... | collective-permute-start | bytes 786440 | tf_op jit(solution)/shard_map/ppermute | solution.py:210
  18.8 7.3 %collective-permute-start.1 = (bf16[2,256,256]{2,1,0:T(8,128)(2,1)S(1)}, bf16[2,256,256]{2,1,0:T(8,128)(2,1)S(1)}, u32[]{:S(2)}, u32[]{:S(2)}) collective-permute-start(bf16[2,256,256]{2,1,0:T(8,128)(2,1)S(1)} %collective-permute-done.refs_0_), channel_id=1, source_target_pairs={{0,16},{8,72},{16,32},{24,88},{32,48},{40,104},{48,0},{56,120},{64... | collective-permute-start | bytes 786440 | tf_op jit(solution)/shard_map/ppermute | solution.py:210
  26.1 13.7 %collective-permute-start.10 = (bf16[2,256,256]{2,1,0:T(8,128)(2,1)S(1)}, bf16[2,256,256]{2,1,0:T(8,128)(2,1)S(1)}, u32[]{:S(2)}, u32[]{:S(2)}) collective-permute-start(bf16[2,256,256]{2,1,0:T(8,128)(2,1)S(1)} %collective-permute-done.4.refs_7_), channel_id=1, source_target_pairs={{0,1},{1,2},{2,3},{3,4},{4,5},{5,6},{6,7},{7,0},{8,9},{9,10},{10,1... | collective-permute-start | bytes 786440 | tf_op jit(solution)/shard_map/ppermute | solution.py:219
  30.1 14.0 %collective-permute-start.12 = (bf16[2,256,256]{2,1,0:T(8,128)(2,1)S(1)}, bf16[2,256,256]{2,1,0:T(8,128)(2,1)S(1)}, u32[]{:S(2)}, u32[]{:S(2)}) collective-permute-start(bf16[2,256,256]{2,1,0:T(8,128)(2,1)S(1)} %collective-permute-done.5.refs_1_), channel_id=1, source_target_pairs={{0,7},{1,0},{2,1},{3,2},{4,3},{5,4},{6,5},{7,6},{8,15},{9,8},{10,9... | collective-permute-start | bytes 786440 | tf_op jit(solution)/shard_map/ppermute | solution.py:222
  36.1 18.0 %collective-permute-start.9 = (bf16[2,2,256,256]{3,2,1,0:T(8,128)(2,1)S(1)}, bf16[2,2,256,256]{3,2,1,0:T(8,128)(2,1)S(1)}, u32[]{:S(2)}, u32[]{:S(2)}) collective-permute-start(bf16[2,2,256,256]{3,2,1,0:T(8,128)(2,1)S(1)} %shard_map.57.refs_3_), channel_id=1, source_target_pairs={{0,192},{8,56},{16,208},{24,8},{32,224},{40,24},{48,240},{56,40},{... | collective-permute-start | bytes 1572872 | tf_op jit(solution)/shard_map/ppermute | solution.py:213
  39.7 8.8 %collective-permute-start.11 = (bf16[2,256,256]{2,1,0:T(8,128)(2,1)S(1)}, bf16[2,256,256]{2,1,0:T(8,128)(2,1)S(1)}, u32[]{:S(2)}, u32[]{:S(2)}) collective-permute-start(bf16[2,256,256]{2,1,0:T(8,128)(2,1)S(1)} %collective-permute-done.10.refs_6_), channel_id=1, source_target_pairs={{0,1},{1,2},{2,3},{3,4},{4,5},{5,6},{6,7},{7,0},{8,9},{9,10},{10,1... | collective-permute-start | bytes 786440 | tf_op jit(solution)/shard_map/ppermute | solution.py:219
  39.7 14.3 %collective-permute-start.8 = (bf16[2,2,256,256]{3,2,1,0:T(8,128)(2,1)S(1)}, bf16[2,2,256,256]{3,2,1,0:T(8,128)(2,1)S(1)}, u32[]{:S(2)}, u32[]{:S(2)}) collective-permute-start(bf16[2,2,256,256]{3,2,1,0:T(8,128)(2,1)S(1)} %shard_map.57.refs_3_), channel_id=1, source_target_pairs={{0,64},{8,24},{16,80},{24,40},{32,96},{40,56},{48,112},{56,8},{64,... | collective-permute-start | bytes 1572872 | tf_op jit(solution)/shard_map/ppermute | solution.py:213
  41.3 35.7 %copy-start.1 = (bf16[2,256,256]{2,1,0:T(8,128)(2,1)S(1)}, bf16[2,256,256]{2,1,0:T(8,128)(2,1)}, u32[]{:S(2)}) copy-start(bf16[2,256,256]{2,1,0:T(8,128)(2,1)} %get-tuple-element.42.refs_9_) | copy-start | bytes 786436
  41.4 12.7 %collective-permute-start.7 = (bf16[2,2,256,256]{3,2,1,0:T(8,128)(2,1)S(1)}, bf16[2,2,256,256]{3,2,1,0:T(8,128)(2,1)S(1)}, u32[]{:S(2)}, u32[]{:S(2)}) collective-permute-start(bf16[2,2,256,256]{3,2,1,0:T(8,128)(2,1)S(1)} %shard_map.56.refs_0_), channel_id=1, source_target_pairs={{0,192},{8,56},{16,208},{24,8},{32,224},{40,24},{48,240},{56,40},{... | collective-permute-start | bytes 1572872 | tf_op jit(solution)/shard_map/ppermute | solution.py:213
  44.1 12.3 %collective-permute-start.6 = (bf16[2,2,256,256]{3,2,1,0:T(8,128)(2,1)S(1)}, bf16[2,2,256,256]{3,2,1,0:T(8,128)(2,1)S(1)}, u32[]{:S(2)}, u32[]{:S(2)}) collective-permute-start(bf16[2,2,256,256]{3,2,1,0:T(8,128)(2,1)S(1)} %shard_map.56.refs_0_), channel_id=1, source_target_pairs={{0,64},{8,24},{16,80},{24,40},{32,96},{40,56},{48,112},{56,8},{64,... | collective-permute-start | bytes 1572872 | tf_op jit(solution)/shard_map/ppermute | solution.py:213
  48.6 5.5 %collective-permute-start.13 = (bf16[2,256,256]{2,1,0:T(8,128)(2,1)S(1)}, bf16[2,256,256]{2,1,0:T(8,128)(2,1)S(1)}, u32[]{:S(2)}, u32[]{:S(2)}) collective-permute-start(bf16[2,256,256]{2,1,0:T(8,128)(2,1)S(1)} %collective-permute-done.12.refs_2_), channel_id=1, source_target_pairs={{0,7},{1,0},{2,1},{3,2},{4,3},{5,4},{6,5},{7,6},{8,15},{9,8},{10,9... | collective-permute-start | bytes 786440 | tf_op jit(solution)/shard_map/ppermute | solution.py:222
  56.4 10.3 %collective-permute-start.15 = (bf16[2,2,256,256]{3,2,1,0:T(8,128)(2,1)S(1)}, bf16[2,2,256,256]{3,2,1,0:T(8,128)(2,1)S(1)}, u32[]{:S(2)}, u32[]{:S(2)}) collective-permute-start(bf16[2,2,256,256]{3,2,1,0:T(8,128)(2,1)S(1)} %collective-permute-done.6.refs_1_), channel_id=1, source_target_pairs={{0,64},{8,24},{16,80},{24,40},{32,96},{40,56},{48,112},{56,8},{64,... | collective-permute-start | bytes 1572872 | tf_op jit(solution)/shard_map/ppermute | solution.py:213
  56.4 10.3 %collective-permute-start.16 = (bf16[2,2,256,256]{3,2,1,0:T(8,128)(2,1)S(1)}, bf16[2,2,256,256]{3,2,1,0:T(8,128)(2,1)S(1)}, u32[]{:S(2)}, u32[]{:S(2)}) collective-permute-start(bf16[2,2,256,256]{3,2,1,0:T(8,128)(2,1)S(1)} %collective-permute-done.9.refs_5_), channel_id=1, source_target_pairs={{0,192},{8,56},{16,208},{24,8},{32,224},{40,24},{48,240},{56,40},{... | collective-permute-start | bytes 1572872 | tf_op jit(solution)/shard_map/ppermute | solution.py:213
  59.1 6.4 %collective-permute-start.14 = (bf16[2,256,256]{2,1,0:T(8,128)(2,1)S(1)}, bf16[2,256,256]{2,1,0:T(8,128)(2,1)S(1)}, u32[]{:S(2)}, u32[]{:S(2)}) collective-permute-start(bf16[2,256,256]{2,1,0:T(8,128)(2,1)S(1)} %collective-permute-done.11.refs_5_), channel_id=1, source_target_pairs={{0,1},{1,2},{2,3},{3,4},{4,5},{5,6},{6,7},{7,0},{8,9},{9,10},{10,1... | collective-permute-start | bytes 786440 | tf_op jit(solution)/shard_map/ppermute | solution.py:219
  65.6 1.0 copy-start.2
  66.8 14.7 %collective-permute-start.17 = (bf16[9,2,256,256]{3,2,1,0:T(8,128)(2,1)S(1)}, bf16[9,2,256,256]{3,2,1,0:T(8,128)(2,1)S(1)}, u32[]{:S(2)}, u32[]{:S(2)}) collective-permute-start(bf16[9,2,256,256]{3,2,1,0:T(8,128)(2,1)S(1)} %shard_map.58.refs_8_), channel_id=1, source_target_pairs={{0,8},{8,0},{16,24},{24,16},{32,40},{40,32},{48,56},{56,48},{64,72... | collective-permute-start | bytes 7077896 | tf_op jit(solution)/shard_map/ppermute | solution.py:216
  81.5 4.5 %copy-start.3 = (s32[32]{0:T(128)S(1)}, s32[32]{0:T(128)}, u32[]{:S(2)}) copy-start(s32[32]{0:T(128)} %left_sizes.3) | copy-start | bytes 388
  81.5 4.5 %copy-start.4 = (s32[32]{0:T(128)S(1)}, s32[32]{0:T(128)}, u32[]{:S(2)}) copy-start(s32[32]{0:T(128)} %right_sizes.3) | copy-start | bytes 388

commit v15 on v14

--- a/solution.py
+++ b/solution.py
@@ -85,12 +85,12 @@
 
 def half_kernel(pieces, *refs):
     ins, (out_ref, held, left_held, psi_held, middle, sems) = refs[:-6], refs[-6:]
-    shards, (lefts, psi) = ins[: len(pieces)], ins[len(pieces) :]
+    shards, lefts, psi = ins[: len(pieces)], ins[len(pieces)], ins[len(pieces) + 1 :]
     _, rank, core, x0, y0 = coordinates()
     ranks, pair, left_dim, inner = left_held.shape
     right_dim = psi_held.shape[2]
     first = [
-        pltpu.make_async_copy(psi, psi_held, sems.at[0]),
+        pltpu.make_async_copy(psi[0] if psi else lefts.at[ranks], psi_held, sems.at[0]),
         pltpu.make_async_copy(lefts.at[pl.ds(0, ranks)], left_held, sems.at[1]),
     ]
     coming = [pltpu.make_async_copy(r, held.at[i], sems.at[2 + i]) for i, r in enumerate(shards)]
@@ -119,50 +119,93 @@
             out_ref[which] += jnp.dot(middle[which, at], shard, preferred_element_type=jnp.float32)
 
 
-def half(pieces, shards, lefts, psi):
-    dtype = psi.dtype
+def half(pieces, shards, lefts, *psi):
+    dtype = lefts.dtype
     slots, pair, left_dim, inner = lefts.shape
-    ranks, right_dim = slots - 1, psi.shape[2]
+    ranks, right_dim = slots - 1, shards[0].shape[-1]
     return pl.pallas_call(
         functools.partial(half_kernel, pieces),
         out_shape=jax.ShapeDtypeStruct((2, left_dim, right_dim), jnp.float32),
-        in_specs=[ANYWHERE] * (len(shards) + 2),
+        in_specs=[ANYWHERE] * (len(shards) + 1 + len(psi)),
         out_specs=VMEM,
         scratch_shapes=[
             pltpu.VMEM((len(shards), *shards[0].shape), dtype),
             pltpu.VMEM((ranks, pair, left_dim, inner), dtype),
-            pltpu.VMEM(psi.shape, dtype),
+            pltpu.VMEM((2, inner, right_dim), dtype),
             pltpu.VMEM((2, ranks, left_dim, pair * right_dim), dtype),
             pltpu.SemaphoreType.DMA((len(shards) + 2,)),
         ],
         compiler_params=pltpu.CompilerParams(vmem_limit_bytes=24 * MIB),
-    )(*shards, lefts, psi)
-
-
-def join_kernel(left_sizes, right_sizes, own_ref, other_ref, out_ref):
-    sector, rank, core, _, _ = coordinates()
+    )(*shards, lefts, *psi)
+
+
+def last_kernel(pieces, left_sizes, right_sizes, mine, theirs, *refs):
+    ins, (out_ref, held, left_held, psi_held, total, sems) = refs[:-6], refs[-6:]
+    shards, (lefts, others, psi) = ins[: len(pieces)], ins[len(pieces) :]
+    sector, rank, core, x0, y0 = coordinates()
     ranks, _, _, rows, right_dim = out_ref.shape
     left_dim = ranks * rows
+    copies = [
+        pltpu.make_async_copy(psi, psi_held.at[0], sems.at[0]),
+        pltpu.make_async_copy(others.at[ranks], psi_held.at[1], sems.at[1]),
+    ]
+    sectors_of = []
+    for i, (far, start) in enumerate(pieces):
+        copies.append(pltpu.make_async_copy(shards[i], held.at[i], sems.at[len(copies)]))
+        for k in range(held.shape[1]):
+            near = OFFSETS[start + k]
+            y = jnp.where(core == 0, y0 + far, y0 + near) & (SIDE - 1)
+            x = jnp.where(core == 0, x0 + near, x0 + far) & (SIDE - 1)
+            at = (x + SIDE * (y & 1) - rank) & (ranks - 1)
+            for a, source in enumerate((lefts, others)):
+                place_in = left_held.at[len(sectors_of), a]
+                copies.append(pltpu.make_async_copy(source.at[at], place_in, sems.at[len(copies)]))
+            sectors_of.append(y // 2)
+    for copy in copies:
+        copy.start()
+    total[0] = mine[...]
+    total[1] = theirs[...]
+    for copy in copies:
+        copy.wait()
+    for i, which in enumerate(sectors_of):
+        shard = held[i // held.shape[1], i % held.shape[1]]
+        for a in range(2):
+            block = left_held[i, a].reshape(2 * left_dim, left_dim)
+            product = jnp.dot(block, psi_held[a, which], preferred_element_type=jnp.float32)
+            product = product.astype(held.dtype)
+            term = jnp.dot(product[:left_dim], shard[0], preferred_element_type=jnp.float32)
+            term += jnp.dot(product[left_dim:], shard[1], preferred_element_type=jnp.float32)
+            total[a, which] += term
     row = lax.broadcasted_iota(jnp.int32, (left_dim, right_dim), 0)
     col = lax.broadcasted_iota(jnp.int32, (left_dim, right_dim), 1)
     for b in range(2):
         own_right = right_sizes[right_sector(rank, core, b)]
-        for total, spot in ((own_ref, core), (other_ref, 1 - core)):
+        for a, spot in enumerate((core, 1 - core)):
             inside = jnp.logical_and(row < left_sizes[sector - core + spot], col < own_right)
-            block = jnp.where(inside, total[b], 0.0)
+            block = jnp.where(inside, total[a, b], 0.0)
             block = block.astype(out_ref.dtype).reshape(ranks, 1, rows, right_dim)
             out_ref[:, b, pl.ds(spot, 1)] = block
 
 
-def join(own, other, left_sizes, right_sizes, ranks, dtype):
-    _, left_dim, right_dim = own.shape
-    return pl.pallas_call(
-        join_kernel,
+def last(pieces, shards, mine, theirs, lefts, others, psi, left_sizes, right_sizes):
+    dtype = psi.dtype
+    slots, pair, left_dim, inner = lefts.shape
+    ranks, right_dim = slots - 1, psi.shape[2]
+    count = len(shards) * shards[0].shape[0]
+    return pl.pallas_call(
+        functools.partial(last_kernel, pieces),
         out_shape=jax.ShapeDtypeStruct((ranks, 2, 2, left_dim // ranks, right_dim), dtype),
-        in_specs=[SMEM, SMEM, VMEM, VMEM],
+        in_specs=[SMEM, SMEM, VMEM, VMEM] + [ANYWHERE] * (len(shards) + 3),
         out_specs=VMEM,
-        compiler_params=pltpu.CompilerParams(vmem_limit_bytes=8 * MIB),
-    )(left_sizes, right_sizes, own, other)
+        scratch_shapes=[
+            pltpu.VMEM((len(shards), *shards[0].shape), dtype),
+            pltpu.VMEM((count, 2, pair, left_dim, inner), dtype),
+            pltpu.VMEM((2, *psi.shape), dtype),
+            pltpu.VMEM((2, *mine.shape), jnp.float32),
+            pltpu.SemaphoreType.DMA((2 + len(shards) + 2 * count,)),
+        ],
+        compiler_params=pltpu.CompilerParams(vmem_limit_bytes=24 * MIB),
+    )(left_sizes, right_sizes, mine, theirs, *shards, lefts, others, psi)
 
 
 def order_kernel(in_ref, out_ref, sems):
@@ -232,29 +275,27 @@
     own = lax.ppermute(right_env, ("blk", "mpo"), turn)
     up1, down1 = up(left_env), down(left_env)
     keep, give = cut(wavefunction, left_sizes, right_sizes)
-    own, keep, give = together(own, keep, give)
+    up2, down2 = up(up1), down(down1)
+    own, keep, give, up2, down2 = together(own, keep, give, up2, down2)
 
     below, above, two = near_step(own, 1), near_step(own, -1), near_step(own, 2)
-    below, above, two, up1, down1 = together(below, above, two, up1, down1)
+    up3, down3 = up(up2), down(down2)
+    below, above, two, up3, down3 = together(below, above, two, up3, down3)
     line_a, line_b = stack(own, below), stack(above, two)
     a_below, a_above = far_step(line_a, 1), far_step(line_a, -1)
     b_below, b_above = far_step(line_b, 1), far_step(line_b, -1)
-    up2, down2 = up(up1), down(down1)
-    up3, down3 = up(up2), down(down2)
-    a_below, a_above, b_below, b_above, up3, down3 = together(
-        a_below, a_above, b_below, b_above, up3, down3
-    )
-    a_two, b_two = far_step(a_below, 1), far_step(b_above, -1)
     up4 = up(up3)
     lefts = stack(left_env, down1, down2, down3, up4, up3, up2, up1, give)
-    lefts, a_two, b_two = together(lefts, a_two, b_two)
+    a_below, a_above, b_below, b_above, lefts = together(a_below, a_above, b_below, b_above, lefts)
+    a_two, b_two = far_step(a_below, 1), far_step(b_above, -1)
     others = swap(lefts)
 
-    pieces = ((0, 0), (SIDE - 1, 0), (1, 0), (0, 2), (SIDE - 1, 2), (1, 2), (2, 0), (2, 2))
-    shards = (line_a, a_below, a_above, line_b, b_below, b_above, a_two, b_two)
-    mine = half(pieces, shards, lefts, keep)
-    theirs = half(pieces, shards, others, others[ranks])
-    done = join(mine, theirs, left_sizes, right_sizes, ranks, wavefunction.dtype)
+    early = ((0, 0), (SIDE - 1, 0), (1, 0), (0, 2), (SIDE - 1, 2), (1, 2))
+    shards = (line_a, a_below, a_above, line_b, b_below, b_above)
+    mine = half(early, shards, lefts, keep)
+    theirs = half(early, shards, others)
+    late = ((2, 0), (2, 2))
+    done = last(late, (a_two, b_two), mine, theirs, lefts, others, keep, left_sizes, right_sizes)
 
     by_plane = lax.all_to_all(done, "mpo", 0, 0)
     chips = SIDE * SIDE

time: 124 us -> 115 us (0.927)
  starting transfers between devices: 50.1 us -> 37.2 us
  blocking collectives: 35.1 us -> 37.2 us
    ppermute x1, starting transfers between devices: 10.3 us -> 5.59 us  [swap(): return lax.ppermute(block, 'blk', [(i, i ^ 1) for i in range(sectors)])]
    ppermute x1, starting transfers between devices: 9.77 us -> 5.83 us  [local(): own = lax.ppermute(right_env, ('blk', 'mpo'), turn)]
    ppermute x3, waiting for transfers between devices: 3.85 us -> 0.01 us  [down(): lax.ppermute(block, 'mpo', [(z, (z - 1) % ranks) for z in range(ranks)])]
    ppermute x3, waiting for transfers between devices: 0.01 us -> 3.77 us  [near_step(): return lax.ppermute(block, 'blk', step(False, by))]
    all_to_all x1, blocking collectives: 13.9 us -> 16.2 us  [local(): out = order(lax.all_to_all(by_plane, 'blk', 0, 0, axis_index_groups=groups))]
    ppermute x4, waiting for transfers between devices: 16.6 us -> 18.9 us  [up(): lax.ppermute(block, 'mpo', [(z, (z + 1) % ranks) for z in range(ranks)])]
    ppermute x4, starting transfers between devices: 6.43 us -> 4.44 us  [up(): lax.ppermute(block, 'mpo', [(z, (z + 1) % ranks) for z in range(ranks)])]
    pallas_call x1, Pallas kernels: 0.67 us -> 2.62 us  [last(): pl.pallas_call(functools.partial(last_kernel, pieces), out_shape=jax.Shap...]
  transfers between devices with their start and end apart: 18 -> 18, of which waited for: 6 -> 6; matrix products, arithmetic and copies ran while one was open for 0% -> 0% of each run, Pallas kernels for 6% -> 9%
where the time goes in v15:
time: 115 us; the launch traced here: 114 us
  starting transfers between devices  37.2 us (32%)
  blocking collectives  37.2 us (32%)
  waiting for transfers between devices  24.1 us (21%)
  Pallas kernels  13.9 us (12%)
    all_to_all x1, blocking collectives, local(): by_plane = lax.all_to_all(done, 'mpo', 0, 0)  21 us
    ppermute x4, waiting for transfers between devices, up(): lax.ppermute(block, 'mpo', [(z, (z + 1) % ranks) for z in range(ranks)])  18.9 us
    all_to_all x1, blocking collectives, local(): out = order(lax.all_to_all(by_plane, 'blk', 0, 0, axis_index_groups=groups))  16.2 us
    ppermute x3, starting transfers between devices, down(): lax.ppermute(block, 'mpo', [(z, (z - 1) % ranks) for z in range(ranks)])  9.06 us
    ppermute x6, starting transfers between devices, far_step(): return lax.ppermute(block, 'blk', step(True, by))  8.17 us
    pallas_call x2, Pallas kernels, half(): pl.pallas_call(functools.partial(half_kernel, pieces), out_shape=jax.Shap...  7.38 us
    ppermute x1, starting transfers between devices, local(): own = lax.ppermute(right_env, ('blk', 'mpo'), turn)  5.83 us
    ppermute x1, starting transfers between devices, swap(): return lax.ppermute(block, 'blk', [(i, i ^ 1) for i in range(sectors)])  5.59 us
  transfers between devices with their start and end apart: 18, of which 6 were waited for; matrix products, arithmetic and copies ran while one was open for 0% of the time, Pallas kernels for 9%

profile of v15, /device:TPU:1, one launch (start us, length us, event | category | flops | bytes accessed | tf_op | source)
XLA Modules:
  0.0 113.7 jit_solution(2851171584662287693)
XLA Ops:
  0.0 0.0 copy-start.1
  0.0 2.5 %collective-permute-start.1 = (bf16[2,256,256]{2,1,0:T(8,128)(2,1)}, bf16[2,256,256]{2,1,0:T(8,128)(2,1)S(1)}, u32[]{:S(2)}, u32[]{:S(2)}) collective-permute-start(bf16[2,256,256]{2,1,0:T(8,128)(2,1)} %refs_0_.1), channel_id=1, source_target_pairs={{0,1},{1,2},{2,3},{3,4},{4,5},{5,6},{6,7},{7,0},{8,9},{9,10},{10,1... | collective-permute-start | bytes 786440 | tf_op jit(solution)/shard_map/ppermute | solution.py:262
  2.5 4.0 %collective-permute-start.3 = (bf16[2,256,256]{2,1,0:T(8,128)(2,1)}, bf16[2,256,256]{2,1,0:T(8,128)(2,1)S(1)}, u32[]{:S(2)}, u32[]{:S(2)}) collective-permute-start(bf16[2,256,256]{2,1,0:T(8,128)(2,1)} %refs_0_.1), channel_id=1, source_target_pairs={{0,7},{1,0},{2,1},{3,2},{4,3},{5,4},{6,5},{7,6},{8,15},{9,8},{10,9... | collective-permute-start | bytes 786440 | tf_op jit(solution)/shard_map/ppermute | solution.py:265
  6.5 5.8 %collective-permute-start = (bf16[2,256,256]{2,1,0:T(8,128)(2,1)}, bf16[2,256,256]{2,1,0:T(8,128)(2,1)S(1)}, u32[]{:S(2)}, u32[]{:S(2)}) collective-permute-start(bf16[2,256,256]{2,1,0:T(8,128)(2,1)} %param.7), channel_id=1, source_target_pairs={{0,0},{1,16},{2,32},{3,48},{4,64},{5,80},{6,96},{7,112},{8,12},{9,... | collective-permute-start | bytes 786440 | tf_op jit(solution)/shard_map/ppermute | solution.py:275
  12.3 0.4 collective-permute-done.1.refs_7_
  12.7 0.9 collective-permute-start.2
  13.6 0.0 collective-permute-done.3.refs_1_
  13.6 2.4 %collective-permute-start.4 = (bf16[2,256,256]{2,1,0:T(8,128)(2,1)S(1)}, bf16[2,256,256]{2,1,0:T(8,128)(2,1)S(1)}, u32[]{:S(2)}, u32[]{:S(2)}) collective-permute-start(bf16[2,256,256]{2,1,0:T(8,128)(2,1)S(1)} %collective-permute-done.3.refs_1_), channel_id=1, source_target_pairs={{0,7},{1,0},{2,1},{3,2},{4,3},{5,4},{6,5},{7,6},{8,15},{9,8},{10,9... | collective-permute-start | bytes 786440 | tf_op jit(solution)/shard_map/ppermute | solution.py:265
  16.0 2.6 %shard_map.55 = (bf16[2,256,256]{2,1,0:T(8,128)(2,1)}, bf16[2,256,256]{2,1,0:T(8,128)(2,1)}) custom-call(s32[32]{0:T(128)} %left_sizes.3, s32[32]{0:T(128)} %right_sizes.3, bf16[256,8192]{1,0:T(8,128)(2,1)} %psi_ref.1), custom_call_target="tpu_custom_call" | custom-call | tf_op jit(solution)/shard_map/pallas_call | solution.py:76
  18.6 0.0 collective-permute-done.refs_0_
  18.6 12.6 %collective-permute-done.2.refs_6_ = bf16[2,256,256]{2,1,0:T(8,128)(2,1)S(1)} collective-permute-done((bf16[2,256,256]{2,1,0:T(8,128)(2,1)S(1)}, bf16[2,256,256]{2,1,0:T(8,128)(2,1)S(1)}, u32[]{:S(2)}, u32[]{:S(2)}) %collective-permute-start.2) | collective-permute-done | bytes 262176 | tf_op jit(solution)/shard_map/ppermute | solution.py:262
  31.2 0.0 collective-permute-done.4.refs_2_
  31.2 1.4 %collective-permute-start.5 = (bf16[2,256,256]{2,1,0:T(8,128)(2,1)S(1)}, bf16[2,256,256]{2,1,0:T(8,128)(2,1)S(1)}, u32[]{:S(2)}, u32[]{:S(2)}) collective-permute-start(bf16[2,256,256]{2,1,0:T(8,128)(2,1)S(1)} %collective-permute-done.refs_0_), channel_id=1, source_target_pairs={{0,16},{8,72},{16,32},{24,88},{32,48},{40,104},{48,0},{56,120},{64... | collective-permute-start | bytes 786440 | tf_op jit(solution)/shard_map/ppermute | solution.py:253
  32.5 1.4 %collective-permute-start.6 = (bf16[2,256,256]{2,1,0:T(8,128)(2,1)S(1)}, bf16[2,256,256]{2,1,0:T(8,128)(2,1)S(1)}, u32[]{:S(2)}, u32[]{:S(2)}) collective-permute-start(bf16[2,256,256]{2,1,0:T(8,128)(2,1)S(1)} %collective-permute-done.refs_0_), channel_id=1, source_target_pairs={{0,48},{8,200},{16,0},{24,216},{32,16},{40,232},{48,32},{56,248},{... | collective-permute-start | bytes 786440 | tf_op jit(solution)/shard_map/ppermute | solution.py:253
  34.0 1.3 %collective-permute-start.7 = (bf16[2,256,256]{2,1,0:T(8,128)(2,1)S(1)}, bf16[2,256,256]{2,1,0:T(8,128)(2,1)S(1)}, u32[]{:S(2)}, u32[]{:S(2)}) collective-permute-start(bf16[2,256,256]{2,1,0:T(8,128)(2,1)S(1)} %collective-permute-done.refs_0_), channel_id=1, source_target_pairs={{0,32},{8,136},{16,48},{24,152},{32,0},{40,168},{48,16},{56,184},{... | collective-permute-start | bytes 786440 | tf_op jit(solution)/shard_map/ppermute | solution.py:253
  35.3 0.0 collective-permute-start.8
  35.3 2.7 %collective-permute-start.9 = (bf16[2,256,256]{2,1,0:T(8,128)(2,1)S(1)}, bf16[2,256,256]{2,1,0:T(8,128)(2,1)S(1)}, u32[]{:S(2)}, u32[]{:S(2)}) collective-permute-start(bf16[2,256,256]{2,1,0:T(8,128)(2,1)S(1)} %collective-permute-done.4.refs_2_), channel_id=1, source_target_pairs={{0,7},{1,0},{2,1},{3,2},{4,3},{5,4},{6,5},{7,6},{8,15},{9,8},{10,9... | collective-permute-start | bytes 786440 | tf_op jit(solution)/shard_map/ppermute | solution.py:265
  38.0 0.0 collective-permute-done.5.refs_1_
  38.0 0.1 collective-permute-done.6.refs_0_
  38.1 3.7 %collective-permute-done.7.refs_1_ = bf16[2,256,256]{2,1,0:T(8,128)(2,1)S(1)} collective-permute-done((bf16[2,256,256]{2,1,0:T(8,128)(2,1)S(1)}, bf16[2,256,256]{2,1,0:T(8,128)(2,1)S(1)}, u32[]{:S(2)}, u32[]{:S(2)}) %collective-permute-start.7) | collective-permute-done | bytes 262176 | tf_op jit(solution)/shard_map/ppermute | solution.py:253
  41.7 0.0 collective-permute-done.8.refs_5_
  41.7 0.0 collective-permute-done.9.refs_3_
  41.7 0.1 shard_map.56.refs_0_
  41.8 0.1 collective-permute-start.10
  41.9 2.7 %collective-permute-start.11 = (bf16[2,2,256,256]{3,2,1,0:T(8,128)(2,1)S(1)}, bf16[2,2,256,256]{3,2,1,0:T(8,128)(2,1)S(1)}, u32[]{:S(2)}, u32[]{:S(2)}) collective-permute-start(bf16[2,2,256,256]{3,2,1,0:T(8,128)(2,1)S(1)} %shard_map.56.refs_0_), channel_id=1, source_target_pairs={{0,192},{8,56},{16,208},{24,8},{32,224},{40,24},{48,240},{56,40},{... | collective-permute-start | bytes 1572872 | tf_op jit(solution)/shard_map/ppermute | solution.py:256
  44.6 0.1 shard_map.57.refs_3_
  44.6 0.0 copy-start
  44.6 0.1 collective-permute-start.12
  44.7 2.7 %collective-permute-start.13 = (bf16[2,2,256,256]{3,2,1,0:T(8,128)(2,1)S(1)}, bf16[2,2,256,256]{3,2,1,0:T(8,128)(2,1)S(1)}, u32[]{:S(2)}, u32[]{:S(2)}) collective-permute-start(bf16[2,2,256,256]{3,2,1,0:T(8,128)(2,1)S(1)} %shard_map.57.refs_3_), channel_id=1, source_target_pairs={{0,192},{8,56},{16,208},{24,8},{32,224},{40,24},{48,240},{56,40},{... | collective-permute-start | bytes 1572872 | tf_op jit(solution)/shard_map/ppermute | solution.py:256
  47.4 1.1 collective-permute-start.14
  48.5 5.9 %collective-permute-done.14.refs_4_ = bf16[2,256,256]{2,1,0:T(8,128)(2,1)S(1)} collective-permute-done((bf16[2,256,256]{2,1,0:T(8,128)(2,1)S(1)}, bf16[2,256,256]{2,1,0:T(8,128)(2,1)S(1)}, u32[]{:S(2)}, u32[]{:S(2)}) %collective-permute-start.14) | collective-permute-done | bytes 262176 | tf_op jit(solution)/shard_map/ppermute | solution.py:262
  54.4 0.0 copy-done.1
  54.4 0.0 copy-start.2
  54.4 0.9 copy-done.2
  55.3 0.3 shard_map.58.refs_6_.refs_2_
  55.6 0.0 collective-permute-done.10.refs_1_
  55.6 0.0 collective-permute-done.11.refs_2_
  55.6 1.4 %collective-permute-done.12.refs_4_ = bf16[2,2,256,256]{3,2,1,0:T(8,128)(2,1)S(1)} collective-permute-done((bf16[2,2,256,256]{3,2,1,0:T(8,128)(2,1)S(1)}, bf16[2,2,256,256]{3,2,1,0:T(8,128)(2,1)S(1)}, u32[]{:S(2)}, u32[]{:S(2)}) %collective-permute-start.12) | collective-permute-done | bytes 524320 | tf_op jit(solution)/shard_map/ppermute | solution.py:256
  57.0 0.0 collective-permute-done.13.refs_5_
  57.0 5.6 %collective-permute-start.15 = (bf16[9,2,256,256]{3,2,1,0:T(8,128)(2,1)S(1)}, bf16[9,2,256,256]{3,2,1,0:T(8,128)(2,1)S(1)}, u32[]{:S(2)}, u32[]{:S(2)}) collective-permute-start(bf16[9,2,256,256]{3,2,1,0:T(8,128)(2,1)S(1)} %shard_map.58.refs_6_.refs_2_), channel_id=1, source_target_pairs={{0,8},{8,0},{16,24},{24,16},{32,40},{40,32},{48,56},{56,48},{64,72... | collective-permute-start | bytes 7077896 | tf_op jit(solution)/shard_map/ppermute | solution.py:259
  62.6 0.0 collective-permute-start.16
  62.6 2.7 %collective-permute-start.17 = (bf16[2,2,256,256]{3,2,1,0:T(8,128)(2,1)S(1)}, bf16[2,2,256,256]{3,2,1,0:T(8,128)(2,1)S(1)}, u32[]{:S(2)}, u32[]{:S(2)}) collective-permute-start(bf16[2,2,256,256]{3,2,1,0:T(8,128)(2,1)S(1)} %collective-permute-done.13.refs_5_), channel_id=1, source_target_pairs={{0,192},{8,56},{16,208},{24,8},{32,224},{40,24},{48,240},{56,40},{... | collective-permute-start | bytes 1572872 | tf_op jit(solution)/shard_map/ppermute | solution.py:256
  65.3 0.0 copy-done
  65.3 3.7 %shard_map.59.mine = f32[2,256,256]{2,1,0:T(8,128)S(1)} custom-call(bf16[2,2,256,256]{3,2,1,0:T(8,128)(2,1)S(1)} %shard_map.56.refs_0_, bf16[2,2,256,256]{3,2,1,0:T(8,128)(2,1)S(1)} %collective-permute-done.10.refs_1_, bf16[2,2,256,256]{3,2,1,0:T(8,128)(2,1)S(1)} %collective-permute-done.11.refs_2_, bf16[2,2,256,256]{3,2,1,0:T(8,128)(2,1)S(1)} %shard_map.57.refs_3_, ...), custom_call_target="tpu_custom_call" | custom-call | tf_op jit(solution)/shard_map/pallas_call | solution.py:126
  69.0 0.0 copy-start.3
  69.0 0.0 copy-start.4
  69.0 0.0 collective-permute-done.15.refs_6_.refs_3_
  69.0 3.7 %shard_map.60.theirs = f32[2,256,256]{2,1,0:T(8,128)S(1)} custom-call(bf16[2,2,256,256]{3,2,1,0:T(8,128)(2,1)S(1)} %shard_map.56.refs_0_, bf16[2,2,256,256]{3,2,1,0:T(8,128)(2,1)S(1)} %collective-permute-done.10.refs_1_, bf16[2,2,256,256]{3,2,1,0:T(8,128)(2,1)S(1)} %collective-permute-done.11.refs_2_, bf16[2,2,256,256]{3,2,1,0:T(8,128)(2,1)S(1)} %shard_map.57.refs_3_, ...), custom_call_target="tpu_custom_call" | custom-call | tf_op jit(solution)/shard_map/pallas_call | solution.py:126
  72.7 0.0 collective-permute-done.16.refs_0_
  72.8 0.0 collective-permute-done.17.refs_1_
  72.8 0.0 copy-done.3
  72.8 0.0 copy-done.4
  72.8 2.6 %shard_map.61 = bf16[8,2,2,32,256]{4,3,2,1,0:T(8,128)(2,1)S(1)} custom-call(s32[32]{0:T(128)S(1)} %copy-done.3, s32[32]{0:T(128)S(1)} %copy-done.4, f32[2,256,256]{2,1,0:T(8,128)S(1)} %shard_map.59.mine, f32[2,256,256]{2,1,0:T(8,128)S(1)} %shard_map.60.theirs, bf16[2,2,256,256]{3,2,1,0:T(8,128)(2,1)S(1)} %collective-permute-done.16.refs_0_, ...), custom_call_target="tpu_custom_call" | custom-call | tf_op jit(solution)/shard_map/pallas_call | solution.py:195
  75.4 21.0 %all_to_all.10 = bf16[8,2,2,32,256]{4,3,2,1,0:T(8,128)(2,1)S(1)} all-to-all(bf16[8,2,2,32,256]{4,3,2,1,0:T(8,128)(2,1)S(1)} %shard_map.61), channel_id=1, replica_groups=mesh['blk'=32,'mpo'=8] {'mpo'}, dimensions={0} | all-to-all | bytes 1048576 | tf_op jit(solution)/shard_map/all_to_all | solution.py:300
  96.4 16.2 %all_to_all.11.in_ref = bf16[16,2,32,256]{3,2,1,0:T(8,128)(2,1)S(1)} all-to-all(bf16[16,2,32,256]{3,2,1,0:T(8,128)(2,1)S(1)} %bitcast.2), channel_id=1, replica_groups={{0,128,16,144,32,160,48,176,64,192,80,208,96,224,112,240},{72,200,88,21..., dimensions={0} | all-to-all | bytes 1048576 | tf_op jit(solution)/shard_map/all_to_all | solution.py:307
  112.7 0.9 shard_map.62
Async XLA Ops:
  0.0 54.4 %copy-start.1 = (bf16[2,256,256]{2,1,0:T(8,128)(2,1)S(1)}, bf16[2,256,256]{2,1,0:T(8,128)(2,1)}, u32[]{:S(2)}) copy-start(bf16[2,256,256]{2,1,0:T(8,128)(2,1)} %refs_0_.1) | copy-start | bytes 786436
  0.0 12.7 %collective-permute-start.1 = (bf16[2,256,256]{2,1,0:T(8,128)(2,1)}, bf16[2,256,256]{2,1,0:T(8,128)(2,1)S(1)}, u32[]{:S(2)}, u32[]{:S(2)}) collective-permute-start(bf16[2,256,256]{2,1,0:T(8,128)(2,1)} %refs_0_.1), channel_id=1, source_target_pairs={{0,1},{1,2},{2,3},{3,4},{4,5},{5,6},{6,7},{7,0},{8,9},{9,10},{10,1... | collective-permute-start | bytes 786440 | tf_op jit(solution)/shard_map/ppermute | solution.py:262
  2.5 11.2 %collective-permute-start.3 = (bf16[2,256,256]{2,1,0:T(8,128)(2,1)}, bf16[2,256,256]{2,1,0:T(8,128)(2,1)S(1)}, u32[]{:S(2)}, u32[]{:S(2)}) collective-permute-start(bf16[2,256,256]{2,1,0:T(8,128)(2,1)} %refs_0_.1), channel_id=1, source_target_pairs={{0,7},{1,0},{2,1},{3,2},{4,3},{5,4},{6,5},{7,6},{8,15},{9,8},{10,9... | collective-permute-start | bytes 786440 | tf_op jit(solution)/shard_map/ppermute | solution.py:265
  6.5 12.1 %collective-permute-start = (bf16[2,256,256]{2,1,0:T(8,128)(2,1)}, bf16[2,256,256]{2,1,0:T(8,128)(2,1)S(1)}, u32[]{:S(2)}, u32[]{:S(2)}) collective-permute-start(bf16[2,256,256]{2,1,0:T(8,128)(2,1)} %param.7), channel_id=1, source_target_pairs={{0,0},{1,16},{2,32},{3,48},{4,64},{5,80},{6,96},{7,112},{8,12},{9,... | collective-permute-start | bytes 786440 | tf_op jit(solution)/shard_map/ppermute | solution.py:275
  12.7 18.5 %collective-permute-start.2 = (bf16[2,256,256]{2,1,0:T(8,128)(2,1)S(1)}, bf16[2,256,256]{2,1,0:T(8,128)(2,1)S(1)}, u32[]{:S(2)}, u32[]{:S(2)}) collective-permute-start(bf16[2,256,256]{2,1,0:T(8,128)(2,1)S(1)} %collective-permute-done.1.refs_7_), channel_id=1, source_target_pairs={{0,1},{1,2},{2,3},{3,4},{4,5},{5,6},{6,7},{7,0},{8,9},{9,10},{10,1... | collective-permute-start | bytes 786440 | tf_op jit(solution)/shard_map/ppermute | solution.py:262
  13.6 17.6 %collective-permute-start.4 = (bf16[2,256,256]{2,1,0:T(8,128)(2,1)S(1)}, bf16[2,256,256]{2,1,0:T(8,128)(2,1)S(1)}, u32[]{:S(2)}, u32[]{:S(2)}) collective-permute-start(bf16[2,256,256]{2,1,0:T(8,128)(2,1)S(1)} %collective-permute-done.3.refs_1_), channel_id=1, source_target_pairs={{0,7},{1,0},{2,1},{3,2},{4,3},{5,4},{6,5},{7,6},{8,15},{9,8},{10,9... | collective-permute-start | bytes 786440 | tf_op jit(solution)/shard_map/ppermute | solution.py:265
  31.2 6.8 %collective-permute-start.5 = (bf16[2,256,256]{2,1,0:T(8,128)(2,1)S(1)}, bf16[2,256,256]{2,1,0:T(8,128)(2,1)S(1)}, u32[]{:S(2)}, u32[]{:S(2)}) collective-permute-start(bf16[2,256,256]{2,1,0:T(8,128)(2,1)S(1)} %collective-permute-done.refs_0_), channel_id=1, source_target_pairs={{0,16},{8,72},{16,32},{24,88},{32,48},{40,104},{48,0},{56,120},{64... | collective-permute-start | bytes 786440 | tf_op jit(solution)/shard_map/ppermute | solution.py:253
  32.5 5.5 %collective-permute-start.6 = (bf16[2,256,256]{2,1,0:T(8,128)(2,1)S(1)}, bf16[2,256,256]{2,1,0:T(8,128)(2,1)S(1)}, u32[]{:S(2)}, u32[]{:S(2)}) collective-permute-start(bf16[2,256,256]{2,1,0:T(8,128)(2,1)S(1)} %collective-permute-done.refs_0_), channel_id=1, source_target_pairs={{0,48},{8,200},{16,0},{24,216},{32,16},{40,232},{48,32},{56,248},{... | collective-permute-start | bytes 786440 | tf_op jit(solution)/shard_map/ppermute | solution.py:253
  34.0 7.7 %collective-permute-start.7 = (bf16[2,256,256]{2,1,0:T(8,128)(2,1)S(1)}, bf16[2,256,256]{2,1,0:T(8,128)(2,1)S(1)}, u32[]{:S(2)}, u32[]{:S(2)}) collective-permute-start(bf16[2,256,256]{2,1,0:T(8,128)(2,1)S(1)} %collective-permute-done.refs_0_), channel_id=1, source_target_pairs={{0,32},{8,136},{16,48},{24,152},{32,0},{40,168},{48,16},{56,184},{... | collective-permute-start | bytes 786440 | tf_op jit(solution)/shard_map/ppermute | solution.py:253
  35.3 6.5 %collective-permute-start.8 = (bf16[2,256,256]{2,1,0:T(8,128)(2,1)S(1)}, bf16[2,256,256]{2,1,0:T(8,128)(2,1)S(1)}, u32[]{:S(2)}, u32[]{:S(2)}) collective-permute-start(bf16[2,256,256]{2,1,0:T(8,128)(2,1)S(1)} %collective-permute-done.2.refs_6_), channel_id=1, source_target_pairs={{0,1},{1,2},{2,3},{3,4},{4,5},{5,6},{6,7},{7,0},{8,9},{9,10},{10,1... | collective-permute-start | bytes 786440 | tf_op jit(solution)/shard_map/ppermute | solution.py:262
  35.3 6.5 %collective-permute-start.9 = (bf16[2,256,256]{2,1,0:T(8,128)(2,1)S(1)}, bf16[2,256,256]{2,1,0:T(8,128)(2,1)S(1)}, u32[]{:S(2)}, u32[]{:S(2)}) collective-permute-start(bf16[2,256,256]{2,1,0:T(8,128)(2,1)S(1)} %collective-permute-done.4.refs_2_), channel_id=1, source_target_pairs={{0,7},{1,0},{2,1},{3,2},{4,3},{5,4},{6,5},{7,6},{8,15},{9,8},{10,9... | collective-permute-start | bytes 786440 | tf_op jit(solution)/shard_map/ppermute | solution.py:265
  41.8 13.8 %collective-permute-start.10 = (bf16[2,2,256,256]{3,2,1,0:T(8,128)(2,1)S(1)}, bf16[2,2,256,256]{3,2,1,0:T(8,128)(2,1)S(1)}, u32[]{:S(2)}, u32[]{:S(2)}) collective-permute-start(bf16[2,2,256,256]{3,2,1,0:T(8,128)(2,1)S(1)} %shard_map.56.refs_0_), channel_id=1, source_target_pairs={{0,64},{8,24},{16,80},{24,40},{32,96},{40,56},{48,112},{56,8},{64,... | collective-permute-start | bytes 1572872 | tf_op jit(solution)/shard_map/ppermute | solution.py:256
  41.9 13.7 %collective-permute-start.11 = (bf16[2,2,256,256]{3,2,1,0:T(8,128)(2,1)S(1)}, bf16[2,2,256,256]{3,2,1,0:T(8,128)(2,1)S(1)}, u32[]{:S(2)}, u32[]{:S(2)}) collective-permute-start(bf16[2,2,256,256]{3,2,1,0:T(8,128)(2,1)S(1)} %shard_map.56.refs_0_), channel_id=1, source_target_pairs={{0,192},{8,56},{16,208},{24,8},{32,224},{40,24},{48,240},{56,40},{... | collective-permute-start | bytes 1572872 | tf_op jit(solution)/shard_map/ppermute | solution.py:256
  44.6 20.7 %copy-start = (bf16[2,256,256]{2,1,0:T(8,128)(2,1)S(1)}, bf16[2,256,256]{2,1,0:T(8,128)(2,1)}, u32[]{:S(2)}) copy-start(bf16[2,256,256]{2,1,0:T(8,128)(2,1)} %get-tuple-element.38.refs_7_.refs_4_) | copy-start | bytes 786436
  44.6 12.4 %collective-permute-start.12 = (bf16[2,2,256,256]{3,2,1,0:T(8,128)(2,1)S(1)}, bf16[2,2,256,256]{3,2,1,0:T(8,128)(2,1)S(1)}, u32[]{:S(2)}, u32[]{:S(2)}) collective-permute-start(bf16[2,2,256,256]{3,2,1,0:T(8,128)(2,1)S(1)} %shard_map.57.refs_3_), channel_id=1, source_target_pairs={{0,64},{8,24},{16,80},{24,40},{32,96},{40,56},{48,112},{56,8},{64,... | collective-permute-start | bytes 1572872 | tf_op jit(solution)/shard_map/ppermute | solution.py:256
  44.7 12.3 %collective-permute-start.13 = (bf16[2,2,256,256]{3,2,1,0:T(8,128)(2,1)S(1)}, bf16[2,2,256,256]{3,2,1,0:T(8,128)(2,1)S(1)}, u32[]{:S(2)}, u32[]{:S(2)}) collective-permute-start(bf16[2,2,256,256]{3,2,1,0:T(8,128)(2,1)S(1)} %shard_map.57.refs_3_), channel_id=1, source_target_pairs={{0,192},{8,56},{16,208},{24,8},{32,224},{40,24},{48,240},{56,40},{... | collective-permute-start | bytes 1572872 | tf_op jit(solution)/shard_map/ppermute | solution.py:256
  47.4 7.0 %collective-permute-start.14 = (bf16[2,256,256]{2,1,0:T(8,128)(2,1)S(1)}, bf16[2,256,256]{2,1,0:T(8,128)(2,1)S(1)}, u32[]{:S(2)}, u32[]{:S(2)}) collective-permute-start(bf16[2,256,256]{2,1,0:T(8,128)(2,1)S(1)} %collective-permute-done.8.refs_5_), channel_id=1, source_target_pairs={{0,1},{1,2},{2,3},{3,4},{4,5},{5,6},{6,7},{7,0},{8,9},{9,10},{10,1... | collective-permute-start | bytes 786440 | tf_op jit(solution)/shard_map/ppermute | solution.py:262
  54.4 1.0 copy-start.2
  57.0 12.0 %collective-permute-start.15 = (bf16[9,2,256,256]{3,2,1,0:T(8,128)(2,1)S(1)}, bf16[9,2,256,256]{3,2,1,0:T(8,128)(2,1)S(1)}, u32[]{:S(2)}, u32[]{:S(2)}) collective-permute-start(bf16[9,2,256,256]{3,2,1,0:T(8,128)(2,1)S(1)} %shard_map.58.refs_6_.refs_2_), channel_id=1, source_target_pairs={{0,8},{8,0},{16,24},{24,16},{32,40},{40,32},{48,56},{56,48},{64,72... | collective-permute-start | bytes 7077896 | tf_op jit(solution)/shard_map/ppermute | solution.py:259
  62.6 10.1 %collective-permute-start.16 = (bf16[2,2,256,256]{3,2,1,0:T(8,128)(2,1)S(1)}, bf16[2,2,256,256]{3,2,1,0:T(8,128)(2,1)S(1)}, u32[]{:S(2)}, u32[]{:S(2)}) collective-permute-start(bf16[2,2,256,256]{3,2,1,0:T(8,128)(2,1)S(1)} %collective-permute-done.10.refs_1_), channel_id=1, source_target_pairs={{0,64},{8,24},{16,80},{24,40},{32,96},{40,56},{48,112},{56,8},{64,... | collective-permute-start | bytes 1572872 | tf_op jit(solution)/shard_map/ppermute | solution.py:256
  62.6 10.1 %collective-permute-start.17 = (bf16[2,2,256,256]{3,2,1,0:T(8,128)(2,1)S(1)}, bf16[2,2,256,256]{3,2,1,0:T(8,128)(2,1)S(1)}, u32[]{:S(2)}, u32[]{:S(2)}) collective-permute-start(bf16[2,2,256,256]{3,2,1,0:T(8,128)(2,1)S(1)} %collective-permute-done.13.refs_5_), channel_id=1, source_target_pairs={{0,192},{8,56},{16,208},{24,8},{32,224},{40,24},{48,240},{56,40},{... | collective-permute-start | bytes 1572872 | tf_op jit(solution)/shard_map/ppermute | solution.py:256
  69.0 3.8 %copy-start.3 = (s32[32]{0:T(128)S(1)}, s32[32]{0:T(128)}, u32[]{:S(2)}) copy-start(s32[32]{0:T(128)} %left_sizes.3) | copy-start | bytes 388
  69.0 3.8 %copy-start.4 = (s32[32]{0:T(128)S(1)}, s32[32]{0:T(128)}, u32[]{:S(2)}) copy-start(s32[32]{0:T(128)} %right_sizes.3) | copy-start | bytes 388

commit v16 on v15

--- a/solution.py
+++ b/solution.py
@@ -276,14 +276,14 @@
     up1, down1 = up(left_env), down(left_env)
     keep, give = cut(wavefunction, left_sizes, right_sizes)
     up2, down2 = up(up1), down(down1)
-    own, keep, give, up2, down2 = together(own, keep, give, up2, down2)
+    own, keep, give = together(own, keep, give)
 
     below, above, two = near_step(own, 1), near_step(own, -1), near_step(own, 2)
-    up3, down3 = up(up2), down(down2)
-    below, above, two, up3, down3 = together(below, above, two, up3, down3)
+    below, above, two, up2, down2 = together(below, above, two, up2, down2)
     line_a, line_b = stack(own, below), stack(above, two)
     a_below, a_above = far_step(line_a, 1), far_step(line_a, -1)
     b_below, b_above = far_step(line_b, 1), far_step(line_b, -1)
+    up3, down3 = up(up2), down(down2)
     up4 = up(up3)
     lefts = stack(left_env, down1, down2, down3, up4, up3, up2, up1, give)
     a_below, a_above, b_below, b_above, lefts = together(a_below, a_above, b_below, b_above, lefts)

time: 115 us -> 114 us (level)
  waiting for transfers between devices: 24.1 us -> 16 us
  starting transfers between devices: 37.2 us -> 43.8 us
    ppermute x1, starting transfers between devices: 5.83 us -> 9.77 us  [local(): own = lax.ppermute(right_env, ('blk', 'mpo'), turn)]
    ppermute x3, waiting for transfers between devices: 3.77 us -> 0.01 us  [near_step(): return lax.ppermute(block, 'blk', step(False, by))]
    ppermute x4, waiting for transfers between devices: 18.9 us -> 15.7 us  [up(): lax.ppermute(block, 'mpo', [(z, (z + 1) % ranks) for z in range(ranks)])]
    all_to_all x1, blocking collectives: 16.2 us -> 14.8 us  [local(): out = order(lax.all_to_all(by_plane, 'blk', 0, 0, axis_index_groups=groups))]
    ppermute x1, starting transfers between devices: 5.59 us -> 6.93 us  [swap(): return lax.ppermute(block, 'blk', [(i, i ^ 1) for i in range(sectors)])]
    all_to_all x1, blocking collectives: 21 us -> 22.4 us  [local(): by_plane = lax.all_to_all(done, 'mpo', 0, 0)]
    ppermute x6, waiting for transfers between devices: 1.42 us -> 0.21 us  [far_step(): return lax.ppermute(block, 'blk', step(True, by))]
  transfers between devices with their start and end apart: 18 -> 18, of which waited for: 6 -> 5; matrix products, arithmetic and copies ran while one was open for 0% -> 0% of each run, Pallas kernels for 9% -> 9%
where the time goes in v16:
time: 114 us; the launch traced here: 112 us
  starting transfers between devices  43.8 us (38%)
  blocking collectives  37.2 us (33%)
  waiting for transfers between devices  16 us (14%)
  Pallas kernels  13.9 us (12%)
    all_to_all x1, blocking collectives, local(): by_plane = lax.all_to_all(done, 'mpo', 0, 0)  22.4 us
    ppermute x4, waiting for transfers between devices, up(): lax.ppermute(block, 'mpo', [(z, (z + 1) % ranks) for z in range(ranks)])  15.7 us
    all_to_all x1, blocking collectives, local(): out = order(lax.all_to_all(by_plane, 'blk', 0, 0, axis_index_groups=groups))  14.8 us
    ppermute x3, starting transfers between devices, down(): lax.ppermute(block, 'mpo', [(z, (z - 1) % ranks) for z in range(ranks)])  9.98 us
    ppermute x1, starting transfers between devices, local(): own = lax.ppermute(right_env, ('blk', 'mpo'), turn)  9.77 us
    ppermute x6, starting transfers between devices, far_step(): return lax.ppermute(block, 'blk', step(True, by))  8.53 us
    pallas_call x2, Pallas kernels, half(): pl.pallas_call(functools.partial(half_kernel, pieces), out_shape=jax.Shap...  7.38 us
    ppermute x1, starting transfers between devices, swap(): return lax.ppermute(block, 'blk', [(i, i ^ 1) for i in range(sectors)])  6.93 us
  transfers between devices with their start and end apart: 18, of which 5 were waited for; matrix products, arithmetic and copies ran while one was open for 0% of the time, Pallas kernels for 9%

profile of v16, /device:TPU:1, one launch (start us, length us, event | category | flops | bytes accessed | tf_op | source)
XLA Modules:
  0.0 112.1 jit_solution(16673847585191855451)
XLA Ops:
  0.0 0.0 copy-start.1
  0.0 9.8 %collective-permute-start = (bf16[2,256,256]{2,1,0:T(8,128)(2,1)}, bf16[2,256,256]{2,1,0:T(8,128)(2,1)S(1)}, u32[]{:S(2)}, u32[]{:S(2)}) collective-permute-start(bf16[2,256,256]{2,1,0:T(8,128)(2,1)} %param.7), channel_id=1, source_target_pairs={{0,0},{1,16},{2,32},{3,48},{4,64},{5,80},{6,96},{7,112},{8,12},{9,... | collective-permute-start | bytes 786440 | tf_op jit(solution)/shard_map/ppermute | solution.py:275
  9.8 1.3 %collective-permute-start.4 = (bf16[2,256,256]{2,1,0:T(8,128)(2,1)}, bf16[2,256,256]{2,1,0:T(8,128)(2,1)S(1)}, u32[]{:S(2)}, u32[]{:S(2)}) collective-permute-start(bf16[2,256,256]{2,1,0:T(8,128)(2,1)} %refs_0_.1), channel_id=1, source_target_pairs={{0,1},{1,2},{2,3},{3,4},{4,5},{5,6},{6,7},{7,0},{8,9},{9,10},{10,1... | collective-permute-start | bytes 786440 | tf_op jit(solution)/shard_map/ppermute | solution.py:262
  11.1 2.4 %collective-permute-start.6 = (bf16[2,256,256]{2,1,0:T(8,128)(2,1)}, bf16[2,256,256]{2,1,0:T(8,128)(2,1)S(1)}, u32[]{:S(2)}, u32[]{:S(2)}) collective-permute-start(bf16[2,256,256]{2,1,0:T(8,128)(2,1)} %refs_0_.1), channel_id=1, source_target_pairs={{0,7},{1,0},{2,1},{3,2},{4,3},{5,4},{6,5},{7,6},{8,15},{9,8},{10,9... | collective-permute-start | bytes 786440 | tf_op jit(solution)/shard_map/ppermute | solution.py:265
  13.4 2.6 %shard_map.55 = (bf16[2,256,256]{2,1,0:T(8,128)(2,1)}, bf16[2,256,256]{2,1,0:T(8,128)(2,1)}) custom-call(s32[32]{0:T(128)} %left_sizes.3, s32[32]{0:T(128)} %right_sizes.3, bf16[256,8192]{1,0:T(8,128)(2,1)} %psi_ref.1), custom_call_target="tpu_custom_call" | custom-call | tf_op jit(solution)/shard_map/pallas_call | solution.py:76
  16.1 0.0 collective-permute-done.refs_0_
  16.1 0.1 collective-permute-start.1
  16.2 2.7 %collective-permute-start.2 = (bf16[2,256,256]{2,1,0:T(8,128)(2,1)S(1)}, bf16[2,256,256]{2,1,0:T(8,128)(2,1)S(1)}, u32[]{:S(2)}, u32[]{:S(2)}) collective-permute-start(bf16[2,256,256]{2,1,0:T(8,128)(2,1)S(1)} %collective-permute-done.refs_0_), channel_id=1, source_target_pairs={{0,48},{8,200},{16,0},{24,216},{32,16},{40,232},{48,32},{56,248},{... | collective-permute-start | bytes 786440 | tf_op jit(solution)/shard_map/ppermute | solution.py:253
  18.8 1.4 %collective-permute-start.3 = (bf16[2,256,256]{2,1,0:T(8,128)(2,1)S(1)}, bf16[2,256,256]{2,1,0:T(8,128)(2,1)S(1)}, u32[]{:S(2)}, u32[]{:S(2)}) collective-permute-start(bf16[2,256,256]{2,1,0:T(8,128)(2,1)S(1)} %collective-permute-done.refs_0_), channel_id=1, source_target_pairs={{0,32},{8,136},{16,48},{24,152},{32,0},{40,168},{48,16},{56,184},{... | collective-permute-start | bytes 786440 | tf_op jit(solution)/shard_map/ppermute | solution.py:253
  20.2 5.8 %collective-permute-done.4.refs_7_ = bf16[2,256,256]{2,1,0:T(8,128)(2,1)S(1)} collective-permute-done((bf16[2,256,256]{2,1,0:T(8,128)(2,1)}, bf16[2,256,256]{2,1,0:T(8,128)(2,1)S(1)}, u32[]{:S(2)}, u32[]{:S(2)}) %collective-permute-start.4) | collective-permute-done | bytes 262176 | tf_op jit(solution)/shard_map/ppermute | solution.py:262
  26.1 0.0 collective-permute-start.5
  26.1 0.0 collective-permute-done.6.refs_1_
  26.1 4.6 %collective-permute-start.7 = (bf16[2,256,256]{2,1,0:T(8,128)(2,1)S(1)}, bf16[2,256,256]{2,1,0:T(8,128)(2,1)S(1)}, u32[]{:S(2)}, u32[]{:S(2)}) collective-permute-start(bf16[2,256,256]{2,1,0:T(8,128)(2,1)S(1)} %collective-permute-done.6.refs_1_), channel_id=1, source_target_pairs={{0,7},{1,0},{2,1},{3,2},{4,3},{5,4},{6,5},{7,6},{8,15},{9,8},{10,9... | collective-permute-start | bytes 786440 | tf_op jit(solution)/shard_map/ppermute | solution.py:265
  30.6 0.0 collective-permute-done.1.refs_1_
  30.6 0.0 collective-permute-done.2.refs_0_
  30.6 0.0 collective-permute-done.3.refs_1_
  30.6 3.7 %collective-permute-done.5.refs_6_ = bf16[2,256,256]{2,1,0:T(8,128)(2,1)S(1)} collective-permute-done((bf16[2,256,256]{2,1,0:T(8,128)(2,1)S(1)}, bf16[2,256,256]{2,1,0:T(8,128)(2,1)S(1)}, u32[]{:S(2)}, u32[]{:S(2)}) %collective-permute-start.5) | collective-permute-done | bytes 262176 | tf_op jit(solution)/shard_map/ppermute | solution.py:262
  34.3 0.0 collective-permute-done.7.refs_2_
  34.3 3.0 %collective-permute-start.12 = (bf16[2,256,256]{2,1,0:T(8,128)(2,1)S(1)}, bf16[2,256,256]{2,1,0:T(8,128)(2,1)S(1)}, u32[]{:S(2)}, u32[]{:S(2)}) collective-permute-start(bf16[2,256,256]{2,1,0:T(8,128)(2,1)S(1)} %collective-permute-done.7.refs_2_), channel_id=1, source_target_pairs={{0,7},{1,0},{2,1},{3,2},{4,3},{5,4},{6,5},{7,6},{8,15},{9,8},{10,9... | collective-permute-start | bytes 786440 | tf_op jit(solution)/shard_map/ppermute | solution.py:265
  37.4 0.1 shard_map.56.refs_0_
  37.4 0.1 collective-permute-start.13
  37.5 1.6 %collective-permute-start.8 = (bf16[2,2,256,256]{3,2,1,0:T(8,128)(2,1)S(1)}, bf16[2,2,256,256]{3,2,1,0:T(8,128)(2,1)S(1)}, u32[]{:S(2)}, u32[]{:S(2)}) collective-permute-start(bf16[2,2,256,256]{3,2,1,0:T(8,128)(2,1)S(1)} %shard_map.56.refs_0_), channel_id=1, source_target_pairs={{0,64},{8,24},{16,80},{24,40},{32,96},{40,56},{48,112},{56,8},{64,... | collective-permute-start | bytes 1572872 | tf_op jit(solution)/shard_map/ppermute | solution.py:256
  39.1 1.1 %collective-permute-start.9 = (bf16[2,2,256,256]{3,2,1,0:T(8,128)(2,1)S(1)}, bf16[2,2,256,256]{3,2,1,0:T(8,128)(2,1)S(1)}, u32[]{:S(2)}, u32[]{:S(2)}) collective-permute-start(bf16[2,2,256,256]{3,2,1,0:T(8,128)(2,1)S(1)} %shard_map.56.refs_0_), channel_id=1, source_target_pairs={{0,192},{8,56},{16,208},{24,8},{32,224},{40,24},{48,240},{56,40},{... | collective-permute-start | bytes 1572872 | tf_op jit(solution)/shard_map/ppermute | solution.py:256
  40.3 0.1 shard_map.57.refs_3_
  40.3 0.0 copy-start
  40.3 0.4 collective-permute-start.10
  40.7 0.0 collective-permute-done.12.refs_3_
  40.7 2.4 %collective-permute-start.11 = (bf16[2,2,256,256]{3,2,1,0:T(8,128)(2,1)S(1)}, bf16[2,2,256,256]{3,2,1,0:T(8,128)(2,1)S(1)}, u32[]{:S(2)}, u32[]{:S(2)}) collective-permute-start(bf16[2,2,256,256]{3,2,1,0:T(8,128)(2,1)S(1)} %shard_map.57.refs_3_), channel_id=1, source_target_pairs={{0,192},{8,56},{16,208},{24,8},{32,224},{40,24},{48,240},{56,40},{... | collective-permute-start | bytes 1572872 | tf_op jit(solution)/shard_map/ppermute | solution.py:256
  43.1 0.8 collective-permute-done.13.refs_5_
  43.9 3.0 %collective-permute-start.14 = (bf16[2,256,256]{2,1,0:T(8,128)(2,1)S(1)}, bf16[2,256,256]{2,1,0:T(8,128)(2,1)S(1)}, u32[]{:S(2)}, u32[]{:S(2)}) collective-permute-start(bf16[2,256,256]{2,1,0:T(8,128)(2,1)S(1)} %collective-permute-done.13.refs_5_), channel_id=1, source_target_pairs={{0,1},{1,2},{2,3},{3,4},{4,5},{5,6},{6,7},{7,0},{8,9},{9,10},{10,1... | collective-permute-start | bytes 786440 | tf_op jit(solution)/shard_map/ppermute | solution.py:262
  46.9 5.4 %collective-permute-done.14.refs_4_ = bf16[2,256,256]{2,1,0:T(8,128)(2,1)S(1)} collective-permute-done((bf16[2,256,256]{2,1,0:T(8,128)(2,1)S(1)}, bf16[2,256,256]{2,1,0:T(8,128)(2,1)S(1)}, u32[]{:S(2)}, u32[]{:S(2)}) %collective-permute-start.14) | collective-permute-done | bytes 262176 | tf_op jit(solution)/shard_map/ppermute | solution.py:262
  52.3 0.0 copy-done.1
  52.4 0.0 copy-start.2
  52.4 0.9 copy-done.2
  53.3 0.3 shard_map.58.refs_6_.refs_2_
  53.6 0.0 collective-permute-done.8.refs_1_
  53.6 0.0 collective-permute-done.9.refs_2_
  53.6 0.0 collective-permute-done.10.refs_4_
  53.6 0.0 collective-permute-done.11.refs_5_
  53.6 6.9 %collective-permute-start.15 = (bf16[9,2,256,256]{3,2,1,0:T(8,128)(2,1)S(1)}, bf16[9,2,256,256]{3,2,1,0:T(8,128)(2,1)S(1)}, u32[]{:S(2)}, u32[]{:S(2)}) collective-permute-start(bf16[9,2,256,256]{3,2,1,0:T(8,128)(2,1)S(1)} %shard_map.58.refs_6_.refs_2_), channel_id=1, source_target_pairs={{0,8},{8,0},{16,24},{24,16},{32,40},{40,32},{48,56},{56,48},{64,72... | collective-permute-start | bytes 7077896 | tf_op jit(solution)/shard_map/ppermute | solution.py:259
  60.5 0.0 collective-permute-start.16
  60.5 3.0 %collective-permute-start.17 = (bf16[2,2,256,256]{3,2,1,0:T(8,128)(2,1)S(1)}, bf16[2,2,256,256]{3,2,1,0:T(8,128)(2,1)S(1)}, u32[]{:S(2)}, u32[]{:S(2)}) collective-permute-start(bf16[2,2,256,256]{3,2,1,0:T(8,128)(2,1)S(1)} %collective-permute-done.11.refs_5_), channel_id=1, source_target_pairs={{0,192},{8,56},{16,208},{24,8},{32,224},{40,24},{48,240},{56,40},{... | collective-permute-start | bytes 1572872 | tf_op jit(solution)/shard_map/ppermute | solution.py:256
  63.6 0.0 copy-done
  63.6 3.7 %shard_map.59.mine = f32[2,256,256]{2,1,0:T(8,128)S(1)} custom-call(bf16[2,2,256,256]{3,2,1,0:T(8,128)(2,1)S(1)} %shard_map.56.refs_0_, bf16[2,2,256,256]{3,2,1,0:T(8,128)(2,1)S(1)} %collective-permute-done.8.refs_1_, bf16[2,2,256,256]{3,2,1,0:T(8,128)(2,1)S(1)} %collective-permute-done.9.refs_2_, bf16[2,2,256,256]{3,2,1,0:T(8,128)(2,1)S(1)} %shard_map.57.refs_3_, ...), custom_call_target="tpu_custom_call" | custom-call | tf_op jit(solution)/shard_map/pallas_call | solution.py:126
  67.3 0.0 copy-start.3
  67.3 0.0 copy-start.4
  67.3 0.0 collective-permute-done.15.refs_6_.refs_3_
  67.3 3.7 %shard_map.60.theirs = f32[2,256,256]{2,1,0:T(8,128)S(1)} custom-call(bf16[2,2,256,256]{3,2,1,0:T(8,128)(2,1)S(1)} %shard_map.56.refs_0_, bf16[2,2,256,256]{3,2,1,0:T(8,128)(2,1)S(1)} %collective-permute-done.8.refs_1_, bf16[2,2,256,256]{3,2,1,0:T(8,128)(2,1)S(1)} %collective-permute-done.9.refs_2_, bf16[2,2,256,256]{3,2,1,0:T(8,128)(2,1)S(1)} %shard_map.57.refs_3_, ...), custom_call_target="tpu_custom_call" | custom-call | tf_op jit(solution)/shard_map/pallas_call | solution.py:126
  71.0 0.0 collective-permute-done.16.refs_0_
  71.0 0.2 collective-permute-done.17.refs_1_
  71.2 0.0 copy-done.3
  71.2 0.0 copy-done.4
  71.2 2.6 %shard_map.61 = bf16[8,2,2,32,256]{4,3,2,1,0:T(8,128)(2,1)S(1)} custom-call(s32[32]{0:T(128)S(1)} %copy-done.3, s32[32]{0:T(128)S(1)} %copy-done.4, f32[2,256,256]{2,1,0:T(8,128)S(1)} %shard_map.59.mine, f32[2,256,256]{2,1,0:T(8,128)S(1)} %shard_map.60.theirs, bf16[2,2,256,256]{3,2,1,0:T(8,128)(2,1)S(1)} %collective-permute-done.16.refs_0_, ...), custom_call_target="tpu_custom_call" | custom-call | tf_op jit(solution)/shard_map/pallas_call | solution.py:195
  73.8 22.4 %all_to_all.10 = bf16[8,2,2,32,256]{4,3,2,1,0:T(8,128)(2,1)S(1)} all-to-all(bf16[8,2,2,32,256]{4,3,2,1,0:T(8,128)(2,1)S(1)} %shard_map.61), channel_id=1, replica_groups=mesh['blk'=32,'mpo'=8] {'mpo'}, dimensions={0} | all-to-all | bytes 1048576 | tf_op jit(solution)/shard_map/all_to_all | solution.py:300
  96.2 14.8 %all_to_all.11.in_ref = bf16[16,2,32,256]{3,2,1,0:T(8,128)(2,1)S(1)} all-to-all(bf16[16,2,32,256]{3,2,1,0:T(8,128)(2,1)S(1)} %bitcast.2), channel_id=1, replica_groups={{0,128,16,144,32,160,48,176,64,192,80,208,96,224,112,240},{72,200,88,21..., dimensions={0} | all-to-all | bytes 1048576 | tf_op jit(solution)/shard_map/all_to_all | solution.py:307
  111.0 0.9 shard_map.62
Async XLA Ops:
  0.0 52.3 %copy-start.1 = (bf16[2,256,256]{2,1,0:T(8,128)(2,1)S(1)}, bf16[2,256,256]{2,1,0:T(8,128)(2,1)}, u32[]{:S(2)}) copy-start(bf16[2,256,256]{2,1,0:T(8,128)(2,1)} %refs_0_.1) | copy-start | bytes 786436
  0.0 16.1 %collective-permute-start = (bf16[2,256,256]{2,1,0:T(8,128)(2,1)}, bf16[2,256,256]{2,1,0:T(8,128)(2,1)S(1)}, u32[]{:S(2)}, u32[]{:S(2)}) collective-permute-start(bf16[2,256,256]{2,1,0:T(8,128)(2,1)} %param.7), channel_id=1, source_target_pairs={{0,0},{1,16},{2,32},{3,48},{4,64},{5,80},{6,96},{7,112},{8,12},{9,... | collective-permute-start | bytes 786440 | tf_op jit(solution)/shard_map/ppermute | solution.py:275
  9.8 16.3 %collective-permute-start.4 = (bf16[2,256,256]{2,1,0:T(8,128)(2,1)}, bf16[2,256,256]{2,1,0:T(8,128)(2,1)S(1)}, u32[]{:S(2)}, u32[]{:S(2)}) collective-permute-start(bf16[2,256,256]{2,1,0:T(8,128)(2,1)} %refs_0_.1), channel_id=1, source_target_pairs={{0,1},{1,2},{2,3},{3,4},{4,5},{5,6},{6,7},{7,0},{8,9},{9,10},{10,1... | collective-permute-start | bytes 786440 | tf_op jit(solution)/shard_map/ppermute | solution.py:262
  11.1 15.0 %collective-permute-start.6 = (bf16[2,256,256]{2,1,0:T(8,128)(2,1)}, bf16[2,256,256]{2,1,0:T(8,128)(2,1)S(1)}, u32[]{:S(2)}, u32[]{:S(2)}) collective-permute-start(bf16[2,256,256]{2,1,0:T(8,128)(2,1)} %refs_0_.1), channel_id=1, source_target_pairs={{0,7},{1,0},{2,1},{3,2},{4,3},{5,4},{6,5},{7,6},{8,15},{9,8},{10,9... | collective-permute-start | bytes 786440 | tf_op jit(solution)/shard_map/ppermute | solution.py:265
  16.1 14.6 %collective-permute-start.1 = (bf16[2,256,256]{2,1,0:T(8,128)(2,1)S(1)}, bf16[2,256,256]{2,1,0:T(8,128)(2,1)S(1)}, u32[]{:S(2)}, u32[]{:S(2)}) collective-permute-start(bf16[2,256,256]{2,1,0:T(8,128)(2,1)S(1)} %collective-permute-done.refs_0_), channel_id=1, source_target_pairs={{0,16},{8,72},{16,32},{24,88},{32,48},{40,104},{48,0},{56,120},{64... | collective-permute-start | bytes 786440 | tf_op jit(solution)/shard_map/ppermute | solution.py:253
  16.2 14.5 %collective-permute-start.2 = (bf16[2,256,256]{2,1,0:T(8,128)(2,1)S(1)}, bf16[2,256,256]{2,1,0:T(8,128)(2,1)S(1)}, u32[]{:S(2)}, u32[]{:S(2)}) collective-permute-start(bf16[2,256,256]{2,1,0:T(8,128)(2,1)S(1)} %collective-permute-done.refs_0_), channel_id=1, source_target_pairs={{0,48},{8,200},{16,0},{24,216},{32,16},{40,232},{48,32},{56,248},{... | collective-permute-start | bytes 786440 | tf_op jit(solution)/shard_map/ppermute | solution.py:253
  18.8 11.8 %collective-permute-start.3 = (bf16[2,256,256]{2,1,0:T(8,128)(2,1)S(1)}, bf16[2,256,256]{2,1,0:T(8,128)(2,1)S(1)}, u32[]{:S(2)}, u32[]{:S(2)}) collective-permute-start(bf16[2,256,256]{2,1,0:T(8,128)(2,1)S(1)} %collective-permute-done.refs_0_), channel_id=1, source_target_pairs={{0,32},{8,136},{16,48},{24,152},{32,0},{40,168},{48,16},{56,184},{... | collective-permute-start | bytes 786440 | tf_op jit(solution)/shard_map/ppermute | solution.py:253
  26.1 8.2 %collective-permute-start.5 = (bf16[2,256,256]{2,1,0:T(8,128)(2,1)S(1)}, bf16[2,256,256]{2,1,0:T(8,128)(2,1)S(1)}, u32[]{:S(2)}, u32[]{:S(2)}) collective-permute-start(bf16[2,256,256]{2,1,0:T(8,128)(2,1)S(1)} %collective-permute-done.4.refs_7_), channel_id=1, source_target_pairs={{0,1},{1,2},{2,3},{3,4},{4,5},{5,6},{6,7},{7,0},{8,9},{9,10},{10,1... | collective-permute-start | bytes 786440 | tf_op jit(solution)/shard_map/ppermute | solution.py:262
  26.1 8.2 %collective-permute-start.7 = (bf16[2,256,256]{2,1,0:T(8,128)(2,1)S(1)}, bf16[2,256,256]{2,1,0:T(8,128)(2,1)S(1)}, u32[]{:S(2)}, u32[]{:S(2)}) collective-permute-start(bf16[2,256,256]{2,1,0:T(8,128)(2,1)S(1)} %collective-permute-done.6.refs_1_), channel_id=1, source_target_pairs={{0,7},{1,0},{2,1},{3,2},{4,3},{5,4},{6,5},{7,6},{8,15},{9,8},{10,9... | collective-permute-start | bytes 786440 | tf_op jit(solution)/shard_map/ppermute | solution.py:265
  34.3 6.4 %collective-permute-start.12 = (bf16[2,256,256]{2,1,0:T(8,128)(2,1)S(1)}, bf16[2,256,256]{2,1,0:T(8,128)(2,1)S(1)}, u32[]{:S(2)}, u32[]{:S(2)}) collective-permute-start(bf16[2,256,256]{2,1,0:T(8,128)(2,1)S(1)} %collective-permute-done.7.refs_2_), channel_id=1, source_target_pairs={{0,7},{1,0},{2,1},{3,2},{4,3},{5,4},{6,5},{7,6},{8,15},{9,8},{10,9... | collective-permute-start | bytes 786440 | tf_op jit(solution)/shard_map/ppermute | solution.py:265
  37.4 6.5 %collective-permute-start.13 = (bf16[2,256,256]{2,1,0:T(8,128)(2,1)S(1)}, bf16[2,256,256]{2,1,0:T(8,128)(2,1)S(1)}, u32[]{:S(2)}, u32[]{:S(2)}) collective-permute-start(bf16[2,256,256]{2,1,0:T(8,128)(2,1)S(1)} %collective-permute-done.5.refs_6_), channel_id=1, source_target_pairs={{0,1},{1,2},{2,3},{3,4},{4,5},{5,6},{6,7},{7,0},{8,9},{9,10},{10,1... | collective-permute-start | bytes 786440 | tf_op jit(solution)/shard_map/ppermute | solution.py:262
  37.5 16.1 %collective-permute-start.8 = (bf16[2,2,256,256]{3,2,1,0:T(8,128)(2,1)S(1)}, bf16[2,2,256,256]{3,2,1,0:T(8,128)(2,1)S(1)}, u32[]{:S(2)}, u32[]{:S(2)}) collective-permute-start(bf16[2,2,256,256]{3,2,1,0:T(8,128)(2,1)S(1)} %shard_map.56.refs_0_), channel_id=1, source_target_pairs={{0,64},{8,24},{16,80},{24,40},{32,96},{40,56},{48,112},{56,8},{64,... | collective-permute-start | bytes 1572872 | tf_op jit(solution)/shard_map/ppermute | solution.py:256
  39.1 14.5 %collective-permute-start.9 = (bf16[2,2,256,256]{3,2,1,0:T(8,128)(2,1)S(1)}, bf16[2,2,256,256]{3,2,1,0:T(8,128)(2,1)S(1)}, u32[]{:S(2)}, u32[]{:S(2)}) collective-permute-start(bf16[2,2,256,256]{3,2,1,0:T(8,128)(2,1)S(1)} %shard_map.56.refs_0_), channel_id=1, source_target_pairs={{0,192},{8,56},{16,208},{24,8},{32,224},{40,24},{48,240},{56,40},{... | collective-permute-start | bytes 1572872 | tf_op jit(solution)/shard_map/ppermute | solution.py:256
  40.3 23.2 %copy-start = (bf16[2,256,256]{2,1,0:T(8,128)(2,1)S(1)}, bf16[2,256,256]{2,1,0:T(8,128)(2,1)}, u32[]{:S(2)}) copy-start(bf16[2,256,256]{2,1,0:T(8,128)(2,1)} %get-tuple-element.34.refs_7_.refs_4_) | copy-start | bytes 786436
  40.3 13.2 %collective-permute-start.10 = (bf16[2,2,256,256]{3,2,1,0:T(8,128)(2,1)S(1)}, bf16[2,2,256,256]{3,2,1,0:T(8,128)(2,1)S(1)}, u32[]{:S(2)}, u32[]{:S(2)}) collective-permute-start(bf16[2,2,256,256]{3,2,1,0:T(8,128)(2,1)S(1)} %shard_map.57.refs_3_), channel_id=1, source_target_pairs={{0,64},{8,24},{16,80},{24,40},{32,96},{40,56},{48,112},{56,8},{64,... | collective-permute-start | bytes 1572872 | tf_op jit(solution)/shard_map/ppermute | solution.py:256
  40.7 12.9 %collective-permute-start.11 = (bf16[2,2,256,256]{3,2,1,0:T(8,128)(2,1)S(1)}, bf16[2,2,256,256]{3,2,1,0:T(8,128)(2,1)S(1)}, u32[]{:S(2)}, u32[]{:S(2)}) collective-permute-start(bf16[2,2,256,256]{3,2,1,0:T(8,128)(2,1)S(1)} %shard_map.57.refs_3_), channel_id=1, source_target_pairs={{0,192},{8,56},{16,208},{24,8},{32,224},{40,24},{48,240},{56,40},{... | collective-permute-start | bytes 1572872 | tf_op jit(solution)/shard_map/ppermute | solution.py:256
  43.9 8.4 %collective-permute-start.14 = (bf16[2,256,256]{2,1,0:T(8,128)(2,1)S(1)}, bf16[2,256,256]{2,1,0:T(8,128)(2,1)S(1)}, u32[]{:S(2)}, u32[]{:S(2)}) collective-permute-start(bf16[2,256,256]{2,1,0:T(8,128)(2,1)S(1)} %collective-permute-done.13.refs_5_), channel_id=1, source_target_pairs={{0,1},{1,2},{2,3},{3,4},{4,5},{5,6},{6,7},{7,0},{8,9},{9,10},{10,1... | collective-permute-start | bytes 786440 | tf_op jit(solution)/shard_map/ppermute | solution.py:262
  52.4 1.0 copy-start.2
  53.6 13.7 %collective-permute-start.15 = (bf16[9,2,256,256]{3,2,1,0:T(8,128)(2,1)S(1)}, bf16[9,2,256,256]{3,2,1,0:T(8,128)(2,1)S(1)}, u32[]{:S(2)}, u32[]{:S(2)}) collective-permute-start(bf16[9,2,256,256]{3,2,1,0:T(8,128)(2,1)S(1)} %shard_map.58.refs_6_.refs_2_), channel_id=1, source_target_pairs={{0,8},{8,0},{16,24},{24,16},{32,40},{40,32},{48,56},{56,48},{64,72... | collective-permute-start | bytes 7077896 | tf_op jit(solution)/shard_map/ppermute | solution.py:259
  60.5 10.5 %collective-permute-start.16 = (bf16[2,2,256,256]{3,2,1,0:T(8,128)(2,1)S(1)}, bf16[2,2,256,256]{3,2,1,0:T(8,128)(2,1)S(1)}, u32[]{:S(2)}, u32[]{:S(2)}) collective-permute-start(bf16[2,2,256,256]{3,2,1,0:T(8,128)(2,1)S(1)} %collective-permute-done.8.refs_1_), channel_id=1, source_target_pairs={{0,64},{8,24},{16,80},{24,40},{32,96},{40,56},{48,112},{56,8},{64,... | collective-permute-start | bytes 1572872 | tf_op jit(solution)/shard_map/ppermute | solution.py:256
  60.5 10.7 %collective-permute-start.17 = (bf16[2,2,256,256]{3,2,1,0:T(8,128)(2,1)S(1)}, bf16[2,2,256,256]{3,2,1,0:T(8,128)(2,1)S(1)}, u32[]{:S(2)}, u32[]{:S(2)}) collective-permute-start(bf16[2,2,256,256]{3,2,1,0:T(8,128)(2,1)S(1)} %collective-permute-done.11.refs_5_), channel_id=1, source_target_pairs={{0,192},{8,56},{16,208},{24,8},{32,224},{40,24},{48,240},{56,40},{... | collective-permute-start | bytes 1572872 | tf_op jit(solution)/shard_map/ppermute | solution.py:256
  67.3 4.0 %copy-start.3 = (s32[32]{0:T(128)S(1)}, s32[32]{0:T(128)}, u32[]{:S(2)}) copy-start(s32[32]{0:T(128)} %left_sizes.3) | copy-start | bytes 388
  67.3 3.9 %copy-start.4 = (s32[32]{0:T(128)S(1)}, s32[32]{0:T(128)}, u32[]{:S(2)}) copy-start(s32[32]{0:T(128)} %right_sizes.3) | copy-start | bytes 388

commit v17 on v15

--- a/solution.py
+++ b/solution.py
@@ -272,11 +272,11 @@
         for y, x, c in spots
         for z in range(ranks)
     ]
+    keep, give = cut(wavefunction, left_sizes, right_sizes)
+    up1, down1 = up(left_env), down(left_env)
+    right_env, keep, give = together(right_env, keep, give)
     own = lax.ppermute(right_env, ("blk", "mpo"), turn)
-    up1, down1 = up(left_env), down(left_env)
-    keep, give = cut(wavefunction, left_sizes, right_sizes)
     up2, down2 = up(up1), down(down1)
-    own, keep, give, up2, down2 = together(own, keep, give, up2, down2)
 
     below, above, two = near_step(own, 1), near_step(own, -1), near_step(own, 2)
     up3, down3 = up(up2), down(down2)

time: 115 us -> 113 us (0.983)
  waiting for transfers between devices: 24.1 us -> 22.9 us
    ppermute x3, waiting for transfers between devices: 3.77 us -> 0.01 us  [near_step(): return lax.ppermute(block, 'blk', step(False, by))]
    ppermute x6, starting transfers between devices: 8.17 us -> 11.4 us  [far_step(): return lax.ppermute(block, 'blk', step(True, by))]
    ppermute x1, starting transfers between devices: 5.59 us -> 3.19 us  [swap(): return lax.ppermute(block, 'blk', [(i, i ^ 1) for i in range(sectors)])]
    ppermute x1, waiting for transfers between devices: 0.01 us -> 2.15 us  [local(): own = lax.ppermute(right_env, ('blk', 'mpo'), turn)]
  transfers between devices with their start and end apart: 18 -> 18, of which waited for: 6 -> 5; matrix products, arithmetic and copies ran while one was open for 0% -> 0% of each run, Pallas kernels for 9% -> 9%
where the time goes in v17:
time: 113 us; the launch traced here: 112 us
  starting transfers between devices  37.6 us (33%)
  blocking collectives  36.3 us (32%)
  waiting for transfers between devices  22.9 us (20%)
  Pallas kernels  13.9 us (12%)
    all_to_all x1, blocking collectives, local(): by_plane = lax.all_to_all(done, 'mpo', 0, 0)  20.3 us
    ppermute x4, waiting for transfers between devices, up(): lax.ppermute(block, 'mpo', [(z, (z + 1) % ranks) for z in range(ranks)])  19.2 us
    all_to_all x1, blocking collectives, local(): out = order(lax.all_to_all(by_plane, 'blk', 0, 0, axis_index_groups=groups))  15.9 us
    ppermute x6, starting transfers between devices, far_step(): return lax.ppermute(block, 'blk', step(True, by))  11.4 us
    ppermute x3, starting transfers between devices, down(): lax.ppermute(block, 'mpo', [(z, (z - 1) % ranks) for z in range(ranks)])  9.07 us
    pallas_call x2, Pallas kernels, half(): pl.pallas_call(functools.partial(half_kernel, pieces), out_shape=jax.Shap...  7.38 us
    ppermute x1, starting transfers between devices, local(): own = lax.ppermute(right_env, ('blk', 'mpo'), turn)  5.83 us
    ppermute x3, starting transfers between devices, near_step(): return lax.ppermute(block, 'blk', step(False, by))  4.38 us
  transfers between devices with their start and end apart: 18, of which 5 were waited for; matrix products, arithmetic and copies ran while one was open for 0% of the time, Pallas kernels for 9%

profile of v17, /device:TPU:1, one launch (start us, length us, event | category | flops | bytes accessed | tf_op | source)
XLA Modules:
  0.0 112.0 jit_solution(13773066229778426366)
XLA Ops:
  0.0 0.0 copy-start.1
  0.0 0.0 copy-start.5
  0.0 2.5 %collective-permute-start.4 = (bf16[2,256,256]{2,1,0:T(8,128)(2,1)}, bf16[2,256,256]{2,1,0:T(8,128)(2,1)S(1)}, u32[]{:S(2)}, u32[]{:S(2)}) collective-permute-start(bf16[2,256,256]{2,1,0:T(8,128)(2,1)} %refs_0_.1), channel_id=1, source_target_pairs={{0,1},{1,2},{2,3},{3,4},{4,5},{5,6},{6,7},{7,0},{8,9},{9,10},{10,1... | collective-permute-start | bytes 786440 | tf_op jit(solution)/shard_map/ppermute | solution.py:262
  2.5 4.0 %collective-permute-start.7 = (bf16[2,256,256]{2,1,0:T(8,128)(2,1)}, bf16[2,256,256]{2,1,0:T(8,128)(2,1)S(1)}, u32[]{:S(2)}, u32[]{:S(2)}) collective-permute-start(bf16[2,256,256]{2,1,0:T(8,128)(2,1)} %refs_0_.1), channel_id=1, source_target_pairs={{0,7},{1,0},{2,1},{3,2},{4,3},{5,4},{6,5},{7,6},{8,15},{9,8},{10,9... | collective-permute-start | bytes 786440 | tf_op jit(solution)/shard_map/ppermute | solution.py:265
  6.5 2.6 %shard_map.55 = (bf16[2,256,256]{2,1,0:T(8,128)(2,1)}, bf16[2,256,256]{2,1,0:T(8,128)(2,1)}) custom-call(s32[32]{0:T(128)} %left_sizes.3, s32[32]{0:T(128)} %right_sizes.3, bf16[256,8192]{1,0:T(8,128)(2,1)} %psi_ref.1), custom_call_target="tpu_custom_call" | custom-call | tf_op jit(solution)/shard_map/pallas_call | solution.py:76
  9.1 0.0 copy-done.5
  9.1 5.8 %collective-permute-start = (bf16[2,256,256]{2,1,0:T(8,128)(2,1)S(1)}, bf16[2,256,256]{2,1,0:T(8,128)(2,1)S(1)}, u32[]{:S(2)}, u32[]{:S(2)}) collective-permute-start(bf16[2,256,256]{2,1,0:T(8,128)(2,1)S(1)} %copy-done.5), channel_id=1, source_target_pairs={{0,0},{1,16},{2,32},{3,48},{4,64},{5,80},{6,96},{7,112},{8,12},{9,... | collective-permute-start | bytes 786440 | tf_op jit(solution)/shard_map/ppermute | solution.py:278
  15.0 0.0 collective-permute-done.4.refs_7_
  15.0 1.3 %collective-permute-start.5 = (bf16[2,256,256]{2,1,0:T(8,128)(2,1)S(1)}, bf16[2,256,256]{2,1,0:T(8,128)(2,1)S(1)}, u32[]{:S(2)}, u32[]{:S(2)}) collective-permute-start(bf16[2,256,256]{2,1,0:T(8,128)(2,1)S(1)} %collective-permute-done.4.refs_7_), channel_id=1, source_target_pairs={{0,1},{1,2},{2,3},{3,4},{4,5},{5,6},{6,7},{7,0},{8,9},{9,10},{10,1... | collective-permute-start | bytes 786440 | tf_op jit(solution)/shard_map/ppermute | solution.py:262
  16.3 0.0 collective-permute-done.7.refs_1_
  16.3 2.4 %collective-permute-start.8 = (bf16[2,256,256]{2,1,0:T(8,128)(2,1)S(1)}, bf16[2,256,256]{2,1,0:T(8,128)(2,1)S(1)}, u32[]{:S(2)}, u32[]{:S(2)}) collective-permute-start(bf16[2,256,256]{2,1,0:T(8,128)(2,1)S(1)} %collective-permute-done.7.refs_1_), channel_id=1, source_target_pairs={{0,7},{1,0},{2,1},{3,2},{4,3},{5,4},{6,5},{7,6},{8,15},{9,8},{10,9... | collective-permute-start | bytes 786440 | tf_op jit(solution)/shard_map/ppermute | solution.py:265
  18.7 2.2 %collective-permute-done.refs_0_ = bf16[2,256,256]{2,1,0:T(8,128)(2,1)S(1)} collective-permute-done((bf16[2,256,256]{2,1,0:T(8,128)(2,1)S(1)}, bf16[2,256,256]{2,1,0:T(8,128)(2,1)S(1)}, u32[]{:S(2)}, u32[]{:S(2)}) %collective-permute-start) | collective-permute-done | bytes 262176 | tf_op jit(solution)/shard_map/ppermute | solution.py:278
  20.8 1.0 collective-permute-start.1
  21.8 1.7 %collective-permute-start.2 = (bf16[2,256,256]{2,1,0:T(8,128)(2,1)S(1)}, bf16[2,256,256]{2,1,0:T(8,128)(2,1)S(1)}, u32[]{:S(2)}, u32[]{:S(2)}) collective-permute-start(bf16[2,256,256]{2,1,0:T(8,128)(2,1)S(1)} %collective-permute-done.refs_0_), channel_id=1, source_target_pairs={{0,48},{8,200},{16,0},{24,216},{32,16},{40,232},{48,32},{56,248},{... | collective-permute-start | bytes 786440 | tf_op jit(solution)/shard_map/ppermute | solution.py:253
  23.5 1.7 %collective-permute-start.3 = (bf16[2,256,256]{2,1,0:T(8,128)(2,1)S(1)}, bf16[2,256,256]{2,1,0:T(8,128)(2,1)S(1)}, u32[]{:S(2)}, u32[]{:S(2)}) collective-permute-start(bf16[2,256,256]{2,1,0:T(8,128)(2,1)S(1)} %collective-permute-done.refs_0_), channel_id=1, source_target_pairs={{0,32},{8,136},{16,48},{24,152},{32,0},{40,168},{48,16},{56,184},{... | collective-permute-start | bytes 786440 | tf_op jit(solution)/shard_map/ppermute | solution.py:253
  25.2 8.7 %collective-permute-done.5.refs_6_ = bf16[2,256,256]{2,1,0:T(8,128)(2,1)S(1)} collective-permute-done((bf16[2,256,256]{2,1,0:T(8,128)(2,1)S(1)}, bf16[2,256,256]{2,1,0:T(8,128)(2,1)S(1)}, u32[]{:S(2)}, u32[]{:S(2)}) %collective-permute-start.5) | collective-permute-done | bytes 262176 | tf_op jit(solution)/shard_map/ppermute | solution.py:262
  33.9 0.0 collective-permute-start.6
  33.9 0.0 collective-permute-done.8.refs_2_
  33.9 2.7 %collective-permute-start.9 = (bf16[2,256,256]{2,1,0:T(8,128)(2,1)S(1)}, bf16[2,256,256]{2,1,0:T(8,128)(2,1)S(1)}, u32[]{:S(2)}, u32[]{:S(2)}) collective-permute-start(bf16[2,256,256]{2,1,0:T(8,128)(2,1)S(1)} %collective-permute-done.8.refs_2_), channel_id=1, source_target_pairs={{0,7},{1,0},{2,1},{3,2},{4,3},{5,4},{6,5},{7,6},{8,15},{9,8},{10,9... | collective-permute-start | bytes 786440 | tf_op jit(solution)/shard_map/ppermute | solution.py:265
  36.5 0.0 collective-permute-done.1.refs_1_
  36.5 0.0 collective-permute-done.2.refs_0_
  36.5 0.0 collective-permute-done.3.refs_1_
  36.5 3.7 %collective-permute-done.6.refs_5_ = bf16[2,256,256]{2,1,0:T(8,128)(2,1)S(1)} collective-permute-done((bf16[2,256,256]{2,1,0:T(8,128)(2,1)S(1)}, bf16[2,256,256]{2,1,0:T(8,128)(2,1)S(1)}, u32[]{:S(2)}, u32[]{:S(2)}) %collective-permute-start.6) | collective-permute-done | bytes 262176 | tf_op jit(solution)/shard_map/ppermute | solution.py:262
  40.3 0.0 collective-permute-done.9.refs_3_
  40.3 0.1 shard_map.56.refs_0_
  40.4 0.9 collective-permute-start.10
  41.3 5.1 %collective-permute-start.11 = (bf16[2,2,256,256]{3,2,1,0:T(8,128)(2,1)S(1)}, bf16[2,2,256,256]{3,2,1,0:T(8,128)(2,1)S(1)}, u32[]{:S(2)}, u32[]{:S(2)}) collective-permute-start(bf16[2,2,256,256]{3,2,1,0:T(8,128)(2,1)S(1)} %shard_map.56.refs_0_), channel_id=1, source_target_pairs={{0,192},{8,56},{16,208},{24,8},{32,224},{40,24},{48,240},{56,40},{... | collective-permute-start | bytes 1572872 | tf_op jit(solution)/shard_map/ppermute | solution.py:256
  46.3 0.1 shard_map.57.refs_3_
  46.4 0.0 copy-start
  46.4 0.1 collective-permute-start.12
  46.5 2.7 %collective-permute-start.13 = (bf16[2,2,256,256]{3,2,1,0:T(8,128)(2,1)S(1)}, bf16[2,2,256,256]{3,2,1,0:T(8,128)(2,1)S(1)}, u32[]{:S(2)}, u32[]{:S(2)}) collective-permute-start(bf16[2,2,256,256]{3,2,1,0:T(8,128)(2,1)S(1)} %shard_map.57.refs_3_), channel_id=1, source_target_pairs={{0,192},{8,56},{16,208},{24,8},{32,224},{40,24},{48,240},{56,40},{... | collective-permute-start | bytes 1572872 | tf_op jit(solution)/shard_map/ppermute | solution.py:256
  49.2 0.0 collective-permute-start.14
  49.2 6.8 %collective-permute-done.14.refs_4_ = bf16[2,256,256]{2,1,0:T(8,128)(2,1)S(1)} collective-permute-done((bf16[2,256,256]{2,1,0:T(8,128)(2,1)S(1)}, bf16[2,256,256]{2,1,0:T(8,128)(2,1)S(1)}, u32[]{:S(2)}, u32[]{:S(2)}) %collective-permute-start.14) | collective-permute-done | bytes 262176 | tf_op jit(solution)/shard_map/ppermute | solution.py:262
  56.0 0.0 copy-done.1
  56.0 0.0 copy-start.2
  56.0 0.9 copy-done.2
  56.9 0.3 shard_map.58.refs_6_.refs_2_
  57.2 0.0 collective-permute-done.10.refs_1_
  57.2 0.0 collective-permute-done.11.refs_2_
  57.2 1.5 %collective-permute-done.12.refs_4_ = bf16[2,2,256,256]{3,2,1,0:T(8,128)(2,1)S(1)} collective-permute-done((bf16[2,2,256,256]{3,2,1,0:T(8,128)(2,1)S(1)}, bf16[2,2,256,256]{3,2,1,0:T(8,128)(2,1)S(1)}, u32[]{:S(2)}, u32[]{:S(2)}) %collective-permute-start.12) | collective-permute-done | bytes 524320 | tf_op jit(solution)/shard_map/ppermute | solution.py:256
  58.7 0.0 collective-permute-done.13.refs_5_
  58.7 3.2 %collective-permute-start.15 = (bf16[9,2,256,256]{3,2,1,0:T(8,128)(2,1)S(1)}, bf16[9,2,256,256]{3,2,1,0:T(8,128)(2,1)S(1)}, u32[]{:S(2)}, u32[]{:S(2)}) collective-permute-start(bf16[9,2,256,256]{3,2,1,0:T(8,128)(2,1)S(1)} %shard_map.58.refs_6_.refs_2_), channel_id=1, source_target_pairs={{0,8},{8,0},{16,24},{24,16},{32,40},{40,32},{48,56},{56,48},{64,72... | collective-permute-start | bytes 7077896 | tf_op jit(solution)/shard_map/ppermute | solution.py:259
  61.9 1.1 %collective-permute-start.16 = (bf16[2,2,256,256]{3,2,1,0:T(8,128)(2,1)S(1)}, bf16[2,2,256,256]{3,2,1,0:T(8,128)(2,1)S(1)}, u32[]{:S(2)}, u32[]{:S(2)}) collective-permute-start(bf16[2,2,256,256]{3,2,1,0:T(8,128)(2,1)S(1)} %collective-permute-done.10.refs_1_), channel_id=1, source_target_pairs={{0,64},{8,24},{16,80},{24,40},{32,96},{40,56},{48,112},{56,8},{64,... | collective-permute-start | bytes 1572872 | tf_op jit(solution)/shard_map/ppermute | solution.py:256
  63.1 1.5 %collective-permute-start.17 = (bf16[2,2,256,256]{3,2,1,0:T(8,128)(2,1)S(1)}, bf16[2,2,256,256]{3,2,1,0:T(8,128)(2,1)S(1)}, u32[]{:S(2)}, u32[]{:S(2)}) collective-permute-start(bf16[2,2,256,256]{3,2,1,0:T(8,128)(2,1)S(1)} %collective-permute-done.13.refs_5_), channel_id=1, source_target_pairs={{0,192},{8,56},{16,208},{24,8},{32,224},{40,24},{48,240},{56,40},{... | collective-permute-start | bytes 1572872 | tf_op jit(solution)/shard_map/ppermute | solution.py:256
  64.6 0.0 copy-done
  64.6 3.7 %shard_map.59.mine = f32[2,256,256]{2,1,0:T(8,128)S(1)} custom-call(bf16[2,2,256,256]{3,2,1,0:T(8,128)(2,1)S(1)} %shard_map.56.refs_0_, bf16[2,2,256,256]{3,2,1,0:T(8,128)(2,1)S(1)} %collective-permute-done.10.refs_1_, bf16[2,2,256,256]{3,2,1,0:T(8,128)(2,1)S(1)} %collective-permute-done.11.refs_2_, bf16[2,2,256,256]{3,2,1,0:T(8,128)(2,1)S(1)} %shard_map.57.refs_3_, ...), custom_call_target="tpu_custom_call" | custom-call | tf_op jit(solution)/shard_map/pallas_call | solution.py:126
  68.3 0.0 copy-start.3
  68.3 0.0 copy-start.4
  68.3 0.0 collective-permute-done.15.refs_6_.refs_3_
  68.3 3.7 %shard_map.60.theirs = f32[2,256,256]{2,1,0:T(8,128)S(1)} custom-call(bf16[2,2,256,256]{3,2,1,0:T(8,128)(2,1)S(1)} %shard_map.56.refs_0_, bf16[2,2,256,256]{3,2,1,0:T(8,128)(2,1)S(1)} %collective-permute-done.10.refs_1_, bf16[2,2,256,256]{3,2,1,0:T(8,128)(2,1)S(1)} %collective-permute-done.11.refs_2_, bf16[2,2,256,256]{3,2,1,0:T(8,128)(2,1)S(1)} %shard_map.57.refs_3_, ...), custom_call_target="tpu_custom_call" | custom-call | tf_op jit(solution)/shard_map/pallas_call | solution.py:126
  72.0 0.0 collective-permute-done.16.refs_0_
  72.0 0.0 collective-permute-done.17.refs_1_
  72.1 0.0 copy-done.3
  72.1 0.0 copy-done.4
  72.1 2.6 %shard_map.61 = bf16[8,2,2,32,256]{4,3,2,1,0:T(8,128)(2,1)S(1)} custom-call(s32[32]{0:T(128)S(1)} %copy-done.3, s32[32]{0:T(128)S(1)} %copy-done.4, f32[2,256,256]{2,1,0:T(8,128)S(1)} %shard_map.59.mine, f32[2,256,256]{2,1,0:T(8,128)S(1)} %shard_map.60.theirs, bf16[2,2,256,256]{3,2,1,0:T(8,128)(2,1)S(1)} %collective-permute-done.16.refs_0_, ...), custom_call_target="tpu_custom_call" | custom-call | tf_op jit(solution)/shard_map/pallas_call | solution.py:195
  74.7 20.3 %all_to_all.10 = bf16[8,2,2,32,256]{4,3,2,1,0:T(8,128)(2,1)S(1)} all-to-all(bf16[8,2,2,32,256]{4,3,2,1,0:T(8,128)(2,1)S(1)} %shard_map.61), channel_id=1, replica_groups=mesh['blk'=32,'mpo'=8] {'mpo'}, dimensions={0} | all-to-all | bytes 1048576 | tf_op jit(solution)/shard_map/all_to_all | solution.py:300
  95.0 15.9 %all_to_all.11.in_ref = bf16[16,2,32,256]{3,2,1,0:T(8,128)(2,1)S(1)} all-to-all(bf16[16,2,32,256]{3,2,1,0:T(8,128)(2,1)S(1)} %bitcast.2), channel_id=1, replica_groups={{0,128,16,144,32,160,48,176,64,192,80,208,96,224,112,240},{72,200,88,21..., dimensions={0} | all-to-all | bytes 1048576 | tf_op jit(solution)/shard_map/all_to_all | solution.py:307
  111.0 0.9 shard_map.62
Async XLA Ops:
  0.0 56.0 %copy-start.1 = (bf16[2,256,256]{2,1,0:T(8,128)(2,1)S(1)}, bf16[2,256,256]{2,1,0:T(8,128)(2,1)}, u32[]{:S(2)}) copy-start(bf16[2,256,256]{2,1,0:T(8,128)(2,1)} %refs_0_.1) | copy-start | bytes 786436
  0.0 9.1 %copy-start.5 = (bf16[2,256,256]{2,1,0:T(8,128)(2,1)S(1)}, bf16[2,256,256]{2,1,0:T(8,128)(2,1)}, u32[]{:S(2)}) copy-start(bf16[2,256,256]{2,1,0:T(8,128)(2,1)} %param.7) | copy-start | bytes 786436
  0.0 15.0 %collective-permute-start.4 = (bf16[2,256,256]{2,1,0:T(8,128)(2,1)}, bf16[2,256,256]{2,1,0:T(8,128)(2,1)S(1)}, u32[]{:S(2)}, u32[]{:S(2)}) collective-permute-start(bf16[2,256,256]{2,1,0:T(8,128)(2,1)} %refs_0_.1), channel_id=1, source_target_pairs={{0,1},{1,2},{2,3},{3,4},{4,5},{5,6},{6,7},{7,0},{8,9},{9,10},{10,1... | collective-permute-start | bytes 786440 | tf_op jit(solution)/shard_map/ppermute | solution.py:262
  2.5 13.8 %collective-permute-start.7 = (bf16[2,256,256]{2,1,0:T(8,128)(2,1)}, bf16[2,256,256]{2,1,0:T(8,128)(2,1)S(1)}, u32[]{:S(2)}, u32[]{:S(2)}) collective-permute-start(bf16[2,256,256]{2,1,0:T(8,128)(2,1)} %refs_0_.1), channel_id=1, source_target_pairs={{0,7},{1,0},{2,1},{3,2},{4,3},{5,4},{6,5},{7,6},{8,15},{9,8},{10,9... | collective-permute-start | bytes 786440 | tf_op jit(solution)/shard_map/ppermute | solution.py:265
  9.1 11.7 %collective-permute-start = (bf16[2,256,256]{2,1,0:T(8,128)(2,1)S(1)}, bf16[2,256,256]{2,1,0:T(8,128)(2,1)S(1)}, u32[]{:S(2)}, u32[]{:S(2)}) collective-permute-start(bf16[2,256,256]{2,1,0:T(8,128)(2,1)S(1)} %copy-done.5), channel_id=1, source_target_pairs={{0,0},{1,16},{2,32},{3,48},{4,64},{5,80},{6,96},{7,112},{8,12},{9,... | collective-permute-start | bytes 786440 | tf_op jit(solution)/shard_map/ppermute | solution.py:278
  15.0 18.9 %collective-permute-start.5 = (bf16[2,256,256]{2,1,0:T(8,128)(2,1)S(1)}, bf16[2,256,256]{2,1,0:T(8,128)(2,1)S(1)}, u32[]{:S(2)}, u32[]{:S(2)}) collective-permute-start(bf16[2,256,256]{2,1,0:T(8,128)(2,1)S(1)} %collective-permute-done.4.refs_7_), channel_id=1, source_target_pairs={{0,1},{1,2},{2,3},{3,4},{4,5},{5,6},{6,7},{7,0},{8,9},{9,10},{10,1... | collective-permute-start | bytes 786440 | tf_op jit(solution)/shard_map/ppermute | solution.py:262
  16.3 17.6 %collective-permute-start.8 = (bf16[2,256,256]{2,1,0:T(8,128)(2,1)S(1)}, bf16[2,256,256]{2,1,0:T(8,128)(2,1)S(1)}, u32[]{:S(2)}, u32[]{:S(2)}) collective-permute-start(bf16[2,256,256]{2,1,0:T(8,128)(2,1)S(1)} %collective-permute-done.7.refs_1_), channel_id=1, source_target_pairs={{0,7},{1,0},{2,1},{3,2},{4,3},{5,4},{6,5},{7,6},{8,15},{9,8},{10,9... | collective-permute-start | bytes 786440 | tf_op jit(solution)/shard_map/ppermute | solution.py:265
  20.8 15.7 %collective-permute-start.1 = (bf16[2,256,256]{2,1,0:T(8,128)(2,1)S(1)}, bf16[2,256,256]{2,1,0:T(8,128)(2,1)S(1)}, u32[]{:S(2)}, u32[]{:S(2)}) collective-permute-start(bf16[2,256,256]{2,1,0:T(8,128)(2,1)S(1)} %collective-permute-done.refs_0_), channel_id=1, source_target_pairs={{0,16},{8,72},{16,32},{24,88},{32,48},{40,104},{48,0},{56,120},{64... | collective-permute-start | bytes 786440 | tf_op jit(solution)/shard_map/ppermute | solution.py:253
  21.8 14.7 %collective-permute-start.2 = (bf16[2,256,256]{2,1,0:T(8,128)(2,1)S(1)}, bf16[2,256,256]{2,1,0:T(8,128)(2,1)S(1)}, u32[]{:S(2)}, u32[]{:S(2)}) collective-permute-start(bf16[2,256,256]{2,1,0:T(8,128)(2,1)S(1)} %collective-permute-done.refs_0_), channel_id=1, source_target_pairs={{0,48},{8,200},{16,0},{24,216},{32,16},{40,232},{48,32},{56,248},{... | collective-permute-start | bytes 786440 | tf_op jit(solution)/shard_map/ppermute | solution.py:253
  23.5 13.1 %collective-permute-start.3 = (bf16[2,256,256]{2,1,0:T(8,128)(2,1)S(1)}, bf16[2,256,256]{2,1,0:T(8,128)(2,1)S(1)}, u32[]{:S(2)}, u32[]{:S(2)}) collective-permute-start(bf16[2,256,256]{2,1,0:T(8,128)(2,1)S(1)} %collective-permute-done.refs_0_), channel_id=1, source_target_pairs={{0,32},{8,136},{16,48},{24,152},{32,0},{40,168},{48,16},{56,184},{... | collective-permute-start | bytes 786440 | tf_op jit(solution)/shard_map/ppermute | solution.py:253
  33.9 6.4 %collective-permute-start.6 = (bf16[2,256,256]{2,1,0:T(8,128)(2,1)S(1)}, bf16[2,256,256]{2,1,0:T(8,128)(2,1)S(1)}, u32[]{:S(2)}, u32[]{:S(2)}) collective-permute-start(bf16[2,256,256]{2,1,0:T(8,128)(2,1)S(1)} %collective-permute-done.5.refs_6_), channel_id=1, source_target_pairs={{0,1},{1,2},{2,3},{3,4},{4,5},{5,6},{6,7},{7,0},{8,9},{9,10},{10,1... | collective-permute-start | bytes 786440 | tf_op jit(solution)/shard_map/ppermute | solution.py:262
  33.9 6.4 %collective-permute-start.9 = (bf16[2,256,256]{2,1,0:T(8,128)(2,1)S(1)}, bf16[2,256,256]{2,1,0:T(8,128)(2,1)S(1)}, u32[]{:S(2)}, u32[]{:S(2)}) collective-permute-start(bf16[2,256,256]{2,1,0:T(8,128)(2,1)S(1)} %collective-permute-done.8.refs_2_), channel_id=1, source_target_pairs={{0,7},{1,0},{2,1},{3,2},{4,3},{5,4},{6,5},{7,6},{8,15},{9,8},{10,9... | collective-permute-start | bytes 786440 | tf_op jit(solution)/shard_map/ppermute | solution.py:265
  40.4 16.8 %collective-permute-start.10 = (bf16[2,2,256,256]{3,2,1,0:T(8,128)(2,1)S(1)}, bf16[2,2,256,256]{3,2,1,0:T(8,128)(2,1)S(1)}, u32[]{:S(2)}, u32[]{:S(2)}) collective-permute-start(bf16[2,2,256,256]{3,2,1,0:T(8,128)(2,1)S(1)} %shard_map.56.refs_0_), channel_id=1, source_target_pairs={{0,64},{8,24},{16,80},{24,40},{32,96},{40,56},{48,112},{56,8},{64,... | collective-permute-start | bytes 1572872 | tf_op jit(solution)/shard_map/ppermute | solution.py:256
  41.3 15.9 %collective-permute-start.11 = (bf16[2,2,256,256]{3,2,1,0:T(8,128)(2,1)S(1)}, bf16[2,2,256,256]{3,2,1,0:T(8,128)(2,1)S(1)}, u32[]{:S(2)}, u32[]{:S(2)}) collective-permute-start(bf16[2,2,256,256]{3,2,1,0:T(8,128)(2,1)S(1)} %shard_map.56.refs_0_), channel_id=1, source_target_pairs={{0,192},{8,56},{16,208},{24,8},{32,224},{40,24},{48,240},{56,40},{... | collective-permute-start | bytes 1572872 | tf_op jit(solution)/shard_map/ppermute | solution.py:256
  46.4 18.2 %copy-start = (bf16[2,256,256]{2,1,0:T(8,128)(2,1)S(1)}, bf16[2,256,256]{2,1,0:T(8,128)(2,1)}, u32[]{:S(2)}) copy-start(bf16[2,256,256]{2,1,0:T(8,128)(2,1)} %get-tuple-element.34.refs_7_.refs_4_) | copy-start | bytes 786436
  46.4 12.3 %collective-permute-start.12 = (bf16[2,2,256,256]{3,2,1,0:T(8,128)(2,1)S(1)}, bf16[2,2,256,256]{3,2,1,0:T(8,128)(2,1)S(1)}, u32[]{:S(2)}, u32[]{:S(2)}) collective-permute-start(bf16[2,2,256,256]{3,2,1,0:T(8,128)(2,1)S(1)} %shard_map.57.refs_3_), channel_id=1, source_target_pairs={{0,64},{8,24},{16,80},{24,40},{32,96},{40,56},{48,112},{56,8},{64,... | collective-permute-start | bytes 1572872 | tf_op jit(solution)/shard_map/ppermute | solution.py:256
  46.5 12.2 %collective-permute-start.13 = (bf16[2,2,256,256]{3,2,1,0:T(8,128)(2,1)S(1)}, bf16[2,2,256,256]{3,2,1,0:T(8,128)(2,1)S(1)}, u32[]{:S(2)}, u32[]{:S(2)}) collective-permute-start(bf16[2,2,256,256]{3,2,1,0:T(8,128)(2,1)S(1)} %shard_map.57.refs_3_), channel_id=1, source_target_pairs={{0,192},{8,56},{16,208},{24,8},{32,224},{40,24},{48,240},{56,40},{... | collective-permute-start | bytes 1572872 | tf_op jit(solution)/shard_map/ppermute | solution.py:256
  49.2 6.8 %collective-permute-start.14 = (bf16[2,256,256]{2,1,0:T(8,128)(2,1)S(1)}, bf16[2,256,256]{2,1,0:T(8,128)(2,1)S(1)}, u32[]{:S(2)}, u32[]{:S(2)}) collective-permute-start(bf16[2,256,256]{2,1,0:T(8,128)(2,1)S(1)} %collective-permute-done.6.refs_5_), channel_id=1, source_target_pairs={{0,1},{1,2},{2,3},{3,4},{4,5},{5,6},{6,7},{7,0},{8,9},{9,10},{10,1... | collective-permute-start | bytes 786440 | tf_op jit(solution)/shard_map/ppermute | solution.py:262
  56.0 1.0 copy-start.2
  58.7 9.6 %collective-permute-start.15 = (bf16[9,2,256,256]{3,2,1,0:T(8,128)(2,1)S(1)}, bf16[9,2,256,256]{3,2,1,0:T(8,128)(2,1)S(1)}, u32[]{:S(2)}, u32[]{:S(2)}) collective-permute-start(bf16[9,2,256,256]{3,2,1,0:T(8,128)(2,1)S(1)} %shard_map.58.refs_6_.refs_2_), channel_id=1, source_target_pairs={{0,8},{8,0},{16,24},{24,16},{32,40},{40,32},{48,56},{56,48},{64,72... | collective-permute-start | bytes 7077896 | tf_op jit(solution)/shard_map/ppermute | solution.py:259
  61.9 10.1 %collective-permute-start.16 = (bf16[2,2,256,256]{3,2,1,0:T(8,128)(2,1)S(1)}, bf16[2,2,256,256]{3,2,1,0:T(8,128)(2,1)S(1)}, u32[]{:S(2)}, u32[]{:S(2)}) collective-permute-start(bf16[2,2,256,256]{3,2,1,0:T(8,128)(2,1)S(1)} %collective-permute-done.10.refs_1_), channel_id=1, source_target_pairs={{0,64},{8,24},{16,80},{24,40},{32,96},{40,56},{48,112},{56,8},{64,... | collective-permute-start | bytes 1572872 | tf_op jit(solution)/shard_map/ppermute | solution.py:256
  63.1 9.0 %collective-permute-start.17 = (bf16[2,2,256,256]{3,2,1,0:T(8,128)(2,1)S(1)}, bf16[2,2,256,256]{3,2,1,0:T(8,128)(2,1)S(1)}, u32[]{:S(2)}, u32[]{:S(2)}) collective-permute-start(bf16[2,2,256,256]{3,2,1,0:T(8,128)(2,1)S(1)} %collective-permute-done.13.refs_5_), channel_id=1, source_target_pairs={{0,192},{8,56},{16,208},{24,8},{32,224},{40,24},{48,240},{56,40},{... | collective-permute-start | bytes 1572872 | tf_op jit(solution)/shard_map/ppermute | solution.py:256
  68.3 3.8 %copy-start.3 = (s32[32]{0:T(128)S(1)}, s32[32]{0:T(128)}, u32[]{:S(2)}) copy-start(s32[32]{0:T(128)} %left_sizes.3) | copy-start | bytes 388
  68.3 3.8 %copy-start.4 = (s32[32]{0:T(128)S(1)}, s32[32]{0:T(128)}, u32[]{:S(2)}) copy-start(s32[32]{0:T(128)} %right_sizes.3) | copy-start | bytes 388

commit v18 on v17

--- a/solution.py
+++ b/solution.py
@@ -279,11 +279,11 @@
     up2, down2 = up(up1), down(down1)
 
     below, above, two = near_step(own, 1), near_step(own, -1), near_step(own, 2)
-    up3, down3 = up(up2), down(down2)
-    below, above, two, up3, down3 = together(below, above, two, up3, down3)
+    below, above, two, up2, down2 = together(below, above, two, up2, down2)
     line_a, line_b = stack(own, below), stack(above, two)
     a_below, a_above = far_step(line_a, 1), far_step(line_a, -1)
     b_below, b_above = far_step(line_b, 1), far_step(line_b, -1)
+    up3, down3 = up(up2), down(down2)
     up4 = up(up3)
     lefts = stack(left_env, down1, down2, down3, up4, up3, up2, up1, give)
     a_below, a_above, b_below, b_above, lefts = together(a_below, a_above, b_below, b_above, lefts)

time: 113 us -> 116 us (1.027)
  starting transfers between devices: 37.6 us -> 43.9 us
  waiting for transfers between devices: 22.9 us -> 17.9 us
    ppermute x1, starting transfers between devices: 5.83 us -> 9.65 us  [local(): own = lax.ppermute(right_env, ('blk', 'mpo'), turn)]
    ppermute x1, starting transfers between devices: 3.19 us -> 6.92 us  [swap(): return lax.ppermute(block, 'blk', [(i, i ^ 1) for i in range(sectors)])]
    ppermute x6, starting transfers between devices: 11.4 us -> 8.48 us  [far_step(): return lax.ppermute(block, 'blk', step(True, by))]
    ppermute x1, waiting for transfers between devices: 2.15 us -> 0.01 us  [local(): own = lax.ppermute(right_env, ('blk', 'mpo'), turn)]
    all_to_all x1, blocking collectives: 20.3 us -> 22.2 us  [local(): by_plane = lax.all_to_all(done, 'mpo', 0, 0)]
    ppermute x4, waiting for transfers between devices: 19.2 us -> 17.6 us  [up(): lax.ppermute(block, 'mpo', [(z, (z + 1) % ranks) for z in range(ranks)])]
    ppermute x6, waiting for transfers between devices: 1.53 us -> 0.22 us  [far_step(): return lax.ppermute(block, 'blk', step(True, by))]
  transfers between devices with their start and end apart: 18 -> 18, of which waited for: 5 -> 6; matrix products, arithmetic and copies ran while one was open for 0% -> 0% of each run, Pallas kernels for 9% -> 7%
where the time goes in v18:
time: 116 us; the launch traced here: 114 us
  starting transfers between devices  43.9 us (38%)
  blocking collectives  37.1 us (32%)
  waiting for transfers between devices  17.9 us (15%)
  Pallas kernels  14 us (12%)
    all_to_all x1, blocking collectives, local(): by_plane = lax.all_to_all(done, 'mpo', 0, 0)  22.2 us
    ppermute x4, waiting for transfers between devices, up(): lax.ppermute(block, 'mpo', [(z, (z + 1) % ranks) for z in range(ranks)])  17.6 us
    all_to_all x1, blocking collectives, local(): out = order(lax.all_to_all(by_plane, 'blk', 0, 0, axis_index_groups=groups))  14.9 us
    ppermute x3, starting transfers between devices, down(): lax.ppermute(block, 'mpo', [(z, (z - 1) % ranks) for z in range(ranks)])  9.98 us
    ppermute x1, starting transfers between devices, local(): own = lax.ppermute(right_env, ('blk', 'mpo'), turn)  9.65 us
    ppermute x6, starting transfers between devices, far_step(): return lax.ppermute(block, 'blk', step(True, by))  8.48 us
    pallas_call x2, Pallas kernels, half(): pl.pallas_call(functools.partial(half_kernel, pieces), out_shape=jax.Shap...  7.38 us
    ppermute x1, starting transfers between devices, swap(): return lax.ppermute(block, 'blk', [(i, i ^ 1) for i in range(sectors)])  6.92 us
  transfers between devices with their start and end apart: 18, of which 6 were waited for; matrix products, arithmetic and copies ran while one was open for 0% of the time, Pallas kernels for 7%

profile of v18, /device:TPU:1, one launch (start us, length us, event | category | flops | bytes accessed | tf_op | source)
XLA Modules:
  0.0 114.3 jit_solution(2647049869089744902)
XLA Ops:
  0.0 0.0 copy-start.5
  0.0 0.0 copy-start.1
  0.0 2.8 %shard_map.55 = (bf16[2,256,256]{2,1,0:T(8,128)(2,1)}, bf16[2,256,256]{2,1,0:T(8,128)(2,1)}) custom-call(s32[32]{0:T(128)} %left_sizes.3, s32[32]{0:T(128)} %right_sizes.3, bf16[256,8192]{1,0:T(8,128)(2,1)} %psi_ref.1), custom_call_target="tpu_custom_call" | custom-call | tf_op jit(solution)/shard_map/pallas_call | solution.py:76
  2.8 0.0 copy-done.5
  2.8 9.6 %collective-permute-start = (bf16[2,256,256]{2,1,0:T(8,128)(2,1)S(1)}, bf16[2,256,256]{2,1,0:T(8,128)(2,1)S(1)}, u32[]{:S(2)}, u32[]{:S(2)}) collective-permute-start(bf16[2,256,256]{2,1,0:T(8,128)(2,1)S(1)} %copy-done.5), channel_id=1, source_target_pairs={{0,0},{1,16},{2,32},{3,48},{4,64},{5,80},{6,96},{7,112},{8,12},{9,... | collective-permute-start | bytes 786440 | tf_op jit(solution)/shard_map/ppermute | solution.py:278
  12.4 0.0 copy-done.1
  12.4 1.3 %collective-permute-start.4 = (bf16[2,256,256]{2,1,0:T(8,128)(2,1)S(1)}, bf16[2,256,256]{2,1,0:T(8,128)(2,1)S(1)}, u32[]{:S(2)}, u32[]{:S(2)}) collective-permute-start(bf16[2,256,256]{2,1,0:T(8,128)(2,1)S(1)} %copy-done.1), channel_id=1, source_target_pairs={{0,1},{1,2},{2,3},{3,4},{4,5},{5,6},{6,7},{7,0},{8,9},{9,10},{10,1... | collective-permute-start | bytes 786440 | tf_op jit(solution)/shard_map/ppermute | solution.py:262
  13.7 2.4 %collective-permute-start.6 = (bf16[2,256,256]{2,1,0:T(8,128)(2,1)S(1)}, bf16[2,256,256]{2,1,0:T(8,128)(2,1)S(1)}, u32[]{:S(2)}, u32[]{:S(2)}) collective-permute-start(bf16[2,256,256]{2,1,0:T(8,128)(2,1)S(1)} %copy-done.1), channel_id=1, source_target_pairs={{0,7},{1,0},{2,1},{3,2},{4,3},{5,4},{6,5},{7,6},{8,15},{9,8},{10,9... | collective-permute-start | bytes 786440 | tf_op jit(solution)/shard_map/ppermute | solution.py:265
  16.1 0.0 collective-permute-done.refs_0_
  16.1 1.8 %collective-permute-start.1 = (bf16[2,256,256]{2,1,0:T(8,128)(2,1)S(1)}, bf16[2,256,256]{2,1,0:T(8,128)(2,1)S(1)}, u32[]{:S(2)}, u32[]{:S(2)}) collective-permute-start(bf16[2,256,256]{2,1,0:T(8,128)(2,1)S(1)} %collective-permute-done.refs_0_), channel_id=1, source_target_pairs={{0,16},{8,72},{16,32},{24,88},{32,48},{40,104},{48,0},{56,120},{64... | collective-permute-start | bytes 786440 | tf_op jit(solution)/shard_map/ppermute | solution.py:253
  17.9 1.4 %collective-permute-start.2 = (bf16[2,256,256]{2,1,0:T(8,128)(2,1)S(1)}, bf16[2,256,256]{2,1,0:T(8,128)(2,1)S(1)}, u32[]{:S(2)}, u32[]{:S(2)}) collective-permute-start(bf16[2,256,256]{2,1,0:T(8,128)(2,1)S(1)} %collective-permute-done.refs_0_), channel_id=1, source_target_pairs={{0,48},{8,200},{16,0},{24,216},{32,16},{40,232},{48,32},{56,248},{... | collective-permute-start | bytes 786440 | tf_op jit(solution)/shard_map/ppermute | solution.py:253
  19.4 1.2 %collective-permute-start.3 = (bf16[2,256,256]{2,1,0:T(8,128)(2,1)S(1)}, bf16[2,256,256]{2,1,0:T(8,128)(2,1)S(1)}, u32[]{:S(2)}, u32[]{:S(2)}) collective-permute-start(bf16[2,256,256]{2,1,0:T(8,128)(2,1)S(1)} %collective-permute-done.refs_0_), channel_id=1, source_target_pairs={{0,32},{8,136},{16,48},{24,152},{32,0},{40,168},{48,16},{56,184},{... | collective-permute-start | bytes 786440 | tf_op jit(solution)/shard_map/ppermute | solution.py:253
  20.5 8.0 %collective-permute-done.4.refs_7_ = bf16[2,256,256]{2,1,0:T(8,128)(2,1)S(1)} collective-permute-done((bf16[2,256,256]{2,1,0:T(8,128)(2,1)S(1)}, bf16[2,256,256]{2,1,0:T(8,128)(2,1)S(1)}, u32[]{:S(2)}, u32[]{:S(2)}) %collective-permute-start.4) | collective-permute-done | bytes 262176 | tf_op jit(solution)/shard_map/ppermute | solution.py:262
  28.5 0.0 collective-permute-start.5
  28.5 0.0 collective-permute-done.6.refs_1_
  28.5 4.6 %collective-permute-start.7 = (bf16[2,256,256]{2,1,0:T(8,128)(2,1)S(1)}, bf16[2,256,256]{2,1,0:T(8,128)(2,1)S(1)}, u32[]{:S(2)}, u32[]{:S(2)}) collective-permute-start(bf16[2,256,256]{2,1,0:T(8,128)(2,1)S(1)} %collective-permute-done.6.refs_1_), channel_id=1, source_target_pairs={{0,7},{1,0},{2,1},{3,2},{4,3},{5,4},{6,5},{7,6},{8,15},{9,8},{10,9... | collective-permute-start | bytes 786440 | tf_op jit(solution)/shard_map/ppermute | solution.py:265
  33.1 0.0 collective-permute-done.1.refs_1_
  33.1 0.0 collective-permute-done.2.refs_0_
  33.1 0.0 collective-permute-done.3.refs_1_
  33.1 3.7 %collective-permute-done.5.refs_6_ = bf16[2,256,256]{2,1,0:T(8,128)(2,1)S(1)} collective-permute-done((bf16[2,256,256]{2,1,0:T(8,128)(2,1)S(1)}, bf16[2,256,256]{2,1,0:T(8,128)(2,1)S(1)}, u32[]{:S(2)}, u32[]{:S(2)}) %collective-permute-start.5) | collective-permute-done | bytes 262176 | tf_op jit(solution)/shard_map/ppermute | solution.py:262
  36.7 0.0 collective-permute-done.7.refs_2_
  36.7 3.0 %collective-permute-start.12 = (bf16[2,256,256]{2,1,0:T(8,128)(2,1)S(1)}, bf16[2,256,256]{2,1,0:T(8,128)(2,1)S(1)}, u32[]{:S(2)}, u32[]{:S(2)}) collective-permute-start(bf16[2,256,256]{2,1,0:T(8,128)(2,1)S(1)} %collective-permute-done.7.refs_2_), channel_id=1, source_target_pairs={{0,7},{1,0},{2,1},{3,2},{4,3},{5,4},{6,5},{7,6},{8,15},{9,8},{10,9... | collective-permute-start | bytes 786440 | tf_op jit(solution)/shard_map/ppermute | solution.py:265
  39.8 0.0 collective-permute-start.13
  39.8 0.1 shard_map.56.refs_0_
  39.9 1.6 %collective-permute-start.8 = (bf16[2,2,256,256]{3,2,1,0:T(8,128)(2,1)S(1)}, bf16[2,2,256,256]{3,2,1,0:T(8,128)(2,1)S(1)}, u32[]{:S(2)}, u32[]{:S(2)}) collective-permute-start(bf16[2,2,256,256]{3,2,1,0:T(8,128)(2,1)S(1)} %shard_map.56.refs_0_), channel_id=1, source_target_pairs={{0,64},{8,24},{16,80},{24,40},{32,96},{40,56},{48,112},{56,8},{64,... | collective-permute-start | bytes 1572872 | tf_op jit(solution)/shard_map/ppermute | solution.py:256
  41.5 1.1 collective-permute-start.9
  42.6 0.1 shard_map.57.refs_3_
  42.7 0.0 copy-start
  42.7 0.4 collective-permute-start.10
  43.1 0.1 collective-permute-done.12.refs_3_
  43.2 2.3 %collective-permute-start.11 = (bf16[2,2,256,256]{3,2,1,0:T(8,128)(2,1)S(1)}, bf16[2,2,256,256]{3,2,1,0:T(8,128)(2,1)S(1)}, u32[]{:S(2)}, u32[]{:S(2)}) collective-permute-start(bf16[2,2,256,256]{3,2,1,0:T(8,128)(2,1)S(1)} %shard_map.57.refs_3_), channel_id=1, source_target_pairs={{0,192},{8,56},{16,208},{24,8},{32,224},{40,24},{48,240},{56,40},{... | collective-permute-start | bytes 1572872 | tf_op jit(solution)/shard_map/ppermute | solution.py:256
  45.5 0.8 collective-permute-done.13.refs_5_
  46.2 3.2 %collective-permute-start.14 = (bf16[2,256,256]{2,1,0:T(8,128)(2,1)S(1)}, bf16[2,256,256]{2,1,0:T(8,128)(2,1)S(1)}, u32[]{:S(2)}, u32[]{:S(2)}) collective-permute-start(bf16[2,256,256]{2,1,0:T(8,128)(2,1)S(1)} %collective-permute-done.13.refs_5_), channel_id=1, source_target_pairs={{0,1},{1,2},{2,3},{3,4},{4,5},{5,6},{6,7},{7,0},{8,9},{9,10},{10,1... | collective-permute-start | bytes 786440 | tf_op jit(solution)/shard_map/ppermute | solution.py:262
  49.4 5.2 %collective-permute-done.14.refs_4_ = bf16[2,256,256]{2,1,0:T(8,128)(2,1)S(1)} collective-permute-done((bf16[2,256,256]{2,1,0:T(8,128)(2,1)S(1)}, bf16[2,256,256]{2,1,0:T(8,128)(2,1)S(1)}, u32[]{:S(2)}, u32[]{:S(2)}) %collective-permute-start.14) | collective-permute-done | bytes 262176 | tf_op jit(solution)/shard_map/ppermute | solution.py:262
  54.6 0.0 copy-start.2
  54.6 0.9 copy-done.2
  55.6 0.3 shard_map.58.refs_6_.refs_2_
  55.9 0.0 collective-permute-done.8.refs_1_
  55.9 0.0 collective-permute-done.9.refs_2_
  55.9 0.0 collective-permute-done.10.refs_4_
  55.9 0.0 collective-permute-done.11.refs_5_
  55.9 6.9 %collective-permute-start.15 = (bf16[9,2,256,256]{3,2,1,0:T(8,128)(2,1)S(1)}, bf16[9,2,256,256]{3,2,1,0:T(8,128)(2,1)S(1)}, u32[]{:S(2)}, u32[]{:S(2)}) collective-permute-start(bf16[9,2,256,256]{3,2,1,0:T(8,128)(2,1)S(1)} %shard_map.58.refs_6_.refs_2_), channel_id=1, source_target_pairs={{0,8},{8,0},{16,24},{24,16},{32,40},{40,32},{48,56},{56,48},{64,72... | collective-permute-start | bytes 7077896 | tf_op jit(solution)/shard_map/ppermute | solution.py:259
  62.8 0.0 collective-permute-start.16
  62.8 3.0 %collective-permute-start.17 = (bf16[2,2,256,256]{3,2,1,0:T(8,128)(2,1)S(1)}, bf16[2,2,256,256]{3,2,1,0:T(8,128)(2,1)S(1)}, u32[]{:S(2)}, u32[]{:S(2)}) collective-permute-start(bf16[2,2,256,256]{3,2,1,0:T(8,128)(2,1)S(1)} %collective-permute-done.11.refs_5_), channel_id=1, source_target_pairs={{0,192},{8,56},{16,208},{24,8},{32,224},{40,24},{48,240},{56,40},{... | collective-permute-start | bytes 1572872 | tf_op jit(solution)/shard_map/ppermute | solution.py:256
  65.8 0.0 copy-done
  65.8 3.7 %shard_map.59.mine = f32[2,256,256]{2,1,0:T(8,128)S(1)} custom-call(bf16[2,2,256,256]{3,2,1,0:T(8,128)(2,1)S(1)} %shard_map.56.refs_0_, bf16[2,2,256,256]{3,2,1,0:T(8,128)(2,1)S(1)} %collective-permute-done.8.refs_1_, bf16[2,2,256,256]{3,2,1,0:T(8,128)(2,1)S(1)} %collective-permute-done.9.refs_2_, bf16[2,2,256,256]{3,2,1,0:T(8,128)(2,1)S(1)} %shard_map.57.refs_3_, ...), custom_call_target="tpu_custom_call" | custom-call | tf_op jit(solution)/shard_map/pallas_call | solution.py:126
  69.5 0.0 copy-start.3
  69.5 0.0 copy-start.4
  69.6 0.0 collective-permute-done.15.refs_6_.refs_3_
  69.6 3.7 %shard_map.60.theirs = f32[2,256,256]{2,1,0:T(8,128)S(1)} custom-call(bf16[2,2,256,256]{3,2,1,0:T(8,128)(2,1)S(1)} %shard_map.56.refs_0_, bf16[2,2,256,256]{3,2,1,0:T(8,128)(2,1)S(1)} %collective-permute-done.8.refs_1_, bf16[2,2,256,256]{3,2,1,0:T(8,128)(2,1)S(1)} %collective-permute-done.9.refs_2_, bf16[2,2,256,256]{3,2,1,0:T(8,128)(2,1)S(1)} %shard_map.57.refs_3_, ...), custom_call_target="tpu_custom_call" | custom-call | tf_op jit(solution)/shard_map/pallas_call | solution.py:126
  73.3 0.0 collective-permute-done.16.refs_0_
  73.3 0.2 collective-permute-done.17.refs_1_
  73.5 0.0 copy-done.3
  73.5 0.0 copy-done.4
  73.5 2.6 %shard_map.61 = bf16[8,2,2,32,256]{4,3,2,1,0:T(8,128)(2,1)S(1)} custom-call(s32[32]{0:T(128)S(1)} %copy-done.3, s32[32]{0:T(128)S(1)} %copy-done.4, f32[2,256,256]{2,1,0:T(8,128)S(1)} %shard_map.59.mine, f32[2,256,256]{2,1,0:T(8,128)S(1)} %shard_map.60.theirs, bf16[2,2,256,256]{3,2,1,0:T(8,128)(2,1)S(1)} %collective-permute-done.16.refs_0_, ...), custom_call_target="tpu_custom_call" | custom-call | tf_op jit(solution)/shard_map/pallas_call | solution.py:195
  76.1 22.2 %all_to_all.10 = bf16[8,2,2,32,256]{4,3,2,1,0:T(8,128)(2,1)S(1)} all-to-all(bf16[8,2,2,32,256]{4,3,2,1,0:T(8,128)(2,1)S(1)} %shard_map.61), channel_id=1, replica_groups=mesh['blk'=32,'mpo'=8] {'mpo'}, dimensions={0} | all-to-all | bytes 1048576 | tf_op jit(solution)/shard_map/all_to_all | solution.py:300
  98.3 14.9 %all_to_all.11.in_ref = bf16[16,2,32,256]{3,2,1,0:T(8,128)(2,1)S(1)} all-to-all(bf16[16,2,32,256]{3,2,1,0:T(8,128)(2,1)S(1)} %bitcast.2), channel_id=1, replica_groups={{0,128,16,144,32,160,48,176,64,192,80,208,96,224,112,240},{72,200,88,21..., dimensions={0} | all-to-all | bytes 1048576 | tf_op jit(solution)/shard_map/all_to_all | solution.py:307
  113.2 0.9 shard_map.62
Async XLA Ops:
  0.0 2.8 %copy-start.5 = (bf16[2,256,256]{2,1,0:T(8,128)(2,1)S(1)}, bf16[2,256,256]{2,1,0:T(8,128)(2,1)}, u32[]{:S(2)}) copy-start(bf16[2,256,256]{2,1,0:T(8,128)(2,1)} %param.7) | copy-start | bytes 786436
  0.0 12.4 %copy-start.1 = (bf16[2,256,256]{2,1,0:T(8,128)(2,1)S(1)}, bf16[2,256,256]{2,1,0:T(8,128)(2,1)}, u32[]{:S(2)}) copy-start(bf16[2,256,256]{2,1,0:T(8,128)(2,1)} %refs_0_.1) | copy-start | bytes 786436
  2.8 13.3 %collective-permute-start = (bf16[2,256,256]{2,1,0:T(8,128)(2,1)S(1)}, bf16[2,256,256]{2,1,0:T(8,128)(2,1)S(1)}, u32[]{:S(2)}, u32[]{:S(2)}) collective-permute-start(bf16[2,256,256]{2,1,0:T(8,128)(2,1)S(1)} %copy-done.5), channel_id=1, source_target_pairs={{0,0},{1,16},{2,32},{3,48},{4,64},{5,80},{6,96},{7,112},{8,12},{9,... | collective-permute-start | bytes 786440 | tf_op jit(solution)/shard_map/ppermute | solution.py:278
  12.4 16.1 %collective-permute-start.4 = (bf16[2,256,256]{2,1,0:T(8,128)(2,1)S(1)}, bf16[2,256,256]{2,1,0:T(8,128)(2,1)S(1)}, u32[]{:S(2)}, u32[]{:S(2)}) collective-permute-start(bf16[2,256,256]{2,1,0:T(8,128)(2,1)S(1)} %copy-done.1), channel_id=1, source_target_pairs={{0,1},{1,2},{2,3},{3,4},{4,5},{5,6},{6,7},{7,0},{8,9},{9,10},{10,1... | collective-permute-start | bytes 786440 | tf_op jit(solution)/shard_map/ppermute | solution.py:262
  13.7 14.8 %collective-permute-start.6 = (bf16[2,256,256]{2,1,0:T(8,128)(2,1)S(1)}, bf16[2,256,256]{2,1,0:T(8,128)(2,1)S(1)}, u32[]{:S(2)}, u32[]{:S(2)}) collective-permute-start(bf16[2,256,256]{2,1,0:T(8,128)(2,1)S(1)} %copy-done.1), channel_id=1, source_target_pairs={{0,7},{1,0},{2,1},{3,2},{4,3},{5,4},{6,5},{7,6},{8,15},{9,8},{10,9... | collective-permute-start | bytes 786440 | tf_op jit(solution)/shard_map/ppermute | solution.py:265
  16.1 17.0 %collective-permute-start.1 = (bf16[2,256,256]{2,1,0:T(8,128)(2,1)S(1)}, bf16[2,256,256]{2,1,0:T(8,128)(2,1)S(1)}, u32[]{:S(2)}, u32[]{:S(2)}) collective-permute-start(bf16[2,256,256]{2,1,0:T(8,128)(2,1)S(1)} %collective-permute-done.refs_0_), channel_id=1, source_target_pairs={{0,16},{8,72},{16,32},{24,88},{32,48},{40,104},{48,0},{56,120},{64... | collective-permute-start | bytes 786440 | tf_op jit(solution)/shard_map/ppermute | solution.py:253
  17.9 15.2 %collective-permute-start.2 = (bf16[2,256,256]{2,1,0:T(8,128)(2,1)S(1)}, bf16[2,256,256]{2,1,0:T(8,128)(2,1)S(1)}, u32[]{:S(2)}, u32[]{:S(2)}) collective-permute-start(bf16[2,256,256]{2,1,0:T(8,128)(2,1)S(1)} %collective-permute-done.refs_0_), channel_id=1, source_target_pairs={{0,48},{8,200},{16,0},{24,216},{32,16},{40,232},{48,32},{56,248},{... | collective-permute-start | bytes 786440 | tf_op jit(solution)/shard_map/ppermute | solution.py:253
  19.4 13.7 %collective-permute-start.3 = (bf16[2,256,256]{2,1,0:T(8,128)(2,1)S(1)}, bf16[2,256,256]{2,1,0:T(8,128)(2,1)S(1)}, u32[]{:S(2)}, u32[]{:S(2)}) collective-permute-start(bf16[2,256,256]{2,1,0:T(8,128)(2,1)S(1)} %collective-permute-done.refs_0_), channel_id=1, source_target_pairs={{0,32},{8,136},{16,48},{24,152},{32,0},{40,168},{48,16},{56,184},{... | collective-permute-start | bytes 786440 | tf_op jit(solution)/shard_map/ppermute | solution.py:253
  28.5 8.2 %collective-permute-start.5 = (bf16[2,256,256]{2,1,0:T(8,128)(2,1)S(1)}, bf16[2,256,256]{2,1,0:T(8,128)(2,1)S(1)}, u32[]{:S(2)}, u32[]{:S(2)}) collective-permute-start(bf16[2,256,256]{2,1,0:T(8,128)(2,1)S(1)} %collective-permute-done.4.refs_7_), channel_id=1, source_target_pairs={{0,1},{1,2},{2,3},{3,4},{4,5},{5,6},{6,7},{7,0},{8,9},{9,10},{10,1... | collective-permute-start | bytes 786440 | tf_op jit(solution)/shard_map/ppermute | solution.py:262
  28.5 8.2 %collective-permute-start.7 = (bf16[2,256,256]{2,1,0:T(8,128)(2,1)S(1)}, bf16[2,256,256]{2,1,0:T(8,128)(2,1)S(1)}, u32[]{:S(2)}, u32[]{:S(2)}) collective-permute-start(bf16[2,256,256]{2,1,0:T(8,128)(2,1)S(1)} %collective-permute-done.6.refs_1_), channel_id=1, source_target_pairs={{0,7},{1,0},{2,1},{3,2},{4,3},{5,4},{6,5},{7,6},{8,15},{9,8},{10,9... | collective-permute-start | bytes 786440 | tf_op jit(solution)/shard_map/ppermute | solution.py:265
  36.7 6.4 %collective-permute-start.12 = (bf16[2,256,256]{2,1,0:T(8,128)(2,1)S(1)}, bf16[2,256,256]{2,1,0:T(8,128)(2,1)S(1)}, u32[]{:S(2)}, u32[]{:S(2)}) collective-permute-start(bf16[2,256,256]{2,1,0:T(8,128)(2,1)S(1)} %collective-permute-done.7.refs_2_), channel_id=1, source_target_pairs={{0,7},{1,0},{2,1},{3,2},{4,3},{5,4},{6,5},{7,6},{8,15},{9,8},{10,9... | collective-permute-start | bytes 786440 | tf_op jit(solution)/shard_map/ppermute | solution.py:265
  39.8 6.4 %collective-permute-start.13 = (bf16[2,256,256]{2,1,0:T(8,128)(2,1)S(1)}, bf16[2,256,256]{2,1,0:T(8,128)(2,1)S(1)}, u32[]{:S(2)}, u32[]{:S(2)}) collective-permute-start(bf16[2,256,256]{2,1,0:T(8,128)(2,1)S(1)} %collective-permute-done.5.refs_6_), channel_id=1, source_target_pairs={{0,1},{1,2},{2,3},{3,4},{4,5},{5,6},{6,7},{7,0},{8,9},{9,10},{10,1... | collective-permute-start | bytes 786440 | tf_op jit(solution)/shard_map/ppermute | solution.py:262
  39.9 16.0 %collective-permute-start.8 = (bf16[2,2,256,256]{3,2,1,0:T(8,128)(2,1)S(1)}, bf16[2,2,256,256]{3,2,1,0:T(8,128)(2,1)S(1)}, u32[]{:S(2)}, u32[]{:S(2)}) collective-permute-start(bf16[2,2,256,256]{3,2,1,0:T(8,128)(2,1)S(1)} %shard_map.56.refs_0_), channel_id=1, source_target_pairs={{0,64},{8,24},{16,80},{24,40},{32,96},{40,56},{48,112},{56,8},{64,... | collective-permute-start | bytes 1572872 | tf_op jit(solution)/shard_map/ppermute | solution.py:256
  41.5 14.4 %collective-permute-start.9 = (bf16[2,2,256,256]{3,2,1,0:T(8,128)(2,1)S(1)}, bf16[2,2,256,256]{3,2,1,0:T(8,128)(2,1)S(1)}, u32[]{:S(2)}, u32[]{:S(2)}) collective-permute-start(bf16[2,2,256,256]{3,2,1,0:T(8,128)(2,1)S(1)} %shard_map.56.refs_0_), channel_id=1, source_target_pairs={{0,192},{8,56},{16,208},{24,8},{32,224},{40,24},{48,240},{56,40},{... | collective-permute-start | bytes 1572872 | tf_op jit(solution)/shard_map/ppermute | solution.py:256
  42.7 23.2 %copy-start = (bf16[2,256,256]{2,1,0:T(8,128)(2,1)S(1)}, bf16[2,256,256]{2,1,0:T(8,128)(2,1)}, u32[]{:S(2)}) copy-start(bf16[2,256,256]{2,1,0:T(8,128)(2,1)} %get-tuple-element.34.refs_7_.refs_4_) | copy-start | bytes 786436
  42.7 13.2 %collective-permute-start.10 = (bf16[2,2,256,256]{3,2,1,0:T(8,128)(2,1)S(1)}, bf16[2,2,256,256]{3,2,1,0:T(8,128)(2,1)S(1)}, u32[]{:S(2)}, u32[]{:S(2)}) collective-permute-start(bf16[2,2,256,256]{3,2,1,0:T(8,128)(2,1)S(1)} %shard_map.57.refs_3_), channel_id=1, source_target_pairs={{0,64},{8,24},{16,80},{24,40},{32,96},{40,56},{48,112},{56,8},{64,... | collective-permute-start | bytes 1572872 | tf_op jit(solution)/shard_map/ppermute | solution.py:256
  43.2 12.7 %collective-permute-start.11 = (bf16[2,2,256,256]{3,2,1,0:T(8,128)(2,1)S(1)}, bf16[2,2,256,256]{3,2,1,0:T(8,128)(2,1)S(1)}, u32[]{:S(2)}, u32[]{:S(2)}) collective-permute-start(bf16[2,2,256,256]{3,2,1,0:T(8,128)(2,1)S(1)} %shard_map.57.refs_3_), channel_id=1, source_target_pairs={{0,192},{8,56},{16,208},{24,8},{32,224},{40,24},{48,240},{56,40},{... | collective-permute-start | bytes 1572872 | tf_op jit(solution)/shard_map/ppermute | solution.py:256
  46.2 8.4 %collective-permute-start.14 = (bf16[2,256,256]{2,1,0:T(8,128)(2,1)S(1)}, bf16[2,256,256]{2,1,0:T(8,128)(2,1)S(1)}, u32[]{:S(2)}, u32[]{:S(2)}) collective-permute-start(bf16[2,256,256]{2,1,0:T(8,128)(2,1)S(1)} %collective-permute-done.13.refs_5_), channel_id=1, source_target_pairs={{0,1},{1,2},{2,3},{3,4},{4,5},{5,6},{6,7},{7,0},{8,9},{9,10},{10,1... | collective-permute-start | bytes 786440 | tf_op jit(solution)/shard_map/ppermute | solution.py:262
  54.6 1.0 copy-start.2
  55.9 13.7 %collective-permute-start.15 = (bf16[9,2,256,256]{3,2,1,0:T(8,128)(2,1)S(1)}, bf16[9,2,256,256]{3,2,1,0:T(8,128)(2,1)S(1)}, u32[]{:S(2)}, u32[]{:S(2)}) collective-permute-start(bf16[9,2,256,256]{3,2,1,0:T(8,128)(2,1)S(1)} %shard_map.58.refs_6_.refs_2_), channel_id=1, source_target_pairs={{0,8},{8,0},{16,24},{24,16},{32,40},{40,32},{48,56},{56,48},{64,72... | collective-permute-start | bytes 7077896 | tf_op jit(solution)/shard_map/ppermute | solution.py:259
  62.8 10.5 %collective-permute-start.16 = (bf16[2,2,256,256]{3,2,1,0:T(8,128)(2,1)S(1)}, bf16[2,2,256,256]{3,2,1,0:T(8,128)(2,1)S(1)}, u32[]{:S(2)}, u32[]{:S(2)}) collective-permute-start(bf16[2,2,256,256]{3,2,1,0:T(8,128)(2,1)S(1)} %collective-permute-done.8.refs_1_), channel_id=1, source_target_pairs={{0,64},{8,24},{16,80},{24,40},{32,96},{40,56},{48,112},{56,8},{64,... | collective-permute-start | bytes 1572872 | tf_op jit(solution)/shard_map/ppermute | solution.py:256
  62.8 10.7 %collective-permute-start.17 = (bf16[2,2,256,256]{3,2,1,0:T(8,128)(2,1)S(1)}, bf16[2,2,256,256]{3,2,1,0:T(8,128)(2,1)S(1)}, u32[]{:S(2)}, u32[]{:S(2)}) collective-permute-start(bf16[2,2,256,256]{3,2,1,0:T(8,128)(2,1)S(1)} %collective-permute-done.11.refs_5_), channel_id=1, source_target_pairs={{0,192},{8,56},{16,208},{24,8},{32,224},{40,24},{48,240},{56,40},{... | collective-permute-start | bytes 1572872 | tf_op jit(solution)/shard_map/ppermute | solution.py:256
  69.5 4.0 %copy-start.3 = (s32[32]{0:T(128)S(1)}, s32[32]{0:T(128)}, u32[]{:S(2)}) copy-start(s32[32]{0:T(128)} %left_sizes.3) | copy-start | bytes 388
  69.5 4.0 %copy-start.4 = (s32[32]{0:T(128)S(1)}, s32[32]{0:T(128)}, u32[]{:S(2)}) copy-start(s32[32]{0:T(128)} %right_sizes.3) | copy-start | bytes 388

commit v19 on v18

--- a/solution.py
+++ b/solution.py
@@ -279,12 +279,12 @@
     up2, down2 = up(up1), down(down1)
 
     below, above, two = near_step(own, 1), near_step(own, -1), near_step(own, 2)
-    below, above, two, up2, down2 = together(below, above, two, up2, down2)
+    up3 = up(up2)
+    below, above, two, up3, down2 = together(below, above, two, up3, down2)
     line_a, line_b = stack(own, below), stack(above, two)
     a_below, a_above = far_step(line_a, 1), far_step(line_a, -1)
     b_below, b_above = far_step(line_b, 1), far_step(line_b, -1)
-    up3, down3 = up(up2), down(down2)
-    up4 = up(up3)
+    up4, down3 = up(up3), down(down2)
     lefts = stack(left_env, down1, down2, down3, up4, up3, up2, up1, give)
     a_below, a_above, b_below, b_above, lefts = together(a_below, a_above, b_below, b_above, lefts)
     a_two, b_two = far_step(a_below, 1), far_step(b_above, -1)

time: 116 us -> 116 us (level)
  starting transfers between devices: 43.9 us -> 39.3 us
  blocking collectives: 37.1 us -> 40.7 us
  waiting for transfers between devices: 17.9 us -> 19.6 us
    ppermute x4, waiting for transfers between devices: 17.6 us -> 8.7 us  [up(): lax.ppermute(block, 'mpo', [(z, (z + 1) % ranks) for z in range(ranks)])]
    ppermute x3, waiting for transfers between devices: 0.06 us -> 6.85 us  [down(): lax.ppermute(block, 'mpo', [(z, (z - 1) % ranks) for z in range(ranks)])]
    ppermute x1, starting transfers between devices: 6.92 us -> 2.68 us  [swap(): return lax.ppermute(block, 'blk', [(i, i ^ 1) for i in range(sectors)])]
    ppermute x6, waiting for transfers between devices: 0.22 us -> 3.15 us  [far_step(): return lax.ppermute(block, 'blk', step(True, by))]
    all_to_all x1, blocking collectives: 22.2 us -> 24.1 us  [local(): by_plane = lax.all_to_all(done, 'mpo', 0, 0)]
    ppermute x1, starting transfers between devices: 9.65 us -> 7.92 us  [local(): own = lax.ppermute(right_env, ('blk', 'mpo'), turn)]
    all_to_all x1, blocking collectives: 14.9 us -> 16.5 us  [local(): out = order(lax.all_to_all(by_plane, 'blk', 0, 0, axis_index_groups=groups))]
  transfers between devices with their start and end apart: 18 -> 18, of which waited for: 6 -> 7; matrix products, arithmetic and copies ran while one was open for 0% -> 0% of each run, Pallas kernels for 7% -> 9%
where the time goes in v19:
time: 116 us; the launch traced here: 115 us
  blocking collectives  40.7 us (35%)
  starting transfers between devices  39.3 us (34%)
  waiting for transfers between devices  19.6 us (17%)
  Pallas kernels  13.9 us (12%)
    all_to_all x1, blocking collectives, local(): by_plane = lax.all_to_all(done, 'mpo', 0, 0)  24.1 us
    all_to_all x1, blocking collectives, local(): out = order(lax.all_to_all(by_plane, 'blk', 0, 0, axis_index_groups=groups))  16.5 us
    ppermute x3, starting transfers between devices, down(): lax.ppermute(block, 'mpo', [(z, (z - 1) % ranks) for z in range(ranks)])  10.9 us
    ppermute x6, starting transfers between devices, far_step(): return lax.ppermute(block, 'blk', step(True, by))  9.26 us
    ppermute x4, waiting for transfers between devices, up(): lax.ppermute(block, 'mpo', [(z, (z + 1) % ranks) for z in range(ranks)])  8.7 us
    ppermute x1, starting transfers between devices, local(): own = lax.ppermute(right_env, ('blk', 'mpo'), turn)  7.92 us
    pallas_call x2, Pallas kernels, half(): pl.pallas_call(functools.partial(half_kernel, pieces), out_shape=jax.Shap...  7.38 us
    ppermute x3, waiting for transfers between devices, down(): lax.ppermute(block, 'mpo', [(z, (z - 1) % ranks) for z in range(ranks)])  6.85 us
  transfers between devices with their start and end apart: 18, of which 7 were waited for; matrix products, arithmetic and copies ran while one was open for 0% of the time, Pallas kernels for 9%

profile of v19, /device:TPU:1, one launch (start us, length us, event | category | flops | bytes accessed | tf_op | source)
XLA Modules:
  0.0 114.8 jit_solution(15842119212332531318)
XLA Ops:
  0.0 0.0 copy-start.1
  0.0 0.0 copy-start.5
  0.0 2.5 %collective-permute-start.4 = (bf16[2,256,256]{2,1,0:T(8,128)(2,1)}, bf16[2,256,256]{2,1,0:T(8,128)(2,1)S(1)}, u32[]{:S(2)}, u32[]{:S(2)}) collective-permute-start(bf16[2,256,256]{2,1,0:T(8,128)(2,1)} %refs_0_.1), channel_id=1, source_target_pairs={{0,1},{1,2},{2,3},{3,4},{4,5},{5,6},{6,7},{7,0},{8,9},{9,10},{10,1... | collective-permute-start | bytes 786440 | tf_op jit(solution)/shard_map/ppermute | solution.py:262
  2.5 2.6 %shard_map.55 = (bf16[2,256,256]{2,1,0:T(8,128)(2,1)}, bf16[2,256,256]{2,1,0:T(8,128)(2,1)}) custom-call(s32[32]{0:T(128)} %left_sizes.3, s32[32]{0:T(128)} %right_sizes.3, bf16[256,8192]{1,0:T(8,128)(2,1)} %psi_ref.1), custom_call_target="tpu_custom_call" | custom-call | tf_op jit(solution)/shard_map/pallas_call | solution.py:76
  5.1 0.0 copy-done.5
  5.1 7.9 %collective-permute-start = (bf16[2,256,256]{2,1,0:T(8,128)(2,1)S(1)}, bf16[2,256,256]{2,1,0:T(8,128)(2,1)S(1)}, u32[]{:S(2)}, u32[]{:S(2)}) collective-permute-start(bf16[2,256,256]{2,1,0:T(8,128)(2,1)S(1)} %copy-done.5), channel_id=1, source_target_pairs={{0,0},{1,16},{2,32},{3,48},{4,64},{5,80},{6,96},{7,112},{8,12},{9,... | collective-permute-start | bytes 786440 | tf_op jit(solution)/shard_map/ppermute | solution.py:278
  13.0 0.0 copy-done.1
  13.1 3.6 %collective-permute-start.7 = (bf16[2,256,256]{2,1,0:T(8,128)(2,1)S(1)}, bf16[2,256,256]{2,1,0:T(8,128)(2,1)S(1)}, u32[]{:S(2)}, u32[]{:S(2)}) collective-permute-start(bf16[2,256,256]{2,1,0:T(8,128)(2,1)S(1)} %copy-done.1), channel_id=1, source_target_pairs={{0,7},{1,0},{2,1},{3,2},{4,3},{5,4},{6,5},{7,6},{8,15},{9,8},{10,9... | collective-permute-start | bytes 786440 | tf_op jit(solution)/shard_map/ppermute | solution.py:265
  16.6 0.0 collective-permute-done.4.refs_7_
  16.6 0.0 collective-permute-start.5
  16.6 0.9 collective-permute-done.refs_0_
  17.5 2.2 %collective-permute-start.1 = (bf16[2,256,256]{2,1,0:T(8,128)(2,1)S(1)}, bf16[2,256,256]{2,1,0:T(8,128)(2,1)S(1)}, u32[]{:S(2)}, u32[]{:S(2)}) collective-permute-start(bf16[2,256,256]{2,1,0:T(8,128)(2,1)S(1)} %collective-permute-done.refs_0_), channel_id=1, source_target_pairs={{0,16},{8,72},{16,32},{24,88},{32,48},{40,104},{48,0},{56,120},{64... | collective-permute-start | bytes 786440 | tf_op jit(solution)/shard_map/ppermute | solution.py:253
  19.7 1.4 %collective-permute-start.2 = (bf16[2,256,256]{2,1,0:T(8,128)(2,1)S(1)}, bf16[2,256,256]{2,1,0:T(8,128)(2,1)S(1)}, u32[]{:S(2)}, u32[]{:S(2)}) collective-permute-start(bf16[2,256,256]{2,1,0:T(8,128)(2,1)S(1)} %collective-permute-done.refs_0_), channel_id=1, source_target_pairs={{0,48},{8,200},{16,0},{24,216},{32,16},{40,232},{48,32},{56,248},{... | collective-permute-start | bytes 786440 | tf_op jit(solution)/shard_map/ppermute | solution.py:253
  21.1 1.2 %collective-permute-start.3 = (bf16[2,256,256]{2,1,0:T(8,128)(2,1)S(1)}, bf16[2,256,256]{2,1,0:T(8,128)(2,1)S(1)}, u32[]{:S(2)}, u32[]{:S(2)}) collective-permute-start(bf16[2,256,256]{2,1,0:T(8,128)(2,1)S(1)} %collective-permute-done.refs_0_), channel_id=1, source_target_pairs={{0,32},{8,136},{16,48},{24,152},{32,0},{40,168},{48,16},{56,184},{... | collective-permute-start | bytes 786440 | tf_op jit(solution)/shard_map/ppermute | solution.py:253
  22.3 3.6 %collective-permute-done.7.refs_1_ = bf16[2,256,256]{2,1,0:T(8,128)(2,1)S(1)} collective-permute-done((bf16[2,256,256]{2,1,0:T(8,128)(2,1)S(1)}, bf16[2,256,256]{2,1,0:T(8,128)(2,1)S(1)}, u32[]{:S(2)}, u32[]{:S(2)}) %collective-permute-start.7) | collective-permute-done | bytes 262176 | tf_op jit(solution)/shard_map/ppermute | solution.py:265
  25.9 7.1 %collective-permute-start.8 = (bf16[2,256,256]{2,1,0:T(8,128)(2,1)S(1)}, bf16[2,256,256]{2,1,0:T(8,128)(2,1)S(1)}, u32[]{:S(2)}, u32[]{:S(2)}) collective-permute-start(bf16[2,256,256]{2,1,0:T(8,128)(2,1)S(1)} %collective-permute-done.7.refs_1_), channel_id=1, source_target_pairs={{0,7},{1,0},{2,1},{3,2},{4,3},{5,4},{6,5},{7,6},{8,15},{9,8},{10,9... | collective-permute-start | bytes 786440 | tf_op jit(solution)/shard_map/ppermute | solution.py:265
  33.0 0.0 collective-permute-done.5.refs_6_
  33.0 0.0 collective-permute-start.6
  33.0 0.0 collective-permute-done.1.refs_1_
  33.0 0.0 collective-permute-done.2.refs_0_
  33.0 0.0 collective-permute-done.3.refs_1_
  33.0 3.3 %collective-permute-done.8.refs_2_ = bf16[2,256,256]{2,1,0:T(8,128)(2,1)S(1)} collective-permute-done((bf16[2,256,256]{2,1,0:T(8,128)(2,1)S(1)}, bf16[2,256,256]{2,1,0:T(8,128)(2,1)S(1)}, u32[]{:S(2)}, u32[]{:S(2)}) %collective-permute-start.8) | collective-permute-done | bytes 262176 | tf_op jit(solution)/shard_map/ppermute | solution.py:265
  36.3 3.1 %collective-permute-done.6.refs_5_ = bf16[2,256,256]{2,1,0:T(8,128)(2,1)S(1)} collective-permute-done((bf16[2,256,256]{2,1,0:T(8,128)(2,1)S(1)}, bf16[2,256,256]{2,1,0:T(8,128)(2,1)S(1)}, u32[]{:S(2)}, u32[]{:S(2)}) %collective-permute-start.6) | collective-permute-done | bytes 262176 | tf_op jit(solution)/shard_map/ppermute | solution.py:262
  39.4 0.3 collective-permute-start.13
  39.7 0.1 shard_map.56.refs_0_
  39.8 3.8 %collective-permute-start.9 = (bf16[2,2,256,256]{3,2,1,0:T(8,128)(2,1)S(1)}, bf16[2,2,256,256]{3,2,1,0:T(8,128)(2,1)S(1)}, u32[]{:S(2)}, u32[]{:S(2)}) collective-permute-start(bf16[2,2,256,256]{3,2,1,0:T(8,128)(2,1)S(1)} %shard_map.56.refs_0_), channel_id=1, source_target_pairs={{0,64},{8,24},{16,80},{24,40},{32,96},{40,56},{48,112},{56,8},{64,... | collective-permute-start | bytes 1572872 | tf_op jit(solution)/shard_map/ppermute | solution.py:256
  43.6 0.0 collective-permute-start.10
  43.6 0.1 shard_map.57.refs_3_
  43.7 0.0 copy-start
  43.7 1.5 %collective-permute-start.11 = (bf16[2,2,256,256]{3,2,1,0:T(8,128)(2,1)S(1)}, bf16[2,2,256,256]{3,2,1,0:T(8,128)(2,1)S(1)}, u32[]{:S(2)}, u32[]{:S(2)}) collective-permute-start(bf16[2,2,256,256]{3,2,1,0:T(8,128)(2,1)S(1)} %shard_map.57.refs_3_), channel_id=1, source_target_pairs={{0,64},{8,24},{16,80},{24,40},{32,96},{40,56},{48,112},{56,8},{64,... | collective-permute-start | bytes 1572872 | tf_op jit(solution)/shard_map/ppermute | solution.py:256
  45.2 1.2 %collective-permute-start.12 = (bf16[2,2,256,256]{3,2,1,0:T(8,128)(2,1)S(1)}, bf16[2,2,256,256]{3,2,1,0:T(8,128)(2,1)S(1)}, u32[]{:S(2)}, u32[]{:S(2)}) collective-permute-start(bf16[2,2,256,256]{3,2,1,0:T(8,128)(2,1)S(1)} %shard_map.57.refs_3_), channel_id=1, source_target_pairs={{0,192},{8,56},{16,208},{24,8},{32,224},{40,24},{48,240},{56,40},{... | collective-permute-start | bytes 1572872 | tf_op jit(solution)/shard_map/ppermute | solution.py:256
  46.4 0.0 collective-permute-done.13.refs_3_
  46.4 1.1 %collective-permute-start.14 = (bf16[2,256,256]{2,1,0:T(8,128)(2,1)S(1)}, bf16[2,256,256]{2,1,0:T(8,128)(2,1)S(1)}, u32[]{:S(2)}, u32[]{:S(2)}) collective-permute-start(bf16[2,256,256]{2,1,0:T(8,128)(2,1)S(1)} %collective-permute-done.6.refs_5_), channel_id=1, source_target_pairs={{0,1},{1,2},{2,3},{3,4},{4,5},{5,6},{6,7},{7,0},{8,9},{9,10},{10,1... | collective-permute-start | bytes 786440 | tf_op jit(solution)/shard_map/ppermute | solution.py:262
  47.6 5.6 %collective-permute-done.14.refs_4_ = bf16[2,256,256]{2,1,0:T(8,128)(2,1)S(1)} collective-permute-done((bf16[2,256,256]{2,1,0:T(8,128)(2,1)S(1)}, bf16[2,256,256]{2,1,0:T(8,128)(2,1)S(1)}, u32[]{:S(2)}, u32[]{:S(2)}) %collective-permute-start.14) | collective-permute-done | bytes 262176 | tf_op jit(solution)/shard_map/ppermute | solution.py:262
  53.2 0.0 copy-start.2
  53.2 0.9 copy-done.2
  54.1 0.3 shard_map.58.refs_6_.refs_2_
  54.4 0.0 collective-permute-done.9.refs_1_
  54.4 0.0 collective-permute-done.10.refs_2_
  54.4 0.9 collective-permute-done.11.refs_4_
  55.3 2.2 %collective-permute-done.12.refs_5_ = bf16[2,2,256,256]{3,2,1,0:T(8,128)(2,1)S(1)} collective-permute-done((bf16[2,2,256,256]{3,2,1,0:T(8,128)(2,1)S(1)}, bf16[2,2,256,256]{3,2,1,0:T(8,128)(2,1)S(1)}, u32[]{:S(2)}, u32[]{:S(2)}) %collective-permute-start.12) | collective-permute-done | bytes 524320 | tf_op jit(solution)/shard_map/ppermute | solution.py:256
  57.5 2.7 %collective-permute-start.15 = (bf16[9,2,256,256]{3,2,1,0:T(8,128)(2,1)S(1)}, bf16[9,2,256,256]{3,2,1,0:T(8,128)(2,1)S(1)}, u32[]{:S(2)}, u32[]{:S(2)}) collective-permute-start(bf16[9,2,256,256]{3,2,1,0:T(8,128)(2,1)S(1)} %shard_map.58.refs_6_.refs_2_), channel_id=1, source_target_pairs={{0,8},{8,0},{16,24},{24,16},{32,40},{40,32},{48,56},{56,48},{64,72... | collective-permute-start | bytes 7077896 | tf_op jit(solution)/shard_map/ppermute | solution.py:259
  60.2 0.8 collective-permute-start.16
  61.1 1.8 %collective-permute-start.17 = (bf16[2,2,256,256]{3,2,1,0:T(8,128)(2,1)S(1)}, bf16[2,2,256,256]{3,2,1,0:T(8,128)(2,1)S(1)}, u32[]{:S(2)}, u32[]{:S(2)}) collective-permute-start(bf16[2,2,256,256]{3,2,1,0:T(8,128)(2,1)S(1)} %collective-permute-done.12.refs_5_), channel_id=1, source_target_pairs={{0,192},{8,56},{16,208},{24,8},{32,224},{40,24},{48,240},{56,40},{... | collective-permute-start | bytes 1572872 | tf_op jit(solution)/shard_map/ppermute | solution.py:256
  62.9 0.0 copy-done
  62.9 3.7 %shard_map.59.mine = f32[2,256,256]{2,1,0:T(8,128)S(1)} custom-call(bf16[2,2,256,256]{3,2,1,0:T(8,128)(2,1)S(1)} %shard_map.56.refs_0_, bf16[2,2,256,256]{3,2,1,0:T(8,128)(2,1)S(1)} %collective-permute-done.9.refs_1_, bf16[2,2,256,256]{3,2,1,0:T(8,128)(2,1)S(1)} %collective-permute-done.10.refs_2_, bf16[2,2,256,256]{3,2,1,0:T(8,128)(2,1)S(1)} %shard_map.57.refs_3_, ...), custom_call_target="tpu_custom_call" | custom-call | tf_op jit(solution)/shard_map/pallas_call | solution.py:126
  66.6 0.0 copy-start.3
  66.6 0.0 copy-start.4
  66.6 0.0 collective-permute-done.15.refs_6_.refs_3_
  66.6 3.7 %shard_map.60.theirs = f32[2,256,256]{2,1,0:T(8,128)S(1)} custom-call(bf16[2,2,256,256]{3,2,1,0:T(8,128)(2,1)S(1)} %shard_map.56.refs_0_, bf16[2,2,256,256]{3,2,1,0:T(8,128)(2,1)S(1)} %collective-permute-done.9.refs_1_, bf16[2,2,256,256]{3,2,1,0:T(8,128)(2,1)S(1)} %collective-permute-done.10.refs_2_, bf16[2,2,256,256]{3,2,1,0:T(8,128)(2,1)S(1)} %shard_map.57.refs_3_, ...), custom_call_target="tpu_custom_call" | custom-call | tf_op jit(solution)/shard_map/pallas_call | solution.py:126
  70.3 0.0 collective-permute-done.16.refs_0_
  70.4 0.0 collective-permute-done.17.refs_1_
  70.4 0.0 copy-done.3
  70.4 0.0 copy-done.4
  70.4 2.6 %shard_map.61 = bf16[8,2,2,32,256]{4,3,2,1,0:T(8,128)(2,1)S(1)} custom-call(s32[32]{0:T(128)S(1)} %copy-done.3, s32[32]{0:T(128)S(1)} %copy-done.4, f32[2,256,256]{2,1,0:T(8,128)S(1)} %shard_map.59.mine, f32[2,256,256]{2,1,0:T(8,128)S(1)} %shard_map.60.theirs, bf16[2,2,256,256]{3,2,1,0:T(8,128)(2,1)S(1)} %collective-permute-done.16.refs_0_, ...), custom_call_target="tpu_custom_call" | custom-call | tf_op jit(solution)/shard_map/pallas_call | solution.py:195
  73.0 24.1 %all_to_all.10 = bf16[8,2,2,32,256]{4,3,2,1,0:T(8,128)(2,1)S(1)} all-to-all(bf16[8,2,2,32,256]{4,3,2,1,0:T(8,128)(2,1)S(1)} %shard_map.61), channel_id=1, replica_groups=mesh['blk'=32,'mpo'=8] {'mpo'}, dimensions={0} | all-to-all | bytes 1048576 | tf_op jit(solution)/shard_map/all_to_all | solution.py:300
  97.1 16.5 %all_to_all.11.in_ref = bf16[16,2,32,256]{3,2,1,0:T(8,128)(2,1)S(1)} all-to-all(bf16[16,2,32,256]{3,2,1,0:T(8,128)(2,1)S(1)} %bitcast.2), channel_id=1, replica_groups={{0,128,16,144,32,160,48,176,64,192,80,208,96,224,112,240},{72,200,88,21..., dimensions={0} | all-to-all | bytes 1048576 | tf_op jit(solution)/shard_map/all_to_all | solution.py:307
  113.7 0.9 shard_map.62
Async XLA Ops:
  0.0 13.0 %copy-start.1 = (bf16[2,256,256]{2,1,0:T(8,128)(2,1)S(1)}, bf16[2,256,256]{2,1,0:T(8,128)(2,1)}, u32[]{:S(2)}) copy-start(bf16[2,256,256]{2,1,0:T(8,128)(2,1)} %refs_0_.1) | copy-start | bytes 786436
  0.0 5.1 %copy-start.5 = (bf16[2,256,256]{2,1,0:T(8,128)(2,1)S(1)}, bf16[2,256,256]{2,1,0:T(8,128)(2,1)}, u32[]{:S(2)}) copy-start(bf16[2,256,256]{2,1,0:T(8,128)(2,1)} %param.7) | copy-start | bytes 786436
  0.0 16.6 %collective-permute-start.4 = (bf16[2,256,256]{2,1,0:T(8,128)(2,1)}, bf16[2,256,256]{2,1,0:T(8,128)(2,1)S(1)}, u32[]{:S(2)}, u32[]{:S(2)}) collective-permute-start(bf16[2,256,256]{2,1,0:T(8,128)(2,1)} %refs_0_.1), channel_id=1, source_target_pairs={{0,1},{1,2},{2,3},{3,4},{4,5},{5,6},{6,7},{7,0},{8,9},{9,10},{10,1... | collective-permute-start | bytes 786440 | tf_op jit(solution)/shard_map/ppermute | solution.py:262
  5.1 12.4 %collective-permute-start = (bf16[2,256,256]{2,1,0:T(8,128)(2,1)S(1)}, bf16[2,256,256]{2,1,0:T(8,128)(2,1)S(1)}, u32[]{:S(2)}, u32[]{:S(2)}) collective-permute-start(bf16[2,256,256]{2,1,0:T(8,128)(2,1)S(1)} %copy-done.5), channel_id=1, source_target_pairs={{0,0},{1,16},{2,32},{3,48},{4,64},{5,80},{6,96},{7,112},{8,12},{9,... | collective-permute-start | bytes 786440 | tf_op jit(solution)/shard_map/ppermute | solution.py:278
  13.1 12.8 %collective-permute-start.7 = (bf16[2,256,256]{2,1,0:T(8,128)(2,1)S(1)}, bf16[2,256,256]{2,1,0:T(8,128)(2,1)S(1)}, u32[]{:S(2)}, u32[]{:S(2)}) collective-permute-start(bf16[2,256,256]{2,1,0:T(8,128)(2,1)S(1)} %copy-done.1), channel_id=1, source_target_pairs={{0,7},{1,0},{2,1},{3,2},{4,3},{5,4},{6,5},{7,6},{8,15},{9,8},{10,9... | collective-permute-start | bytes 786440 | tf_op jit(solution)/shard_map/ppermute | solution.py:265
  16.6 16.4 %collective-permute-start.5 = (bf16[2,256,256]{2,1,0:T(8,128)(2,1)S(1)}, bf16[2,256,256]{2,1,0:T(8,128)(2,1)S(1)}, u32[]{:S(2)}, u32[]{:S(2)}) collective-permute-start(bf16[2,256,256]{2,1,0:T(8,128)(2,1)S(1)} %collective-permute-done.4.refs_7_), channel_id=1, source_target_pairs={{0,1},{1,2},{2,3},{3,4},{4,5},{5,6},{6,7},{7,0},{8,9},{9,10},{10,1... | collective-permute-start | bytes 786440 | tf_op jit(solution)/shard_map/ppermute | solution.py:262
  17.5 15.5 %collective-permute-start.1 = (bf16[2,256,256]{2,1,0:T(8,128)(2,1)S(1)}, bf16[2,256,256]{2,1,0:T(8,128)(2,1)S(1)}, u32[]{:S(2)}, u32[]{:S(2)}) collective-permute-start(bf16[2,256,256]{2,1,0:T(8,128)(2,1)S(1)} %collective-permute-done.refs_0_), channel_id=1, source_target_pairs={{0,16},{8,72},{16,32},{24,88},{32,48},{40,104},{48,0},{56,120},{64... | collective-permute-start | bytes 786440 | tf_op jit(solution)/shard_map/ppermute | solution.py:253
  19.7 13.3 %collective-permute-start.2 = (bf16[2,256,256]{2,1,0:T(8,128)(2,1)S(1)}, bf16[2,256,256]{2,1,0:T(8,128)(2,1)S(1)}, u32[]{:S(2)}, u32[]{:S(2)}) collective-permute-start(bf16[2,256,256]{2,1,0:T(8,128)(2,1)S(1)} %collective-permute-done.refs_0_), channel_id=1, source_target_pairs={{0,48},{8,200},{16,0},{24,216},{32,16},{40,232},{48,32},{56,248},{... | collective-permute-start | bytes 786440 | tf_op jit(solution)/shard_map/ppermute | solution.py:253
  21.1 11.9 %collective-permute-start.3 = (bf16[2,256,256]{2,1,0:T(8,128)(2,1)S(1)}, bf16[2,256,256]{2,1,0:T(8,128)(2,1)S(1)}, u32[]{:S(2)}, u32[]{:S(2)}) collective-permute-start(bf16[2,256,256]{2,1,0:T(8,128)(2,1)S(1)} %collective-permute-done.refs_0_), channel_id=1, source_target_pairs={{0,32},{8,136},{16,48},{24,152},{32,0},{40,168},{48,16},{56,184},{... | collective-permute-start | bytes 786440 | tf_op jit(solution)/shard_map/ppermute | solution.py:253
  25.9 10.4 %collective-permute-start.8 = (bf16[2,256,256]{2,1,0:T(8,128)(2,1)S(1)}, bf16[2,256,256]{2,1,0:T(8,128)(2,1)S(1)}, u32[]{:S(2)}, u32[]{:S(2)}) collective-permute-start(bf16[2,256,256]{2,1,0:T(8,128)(2,1)S(1)} %collective-permute-done.7.refs_1_), channel_id=1, source_target_pairs={{0,7},{1,0},{2,1},{3,2},{4,3},{5,4},{6,5},{7,6},{8,15},{9,8},{10,9... | collective-permute-start | bytes 786440 | tf_op jit(solution)/shard_map/ppermute | solution.py:265
  33.0 6.4 %collective-permute-start.6 = (bf16[2,256,256]{2,1,0:T(8,128)(2,1)S(1)}, bf16[2,256,256]{2,1,0:T(8,128)(2,1)S(1)}, u32[]{:S(2)}, u32[]{:S(2)}) collective-permute-start(bf16[2,256,256]{2,1,0:T(8,128)(2,1)S(1)} %collective-permute-done.5.refs_6_), channel_id=1, source_target_pairs={{0,1},{1,2},{2,3},{3,4},{4,5},{5,6},{6,7},{7,0},{8,9},{9,10},{10,1... | collective-permute-start | bytes 786440 | tf_op jit(solution)/shard_map/ppermute | solution.py:262
  39.4 7.0 %collective-permute-start.13 = (bf16[2,256,256]{2,1,0:T(8,128)(2,1)S(1)}, bf16[2,256,256]{2,1,0:T(8,128)(2,1)S(1)}, u32[]{:S(2)}, u32[]{:S(2)}) collective-permute-start(bf16[2,256,256]{2,1,0:T(8,128)(2,1)S(1)} %collective-permute-done.8.refs_2_), channel_id=1, source_target_pairs={{0,7},{1,0},{2,1},{3,2},{4,3},{5,4},{6,5},{7,6},{8,15},{9,8},{10,9... | collective-permute-start | bytes 786440 | tf_op jit(solution)/shard_map/ppermute | solution.py:265
  39.8 14.6 %collective-permute-start.9 = (bf16[2,2,256,256]{3,2,1,0:T(8,128)(2,1)S(1)}, bf16[2,2,256,256]{3,2,1,0:T(8,128)(2,1)S(1)}, u32[]{:S(2)}, u32[]{:S(2)}) collective-permute-start(bf16[2,2,256,256]{3,2,1,0:T(8,128)(2,1)S(1)} %shard_map.56.refs_0_), channel_id=1, source_target_pairs={{0,64},{8,24},{16,80},{24,40},{32,96},{40,56},{48,112},{56,8},{64,... | collective-permute-start | bytes 1572872 | tf_op jit(solution)/shard_map/ppermute | solution.py:256
  43.6 10.8 %collective-permute-start.10 = (bf16[2,2,256,256]{3,2,1,0:T(8,128)(2,1)S(1)}, bf16[2,2,256,256]{3,2,1,0:T(8,128)(2,1)S(1)}, u32[]{:S(2)}, u32[]{:S(2)}) collective-permute-start(bf16[2,2,256,256]{3,2,1,0:T(8,128)(2,1)S(1)} %shard_map.56.refs_0_), channel_id=1, source_target_pairs={{0,192},{8,56},{16,208},{24,8},{32,224},{40,24},{48,240},{56,40},{... | collective-permute-start | bytes 1572872 | tf_op jit(solution)/shard_map/ppermute | solution.py:256
  43.7 19.2 %copy-start = (bf16[2,256,256]{2,1,0:T(8,128)(2,1)S(1)}, bf16[2,256,256]{2,1,0:T(8,128)(2,1)}, u32[]{:S(2)}) copy-start(bf16[2,256,256]{2,1,0:T(8,128)(2,1)} %get-tuple-element.34.refs_7_.refs_4_) | copy-start | bytes 786436
  43.7 11.7 %collective-permute-start.11 = (bf16[2,2,256,256]{3,2,1,0:T(8,128)(2,1)S(1)}, bf16[2,2,256,256]{3,2,1,0:T(8,128)(2,1)S(1)}, u32[]{:S(2)}, u32[]{:S(2)}) collective-permute-start(bf16[2,2,256,256]{3,2,1,0:T(8,128)(2,1)S(1)} %shard_map.57.refs_3_), channel_id=1, source_target_pairs={{0,64},{8,24},{16,80},{24,40},{32,96},{40,56},{48,112},{56,8},{64,... | collective-permute-start | bytes 1572872 | tf_op jit(solution)/shard_map/ppermute | solution.py:256
  45.2 12.3 %collective-permute-start.12 = (bf16[2,2,256,256]{3,2,1,0:T(8,128)(2,1)S(1)}, bf16[2,2,256,256]{3,2,1,0:T(8,128)(2,1)S(1)}, u32[]{:S(2)}, u32[]{:S(2)}) collective-permute-start(bf16[2,2,256,256]{3,2,1,0:T(8,128)(2,1)S(1)} %shard_map.57.refs_3_), channel_id=1, source_target_pairs={{0,192},{8,56},{16,208},{24,8},{32,224},{40,24},{48,240},{56,40},{... | collective-permute-start | bytes 1572872 | tf_op jit(solution)/shard_map/ppermute | solution.py:256
  46.4 6.7 %collective-permute-start.14 = (bf16[2,256,256]{2,1,0:T(8,128)(2,1)S(1)}, bf16[2,256,256]{2,1,0:T(8,128)(2,1)S(1)}, u32[]{:S(2)}, u32[]{:S(2)}) collective-permute-start(bf16[2,256,256]{2,1,0:T(8,128)(2,1)S(1)} %collective-permute-done.6.refs_5_), channel_id=1, source_target_pairs={{0,1},{1,2},{2,3},{3,4},{4,5},{5,6},{6,7},{7,0},{8,9},{9,10},{10,1... | collective-permute-start | bytes 786440 | tf_op jit(solution)/shard_map/ppermute | solution.py:262
  53.2 1.0 copy-start.2
  57.5 9.1 %collective-permute-start.15 = (bf16[9,2,256,256]{3,2,1,0:T(8,128)(2,1)S(1)}, bf16[9,2,256,256]{3,2,1,0:T(8,128)(2,1)S(1)}, u32[]{:S(2)}, u32[]{:S(2)}) collective-permute-start(bf16[9,2,256,256]{3,2,1,0:T(8,128)(2,1)S(1)} %shard_map.58.refs_6_.refs_2_), channel_id=1, source_target_pairs={{0,8},{8,0},{16,24},{24,16},{32,40},{40,32},{48,56},{56,48},{64,72... | collective-permute-start | bytes 7077896 | tf_op jit(solution)/shard_map/ppermute | solution.py:259
  60.2 10.1 %collective-permute-start.16 = (bf16[2,2,256,256]{3,2,1,0:T(8,128)(2,1)S(1)}, bf16[2,2,256,256]{3,2,1,0:T(8,128)(2,1)S(1)}, u32[]{:S(2)}, u32[]{:S(2)}) collective-permute-start(bf16[2,2,256,256]{3,2,1,0:T(8,128)(2,1)S(1)} %collective-permute-done.9.refs_1_), channel_id=1, source_target_pairs={{0,64},{8,24},{16,80},{24,40},{32,96},{40,56},{48,112},{56,8},{64,... | collective-permute-start | bytes 1572872 | tf_op jit(solution)/shard_map/ppermute | solution.py:256
  61.1 9.3 %collective-permute-start.17 = (bf16[2,2,256,256]{3,2,1,0:T(8,128)(2,1)S(1)}, bf16[2,2,256,256]{3,2,1,0:T(8,128)(2,1)S(1)}, u32[]{:S(2)}, u32[]{:S(2)}) collective-permute-start(bf16[2,2,256,256]{3,2,1,0:T(8,128)(2,1)S(1)} %collective-permute-done.12.refs_5_), channel_id=1, source_target_pairs={{0,192},{8,56},{16,208},{24,8},{32,224},{40,24},{48,240},{56,40},{... | collective-permute-start | bytes 1572872 | tf_op jit(solution)/shard_map/ppermute | solution.py:256
  66.6 3.8 %copy-start.3 = (s32[32]{0:T(128)S(1)}, s32[32]{0:T(128)}, u32[]{:S(2)}) copy-start(s32[32]{0:T(128)} %left_sizes.3) | copy-start | bytes 388
  66.6 3.8 %copy-start.4 = (s32[32]{0:T(128)S(1)}, s32[32]{0:T(128)}, u32[]{:S(2)}) copy-start(s32[32]{0:T(128)} %right_sizes.3) | copy-start | bytes 388

commit v20 on v16

--- a/solution.py
+++ b/solution.py
@@ -286,8 +286,9 @@
     up3, down3 = up(up2), down(down2)
     up4 = up(up3)
     lefts = stack(left_env, down1, down2, down3, up4, up3, up2, up1, give)
-    a_below, a_above, b_below, b_above, lefts = together(a_below, a_above, b_below, b_above, lefts)
-    a_two, b_two = far_step(a_below, 1), far_step(b_above, -1)
+    a_two = far_step(a_below, 1)
+    a_above, b_below, b_above, a_two, lefts = together(a_above, b_below, b_above, a_two, lefts)
+    b_two = far_step(b_above, -1)
     others = swap(lefts)
 
     early = ((0, 0), (SIDE - 1, 0), (1, 0), (0, 2), (SIDE - 1, 2), (1, 2))

time: 114 us -> 114 us (level)
  waiting for transfers between devices: 16 us -> 22 us
  starting transfers between devices: 43.8 us -> 40.4 us
  blocking collectives: 37.2 us -> 35 us
    ppermute x4, waiting for transfers between devices: 15.7 us -> 19.8 us  [up(): lax.ppermute(block, 'mpo', [(z, (z + 1) % ranks) for z in range(ranks)])]
    ppermute x4, starting transfers between devices: 4.38 us -> 1.68 us  [up(): lax.ppermute(block, 'mpo', [(z, (z + 1) % ranks) for z in range(ranks)])]
    ppermute x3, waiting for transfers between devices: 0.01 us -> 1.7 us  [down(): lax.ppermute(block, 'mpo', [(z, (z - 1) % ranks) for z in range(ranks)])]
    all_to_all x1, blocking collectives: 22.4 us -> 21 us  [local(): by_plane = lax.all_to_all(done, 'mpo', 0, 0)]
  transfers between devices with their start and end apart: 18 -> 18, of which waited for: 5 -> 6; matrix products, arithmetic and copies ran while one was open for 0% -> 0% of each run, Pallas kernels for 9% -> 9%
where the time goes in v20:
time: 114 us; the launch traced here: 113 us
  starting transfers between devices  40.4 us (35%)
  blocking collectives  35 us (31%)
  waiting for transfers between devices  22 us (19%)
  Pallas kernels  13.9 us (12%)
    all_to_all x1, blocking collectives, local(): by_plane = lax.all_to_all(done, 'mpo', 0, 0)  21 us
    ppermute x4, waiting for transfers between devices, up(): lax.ppermute(block, 'mpo', [(z, (z + 1) % ranks) for z in range(ranks)])  19.8 us
    all_to_all x1, blocking collectives, local(): out = order(lax.all_to_all(by_plane, 'blk', 0, 0, axis_index_groups=groups))  14 us
    ppermute x1, starting transfers between devices, local(): own = lax.ppermute(right_env, ('blk', 'mpo'), turn)  9.77 us
    ppermute x3, starting transfers between devices, down(): lax.ppermute(block, 'mpo', [(z, (z - 1) % ranks) for z in range(ranks)])  9.37 us
    ppermute x6, starting transfers between devices, far_step(): return lax.ppermute(block, 'blk', step(True, by))  8 us
    ppermute x1, starting transfers between devices, swap(): return lax.ppermute(block, 'blk', [(i, i ^ 1) for i in range(sectors)])  7.42 us
    pallas_call x2, Pallas kernels, half(): pl.pallas_call(functools.partial(half_kernel, pieces), out_shape=jax.Shap...  7.38 us
  transfers between devices with their start and end apart: 18, of which 6 were waited for; matrix products, arithmetic and copies ran while one was open for 0% of the time, Pallas kernels for 9%

profile of v20, /device:TPU:1, one launch (start us, length us, event | category | flops | bytes accessed | tf_op | source)
XLA Modules:
  0.0 112.6 jit_solution(7322836173610281910)
XLA Ops:
  0.0 0.0 copy-start.1
  0.0 9.8 %collective-permute-start = (bf16[2,256,256]{2,1,0:T(8,128)(2,1)}, bf16[2,256,256]{2,1,0:T(8,128)(2,1)S(1)}, u32[]{:S(2)}, u32[]{:S(2)}) collective-permute-start(bf16[2,256,256]{2,1,0:T(8,128)(2,1)} %param.7), channel_id=1, source_target_pairs={{0,0},{1,16},{2,32},{3,48},{4,64},{5,80},{6,96},{7,112},{8,12},{9,... | collective-permute-start | bytes 786440 | tf_op jit(solution)/shard_map/ppermute | solution.py:275
  9.8 1.3 %collective-permute-start.4 = (bf16[2,256,256]{2,1,0:T(8,128)(2,1)}, bf16[2,256,256]{2,1,0:T(8,128)(2,1)S(1)}, u32[]{:S(2)}, u32[]{:S(2)}) collective-permute-start(bf16[2,256,256]{2,1,0:T(8,128)(2,1)} %refs_0_.1), channel_id=1, source_target_pairs={{0,1},{1,2},{2,3},{3,4},{4,5},{5,6},{6,7},{7,0},{8,9},{9,10},{10,1... | collective-permute-start | bytes 786440 | tf_op jit(solution)/shard_map/ppermute | solution.py:262
  11.1 2.4 %collective-permute-start.6 = (bf16[2,256,256]{2,1,0:T(8,128)(2,1)}, bf16[2,256,256]{2,1,0:T(8,128)(2,1)S(1)}, u32[]{:S(2)}, u32[]{:S(2)}) collective-permute-start(bf16[2,256,256]{2,1,0:T(8,128)(2,1)} %refs_0_.1), channel_id=1, source_target_pairs={{0,7},{1,0},{2,1},{3,2},{4,3},{5,4},{6,5},{7,6},{8,15},{9,8},{10,9... | collective-permute-start | bytes 786440 | tf_op jit(solution)/shard_map/ppermute | solution.py:265
  13.4 2.6 %shard_map.55 = (bf16[2,256,256]{2,1,0:T(8,128)(2,1)}, bf16[2,256,256]{2,1,0:T(8,128)(2,1)}) custom-call(s32[32]{0:T(128)} %left_sizes.3, s32[32]{0:T(128)} %right_sizes.3, bf16[256,8192]{1,0:T(8,128)(2,1)} %psi_ref.1), custom_call_target="tpu_custom_call" | custom-call | tf_op jit(solution)/shard_map/pallas_call | solution.py:76
  16.1 0.0 collective-permute-done.refs_0_
  16.1 0.1 collective-permute-start.1
  16.2 2.7 %collective-permute-start.2 = (bf16[2,256,256]{2,1,0:T(8,128)(2,1)S(1)}, bf16[2,256,256]{2,1,0:T(8,128)(2,1)S(1)}, u32[]{:S(2)}, u32[]{:S(2)}) collective-permute-start(bf16[2,256,256]{2,1,0:T(8,128)(2,1)S(1)} %collective-permute-done.refs_0_), channel_id=1, source_target_pairs={{0,48},{8,200},{16,0},{24,216},{32,16},{40,232},{48,32},{56,248},{... | collective-permute-start | bytes 786440 | tf_op jit(solution)/shard_map/ppermute | solution.py:253
  18.8 1.4 %collective-permute-start.3 = (bf16[2,256,256]{2,1,0:T(8,128)(2,1)S(1)}, bf16[2,256,256]{2,1,0:T(8,128)(2,1)S(1)}, u32[]{:S(2)}, u32[]{:S(2)}) collective-permute-start(bf16[2,256,256]{2,1,0:T(8,128)(2,1)S(1)} %collective-permute-done.refs_0_), channel_id=1, source_target_pairs={{0,32},{8,136},{16,48},{24,152},{32,0},{40,168},{48,16},{56,184},{... | collective-permute-start | bytes 786440 | tf_op jit(solution)/shard_map/ppermute | solution.py:253
  20.2 5.8 %collective-permute-done.4.refs_7_ = bf16[2,256,256]{2,1,0:T(8,128)(2,1)S(1)} collective-permute-done((bf16[2,256,256]{2,1,0:T(8,128)(2,1)}, bf16[2,256,256]{2,1,0:T(8,128)(2,1)S(1)}, u32[]{:S(2)}, u32[]{:S(2)}) %collective-permute-start.4) | collective-permute-done | bytes 262176 | tf_op jit(solution)/shard_map/ppermute | solution.py:262
  26.1 0.0 collective-permute-start.5
  26.1 0.0 collective-permute-done.6.refs_1_
  26.1 4.6 %collective-permute-start.7 = (bf16[2,256,256]{2,1,0:T(8,128)(2,1)S(1)}, bf16[2,256,256]{2,1,0:T(8,128)(2,1)S(1)}, u32[]{:S(2)}, u32[]{:S(2)}) collective-permute-start(bf16[2,256,256]{2,1,0:T(8,128)(2,1)S(1)} %collective-permute-done.6.refs_1_), channel_id=1, source_target_pairs={{0,7},{1,0},{2,1},{3,2},{4,3},{5,4},{6,5},{7,6},{8,15},{9,8},{10,9... | collective-permute-start | bytes 786440 | tf_op jit(solution)/shard_map/ppermute | solution.py:265
  30.6 0.0 collective-permute-done.1.refs_1_
  30.6 0.0 collective-permute-done.2.refs_0_
  30.6 0.0 collective-permute-done.3.refs_1_
  30.6 3.7 %collective-permute-done.5.refs_6_ = bf16[2,256,256]{2,1,0:T(8,128)(2,1)S(1)} collective-permute-done((bf16[2,256,256]{2,1,0:T(8,128)(2,1)S(1)}, bf16[2,256,256]{2,1,0:T(8,128)(2,1)S(1)}, u32[]{:S(2)}, u32[]{:S(2)}) %collective-permute-start.5) | collective-permute-done | bytes 262176 | tf_op jit(solution)/shard_map/ppermute | solution.py:262
  34.3 0.0 collective-permute-done.7.refs_2_
  34.3 0.1 shard_map.56.refs_0_
  34.4 2.2 %collective-permute-start.8 = (bf16[2,2,256,256]{3,2,1,0:T(8,128)(2,1)S(1)}, bf16[2,2,256,256]{3,2,1,0:T(8,128)(2,1)S(1)}, u32[]{:S(2)}, u32[]{:S(2)}) collective-permute-start(bf16[2,2,256,256]{3,2,1,0:T(8,128)(2,1)S(1)} %shard_map.56.refs_0_), channel_id=1, source_target_pairs={{0,64},{8,24},{16,80},{24,40},{32,96},{40,56},{48,112},{56,8},{64,... | collective-permute-start | bytes 1572872 | tf_op jit(solution)/shard_map/ppermute | solution.py:256
  36.6 2.4 %collective-permute-start.13 = (bf16[2,256,256]{2,1,0:T(8,128)(2,1)S(1)}, bf16[2,256,256]{2,1,0:T(8,128)(2,1)S(1)}, u32[]{:S(2)}, u32[]{:S(2)}) collective-permute-start(bf16[2,256,256]{2,1,0:T(8,128)(2,1)S(1)} %collective-permute-done.7.refs_2_), channel_id=1, source_target_pairs={{0,7},{1,0},{2,1},{3,2},{4,3},{5,4},{6,5},{7,6},{8,15},{9,8},{10,9... | collective-permute-start | bytes 786440 | tf_op jit(solution)/shard_map/ppermute | solution.py:265
  39.0 1.1 %collective-permute-start.9 = (bf16[2,2,256,256]{3,2,1,0:T(8,128)(2,1)S(1)}, bf16[2,2,256,256]{3,2,1,0:T(8,128)(2,1)S(1)}, u32[]{:S(2)}, u32[]{:S(2)}) collective-permute-start(bf16[2,2,256,256]{3,2,1,0:T(8,128)(2,1)S(1)} %shard_map.56.refs_0_), channel_id=1, source_target_pairs={{0,192},{8,56},{16,208},{24,8},{32,224},{40,24},{48,240},{56,40},{... | collective-permute-start | bytes 1572872 | tf_op jit(solution)/shard_map/ppermute | solution.py:256
  40.2 0.0 collective-permute-start.14
  40.2 0.1 shard_map.57.refs_3_
  40.2 0.0 copy-start
  40.3 0.4 collective-permute-start.10
  40.7 1.7 %collective-permute-done.13.refs_3_ = bf16[2,256,256]{2,1,0:T(8,128)(2,1)S(1)} collective-permute-done((bf16[2,256,256]{2,1,0:T(8,128)(2,1)S(1)}, bf16[2,256,256]{2,1,0:T(8,128)(2,1)S(1)}, u32[]{:S(2)}, u32[]{:S(2)}) %collective-permute-start.13) | collective-permute-done | bytes 262176 | tf_op jit(solution)/shard_map/ppermute | solution.py:265
  42.3 1.1 %collective-permute-start.11 = (bf16[2,2,256,256]{3,2,1,0:T(8,128)(2,1)S(1)}, bf16[2,2,256,256]{3,2,1,0:T(8,128)(2,1)S(1)}, u32[]{:S(2)}, u32[]{:S(2)}) collective-permute-start(bf16[2,2,256,256]{3,2,1,0:T(8,128)(2,1)S(1)} %shard_map.57.refs_3_), channel_id=1, source_target_pairs={{0,192},{8,56},{16,208},{24,8},{32,224},{40,24},{48,240},{56,40},{... | collective-permute-start | bytes 1572872 | tf_op jit(solution)/shard_map/ppermute | solution.py:256
  43.5 0.5 collective-permute-done.8.refs_1_
  44.0 0.9 collective-permute-start.12
  44.9 2.0 %collective-permute-done.14.refs_5_ = bf16[2,256,256]{2,1,0:T(8,128)(2,1)S(1)} collective-permute-done((bf16[2,256,256]{2,1,0:T(8,128)(2,1)S(1)}, bf16[2,256,256]{2,1,0:T(8,128)(2,1)S(1)}, u32[]{:S(2)}, u32[]{:S(2)}) %collective-permute-start.14) | collective-permute-done | bytes 262176 | tf_op jit(solution)/shard_map/ppermute | solution.py:262
  46.9 0.4 collective-permute-start.15
  47.3 8.3 %collective-permute-done.15.refs_4_ = bf16[2,256,256]{2,1,0:T(8,128)(2,1)S(1)} collective-permute-done((bf16[2,256,256]{2,1,0:T(8,128)(2,1)S(1)}, bf16[2,256,256]{2,1,0:T(8,128)(2,1)S(1)}, u32[]{:S(2)}, u32[]{:S(2)}) %collective-permute-start.15) | collective-permute-done | bytes 262176 | tf_op jit(solution)/shard_map/ppermute | solution.py:262
  55.6 0.0 copy-done.1
  55.6 0.0 copy-start.2
  55.6 0.9 copy-done.2
  56.5 0.3 shard_map.58.refs_6_.refs_2_
  56.8 0.0 collective-permute-done.9.refs_2_
  56.8 0.0 collective-permute-done.10.refs_4_
  56.8 0.0 collective-permute-done.11.refs_5_
  56.8 0.0 collective-permute-done.12.refs_0_
  56.9 7.4 %collective-permute-start.16 = (bf16[9,2,256,256]{3,2,1,0:T(8,128)(2,1)S(1)}, bf16[9,2,256,256]{3,2,1,0:T(8,128)(2,1)S(1)}, u32[]{:S(2)}, u32[]{:S(2)}) collective-permute-start(bf16[9,2,256,256]{3,2,1,0:T(8,128)(2,1)S(1)} %shard_map.58.refs_6_.refs_2_), channel_id=1, source_target_pairs={{0,8},{8,0},{16,24},{24,16},{32,40},{40,32},{48,56},{56,48},{64,72... | collective-permute-start | bytes 7077896 | tf_op jit(solution)/shard_map/ppermute | solution.py:259
  64.3 2.1 %collective-permute-start.17 = (bf16[2,2,256,256]{3,2,1,0:T(8,128)(2,1)S(1)}, bf16[2,2,256,256]{3,2,1,0:T(8,128)(2,1)S(1)}, u32[]{:S(2)}, u32[]{:S(2)}) collective-permute-start(bf16[2,2,256,256]{3,2,1,0:T(8,128)(2,1)S(1)} %collective-permute-done.11.refs_5_), channel_id=1, source_target_pairs={{0,192},{8,56},{16,208},{24,8},{32,224},{40,24},{48,240},{56,40},{... | collective-permute-start | bytes 1572872 | tf_op jit(solution)/shard_map/ppermute | solution.py:256
  66.4 0.0 copy-done
  66.4 3.7 %shard_map.59.mine = f32[2,256,256]{2,1,0:T(8,128)S(1)} custom-call(bf16[2,2,256,256]{3,2,1,0:T(8,128)(2,1)S(1)} %shard_map.56.refs_0_, bf16[2,2,256,256]{3,2,1,0:T(8,128)(2,1)S(1)} %collective-permute-done.8.refs_1_, bf16[2,2,256,256]{3,2,1,0:T(8,128)(2,1)S(1)} %collective-permute-done.9.refs_2_, bf16[2,2,256,256]{3,2,1,0:T(8,128)(2,1)S(1)} %shard_map.57.refs_3_, ...), custom_call_target="tpu_custom_call" | custom-call | tf_op jit(solution)/shard_map/pallas_call | solution.py:126
  70.1 0.0 copy-start.3
  70.1 0.0 copy-start.4
  70.1 0.0 collective-permute-done.16.refs_6_.refs_3_
  70.2 3.7 %shard_map.60.theirs = f32[2,256,256]{2,1,0:T(8,128)S(1)} custom-call(bf16[2,2,256,256]{3,2,1,0:T(8,128)(2,1)S(1)} %shard_map.56.refs_0_, bf16[2,2,256,256]{3,2,1,0:T(8,128)(2,1)S(1)} %collective-permute-done.8.refs_1_, bf16[2,2,256,256]{3,2,1,0:T(8,128)(2,1)S(1)} %collective-permute-done.9.refs_2_, bf16[2,2,256,256]{3,2,1,0:T(8,128)(2,1)S(1)} %shard_map.57.refs_3_, ...), custom_call_target="tpu_custom_call" | custom-call | tf_op jit(solution)/shard_map/pallas_call | solution.py:126
  73.9 0.0 collective-permute-done.17.refs_1_
  73.9 0.0 copy-done.3
  73.9 0.0 copy-done.4
  73.9 2.6 %shard_map.61 = bf16[8,2,2,32,256]{4,3,2,1,0:T(8,128)(2,1)S(1)} custom-call(s32[32]{0:T(128)S(1)} %copy-done.3, s32[32]{0:T(128)S(1)} %copy-done.4, f32[2,256,256]{2,1,0:T(8,128)S(1)} %shard_map.59.mine, f32[2,256,256]{2,1,0:T(8,128)S(1)} %shard_map.60.theirs, bf16[2,2,256,256]{3,2,1,0:T(8,128)(2,1)S(1)} %collective-permute-done.12.refs_0_, ...), custom_call_target="tpu_custom_call" | custom-call | tf_op jit(solution)/shard_map/pallas_call | solution.py:195
  76.5 21.0 %all_to_all.10 = bf16[8,2,2,32,256]{4,3,2,1,0:T(8,128)(2,1)S(1)} all-to-all(bf16[8,2,2,32,256]{4,3,2,1,0:T(8,128)(2,1)S(1)} %shard_map.61), channel_id=1, replica_groups=mesh['blk'=32,'mpo'=8] {'mpo'}, dimensions={0} | all-to-all | bytes 1048576 | tf_op jit(solution)/shard_map/all_to_all | solution.py:301
  97.5 14.0 %all_to_all.11.in_ref = bf16[16,2,32,256]{3,2,1,0:T(8,128)(2,1)S(1)} all-to-all(bf16[16,2,32,256]{3,2,1,0:T(8,128)(2,1)S(1)} %bitcast.2), channel_id=1, replica_groups={{0,128,16,144,32,160,48,176,64,192,80,208,96,224,112,240},{72,200,88,21..., dimensions={0} | all-to-all | bytes 1048576 | tf_op jit(solution)/shard_map/all_to_all | solution.py:308
  111.5 0.9 shard_map.62
Async XLA Ops:
  0.0 55.6 %copy-start.1 = (bf16[2,256,256]{2,1,0:T(8,128)(2,1)S(1)}, bf16[2,256,256]{2,1,0:T(8,128)(2,1)}, u32[]{:S(2)}) copy-start(bf16[2,256,256]{2,1,0:T(8,128)(2,1)} %refs_0_.1) | copy-start | bytes 786436
  0.0 16.1 %collective-permute-start = (bf16[2,256,256]{2,1,0:T(8,128)(2,1)}, bf16[2,256,256]{2,1,0:T(8,128)(2,1)S(1)}, u32[]{:S(2)}, u32[]{:S(2)}) collective-permute-start(bf16[2,256,256]{2,1,0:T(8,128)(2,1)} %param.7), channel_id=1, source_target_pairs={{0,0},{1,16},{2,32},{3,48},{4,64},{5,80},{6,96},{7,112},{8,12},{9,... | collective-permute-start | bytes 786440 | tf_op jit(solution)/shard_map/ppermute | solution.py:275
  9.8 16.3 %collective-permute-start.4 = (bf16[2,256,256]{2,1,0:T(8,128)(2,1)}, bf16[2,256,256]{2,1,0:T(8,128)(2,1)S(1)}, u32[]{:S(2)}, u32[]{:S(2)}) collective-permute-start(bf16[2,256,256]{2,1,0:T(8,128)(2,1)} %refs_0_.1), channel_id=1, source_target_pairs={{0,1},{1,2},{2,3},{3,4},{4,5},{5,6},{6,7},{7,0},{8,9},{9,10},{10,1... | collective-permute-start | bytes 786440 | tf_op jit(solution)/shard_map/ppermute | solution.py:262
  11.1 15.0 %collective-permute-start.6 = (bf16[2,256,256]{2,1,0:T(8,128)(2,1)}, bf16[2,256,256]{2,1,0:T(8,128)(2,1)S(1)}, u32[]{:S(2)}, u32[]{:S(2)}) collective-permute-start(bf16[2,256,256]{2,1,0:T(8,128)(2,1)} %refs_0_.1), channel_id=1, source_target_pairs={{0,7},{1,0},{2,1},{3,2},{4,3},{5,4},{6,5},{7,6},{8,15},{9,8},{10,9... | collective-permute-start | bytes 786440 | tf_op jit(solution)/shard_map/ppermute | solution.py:265
  16.1 14.6 %collective-permute-start.1 = (bf16[2,256,256]{2,1,0:T(8,128)(2,1)S(1)}, bf16[2,256,256]{2,1,0:T(8,128)(2,1)S(1)}, u32[]{:S(2)}, u32[]{:S(2)}) collective-permute-start(bf16[2,256,256]{2,1,0:T(8,128)(2,1)S(1)} %collective-permute-done.refs_0_), channel_id=1, source_target_pairs={{0,16},{8,72},{16,32},{24,88},{32,48},{40,104},{48,0},{56,120},{64... | collective-permute-start | bytes 786440 | tf_op jit(solution)/shard_map/ppermute | solution.py:253
  16.2 14.5 %collective-permute-start.2 = (bf16[2,256,256]{2,1,0:T(8,128)(2,1)S(1)}, bf16[2,256,256]{2,1,0:T(8,128)(2,1)S(1)}, u32[]{:S(2)}, u32[]{:S(2)}) collective-permute-start(bf16[2,256,256]{2,1,0:T(8,128)(2,1)S(1)} %collective-permute-done.refs_0_), channel_id=1, source_target_pairs={{0,48},{8,200},{16,0},{24,216},{32,16},{40,232},{48,32},{56,248},{... | collective-permute-start | bytes 786440 | tf_op jit(solution)/shard_map/ppermute | solution.py:253
  18.8 11.8 %collective-permute-start.3 = (bf16[2,256,256]{2,1,0:T(8,128)(2,1)S(1)}, bf16[2,256,256]{2,1,0:T(8,128)(2,1)S(1)}, u32[]{:S(2)}, u32[]{:S(2)}) collective-permute-start(bf16[2,256,256]{2,1,0:T(8,128)(2,1)S(1)} %collective-permute-done.refs_0_), channel_id=1, source_target_pairs={{0,32},{8,136},{16,48},{24,152},{32,0},{40,168},{48,16},{56,184},{... | collective-permute-start | bytes 786440 | tf_op jit(solution)/shard_map/ppermute | solution.py:253
  26.1 8.2 %collective-permute-start.5 = (bf16[2,256,256]{2,1,0:T(8,128)(2,1)S(1)}, bf16[2,256,256]{2,1,0:T(8,128)(2,1)S(1)}, u32[]{:S(2)}, u32[]{:S(2)}) collective-permute-start(bf16[2,256,256]{2,1,0:T(8,128)(2,1)S(1)} %collective-permute-done.4.refs_7_), channel_id=1, source_target_pairs={{0,1},{1,2},{2,3},{3,4},{4,5},{5,6},{6,7},{7,0},{8,9},{9,10},{10,1... | collective-permute-start | bytes 786440 | tf_op jit(solution)/shard_map/ppermute | solution.py:262
  26.1 8.2 %collective-permute-start.7 = (bf16[2,256,256]{2,1,0:T(8,128)(2,1)S(1)}, bf16[2,256,256]{2,1,0:T(8,128)(2,1)S(1)}, u32[]{:S(2)}, u32[]{:S(2)}) collective-permute-start(bf16[2,256,256]{2,1,0:T(8,128)(2,1)S(1)} %collective-permute-done.6.refs_1_), channel_id=1, source_target_pairs={{0,7},{1,0},{2,1},{3,2},{4,3},{5,4},{6,5},{7,6},{8,15},{9,8},{10,9... | collective-permute-start | bytes 786440 | tf_op jit(solution)/shard_map/ppermute | solution.py:265
  34.4 9.6 %collective-permute-start.8 = (bf16[2,2,256,256]{3,2,1,0:T(8,128)(2,1)S(1)}, bf16[2,2,256,256]{3,2,1,0:T(8,128)(2,1)S(1)}, u32[]{:S(2)}, u32[]{:S(2)}) collective-permute-start(bf16[2,2,256,256]{3,2,1,0:T(8,128)(2,1)S(1)} %shard_map.56.refs_0_), channel_id=1, source_target_pairs={{0,64},{8,24},{16,80},{24,40},{32,96},{40,56},{48,112},{56,8},{64,... | collective-permute-start | bytes 1572872 | tf_op jit(solution)/shard_map/ppermute | solution.py:256
  36.6 5.8 %collective-permute-start.13 = (bf16[2,256,256]{2,1,0:T(8,128)(2,1)S(1)}, bf16[2,256,256]{2,1,0:T(8,128)(2,1)S(1)}, u32[]{:S(2)}, u32[]{:S(2)}) collective-permute-start(bf16[2,256,256]{2,1,0:T(8,128)(2,1)S(1)} %collective-permute-done.7.refs_2_), channel_id=1, source_target_pairs={{0,7},{1,0},{2,1},{3,2},{4,3},{5,4},{6,5},{7,6},{8,15},{9,8},{10,9... | collective-permute-start | bytes 786440 | tf_op jit(solution)/shard_map/ppermute | solution.py:265
  39.0 17.8 %collective-permute-start.9 = (bf16[2,2,256,256]{3,2,1,0:T(8,128)(2,1)S(1)}, bf16[2,2,256,256]{3,2,1,0:T(8,128)(2,1)S(1)}, u32[]{:S(2)}, u32[]{:S(2)}) collective-permute-start(bf16[2,2,256,256]{3,2,1,0:T(8,128)(2,1)S(1)} %shard_map.56.refs_0_), channel_id=1, source_target_pairs={{0,192},{8,56},{16,208},{24,8},{32,224},{40,24},{48,240},{56,40},{... | collective-permute-start | bytes 1572872 | tf_op jit(solution)/shard_map/ppermute | solution.py:256
  40.2 6.7 %collective-permute-start.14 = (bf16[2,256,256]{2,1,0:T(8,128)(2,1)S(1)}, bf16[2,256,256]{2,1,0:T(8,128)(2,1)S(1)}, u32[]{:S(2)}, u32[]{:S(2)}) collective-permute-start(bf16[2,256,256]{2,1,0:T(8,128)(2,1)S(1)} %collective-permute-done.5.refs_6_), channel_id=1, source_target_pairs={{0,1},{1,2},{2,3},{3,4},{4,5},{5,6},{6,7},{7,0},{8,9},{9,10},{10,1... | collective-permute-start | bytes 786440 | tf_op jit(solution)/shard_map/ppermute | solution.py:262
  40.2 26.2 %copy-start = (bf16[2,256,256]{2,1,0:T(8,128)(2,1)S(1)}, bf16[2,256,256]{2,1,0:T(8,128)(2,1)}, u32[]{:S(2)}) copy-start(bf16[2,256,256]{2,1,0:T(8,128)(2,1)} %get-tuple-element.33.refs_7_.refs_4_) | copy-start | bytes 786436
  40.3 16.6 %collective-permute-start.10 = (bf16[2,2,256,256]{3,2,1,0:T(8,128)(2,1)S(1)}, bf16[2,2,256,256]{3,2,1,0:T(8,128)(2,1)S(1)}, u32[]{:S(2)}, u32[]{:S(2)}) collective-permute-start(bf16[2,2,256,256]{3,2,1,0:T(8,128)(2,1)S(1)} %shard_map.57.refs_3_), channel_id=1, source_target_pairs={{0,64},{8,24},{16,80},{24,40},{32,96},{40,56},{48,112},{56,8},{64,... | collective-permute-start | bytes 1572872 | tf_op jit(solution)/shard_map/ppermute | solution.py:256
  42.3 14.5 %collective-permute-start.11 = (bf16[2,2,256,256]{3,2,1,0:T(8,128)(2,1)S(1)}, bf16[2,2,256,256]{3,2,1,0:T(8,128)(2,1)S(1)}, u32[]{:S(2)}, u32[]{:S(2)}) collective-permute-start(bf16[2,2,256,256]{3,2,1,0:T(8,128)(2,1)S(1)} %shard_map.57.refs_3_), channel_id=1, source_target_pairs={{0,192},{8,56},{16,208},{24,8},{32,224},{40,24},{48,240},{56,40},{... | collective-permute-start | bytes 1572872 | tf_op jit(solution)/shard_map/ppermute | solution.py:256
  44.0 12.9 %collective-permute-start.12 = (bf16[2,2,256,256]{3,2,1,0:T(8,128)(2,1)S(1)}, bf16[2,2,256,256]{3,2,1,0:T(8,128)(2,1)S(1)}, u32[]{:S(2)}, u32[]{:S(2)}) collective-permute-start(bf16[2,2,256,256]{3,2,1,0:T(8,128)(2,1)S(1)} %collective-permute-done.8.refs_1_), channel_id=1, source_target_pairs={{0,64},{8,24},{16,80},{24,40},{32,96},{40,56},{48,112},{56,8},{64,... | collective-permute-start | bytes 1572872 | tf_op jit(solution)/shard_map/ppermute | solution.py:256
  46.9 8.7 %collective-permute-start.15 = (bf16[2,256,256]{2,1,0:T(8,128)(2,1)S(1)}, bf16[2,256,256]{2,1,0:T(8,128)(2,1)S(1)}, u32[]{:S(2)}, u32[]{:S(2)}) collective-permute-start(bf16[2,256,256]{2,1,0:T(8,128)(2,1)S(1)} %collective-permute-done.14.refs_5_), channel_id=1, source_target_pairs={{0,1},{1,2},{2,3},{3,4},{4,5},{5,6},{6,7},{7,0},{8,9},{9,10},{10,1... | collective-permute-start | bytes 786440 | tf_op jit(solution)/shard_map/ppermute | solution.py:262
  55.6 1.0 copy-start.2
  56.9 13.3 %collective-permute-start.16 = (bf16[9,2,256,256]{3,2,1,0:T(8,128)(2,1)S(1)}, bf16[9,2,256,256]{3,2,1,0:T(8,128)(2,1)S(1)}, u32[]{:S(2)}, u32[]{:S(2)}) collective-permute-start(bf16[9,2,256,256]{3,2,1,0:T(8,128)(2,1)S(1)} %shard_map.58.refs_6_.refs_2_), channel_id=1, source_target_pairs={{0,8},{8,0},{16,24},{24,16},{32,40},{40,32},{48,56},{56,48},{64,72... | collective-permute-start | bytes 7077896 | tf_op jit(solution)/shard_map/ppermute | solution.py:259
  64.3 9.6 %collective-permute-start.17 = (bf16[2,2,256,256]{3,2,1,0:T(8,128)(2,1)S(1)}, bf16[2,2,256,256]{3,2,1,0:T(8,128)(2,1)S(1)}, u32[]{:S(2)}, u32[]{:S(2)}) collective-permute-start(bf16[2,2,256,256]{3,2,1,0:T(8,128)(2,1)S(1)} %collective-permute-done.11.refs_5_), channel_id=1, source_target_pairs={{0,192},{8,56},{16,208},{24,8},{32,224},{40,24},{48,240},{56,40},{... | collective-permute-start | bytes 1572872 | tf_op jit(solution)/shard_map/ppermute | solution.py:256
  70.1 3.8 %copy-start.3 = (s32[32]{0:T(128)S(1)}, s32[32]{0:T(128)}, u32[]{:S(2)}) copy-start(s32[32]{0:T(128)} %left_sizes.3) | copy-start | bytes 388
  70.1 3.8 %copy-start.4 = (s32[32]{0:T(128)S(1)}, s32[32]{0:T(128)}, u32[]{:S(2)}) copy-start(s32[32]{0:T(128)} %right_sizes.3) | copy-start | bytes 388
